TPU v7x, 32 devices: a whole 2x2x4 slice. The times are simulated.
32 devices in a mesh: dp: 4 (over x, core), seq: 8 (over z, y).
Axes of the slice: x: 2, y: 2, z: 4, core: 2. Of those that a mesh axis runs over, the one named last changes fastest.
Arguments:
- layer_input: bfloat16 [8192, 2048], P(('dp', 'seq')), may hold values from -6 to 6
- global_keys: bfloat16 [8192, 2048], P(('dp', 'seq')), may hold values from -8 to 8
- global_values: bfloat16 [8192, 2048], P(('dp', 'seq')), may hold values from -6 to 6
- lengths: int32 [4], P('dp'), may hold values from 256 to 2048, as said below
- attn_gain: bfloat16 [2048], P('seq'), may hold values from 0.25 to 1.75
- query_weight: bfloat16 [2048, 2048], P('seq'), may hold values from -0.125 to 0.125
- out_weight: bfloat16 [2048, 2048], P('seq'), may hold values from -2 to 2
- ffn_gain: bfloat16 [2048], P('seq'), may hold values from 0.25 to 1.75
- gate_weight: bfloat16 [5504, 2048], P('seq'), may hold values from -0.125 to 0.125
- up_weight: bfloat16 [5504, 2048], P('seq'), may hold values from -0.125 to 0.125
- down_weight: bfloat16 [5504, 2048], P('seq'), may hold values from -0.078125 to 0.078125
- cotangent: bfloat16 [8192, 2048], P(('dp', 'seq')), may hold values from -6 to 6
Outputs:
- layer_output: bfloat16 [8192, 2048], P(('dp', 'seq'))
- input_grad: bfloat16 [8192, 2048], P(('dp', 'seq'))
- key_grad: bfloat16 [8192, 2048], P(('dp', 'seq'))
- value_grad: bfloat16 [8192, 2048], P(('dp', 'seq'))
- attn_gain_grad: float32 [2048], P('seq')
- query_weight_grad: float32 [2048, 2048], P('seq')
- out_weight_grad: float32 [2048, 2048], P('seq')
- ffn_gain_grad: float32 [2048], P('seq')
- gate_weight_grad: float32 [5504, 2048], P('seq')
- up_weight_grad: float32 [5504, 2048], P('seq')
- down_weight_grad: float32 [5504, 2048], P('seq')
Inputs may be any that keep to these rules, and one draw needn't show every extreme that they name: The first lengths[g] positions of bucket g are live and the rest are padding; in every draw at least one bucket is full.
All inputs are finite; a program needn't handle non-finite values.
Results may differ from a plain program's by a relative error of at most 0.02.
Values may be sent and summed in bfloat16 or wider, within the bound.
No kernel may reach another device: no remote copies, remote signals or barrier semaphores. Data moves between devices by JAX's collectives and lax.ppermute only.
A program may use at most 320 MiB of HBM per device.

v0:
```python
import jax
import jax.numpy as jnp
from jax import lax
from jax.sharding import PartitionSpec as P

HEAD_DIM = 128
ATT_BLOCK = 512


EPSILON = 1e-05


def root_norm(values_in, gain_scale):
    return (
        values_in
        * lax.rsqrt(jnp.mean(values_in * values_in, axis=-1, keepdims=True) + EPSILON)
        * gain_scale
    )


def norm_backward(values_in, gain_scale, upstream):
    result, pullback = jax.vjp(root_norm, values_in, gain_scale)
    return pullback(upstream)


def product(left_side, right_side):
    return jnp.dot(left_side, right_side, preferred_element_type=jnp.float32)


def inner_rows(left_side, right_side):
    return lax.dot_general(
        left_side, right_side, (((0,), (0,)), ((), ())), preferred_element_type=jnp.float32
    )


def outer_cols(left_side, right_side):
    return lax.dot_general(
        left_side, right_side, (((1,), (1,)), ((), ())), preferred_element_type=jnp.float32
    )


def silu_backward(gate_value, up_value, grad_inner):
    sigmoid_gate = jax.nn.sigmoid(gate_value)
    grad_gate = grad_inner * up_value * sigmoid_gate * (1.0 + gate_value * (1.0 - sigmoid_gate))
    grad_up = grad_inner * gate_value * sigmoid_gate
    return (grad_gate.astype(jnp.bfloat16), grad_up.astype(jnp.bfloat16))


def head_view(array_in):
    return array_in.reshape(array_in.shape[0], -1, HEAD_DIM)


def block_scores(query_blk, key_blk, query_first, key_first):
    scores = jnp.einsum(
        "qhd,khd->hqk", query_blk, key_blk, preferred_element_type=jnp.float32
    ) * HEAD_DIM ** (-0.5)
    query_pos = query_first + lax.iota(jnp.int32, ATT_BLOCK)
    key_pos = key_first + lax.iota(jnp.int32, ATT_BLOCK)
    causal = key_pos[None, :] <= query_pos[:, None]
    return (scores, causal[None], query_pos)


def attend_forward(head_query, head_keys, head_values, length):
    query_heads = head_view(head_query)
    key_heads = head_view(head_keys)
    value_heads = head_view(head_values)
    count_blocks = query_heads.shape[0] // ATT_BLOCK
    heads_here = query_heads.shape[1]
    live_blocks = (length + ATT_BLOCK - 1) // ATT_BLOCK

    def one_block(query_index):
        query_first = query_index * ATT_BLOCK
        query_blk = lax.dynamic_slice_in_dim(query_heads, query_first, ATT_BLOCK, 0)
        reach_blocks = jnp.minimum(query_index + 1, live_blocks)

        def stats_step(key_index, loop_state):
            running_max, running_sum = loop_state
            key_first = key_index * ATT_BLOCK
            key_blk = lax.dynamic_slice_in_dim(key_heads, key_first, ATT_BLOCK, 0)
            scores, causal, query_pos = block_scores(query_blk, key_blk, query_first, key_first)
            scores = jnp.where(causal, scores, -jnp.inf)
            new_max = jnp.maximum(running_max, jnp.max(scores, axis=-1))
            new_sum = running_sum * jnp.exp(running_max - new_max) + jnp.sum(
                jnp.exp(scores - new_max[..., None]), axis=-1
            )
            return (new_max, new_sum)

        start_state = (
            jnp.full((heads_here, ATT_BLOCK), -1e30, jnp.float32),
            jnp.zeros((heads_here, ATT_BLOCK), jnp.float32),
        )
        final_max, final_sum = lax.fori_loop(0, reach_blocks, stats_step, start_state)
        log_sum = final_max + jnp.log(final_sum)

        def output_step(key_index, running_total):
            key_first = key_index * ATT_BLOCK
            key_blk = lax.dynamic_slice_in_dim(key_heads, key_first, ATT_BLOCK, 0)
            value_blk = lax.dynamic_slice_in_dim(value_heads, key_first, ATT_BLOCK, 0)
            scores, causal, query_pos = block_scores(query_blk, key_blk, query_first, key_first)
            keep_mask = causal & (query_pos < length)[None, :, None]
            weights_soft = jnp.where(keep_mask, jnp.exp(scores - log_sum[..., None]), 0.0).astype(
                jnp.bfloat16
            )
            return running_total + jnp.einsum(
                "hqk,khd->qhd", weights_soft, value_blk, preferred_element_type=jnp.float32
            )

        start_total = jnp.zeros((ATT_BLOCK, heads_here, HEAD_DIM), jnp.float32)
        blended = lax.fori_loop(0, reach_blocks, output_step, start_total)
        return (blended, log_sum)

    blended, log_sums = lax.map(one_block, jnp.arange(count_blocks, dtype=jnp.int32))
    return (blended.reshape(count_blocks * ATT_BLOCK, heads_here * HEAD_DIM), log_sums)


def attend_backward(head_query, head_keys, head_values, blended, log_sums, grad_heads, length):
    query_heads = head_view(head_query)
    key_heads = head_view(head_keys)
    value_heads = head_view(head_values)
    grad_view = head_view(grad_heads)
    count_blocks = query_heads.shape[0] // ATT_BLOCK
    heads_here = query_heads.shape[1]
    live_blocks = (length + ATT_BLOCK - 1) // ATT_BLOCK
    score_scale = HEAD_DIM ** (-0.5)
    deltas = jnp.sum(grad_view.astype(jnp.float32) * head_view(blended), axis=-1)

    def key_step(grad_queries, key_index):
        key_first = key_index * ATT_BLOCK
        key_blk = lax.dynamic_slice_in_dim(key_heads, key_first, ATT_BLOCK, 0)
        value_blk = lax.dynamic_slice_in_dim(value_heads, key_first, ATT_BLOCK, 0)

        def query_step(query_index, loop_state):
            grad_queries, grad_key, grad_value = loop_state
            query_first = query_index * ATT_BLOCK
            query_blk = lax.dynamic_slice_in_dim(query_heads, query_first, ATT_BLOCK, 0)
            grad_blk = lax.dynamic_slice_in_dim(grad_view, query_first, ATT_BLOCK, 0)
            delta_blk = lax.dynamic_slice_in_dim(deltas, query_first, ATT_BLOCK, 0)
            scores, causal, query_pos = block_scores(query_blk, key_blk, query_first, key_first)
            keep_mask = causal & (query_pos < length)[None, :, None]
            weights_soft = jnp.where(
                keep_mask, jnp.exp(scores - log_sums[query_index][..., None]), 0.0
            )
            grad_value = grad_value + jnp.einsum(
                "hqk,qhd->khd",
                weights_soft.astype(jnp.bfloat16),
                grad_blk,
                preferred_element_type=jnp.float32,
            )
            grad_soft = jnp.einsum(
                "qhd,khd->hqk", grad_blk, value_blk, preferred_element_type=jnp.float32
            )
            grad_scores = (weights_soft * (grad_soft - delta_blk.T[:, :, None])).astype(
                jnp.bfloat16
            )
            grad_key = (
                grad_key
                + jnp.einsum(
                    "hqk,qhd->khd", grad_scores, query_blk, preferred_element_type=jnp.float32
                )
                * score_scale
            )
            update = (
                jnp.einsum("hqk,khd->qhd", grad_scores, key_blk, preferred_element_type=jnp.float32)
                * score_scale
            )
            current = lax.dynamic_slice_in_dim(grad_queries, query_first, ATT_BLOCK, 0)
            grad_queries = lax.dynamic_update_slice_in_dim(
                grad_queries, current + update, query_first, 0
            )
            return (grad_queries, grad_key, grad_value)

        zero_block = jnp.zeros((ATT_BLOCK, heads_here, HEAD_DIM), jnp.float32)
        grad_queries, grad_key, grad_value = lax.fori_loop(
            key_index, live_blocks, query_step, (grad_queries, zero_block, zero_block)
        )
        return (grad_queries, (grad_key, grad_value))

    start_queries = jnp.zeros(query_heads.shape, jnp.float32)
    grad_queries, (grad_keys, grad_values) = lax.scan(
        key_step, start_queries, jnp.arange(count_blocks, dtype=jnp.int32)
    )
    flat_shape = (count_blocks * ATT_BLOCK, heads_here * HEAD_DIM)
    return (
        grad_queries.reshape(flat_shape),
        grad_keys.reshape(flat_shape),
        grad_values.reshape(flat_shape),
    )


def ffn_by_tokens(normed_ffn, cotangent, gate_weight, up_weight, down_weight):
    gathered = lax.all_gather(normed_ffn, "seq", axis=0, tiled=True)
    gate_local = outer_cols(gathered, gate_weight)
    up_local = outer_cols(gathered, up_weight)
    inner_local = (jax.nn.silu(gate_local) * up_local).astype(jnp.bfloat16)
    ffn_out = lax.psum_scatter(
        product(inner_local, down_weight).astype(jnp.bfloat16),
        "seq",
        scatter_dimension=0,
        tiled=True,
    ).astype(jnp.float32)
    grad_rows = lax.all_gather(cotangent, "seq", axis=0, tiled=True)
    grad_inner = outer_cols(grad_rows, down_weight)
    grad_gate, grad_up = silu_backward(gate_local, up_local, grad_inner)
    grad_normed = lax.psum_scatter(
        (product(grad_gate, gate_weight) + product(grad_up, up_weight)).astype(jnp.bfloat16),
        "seq",
        scatter_dimension=0,
        tiled=True,
    ).astype(jnp.float32)
    return (
        ffn_out,
        grad_normed,
        inner_rows(grad_gate, gathered),
        inner_rows(grad_up, gathered),
        inner_rows(inner_local, grad_rows),
    )


def local(
    layer_input,
    global_keys,
    global_values,
    lengths,
    attn_gain,
    query_weight,
    out_weight,
    ffn_gain,
    gate_weight,
    up_weight,
    down_weight,
    cotangent,
):
    length = lengths[0]
    full_query, full_out, gain_attn, gain_ffn = (
        lax.all_gather(query_weight, "seq", axis=0, tiled=True),
        lax.all_gather(out_weight, "seq", axis=0, tiled=True),
        lax.all_gather(attn_gain, "seq", axis=0, tiled=True),
        lax.all_gather(ffn_gain, "seq", axis=0, tiled=True),
    )
    gain_attn = gain_attn.astype(jnp.float32)
    gain_ffn = gain_ffn.astype(jnp.float32)
    input_wide = layer_input.astype(jnp.float32)
    normed = root_norm(input_wide, gain_attn).astype(jnp.bfloat16)
    queries = product(normed, full_query).astype(jnp.bfloat16)
    head_query, head_keys, head_values = (
        lax.all_to_all(queries, "seq", split_axis=1, concat_axis=0, tiled=True),
        lax.all_to_all(global_keys, "seq", split_axis=1, concat_axis=0, tiled=True),
        lax.all_to_all(global_values, "seq", split_axis=1, concat_axis=0, tiled=True),
    )
    blended, log_sums = attend_forward(head_query, head_keys, head_values, length)
    blended_low = blended.astype(jnp.bfloat16)
    mixed_heads = lax.all_to_all(blended_low, "seq", split_axis=0, concat_axis=1, tiled=True)
    hidden = input_wide + product(mixed_heads, full_out)
    normed_ffn = root_norm(hidden, gain_ffn).astype(jnp.bfloat16)
    ffn_out, grad_normed_ffn, gate_part, up_part, down_part = ffn_by_tokens(
        normed_ffn, cotangent, gate_weight, up_weight, down_weight
    )
    layer_output = (hidden + ffn_out).astype(jnp.bfloat16)
    grad_through, grad_gain_ffn = norm_backward(hidden, gain_ffn, grad_normed_ffn)
    grad_hidden = cotangent.astype(jnp.float32) + grad_through
    grad_branch = grad_hidden.astype(jnp.bfloat16)
    grad_mixed = outer_cols(grad_branch, full_out).astype(jnp.bfloat16)
    grad_heads = lax.all_to_all(grad_mixed, "seq", split_axis=1, concat_axis=0, tiled=True)
    grad_query_heads, grad_key_heads, grad_value_heads = attend_backward(
        head_query, head_keys, head_values, blended, log_sums, grad_heads, length
    )
    grad_query_low = grad_query_heads.astype(jnp.bfloat16)
    grad_query, key_grad, value_grad = (
        lax.all_to_all(grad_query_low, "seq", split_axis=0, concat_axis=1, tiled=True),
        lax.all_to_all(
            grad_key_heads.astype(jnp.bfloat16), "seq", split_axis=0, concat_axis=1, tiled=True
        ),
        lax.all_to_all(
            grad_value_heads.astype(jnp.bfloat16), "seq", split_axis=0, concat_axis=1, tiled=True
        ),
    )
    grad_normed = outer_cols(grad_query, full_query)
    grad_input_norm, grad_gain_attn = norm_backward(input_wide, gain_attn, grad_normed)
    input_grad = (grad_hidden + grad_input_norm).astype(jnp.bfloat16)
    query_part, out_part, gain_attn_part, gain_ffn_part = (
        lax.psum_scatter(
            inner_rows(normed, grad_query).astype(jnp.bfloat16),
            "seq",
            scatter_dimension=0,
            tiled=True,
        ).astype(jnp.float32),
        lax.psum_scatter(
            inner_rows(mixed_heads, grad_branch).astype(jnp.bfloat16),
            "seq",
            scatter_dimension=0,
            tiled=True,
        ).astype(jnp.float32),
        lax.psum_scatter(
            grad_gain_attn.astype(jnp.bfloat16), "seq", scatter_dimension=0, tiled=True
        ).astype(jnp.float32),
        lax.psum_scatter(
            grad_gain_ffn.astype(jnp.bfloat16), "seq", scatter_dimension=0, tiled=True
        ).astype(jnp.float32),
    )
    summed = (
        lax.psum(query_part.astype(jnp.bfloat16), "dp").astype(jnp.float32),
        lax.psum(out_part.astype(jnp.bfloat16), "dp").astype(jnp.float32),
        lax.psum(gain_attn_part.astype(jnp.bfloat16), "dp").astype(jnp.float32),
        lax.psum(gain_ffn_part.astype(jnp.bfloat16), "dp").astype(jnp.float32),
        lax.psum(gate_part.astype(jnp.bfloat16), "dp").astype(jnp.float32),
        lax.psum(up_part.astype(jnp.bfloat16), "dp").astype(jnp.float32),
        lax.psum(down_part.astype(jnp.bfloat16), "dp").astype(jnp.float32),
    )
    return (
        layer_output,
        input_grad,
        key_grad,
        value_grad,
        summed[2],
        summed[0],
        summed[1],
        summed[3],
        summed[4],
        summed[5],
        summed[6],
    )


def solution(mesh):
    placed = (
        P(("dp", "seq"), None),
        P(("dp", "seq"), None),
        P(("dp", "seq"), None),
        P("dp"),
        P("seq"),
        P("seq", None),
        P("seq", None),
        P("seq"),
        P("seq", None),
        P("seq", None),
        P("seq", None),
        P(("dp", "seq"), None),
    )
    return jax.shard_map(
        local,
        mesh=mesh,
        in_specs=placed,
        out_specs=(
            P(("dp", "seq"), None),
            P(("dp", "seq"), None),
            P(("dp", "seq"), None),
            P(("dp", "seq"), None),
            P("seq"),
            P("seq", None),
            P("seq", None),
            P("seq"),
            P("seq", None),
            P("seq", None),
            P("seq", None),
        ),
        check_vma=False,
    )
```

profile of v0, /device:TPU:0, one launch (start us, length us, event | category | flops | bytes accessed | tf_op | source)
XLA Modules:
  0.0 1509.8 jit_solution(14060326996942485663)
XLA Ops:
  10.3 7.3 all-to-all-start.1
  19.8 46.7 %all-to-all-done.1 = bf16[256,8,256]{0,2,1:T(8,128)(2,1)} async-done(((bf16[256,8,256]{0,2,1:T(8,128)(2,1)}), bf16[256,8,256]{0,2,1:T(8,128)(2,1)}, u32[]{:S(2)}, u32[]{:S(2)}) %all-to-all-start.1) | async-done | bytes 1048608 | tf_op jit(solution)/shard_map/all_to_all | solution.py:247
  66.6 5.7 all-to-all-start.2
  72.3 35.6 %all-gather = bf16[8,1,256]{2,1,0:T(2,128)(2,1)S(1)} all-gather(bf16[1,1,256]{2,1,0:T(2,128)(2,1)S(1)} %reshape.281), channel_id=1, replica_groups=mesh['dp'=4,'seq'=8] {'seq'}, dimensions={0}, use_global_device_ids=true | all-gather | bytes 4608 | tf_op jit(solution)/shard_map/all_gather | solution.py:237
  110.0 58.8 %all-gather.7.cloned.1.call-done = bf16[2048,2048]{1,0:T(8,128)(2,1)} async-done(((bf16[256,2048]{1,0:T(8,128)(2,1)}), bf16[2048,2048]{1,0:T(8,128)(2,1)}) %all-gather.7.cloned.1.call-update) | async-done | bytes 8388624 | tf_op jit(solution)/shard_map/all_gather | solution.py:235
  168.8 7.1 convolution_convert_fusion.7
  178.1 4.3 all-to-all-start
  196.4 29.3 %all-to-all-done = bf16[256,8,256]{0,2,1:T(8,128)(2,1)} async-done(((bf16[256,8,256]{0,2,1:T(8,128)(2,1)}), bf16[256,8,256]{0,2,1:T(8,128)(2,1)}, u32[]{:S(2)}, u32[]{:S(2)}) %all-to-all-start) | async-done | bytes 1048608 | tf_op jit(solution)/shard_map/all_to_all | solution.py:246
  233.1 65.4 %while.72 = (s32[]{:T(128)}, f32[4,512,2,128]{1,3,2,0:T(8,128)}, f32[4,2,512]{2,1,0:T(2,128)S(1)}, s32[4]{0:T(128)S(1)}, s32[]{:T(128)}, /*index=5*/bf16[2048,2,...) while((s32[]{:T(128)}, f32[4,512,2,128]{1,3,2,0:T(8,128)}, ...), condition=%wide.region_8.9_spmd.clone, body=%wide.region_1.8_spmd.sunk.clone | while | flops 409344000 | bytes 10062657 | solution.py:112
  239.2 3.8 while.71
  247.8 4.6 while.70
  253.3 7.6 while.71
  254.2 2.9 fusion.127
  265.7 4.6 while.70
  271.2 7.6 while.71
  272.1 2.9 fusion.127
  275.9 2.9 fusion.127
  283.5 4.6 while.70
  289.0 7.6 while.71
  293.7 2.9 fusion.127
  301.2 3.7 copy.88
  307.4 4.3 all-to-all-start.3
  311.7 28.5 %all-gather.1 = bf16[8,1,256]{2,1,0:T(2,128)(2,1)S(1)} all-gather(bf16[1,1,256]{2,1,0:T(2,128)(2,1)S(1)} %reshape.283), channel_id=1, replica_groups=mesh['dp'=4,'seq'=8] {'seq'}, dimensions={0}, use_global_device_ids=true | all-gather | bytes 4608 | tf_op jit(solution)/shard_map/all_gather | solution.py:238
  342.5 6.4 multiply_reduce_fusion.1
  352.0 133.5 %all-gather.11.cloned.1.call-done = bf16[2048,2048]{1,0:T(8,128)(2,1)} async-done(((bf16[256,2048]{1,0:T(8,128)(2,1)}), bf16[2048,2048]{1,0:T(8,128)(2,1)}) %all-gather.11.cloned.1.call-update) | async-done | bytes 8388624 | tf_op jit(solution)/shard_map/all_gather | solution.py:191
  485.5 11.0 fusion.55
  496.5 7.8 fusion.54
  504.3 106.3 %all-gather.13.cloned.1.call-done = bf16[2048,2048]{1,0:T(8,128)(2,1)} async-done(((bf16[256,2048]{1,0:T(8,128)(2,1)}), bf16[2048,2048]{1,0:T(8,128)(2,1)}) %all-gather.13.cloned.1.call-update) | async-done | bytes 8388624 | tf_op jit(solution)/shard_map/all_gather | solution.py:201
  610.6 14.4 multiply_convert_fusion.1
  625.0 10.8 fusion.56
  635.9 12.6 add_convert_fusion
  648.5 11.0 convolution_convert_fusion
  659.6 136.2 %reduce-scatter.7.cloned.1.call-done = bf16[256,2048]{1,0:T(8,128)(2,1)} async-done(((bf16[2048,2048]{1,0:T(8,128)(2,1)}), bf16[256,2048]{1,0:T(8,128)(2,1)}) %reduce-scatter.7.cloned.1.call-update) | async-done | bytes 1048592 | tf_op jit(solution)/shard_map/reduce_scatter | solution.py:204
  798.3 149.5 %reduce-scatter.5.cloned.1.call-done = bf16[256,2048]{1,0:T(8,128)(2,1)} async-done(((bf16[2048,2048]{1,0:T(8,128)(2,1)}), bf16[256,2048]{1,0:T(8,128)(2,1)}) %reduce-scatter.5.cloned.1.call-update) | async-done | bytes 1048592 | tf_op jit(solution)/shard_map/reduce_scatter | solution.py:195
  947.8 3.7 fusion.42
  951.5 6.5 convolution_convert_fusion.6
  959.1 4.2 all-to-all-start.4
  965.4 4.3 copy.92
  969.7 6.9 convolution_convert_fusion.1
  976.7 17.9 %all-to-all-done.4 = bf16[256,8,256]{2,0,1:T(8,128)(2,1)} async-done(((bf16[256,8,256]{2,0,1:T(8,128)(2,1)}), bf16[256,8,256]{2,0,1:T(8,128)(2,1)}, u32[]{:S(2)}, u32[]{:S(2)}) %all-to-all-start.4) | async-done | bytes 1048608 | tf_op jit(solution)/shard_map/all_to_all | solution.py:263
  999.0 3.3 reshape.280
  1002.3 4.6 multiply_reduce_fusion
  1008.6 46.9 %while.74 = (s32[]{:T(128)}, f32[2048,2,128]{2,0,1:T(8,128)}, bf16[4,512,2,128]{1,3,2,0:T(8,128)(2,1)}, bf16[4,512,2,128]{1,3,2,0:T(8,128)(2,1)}, s32[4]{0:T(128...) while((s32[]{:T(128)}, f32[2048,2,128]{2,0,1:T(8,128)}, ...), condition=%wide.region_17.18_spmd.clone, body=%wide.region_14.17_spmd.sunk.clone | while | flops 675940352 | bytes 19695292 | solution.py:179
  1012.1 18.5 %while.73 = (s32[]{:T(128)}, f32[2048,2,128]{2,0,1:T(8,128)}, f32[512,2,128]{0,2,1:T(8,128)S(1)}, f32[512,2,128]{0,2,1:T(8,128)S(1)}, s32[]{:T(128)}, /*index=5*...) while((s32[]{:T(128)}, f32[2048,2,128]{2,0,1:T(8,128)}, ...), condition=%wide.region_16.16_spmd, body=%wide.region_15.15_spmd.sunk | while | flops 675940352 | bytes 14976297 | solution.py:173
  1035.0 9.6 while.73
  1058.4 19.8 %all_to_all.128 = bf16[8,256,256]{1,2,0:T(8,128)(2,1)S(1)} all-to-all(bf16[8,256,256]{1,2,0:T(8,128)(2,1)S(1)} %copy.99), channel_id=1, replica_groups=mesh['dp'=4,'seq'=8] {'seq'}, dimensions={0} | all-to-all | bytes 2097152 | tf_op jit(solution)/shard_map/all_to_all | solution.py:269
  1079.1 5.7 convolution_convert_fusion.2
  1085.0 10.9 convolution_convert_fusion.3
  1095.9 10.8 convolution_convert_fusion.4
  1106.7 7.3 convolution_convert_fusion.5
  1113.9 19.8 %reduce-scatter.11.cloned.1.call-done = bf16[256,2048]{1,0:T(8,128)(2,1)} async-done(((bf16[2048,2048]{1,0:T(8,128)(2,1)}), bf16[256,2048]{1,0:T(8,128)(2,1)}) %reduce-scatter.11.cloned.1.call-update) | async-done | bytes 1048592 | tf_op jit(solution)/shard_map/reduce_scatter | solution.py:287
  1133.7 161.8 %reduce-scatter.9.cloned.1.call-done = bf16[256,2048]{1,0:T(8,128)(2,1)} async-done(((bf16[2048,2048]{1,0:T(8,128)(2,1)}), bf16[256,2048]{1,0:T(8,128)(2,1)}) %reduce-scatter.9.cloned.1.call-update) | async-done | bytes 1048592 | tf_op jit(solution)/shard_map/reduce_scatter | solution.py:281
  1301.4 4.3 all-to-all-start.7
  1310.2 21.6 %all-to-all-done.7 = bf16[8,256,256]{2,1,0:T(8,128)(2,1)} async-done(((bf16[8,256,256]{2,1,0:T(8,128)(2,1)}), bf16[8,256,256]{2,1,0:T(8,128)(2,1)}, u32[]{:S(2)}, u32[]{:S(2)}) %all-to-all-start.7) | async-done | bytes 1048608 | tf_op jit(solution)/shard_map/all_to_all | solution.py:273
  1331.8 3.6 all-to-all-start.6
  1341.2 8.0 fusion.39
  1349.3 22.2 %all-reduce.2 = (bf16[2048]{0:T(1024)(128)(2,1)S(1)}, bf16[2048]{0:T(1024)(128)(2,1)S(1)}) all-reduce(bf16[2048]{0:T(1024)(128)(2,1)S(1)} %get-tuple-element.403, bf16[2048]{0:T(1024)(128)(2,1)S(1)} %copy-done.17), channel_id=4, replica_groups=mesh['dp'=4,'seq'=8] {'seq'}, use_global_device_ids=true, to_apply=%region_20.21.clone | all-reduce | flops 4096 | bytes 16384
  1371.6 6.8 all-reduce.3
  1383.2 3.8 fusion.44
  1387.0 100.6 %all-reduce.7.cloned.1.call-done = (bf16[256,2048]{1,0:T(8,128)(2,1)}, bf16[256,2048]{1,0:T(8,128)(2,1)}, bf16[688,2048]{1,0:T(8,128)(2,1)}, bf16[688,2048]{1,0:T(8,128)(2,1)}, bf16[688,2048]{1,0:T(8,128)(2,1)}) async-done(((bf16[256,2048]{1,0:T(8,128)(2,1)}, bf16[256,2048]{1,0:T(8,128)(2,1)}, bf16[688,2048]{1,0:T(8,128)(2,1)}, bf16[688,2048]{1,0:T(8,128)(2,1)}, bf16[688,2048]{1,0:T(8,128)(2,1)}), ...) | async-done | bytes 10551312 | tf_op jit(solution)/shard_map/psum | solution.py:301
  1487.6 2.9 convert_element_type.179
  1493.0 3.2 convert_element_type.185
  1496.3 3.2 convert_element_type.187
  1499.5 3.2 convert_element_type.189
  (310 shorter events, 167.2 us)
Async XLA Ops:
  7.2 603.5 %copy-start = (bf16[688,2048]{1,0:T(8,128)(2,1)S(1)}, bf16[688,2048]{1,0:T(8,128)(2,1)}, u32[]{:S(2)}) copy-start(bf16[688,2048]{1,0:T(8,128)(2,1)} %param.32) | copy-start | bytes 8454148
  7.2 161.6 %all-gather.7.cloned.1.call-start = ((), (), s32[]{:S(2)}) async-start(), calls=%async_computation.12 | async-start | bytes 9437184 | tf_op jit(solution)/shard_map/all_gather | solution.py:235
  10.3 56.3 %all-to-all-start.1 = ((bf16[256,8,256]{0,2,1:T(8,128)(2,1)}), bf16[256,8,256]{0,2,1:T(8,128)(2,1)}, u32[]{:S(2)}, u32[]{:S(2)}) async-start(bf16[256,8,256]{0,2,1:T(8,128)(2,1)} %bitcast.176), calls=%async_computation.1 | async-start | bytes 2097152 | tf_op jit(solution)/shard_map/all_to_all | solution.py:247
  17.6 54.7 %copy-start.26 = (bf16[256]{0:T(256)(128)(2,1)S(1)}, bf16[256]{0:T(256)(128)(2,1)}, u32[]{:S(2)}) copy-start(bf16[256]{0:T(256)(128)(2,1)} %param.26) | copy-start | bytes 1540
  66.6 111.5 %all-to-all-start.2 = ((bf16[256,8,256]{0,2,1:T(8,128)(2,1)}), bf16[256,8,256]{0,2,1:T(8,128)(2,1)}, u32[]{:S(2)}, u32[]{:S(2)}) async-start(bf16[256,8,256]{0,2,1:T(8,128)(2,1)} %bitcast.175), calls=%async_computation.2 | async-start | bytes 2097152 | tf_op jit(solution)/shard_map/all_to_all | solution.py:248
  107.9 68.0 %copy-start.15 = (f32[8,1,256]{2,1,0:T(1,128)}, f32[8,1,256]{2,1,0:T(1,128)S(1)}, u32[]{:S(2)}) copy-start(f32[8,1,256]{2,1,0:T(1,128)S(1)} %convert_element_type.191) | copy-start | bytes 24580
  109.4 0.6 copy-start.20
  110.0 65.9 %copy-start.18 = (f32[256]{0:T(256)}, f32[256]{0:T(256)S(1)}, u32[]{:S(2)}) copy-start(f32[256]{0:T(256)S(1)} %fusion.51) | copy-start | bytes 3076
  178.1 47.6 %all-to-all-start = ((bf16[256,8,256]{0,2,1:T(8,128)(2,1)}), bf16[256,8,256]{0,2,1:T(8,128)(2,1)}, u32[]{:S(2)}, u32[]{:S(2)}) async-start(bf16[256,8,256]{0,2,1:T(8,128)(2,1)} %bitcast.173), calls=%async_computation | async-start | bytes 2097152 | tf_op jit(solution)/shard_map/all_to_all | solution.py:246
  182.4 160.1 %all-gather.9.cloned.1.call-start = ((), (), s32[]{:S(2)}) async-start(), calls=%async_computation.13 | async-start | bytes 9437184 | tf_op jit(solution)/shard_map/all_gather | solution.py:236
  304.8 6.9 copy-start.27
  307.4 32.8 %all-to-all-start.3 = ((bf16[8,256,256]{2,1,0:T(8,128)(2,1)}), bf16[8,256,256]{2,1,0:T(8,128)(2,1)}, u32[]{:S(2)}, u32[]{:S(2)}) async-start(bf16[8,256,256]{2,1,0:T(8,128)(2,1)} %convert_element_type.153), calls=%async_computation.3 | async-start | bytes 2097152 | tf_op jit(solution)/shard_map/all_to_all | solution.py:252
  311.6 173.9 %all-gather.11.cloned.1.call-start = ((), (), s32[]{:S(2)}) async-start(), calls=%async_computation.14 | async-start | bytes 9437184 | tf_op jit(solution)/shard_map/all_gather | solution.py:191
  348.8 1.3 copy-start.2
  351.4 259.2 %all-gather.13.cloned.1.call-start = ((), (), s32[]{:S(2)}) async-start(), calls=%async_computation.16 | async-start | bytes 9437184 | tf_op jit(solution)/shard_map/all_gather | solution.py:201
  352.0 443.9 %reduce-scatter.7.cloned.1.call-start = ((), (), s32[]{:S(2)}) async-start(), calls=%async_computation.17 | async-start | bytes 9437184 | tf_op jit(solution)/shard_map/reduce_scatter | solution.py:204
  485.5 11.0 copy-start.22
  485.5 11.0 copy-start.23
  610.6 14.4 copy-start.24
  625.0 10.9 copy-start.31
  625.0 10.9 copy-start.29
  625.0 10.9 copy-start.25
  648.5 299.3 %reduce-scatter.5.cloned.1.call-start = ((), (), s32[]{:S(2)}) async-start(), calls=%async_computation.15 | async-start | bytes 9437184 | tf_op jit(solution)/shard_map/reduce_scatter | solution.py:195
  659.6 136.3 %copy-start.3 = (f32[256,2048]{1,0:T(8,128)S(1)}, f32[256,2048]{1,0:T(8,128)}, u32[]{:S(2)}) copy-start(f32[256,2048]{1,0:T(8,128)} %copy-done.2) | copy-start | bytes 6291460
  951.5 6.5 copy-start.5
  959.1 35.4 %all-to-all-start.4 = ((bf16[256,8,256]{2,0,1:T(8,128)(2,1)}), bf16[256,8,256]{2,0,1:T(8,128)(2,1)}, u32[]{:S(2)}, u32[]{:S(2)}) async-start(bf16[256,8,256]{2,0,1:T(8,128)(2,1)} %bitcast.118), calls=%async_computation.6 | async-start | bytes 2097152 | tf_op jit(solution)/shard_map/all_to_all | solution.py:263
  963.4 170.4 %reduce-scatter.11.cloned.1.call-start = ((), (), s32[]{:S(2)}) async-start(), calls=%async_computation.19 | async-start | bytes 9437184 | tf_op jit(solution)/shard_map/reduce_scatter | solution.py:287
  963.5 1.0 copy-start.7
  965.4 4.3 copy-start.6
  976.6 318.9 %reduce-scatter.9.cloned.1.call-start = ((), (), s32[]{:S(2)}) async-start(), calls=%async_computation.18 | async-start | bytes 9437184 | tf_op jit(solution)/shard_map/reduce_scatter | solution.py:281
  1058.1 21.0 %copy-start.4 = (bf16[256,2048]{1,0:T(8,128)(2,1)S(1)}, bf16[256,2048]{1,0:T(8,128)(2,1)}, u32[]{:S(2)}) copy-start(bf16[256,2048]{1,0:T(8,128)(2,1)} %param.22) | copy-start | bytes 3145732
  1058.1 21.0 %copy-start.16 = (f32[8,1,256]{2,1,0:T(1,128)S(1)}, f32[8,1,256]{2,1,0:T(1,128)}, u32[]{:S(2)}) copy-start(f32[8,1,256]{2,1,0:T(1,128)} %copy-done.15) | copy-start | bytes 24580
  1058.1 21.0 %copy-start.19 = (f32[256]{0:T(256)S(1)}, f32[256]{0:T(256)}, u32[]{:S(2)}) copy-start(f32[256]{0:T(256)} %copy-done.18) | copy-start | bytes 3076
  1078.1 1.0 copy-start.10
  1084.9 402.7 %all-reduce.7.cloned.1.call-start = ((), (), s32[]{:S(2)}) async-start(), calls=%async_computation.20 | async-start | bytes 21102592 | tf_op jit(solution)/shard_map/psum | solution.py:301
  1084.9 10.9 copy-start.30
  1085.0 21.7 %slice-start = ((s8[8388608]{0:T(1024)(128)(4,1)}), s8[4194304]{0:T(1024)(128)(4,1)S(1)}, s32[]{:S(2)}) async-start(s8[8388608]{0:T(1024)(128)(4,1)} %bitcast.191), calls=%async_computation.21 | async-start | bytes 8388608
  1095.9 10.8 slice-start.1
  1095.9 10.8 copy-start.32
  1295.5 1.2 copy-start.9
  1298.7 6.9 copy-start.8
  1301.4 30.4 %all-to-all-start.7 = ((bf16[8,256,256]{2,1,0:T(8,128)(2,1)}), bf16[8,256,256]{2,1,0:T(8,128)(2,1)}, u32[]{:S(2)}, u32[]{:S(2)}) async-start(bf16[8,256,256]{2,1,0:T(8,128)(2,1)} %convert_element_type.175), calls=%async_computation.9 | async-start | bytes 2097152 | tf_op jit(solution)/shard_map/all_to_all | solution.py:273
  1307.7 27.7 %copy-start.28 = (u32[32]{0:T(128)S(1)}, u32[32]{0:T(128)}, u32[]{:S(2)}) copy-start(u32[32]{0:T(128)} %constant.121) | copy-start | bytes 388
  1331.8 47.8 %all-to-all-start.6 = ((bf16[8,256,256]{2,1,0:T(8,128)(2,1)}), bf16[8,256,256]{2,1,0:T(8,128)(2,1)S(1)}, u32[]{:S(2)}, u32[]{:S(2)}) async-start(bf16[8,256,256]{2,1,0:T(8,128)(2,1)} %convert_element_type.173), calls=%async_computation.8 | async-start | bytes 2097152 | tf_op jit(solution)/shard_map/all_to_all | solution.py:270
  1341.2 8.0 copy-start.17
  1379.6 3.6 copy-start.21
  1487.6 2.9 copy-start.14
  1490.5 2.6 copy-start.13
  1493.0 3.2 copy-start.12
  1496.3 3.2 copy-start.11
  1499.5 3.2 copy-start.1
Sparse Core Ops, SparseCore 0:
  10.2 158.5 all-gather.6
  185.3 136.0 all-gather.8
  351.5 133.9 all-gather.10
  487.5 123.1 all-gather.12
  648.6 147.1 reduce-scatter.6
  799.8 147.9 reduce-scatter.4
  976.7 156.9 reduce-scatter.10
  1137.8 157.6 reduce-scatter.8
  1299.1 188.4 all-reduce.6
where the time goes:
time: 1530 us; the launch traced here: 1510 us
  waiting for transfers between devices  984 us (64%)
  matrix products  186 us (12%)
  blocking collectives  113 us (7%)
  local copies, waits for them, and re-layouts  106 us (7%)
  other arithmetic  54.1 us (4%)
  starting transfers between devices  34 us (2%)
  loops' own time  17.1 us (1%)
  between operations  16 us (1%)
    reduce_scatter x1, waiting for transfers between devices, local(): lax.psum_scatter(inner_rows(normed, grad_query).astype(jnp.bfloat16), 'se...  162 us
    reduce_scatter x1, waiting for transfers between devices, ffn_by_tokens(): lax.psum_scatter(product(inner_local, down_weight).astype(jnp.bfloat16),...  149 us
    reduce_scatter x1, waiting for transfers between devices, ffn_by_tokens(): lax.psum_scatter((product(grad_gate, gate_weight) + product(grad_up, up_w...  136 us
    all_gather x1, waiting for transfers between devices, ffn_by_tokens(): gathered = lax.all_gather(normed_ffn, 'seq', axis=0, tiled=True)  133 us
    all_gather x1, waiting for transfers between devices, ffn_by_tokens(): grad_rows = lax.all_gather(cotangent, 'seq', axis=0, tiled=True)  106 us
    psum x1, waiting for transfers between devices, local(): lax.psum(query_part.astype(jnp.bfloat16), 'dp').astype(jnp.float32)  101 us
    all_gather x1, waiting for transfers between devices, local(): lax.all_gather(query_weight, 'seq', axis=0, tiled=True)  58.8 us
    dot_general x5, matrix products, product(): return jnp.dot(left_side, right_side, preferred_element_type=jnp.float32)  47.9 us
  transfers between devices with their start and end apart: 16, of which 12 were waited for; matrix products, arithmetic and copies ran while one was open for 18% of the time, Pallas kernels for 0%

commit v1 on v0

v1 whole, which is shorter than its diff:
```python
import functools

import jax
import jax.numpy as jnp
from jax import lax
from jax.experimental import pallas as pl
from jax.experimental.pallas import tpu as pltpu
from jax.sharding import PartitionSpec as P

HEAD_DIM = 128
ATT_BLOCK = 512


EPSILON = 1e-05


def product(left_side, right_side):
    return jnp.dot(left_side, right_side, preferred_element_type=jnp.float32)


def inner_rows(left_side, right_side):
    return lax.dot_general(
        left_side, right_side, (((0,), (0,)), ((), ())), preferred_element_type=jnp.float32
    )


def outer_cols(left_side, right_side):
    return lax.dot_general(
        left_side, right_side, (((1,), (1,)), ((), ())), preferred_element_type=jnp.float32
    )


def silu_backward(gate_value, up_value, grad_inner):
    sigmoid_gate = jax.nn.sigmoid(gate_value)
    grad_gate = grad_inner * up_value * sigmoid_gate * (1.0 + gate_value * (1.0 - sigmoid_gate))
    grad_up = grad_inner * gate_value * sigmoid_gate
    return (grad_gate.astype(jnp.bfloat16), grad_up.astype(jnp.bfloat16))


def snake(count):
    deep = 4 if count % 4 == 0 else 1
    wide = count // deep
    if deep == 1 or wide == 1:
        return list(range(count))
    order = []
    for z in range(deep):
        across = range(1, wide) if z % 2 == 0 else range(wide - 1, 0, -1)
        order += [z * wide + y for y in across]
    return order + [z * wide for z in range(deep - 1, -1, -1)]


def after(value, *others):
    return lax.optimization_barrier((value, *others))[0]


def low(value):
    return value.astype(jnp.bfloat16)


def wide(value):
    return value.astype(jnp.float32)


class Links:
    def __init__(self, mesh):
        self.n = mesh.shape["seq"]
        self.nd = mesh.shape["dp"]
        self.order = snake(self.n)
        n = self.n
        self.right = [(self.order[k], self.order[(k + 1) % n]) for k in range(n)]
        self.left = [(b, a) for a, b in self.right]

    def place(self):
        me = lax.axis_index("seq")
        table = [0] * self.n
        for k, i in enumerate(self.order):
            table[i] = k
        return sum(jnp.where(me == i, table[i], 0) for i in range(self.n))

    def owner(self, place, distance):
        spot = (place + distance) % self.n
        return sum(jnp.where(spot == k, self.order[k], 0) for k in range(self.n))

    def to_right(self, x):
        return lax.ppermute(x, "seq", self.right)

    def to_left(self, x):
        return lax.ppermute(x, "seq", self.left)

    def swap(self, x, axis, r):
        count = self.n if axis == "seq" else self.nd
        return lax.ppermute(x, axis, [(k, k ^ r) for k in range(count)])

    def gather(self, x, watch=None):
        half = self.n // 2
        out = {0: x}
        from_left = from_right = x
        rows = x.shape[0] // 2
        for s in range(1, half):
            from_left, from_right = self.to_right(from_left), self.to_left(from_right)
            out[-s], out[s] = from_left, from_right
        out["a"] = self.to_right(from_left[:rows])
        out["b"] = self.to_left(from_right[rows:])
        return out

    def scatter(self, part):
        half = self.n // 2
        going_left = self.to_left(low(part("b")))
        going_right = self.to_right(low(part("a")))
        for s in range(half - 1, 0, -1):
            lshare, rshare = part(-s), part(s)
            if s == half - 1:
                rows = lshare.shape[0] // 2
                lshare = jnp.concatenate([lshare[:rows], lshare[rows:] + wide(going_left)])
                rshare = jnp.concatenate([rshare[:rows] + wide(going_right), rshare[rows:]])
            else:
                lshare = lshare + wide(going_left)
                rshare = rshare + wide(going_right)
            going_left, going_right = self.to_left(low(lshare)), self.to_right(low(rshare))
        return part(0), going_left, going_right


VMEM_LIMIT = 56 * 1024 * 1024
ANYWHERE = pl.BlockSpec(memory_space=pl.ANY)
IN_VMEM = pl.BlockSpec(memory_space=pltpu.VMEM)
IN_SMEM = pl.BlockSpec(memory_space=pltpu.SMEM)
LOG2_E = 1.4426950408889634
DEAD = 1e30


def nt_dot(a, b):
    return lax.dot_general(a, b, (((1,), (1,)), ((), ())), preferred_element_type=jnp.float32)


def tn_dot(a, b):
    return lax.dot_general(a, b, (((0,), (0,)), ((), ())), preferred_element_type=jnp.float32)


def call(body, operands, specs, outs, out_specs, scratch, flops, moved, name):
    return pl.pallas_call(
        body,
        name=name,
        in_specs=specs,
        out_specs=tuple(out_specs),
        out_shape=tuple(jax.ShapeDtypeStruct(s, t) for s, t in outs),
        scratch_shapes=scratch,
        compiler_params=pltpu.CompilerParams(vmem_limit_bytes=VMEM_LIMIT),
        cost_estimate=pl.CostEstimate(flops=flops, bytes_accessed=moved, transcendentals=0),
    )(*operands)


def start_all(copies):
    for copy in copies:
        copy.start()
    return copies


def wait_all(copies):
    for copy in copies:
        copy.wait()


def causal_mask(block):
    key_at = lax.broadcasted_iota(jnp.int32, (block, block), 0)
    query_at = lax.broadcasted_iota(jnp.int32, (block, block), 1)
    return key_at <= query_at


def forward_body(n, info, *refs):
    q_in, kv_in = refs[:n], refs[n : 2 * n]
    outs, stats, ot = refs[2 * n : 3 * n], refs[3 * n], refs[3 * n + 1]
    qs, ks, vs, vt, mixed, sems = refs[3 * n + 2 :]
    me, length = info[0], info[1]
    count, width = q_in[0].shape
    heads = width // HEAD_DIM
    total = n * count
    blocks = total // ATT_BLOCK
    copies = []
    for r in range(n):
        rows = pl.ds(pl.multiple_of((me ^ r) * count, count), count)
        for k, (src, dst) in enumerate(
            (
                (kv_in[r].at[:, pl.ds(0, width)], ks),
                (kv_in[r].at[:, pl.ds(width, width)], vs),
                (q_in[r], qs),
            )
        ):
            copies.append(pltpu.make_async_copy(src, dst.at[rows], sems.at[3 * r + k]))
    wait_all(start_all(copies))
    factor = HEAD_DIM ** (-0.5) * LOG2_E

    def transpose_values(b, _):
        at = pl.ds(pl.multiple_of(b * ATT_BLOCK, ATT_BLOCK), ATT_BLOCK)
        vt[:, at] = vs[at, :].T
        return 0

    lax.fori_loop(0, blocks, transpose_values, 0)
    live = jnp.minimum((length + ATT_BLOCK - 1) // ATT_BLOCK, blocks)

    def tile(qi, kj, state, masked):
        new = []
        q_at = pl.ds(pl.multiple_of(qi * ATT_BLOCK, ATT_BLOCK), ATT_BLOCK)
        k_at = pl.ds(pl.multiple_of(kj * ATT_BLOCK, ATT_BLOCK), ATT_BLOCK)
        for h in range(heads):
            cols = slice(h * HEAD_DIM, (h + 1) * HEAD_DIM)
            top, total_sum, acc = state[h]
            scores = nt_dot(ks[k_at, cols], qs[q_at, cols]) * factor
            if masked:
                scores = jnp.where(causal_mask(ATT_BLOCK), scores, -DEAD)
            higher = jnp.maximum(top, jnp.max(scores, axis=0, keepdims=True))
            weights = jnp.exp2(scores - higher)
            shrink = jnp.exp2(top - higher)
            total_sum = total_sum * shrink + jnp.sum(weights, axis=0, keepdims=True)
            acc = acc * shrink + jnp.dot(
                vt[cols, k_at], weights.astype(jnp.bfloat16), preferred_element_type=jnp.float32
            )
            new.append((higher, total_sum, acc))
        return tuple(new)

    stats[...] = jnp.full(stats.shape, DEAD, jnp.float32)

    def query_block(qi, _):
        first = tuple(
            (
                jnp.full((1, ATT_BLOCK), -DEAD, jnp.float32),
                jnp.zeros((1, ATT_BLOCK), jnp.float32),
                jnp.zeros((HEAD_DIM, ATT_BLOCK), jnp.float32),
            )
            for _ in range(heads)
        )
        state = lax.fori_loop(0, qi, lambda kj, s: tile(qi, kj, s, False), first)
        state = tile(qi, qi, state, True)
        q_at = pl.ds(pl.multiple_of(qi * ATT_BLOCK, ATT_BLOCK), ATT_BLOCK)
        spot = qi * ATT_BLOCK + lax.broadcasted_iota(jnp.int32, (1, ATT_BLOCK), 1)
        alive = spot < length
        for h in range(heads):
            cols = slice(h * HEAD_DIM, (h + 1) * HEAD_DIM)
            top, total_sum, acc = state[h]
            scaled = acc * jnp.where(alive, 1.0 / total_sum, 0.0)
            ot[cols, q_at] = scaled
            mixed[q_at, cols] = scaled.T.astype(jnp.bfloat16)
            stats[h : h + 1, q_at] = jnp.where(alive, top + jnp.log2(total_sum), DEAD)
        return 0

    lax.fori_loop(0, live, query_block, 0)

    def dead_block(qi, _):
        q_at = pl.ds(pl.multiple_of(qi * ATT_BLOCK, ATT_BLOCK), ATT_BLOCK)
        mixed[q_at, :] = jnp.zeros((ATT_BLOCK, width), jnp.bfloat16)
        ot[:, q_at] = jnp.zeros((width, ATT_BLOCK), jnp.float32)
        return 0

    lax.fori_loop(live, blocks, dead_block, 0)
    copies = []
    for r in range(n):
        rows = pl.ds(pl.multiple_of((me ^ r) * count, count), count)
        copies.append(pltpu.make_async_copy(mixed.at[rows], outs[r], sems.at[r]))
    wait_all(start_all(copies))


def attention_forward(info, q_blocks, kv_blocks):
    n = len(q_blocks)
    count, width = q_blocks[0].shape
    total = n * count
    got = call(
        functools.partial(forward_body, n),
        [info, *q_blocks, *kv_blocks],
        [IN_SMEM] + [ANYWHERE] * (2 * n),
        [((count, width), jnp.bfloat16)] * n
        + [((8, total), jnp.float32), ((width, total), jnp.float32)],
        [ANYWHERE] * n + [IN_VMEM] * 2,
        [pltpu.VMEM((total, width), jnp.bfloat16)] * 3
        + [pltpu.VMEM((width, total), jnp.bfloat16), pltpu.VMEM((total, width), jnp.bfloat16)]
        + [pltpu.SemaphoreType.DMA((3 * n,))],
        16 * 2 * total * total * width // 2,
        10 * total * width,
        "attention_forward",
    )
    return got[:n], got[n], got[n + 1]


def backward_body(n, info, *refs):
    q_in, kv_in, g_in = refs[:n], refs[n : 2 * n], refs[2 * n : 3 * n]
    stats, ot = refs[3 * n], refs[3 * n + 1]
    refs = refs[3 * n + 2 :]
    dq_out, dkv_out = refs[:n], refs[n : 2 * n]
    qs, ks, vs, gs, kt, delta, dqt, dk, dv, dq_low, dkv_low, sems = refs[2 * n :]
    me, length = info[0], info[1]
    count, width = q_in[0].shape
    heads = width // HEAD_DIM
    total = n * count
    blocks = total // ATT_BLOCK
    copies = []
    for r in range(n):
        rows = pl.ds(pl.multiple_of((me ^ r) * count, count), count)
        for k, (src, dst) in enumerate(
            (
                (kv_in[r].at[:, pl.ds(0, width)], ks),
                (kv_in[r].at[:, pl.ds(width, width)], vs),
                (q_in[r], qs),
                (g_in[r], gs),
            )
        ):
            copies.append(pltpu.make_async_copy(src, dst.at[rows], sems.at[4 * r + k]))
    start_all(copies)
    live = jnp.minimum((length + ATT_BLOCK - 1) // ATT_BLOCK, blocks)
    scale = HEAD_DIM ** (-0.5)
    factor = scale * LOG2_E

    def clear(b, _):
        at = pl.ds(pl.multiple_of(b * ATT_BLOCK, ATT_BLOCK), ATT_BLOCK)
        dqt[:, at] = jnp.zeros((width, ATT_BLOCK), jnp.float32)
        dk[at, :] = jnp.zeros((ATT_BLOCK, width), jnp.float32)
        dv[at, :] = jnp.zeros((ATT_BLOCK, width), jnp.float32)
        return 0

    lax.fori_loop(0, blocks, clear, 0)
    wait_all(copies)

    def prepare(b, _):
        at = pl.ds(pl.multiple_of(b * ATT_BLOCK, ATT_BLOCK), ATT_BLOCK)
        kt[:, at] = ks[at, :].T
        both = gs[at, :].astype(jnp.float32).T * ot[:, at]
        for h in range(heads):
            cols = slice(h * HEAD_DIM, (h + 1) * HEAD_DIM)
            delta[h : h + 1, at] = jnp.sum(both[cols], axis=0, keepdims=True)
        return 0

    lax.fori_loop(0, blocks, prepare, 0)

    def tile(qi, kj, masked):
        q_at = pl.ds(pl.multiple_of(qi * ATT_BLOCK, ATT_BLOCK), ATT_BLOCK)
        k_at = pl.ds(pl.multiple_of(kj * ATT_BLOCK, ATT_BLOCK), ATT_BLOCK)
        for h in range(heads):
            cols = slice(h * HEAD_DIM, (h + 1) * HEAD_DIM)
            q, g = qs[q_at, cols], gs[q_at, cols]
            scores = nt_dot(ks[k_at, cols], q) * factor - stats[h : h + 1, q_at]
            if masked:
                scores = jnp.where(causal_mask(ATT_BLOCK), scores, -DEAD)
            weights = jnp.exp2(scores)
            grad_weights = nt_dot(vs[k_at, cols], g)
            grad_scores = (weights * (grad_weights - delta[h : h + 1, q_at])).astype(jnp.bfloat16)
            dv[k_at, cols] += jnp.dot(
                weights.astype(jnp.bfloat16), g, preferred_element_type=jnp.float32
            )
            dk[k_at, cols] += jnp.dot(grad_scores, q, preferred_element_type=jnp.float32)
            dqt[cols, q_at] += jnp.dot(
                kt[cols, k_at], grad_scores, preferred_element_type=jnp.float32
            )

    def query_block(qi, _):
        def step(kj, _):
            tile(qi, kj, False)
            return 0

        lax.fori_loop(0, qi, step, 0)
        tile(qi, qi, True)
        return 0

    lax.fori_loop(0, live, query_block, 0)

    def finish(b, _):
        at = pl.ds(pl.multiple_of(b * ATT_BLOCK, ATT_BLOCK), ATT_BLOCK)
        dq_low[at, :] = (dqt[:, at] * scale).T.astype(jnp.bfloat16)
        dkv_low[at, :width] = (dk[at, :] * scale).astype(jnp.bfloat16)
        dkv_low[at, width:] = dv[at, :].astype(jnp.bfloat16)
        return 0

    lax.fori_loop(0, blocks, finish, 0)
    copies = []
    for r in range(n):
        rows = pl.ds(pl.multiple_of((me ^ r) * count, count), count)
        copies.append(pltpu.make_async_copy(dq_low.at[rows], dq_out[r], sems.at[2 * r]))
        copies.append(pltpu.make_async_copy(dkv_low.at[rows], dkv_out[r], sems.at[2 * r + 1]))
    wait_all(start_all(copies))


def attention_backward(info, q_blocks, kv_blocks, g_blocks, stats, ot):
    n = len(q_blocks)
    count, width = q_blocks[0].shape
    total = n * count
    low_all = pltpu.VMEM((total, width), jnp.bfloat16)
    got = call(
        functools.partial(backward_body, n),
        [info, *q_blocks, *kv_blocks, *g_blocks, stats, ot],
        [IN_SMEM] + [ANYWHERE] * (3 * n) + [IN_VMEM] * 2,
        [((count, width), jnp.bfloat16)] * n + [((count, 2 * width), jnp.bfloat16)] * n,
        [ANYWHERE] * (2 * n),
        [low_all] * 4
        + [
            pltpu.VMEM((width, total), jnp.bfloat16),
            pltpu.VMEM((8, total), jnp.float32),
            pltpu.VMEM((width, total), jnp.float32),
            pltpu.VMEM((total, width), jnp.float32),
            pltpu.VMEM((total, width), jnp.float32),
            low_all,
            pltpu.VMEM((total, 2 * width), jnp.bfloat16),
            pltpu.SemaphoreType.DMA((4 * n,)),
        ],
        40 * 2 * total * total * width // 2,
        20 * total * width,
        "attention_backward",
    )
    return got[:n], got[n:]


def aligned(index, unit):
    return pl.multiple_of(index * unit, unit)


def pack_body(n, info, keys, values, *refs):
    outs, sems = refs[:n], refs[n]
    me = info[0]
    width = outs[0].shape[1] // 2
    copies = []
    for r in range(n):
        cols = pl.ds(aligned(me ^ r, width), width)
        copies.append(
            pltpu.make_async_copy(keys.at[:, cols], outs[r].at[:, pl.ds(0, width)], sems.at[2 * r])
        )
        copies.append(
            pltpu.make_async_copy(
                values.at[:, cols], outs[r].at[:, pl.ds(width, width)], sems.at[2 * r + 1]
            )
        )
    wait_all(start_all(copies))


def pack_keys_values(n, info, keys, values):
    count, depth = keys.shape
    return call(
        functools.partial(pack_body, n),
        [info, keys, values],
        [IN_SMEM, ANYWHERE, ANYWHERE],
        [((count, 2 * depth // n), jnp.bfloat16)] * n,
        [IN_VMEM] * n,
        [pltpu.SemaphoreType.DMA((2 * n,))],
        0,
        8 * count * depth,
        "pack_keys_values",
    )


GAIN_ROWS = 32


def norm_parts(v):
    return lax.rsqrt(jnp.mean(v * v, axis=-1, keepdims=True) + EPSILON)


def query_body(n, info, x, *refs):
    pieces = 2 * (n + 1)
    mine, other = refs[: n + 1], refs[n + 1 : pieces]
    q_out = refs[pieces : pieces + n]
    normed, gains, weight_out = refs[pieces + n : pieces + n + 3]
    weight, gain_rows, sems, out_sem = refs[pieces + n + 3 :]
    me, core = info[0], info[2]
    depth = x.shape[1]
    half = mine[0].shape[1]
    wrows = mine[0].shape[0] - GAIN_ROWS
    upper = (wrows + GAIN_ROWS) // 2 - GAIN_ROWS
    copies = []
    for k in range(n + 1):
        who = info[3 + min(k, n - 1)]
        if k < n - 1:
            skip, rows, at = GAIN_ROWS, wrows, who * wrows
        elif k == n - 1:
            skip, rows, at = GAIN_ROWS, upper, who * wrows
        else:
            skip, rows, at = 0, wrows - upper, who * wrows + upper
        at = pl.multiple_of(at, 16)
        for j, (ref, side) in enumerate(((mine, core), (other, 1 - core))):
            copies.append(
                pltpu.make_async_copy(
                    ref[k].at[pl.ds(skip, rows)],
                    weight.at[pl.ds(at, rows), pl.ds(aligned(side, half), half)],
                    sems.at[3 * k + j],
                )
            )
        if k < n:
            copies.append(
                pltpu.make_async_copy(
                    mine[k].at[pl.ds(0, 16)],
                    gain_rows.at[pl.ds(aligned(who, 16), 16)],
                    sems.at[3 * k + 2],
                )
            )
    wait_all(start_all(copies))
    save = pltpu.make_async_copy(weight, weight_out, out_sem)
    save.start()
    share = depth // n
    for o in range(n):
        row = gain_rows[o * 16 : o * 16 + 16, : 2 * share].astype(jnp.float32)
        gains[0:1, o * share : (o + 1) * share] = row[0:1, :share]
        gains[1:2, o * share : (o + 1) * share] = row[0:1, share:]
    v = x[...].astype(jnp.float32)
    normed[...] = (v * norm_parts(v) * gains[0:1, :]).astype(jnp.bfloat16)
    for r in range(n):
        cols = pl.ds(aligned(me ^ r, share), share)
        q_out[r][...] = jnp.dot(
            normed[...], weight[:, cols], preferred_element_type=jnp.float32
        ).astype(jnp.bfloat16)
    save.wait()


def project_queries(n, info, x, mine, other):
    count, depth = x.shape
    got = call(
        functools.partial(query_body, n),
        [info, x, *mine, *other],
        [IN_SMEM, IN_VMEM] + [ANYWHERE] * (2 * n + 2),
        [((count, depth // n), jnp.bfloat16)] * n
        + [
            ((count, depth), jnp.bfloat16),
            ((8, depth), jnp.float32),
            ((depth, depth), jnp.bfloat16),
        ],
        [IN_VMEM] * (n + 2) + [ANYWHERE],
        [
            pltpu.VMEM((depth, depth), jnp.bfloat16),
            pltpu.VMEM((n * 16, mine[0].shape[1]), jnp.bfloat16),
            pltpu.SemaphoreType.DMA((3 * n + 3,)),
            pltpu.SemaphoreType.DMA,
        ],
        2 * count * depth * depth,
        6 * depth * depth,
        "project_queries",
    )
    return got[:n], got[n], got[n + 1], got[n + 2]


def stack_body(n, info, *refs):
    blocks, out, sems = refs[: n + 1], refs[n + 1], refs[n + 2]
    wrows = blocks[0].shape[0]
    copies = []
    for k in range(n + 1):
        who = info[3 + min(k, n - 1)]
        rows = blocks[k].shape[0]
        at = who * wrows + (rows if k == n else 0)
        copies.append(
            pltpu.make_async_copy(
                blocks[k], out.at[pl.ds(pl.multiple_of(at, 16), rows)], sems.at[k]
            )
        )
    wait_all(start_all(copies))


def stack_ring(n, info, blocks):
    wrows, width = blocks[0].shape
    return call(
        functools.partial(stack_body, n),
        [info, *blocks],
        [IN_SMEM] + [ANYWHERE] * (n + 1),
        [((n * wrows, width), jnp.bfloat16)],
        [IN_VMEM],
        [pltpu.SemaphoreType.DMA((n + 1,))],
        0,
        4 * n * wrows * width,
        "stack_ring",
    )[0]


def hidden_body(n, nd, info, x, gains, *refs):
    blocks, parts = refs[:n], refs[n : n + nd]
    hidden, normed, mixed, weight_out = refs[n + nd : n + nd + 4]
    weight, sems, out_sem = refs[n + nd + 4 :]
    me, dp = info[0], info[1]
    share, quarter = blocks[0].shape[1], parts[0].shape[1]
    copies = []
    for r in range(nd):
        cols = pl.ds(aligned(dp ^ r, quarter), quarter)
        copies.append(pltpu.make_async_copy(parts[r], weight.at[:, cols], sems.at[r]))
    for r in range(n):
        cols = pl.ds(aligned(me ^ r, share), share)
        copies.append(pltpu.make_async_copy(blocks[r], mixed.at[:, cols], sems.at[nd + r]))
    wait_all(start_all(copies))
    save = pltpu.make_async_copy(weight, weight_out, out_sem)
    save.start()
    depth = x.shape[1]
    piece = 512

    def step(c, total):
        cols = pl.ds(aligned(c, piece), piece)
        v = x[:, cols].astype(jnp.float32) + jnp.dot(
            mixed[...], weight[:, cols], preferred_element_type=jnp.float32
        )
        hidden[:, cols] = v
        return total + jnp.sum(v * v, axis=-1, keepdims=True)

    total = lax.fori_loop(0, depth // piece, step, jnp.zeros((x.shape[0], 1), jnp.float32))
    normed[...] = (
        hidden[...] * lax.rsqrt(total / depth + EPSILON) * gains[1:2, :]
    ).astype(jnp.bfloat16)
    save.wait()


def project_mixed(n, nd, info, x, gains, blocks, parts):
    count, depth = x.shape
    return call(
        functools.partial(hidden_body, n, nd),
        [info, x, gains, *blocks, *parts],
        [IN_SMEM, IN_VMEM, IN_VMEM] + [ANYWHERE] * (n + nd),
        [
            ((count, depth), jnp.float32),
            ((count, depth), jnp.bfloat16),
            ((count, depth), jnp.bfloat16),
            ((depth, depth), jnp.bfloat16),
        ],
        [IN_VMEM] * 3 + [ANYWHERE],
        [
            pltpu.VMEM((depth, depth), jnp.bfloat16),
            pltpu.SemaphoreType.DMA((n + nd,)),
            pltpu.SemaphoreType.DMA,
        ],
        2 * count * depth * depth,
        6 * depth * depth,
        "project_mixed",
    )


def norm_grad(v, gain, upstream):
    scale = norm_parts(v)
    weighted = upstream * gain
    through = weighted * scale - v * (scale**3) * jnp.mean(weighted * v, axis=-1, keepdims=True)
    return through, jnp.sum(upstream * v * scale, axis=0, keepdims=True)


def branch_body(n, nd, info, hidden, gains, cotangent, own, first, second, weight_in, *refs):
    gm_out, cols_out = refs[:n], refs[n : n + nd]
    grad_hidden, gain_part, branch, weight, sem = refs[n + nd :]
    me, dp = info[0], info[1]
    load = pltpu.make_async_copy(weight_in, weight, sem)
    load.start()
    upstream = own[...] + first[...].astype(jnp.float32) + second[...].astype(jnp.float32)
    through, gain = norm_grad(hidden[...], gains[1:2, :], upstream)
    gain_part[...] = jnp.broadcast_to(gain, gain_part.shape)
    total = cotangent[...].astype(jnp.float32) + through
    grad_hidden[...] = total
    branch[...] = total.astype(jnp.bfloat16)
    quarter = cols_out[0].shape[1]
    for r in range(nd):
        cols_out[r][...] = branch[:, pl.ds(aligned(dp ^ r, quarter), quarter)]
    load.wait()
    share = gm_out[0].shape[1]
    for r in range(n):
        rows = pl.ds(aligned(me ^ r, share), share)
        gm_out[r][...] = nt_dot(branch[...], weight[rows, :]).astype(jnp.bfloat16)


def branch_gradient(n, nd, info, hidden, gains, cotangent, sums, weight):
    count, depth = cotangent.shape
    got = call(
        functools.partial(branch_body, n, nd),
        [info, hidden, gains, cotangent, *sums, weight],
        [IN_SMEM] + [IN_VMEM] * 6 + [ANYWHERE],
        [((count, depth // n), jnp.bfloat16)] * n
        + [((count, depth // nd), jnp.bfloat16)] * nd
        + [((count, depth), jnp.float32), ((8, depth), jnp.float32)],
        [IN_VMEM] * (n + nd + 2),
        [
            pltpu.VMEM((count, depth), jnp.bfloat16),
            pltpu.VMEM((depth, depth), jnp.bfloat16),
            pltpu.SemaphoreType.DMA,
        ],
        2 * count * depth * depth,
        6 * depth * depth,
        "branch_gradient",
    )
    return got[:n], got[n : n + nd], got[n + nd], got[n + nd + 1]


def sort_body(n, nd, info, *refs):
    blocks, out, cols_out = refs[:n], refs[n], refs[n + 1 : n + 1 + nd]
    rows, sems = refs[n + 1 + nd :]
    me, dp = info[0], info[1]
    share, quarter = blocks[0].shape[1], cols_out[0].shape[1]
    copies = []
    for r in range(n):
        cols = pl.ds(aligned(me ^ r, share), share)
        copies.append(pltpu.make_async_copy(blocks[r], rows.at[:, cols], sems.at[r]))
    wait_all(start_all(copies))
    copies = [pltpu.make_async_copy(rows, out, sems.at[0])]
    for r in range(nd):
        cols = pl.ds(aligned(dp ^ r, quarter), quarter)
        copies.append(pltpu.make_async_copy(rows.at[:, cols], cols_out[r], sems.at[1 + r]))
    wait_all(start_all(copies))


def sort_columns(n, nd, info, blocks):
    count, share = blocks[0].shape
    depth = n * share
    got = call(
        functools.partial(sort_body, n, nd),
        [info, *blocks],
        [IN_SMEM] + [ANYWHERE] * n,
        [((count, depth), jnp.bfloat16)] + [((count, depth // nd), jnp.bfloat16)] * nd,
        [ANYWHERE] * (nd + 1),
        [
            pltpu.VMEM((count, depth), jnp.bfloat16),
            pltpu.SemaphoreType.DMA((max(n, nd + 1),)),
        ],
        0,
        6 * count * depth,
        "sort_columns",
    )
    return got[0], got[1:]


def split_body(n, info, *refs):
    blocks, keys, values, sems = refs[:n], refs[n], refs[n + 1], refs[n + 2]
    me = info[0]
    share = blocks[0].shape[1] // 2
    copies = []
    for r in range(n):
        cols = pl.ds(aligned(me ^ r, share), share)
        copies.append(
            pltpu.make_async_copy(blocks[r].at[:, pl.ds(0, share)], keys.at[:, cols], sems.at[2 * r])
        )
        copies.append(
            pltpu.make_async_copy(
                blocks[r].at[:, pl.ds(share, share)], values.at[:, cols], sems.at[2 * r + 1]
            )
        )
    wait_all(start_all(copies))


def split_keys_values(n, info, blocks):
    count, share = blocks[0].shape
    depth = n * share // 2
    return call(
        functools.partial(split_body, n),
        [info, *blocks],
        [IN_SMEM] + [ANYWHERE] * n,
        [((count, depth), jnp.bfloat16)] * 2,
        [IN_VMEM] * 2,
        [pltpu.SemaphoreType.DMA((2 * n,))],
        0,
        8 * count * depth,
        "split_keys_values",
    )


def input_body(x, gains, grad_query, grad_hidden, weight, out, gain_part, upstream):
    piece = 512

    def step(c, _):
        rows = pl.ds(aligned(c, piece), piece)
        upstream[:, rows] = nt_dot(grad_query[...], weight[rows, :])
        return 0

    lax.fori_loop(0, x.shape[1] // piece, step, 0)
    through, gain = norm_grad(x[...].astype(jnp.float32), gains[0:1, :], upstream[...])
    gain_part[...] = jnp.broadcast_to(gain, gain_part.shape)
    out[...] = (grad_hidden[...] + through).astype(jnp.bfloat16)


def input_gradient(x, gains, grad_query, grad_hidden, weight):
    count, depth = x.shape
    return call(
        input_body,
        [x, gains, grad_query, grad_hidden, weight],
        [IN_VMEM] * 5,
        [((count, depth), jnp.bfloat16), ((8, depth), jnp.float32)],
        [IN_VMEM] * 2,
        [pltpu.VMEM((count, depth), jnp.float32)],
        2 * count * depth * depth,
        6 * depth * depth,
        "input_gradient",
    )


def tree_sum(parts):
    while len(parts) > 1:
        parts = [parts[k] + parts[k + 1] for k in range(0, len(parts), 2)]
    return parts[0]


def columns(x, start, width):
    return lax.dynamic_slice_in_dim(x, start, width, 1)


def rows_of(x, start, count):
    return lax.dynamic_slice_in_dim(x, start, count, 0)


def make_local(mesh):
    net = Links(mesh)
    n, nd = net.n, net.nd
    dp_order = list(range(0, nd, 2)) + list(range(1, nd, 2))
    half_way = n // 2
    ring_order = [0] + [s for k in range(1, half_way) for s in (-k, k)] + ["a", "b"]

    def exchange(blocks, axis="seq"):
        return [b if r == 0 else net.swap(b, axis, r) for r, b in enumerate(blocks)]

    def keyed_rows(place, key, count):
        if key in ("a", "b"):
            first = net.owner(place, half_way) * count
            return (first if key == "a" else first + count // 2), count // 2
        return net.owner(place, key) * count, count

    def dp_rows(x):
        near = jnp.concatenate([x] + [net.swap(x, "dp", r) for r in range(2, nd, 2)], 0)
        return jnp.concatenate([near, net.swap(near, "dp", 1)], 0)

    def dp_parts(x):
        near = {0: x}
        for r in range(2, nd, 2):
            near[r] = net.swap(x, "dp", r)
        far = {r + 1: net.swap(v, "dp", 1) for r, v in near.items()}
        return {**near, **far}

    def dp_total(x, mine):
        core = mine % 2
        half = x.shape[1] // 2
        x = low(x)
        kept = wide(columns(x, core * half, half))
        kept = low(kept + wide(net.swap(columns(x, (1 - core) * half, half), "dp", 1)))
        total = low(
            tree_sum([wide(kept)] + [wide(net.swap(kept, "dp", r)) for r in range(2, nd, 2)])
        )
        other = net.swap(total, "dp", 1)
        first = core == 0
        return jnp.concatenate(
            [wide(jnp.where(first, total, other)), wide(jnp.where(first, other, total))], 1
        )

    def local(
        layer_input,
        global_keys,
        global_values,
        lengths,
        attn_gain,
        query_weight,
        out_weight,
        ffn_gain,
        gate_weight,
        up_weight,
        down_weight,
        cotangent,
    ):
        length = lengths[0]
        me, mine = lax.axis_index("seq"), lax.axis_index("dp")
        core = mine % 2
        place = net.place()
        depth = layer_input.shape[1]
        wrows = query_weight.shape[0]
        quarter = depth // nd
        owners = [net.owner(place, key) for key in ring_order[:-2]] + [net.owner(place, half_way)]
        info = jnp.stack([me, mine, core, *owners]).astype(jnp.int32)
        length_info = jnp.stack([me, length]).astype(jnp.int32)

        half = depth // 2
        gains = jnp.concatenate([attn_gain, ffn_gain])
        per_half = jnp.tile(gains, half // gains.shape[0])
        gain_rows = jnp.broadcast_to(per_half[None], (GAIN_ROWS, half))
        piece = jnp.concatenate([gain_rows, columns(query_weight, core * half, half)], 0)
        got = net.gather(piece)
        fetched = [got[k] for k in ring_order]
        kv_sent = pack_keys_values(n, info, global_keys, global_values)
        kv_blocks = exchange(kv_sent)
        q_sent, normed, gains, full_query = project_queries(
            n, info, layer_input, fetched, [net.swap(b, "dp", 1) for b in fetched]
        )
        q_blocks = exchange(q_sent)
        mixed_sent, stats, ot = attention_forward(length_info, q_blocks, kv_blocks)

        out_piece = columns(out_weight, mine * quarter, quarter)
        out_got = net.gather(after(out_piece, got["a"]))
        out_quarter = stack_ring(n, info, [out_got[k] for k in ring_order])
        out_parts = dp_parts(out_quarter)

        mixed_blocks = exchange(mixed_sent)
        hidden, normed_ffn, mixed, full_out = project_mixed(
            n, nd, info, layer_input, gains, mixed_blocks, [out_parts[r] for r in range(nd)]
        )

        cot = net.gather(after(cotangent, q_blocks[n - 1]))
        nf = net.gather(normed_ffn)
        inner, grad_gate, grad_up = {}, {}, {}
        for key in nf:
            gate_value = outer_cols(nf[key], gate_weight)
            up_value = outer_cols(nf[key], up_weight)
            grad_inner = outer_cols(cot[key], down_weight)
            inner[key] = low(jax.nn.silu(gate_value) * up_value)
            grad_gate[key], grad_up[key] = silu_backward(gate_value, up_value, grad_inner)

        def grad_share(key):
            return product(grad_gate[key], gate_weight) + product(grad_up[key], up_weight)

        grad_sums = net.scatter(grad_share)
        gm_sent, branch_cols, grad_hidden, ffn_gain_part = branch_gradient(
            n, nd, info, hidden, gains, cotangent, grad_sums, full_out
        )
        gm_blocks = exchange(gm_sent)

        def joined(blocks):
            return jnp.concatenate([blocks[k] for k in ring_order], 0)

        nf_all, cot_all = joined(nf), joined(cot)
        gate_grad = dp_total(inner_rows(joined(grad_gate), nf_all), mine)
        up_grad = dp_total(inner_rows(joined(grad_up), nf_all), mine)
        down_grad = dp_total(inner_rows(joined(inner), cot_all), mine)

        inner_late = {k: after(v, gm_blocks[n - 1]) for k, v in inner.items()}
        own, first, second = net.scatter(lambda key: product(inner_late[key], down_weight))
        layer_output = low(hidden + (own + wide(first) + wide(second)))

        dq_sent, dkv_sent = attention_backward(
            length_info, q_blocks, kv_blocks, gm_blocks, stats, ot
        )
        grad_query, query_cols = sort_columns(n, nd, info, exchange(dq_sent))
        dkv_late = [after(b, grad_query) for b in dkv_sent]
        key_grad, value_grad = split_keys_values(n, info, exchange(dkv_late))
        input_grad, attn_gain_part = input_gradient(
            layer_input, gains, grad_query, grad_hidden, full_query
        )

        def dp_join(cols):
            got_cols = exchange(cols, "dp")
            return jnp.concatenate([got_cols[r] for r in dp_order], 0)

        out_part = inner_rows(dp_rows(mixed), dp_join(branch_cols))
        query_part = inner_rows(dp_rows(normed), dp_join(query_cols))
        gain_part = jnp.concatenate(
            [attn_gain_part[0].reshape(n, -1), ffn_gain_part[0].reshape(n, -1)], 1
        )

        def out_rows(key):
            return rows_of(out_part, *keyed_rows(place, key, wrows))

        def total_of(sums):
            own, first, second = sums
            return low(own + wide(first) + wide(second))

        out_mine = total_of(net.scatter(out_rows))

        def query_rows(key):
            first, size = keyed_rows(place, key, wrows)
            block = rows_of(query_part, first, size)
            if key == "a":
                return jnp.concatenate([block, jnp.zeros((16, quarter), jnp.float32)], 0)
            row = rows_of(gain_part, first // wrows, 1)
            row = jnp.pad(row, ((0, 0), (0, quarter - row.shape[1])))
            tail = jnp.broadcast_to(row, (16, quarter))
            if key == "b":
                return jnp.concatenate([block, tail], 0)
            middle = jnp.zeros((16, quarter), jnp.float32)
            return jnp.concatenate([block[: size // 2], middle, block[size // 2 :], tail], 0)

        query_mine = total_of(net.scatter(query_rows))

        def whole_rows(parts):
            first = jnp.zeros((), jnp.int32)
            out = jnp.zeros((wrows, depth), jnp.float32)
            for r, part in parts.items():
                out = lax.dynamic_update_slice(out, wide(part), (first, (mine ^ r) * quarter))
            return out

        out_grad = whole_rows(dp_parts(out_mine))
        query_parts = dp_parts(query_mine)
        body = {
            r: jnp.concatenate([v[: wrows // 2], v[wrows // 2 + 16 : wrows + 16]], 0)
            for r, v in query_parts.items()
        }
        query_grad = whole_rows(body)
        gain_sum = tree_sum([wide(query_parts[r][wrows + 16]) for r in range(nd)])
        attn_count = attn_gain.shape[0]
        return (
            layer_output,
            input_grad,
            key_grad,
            value_grad,
            gain_sum[:attn_count],
            query_grad,
            out_grad,
            gain_sum[attn_count : 2 * attn_count],
            gate_grad,
            up_grad,
            down_grad,
        )

    return local


def solution(mesh):
    placed = (
        P(("dp", "seq"), None),
        P(("dp", "seq"), None),
        P(("dp", "seq"), None),
        P("dp"),
        P("seq"),
        P("seq", None),
        P("seq", None),
        P("seq"),
        P("seq", None),
        P("seq", None),
        P("seq", None),
        P(("dp", "seq"), None),
    )
    return jax.shard_map(
        make_local(mesh),
        mesh=mesh,
        in_specs=placed,
        out_specs=(
            P(("dp", "seq"), None),
            P(("dp", "seq"), None),
            P(("dp", "seq"), None),
            P(("dp", "seq"), None),
            P("seq"),
            P("seq", None),
            P("seq", None),
            P("seq"),
            P("seq", None),
            P("seq", None),
            P("seq", None),
        ),
        check_vma=False,
    )
```

time: 1530 us -> 885 us (0.58)
  waiting for transfers between devices: 984 us -> 399 us
  starting transfers between devices: 34 us -> 183 us
  blocking collectives: 113 us -> 0 us
  Pallas kernels: 0 us -> 94.7 us
  matrix products: 186 us -> 111 us
  local copies, waits for them, and re-layouts: 106 us -> 46 us
  loops' own time: 17.1 us -> 0 us
    reduce_scatter x4 -> x0, waiting for transfers between devices: 467 us -> none  [the longest x1 162 us: local(): lax.psum_scatter(inner_rows(normed, grad_query).astype(jnp.bfloat16), 'se...]
    ppermute x0 -> x143, waiting for transfers between devices: none -> 399 us  [the longest x32 184 us: to_right(): return lax.ppermute(x, 'seq', self.right)]
    all_gather x4 -> x0, waiting for transfers between devices: 299 us -> none  [the longest x1 133 us: ffn_by_tokens(): gathered = lax.all_gather(normed_ffn, 'seq', axis=0, tiled=True)]
    ppermute x0 -> x143, starting transfers between devices: none -> 183 us  [the longest x79 115 us: swap(): return lax.ppermute(x, axis, [(k, k ^ r) for k in range(count)])]
    all_to_all x7 -> x0, waiting for transfers between devices: 116 us -> none  [the longest x1 46.7 us: local(): lax.all_to_all(global_keys, 'seq', split_axis=1, concat_axis=0, tiled=True)]
    psum x1 -> x0, waiting for transfers between devices: 101 us -> none  [local(): lax.psum(query_part.astype(jnp.bfloat16), 'dp').astype(jnp.float32)]
    pallas_call x0 -> x10, Pallas kernels: none -> 94.7 us  [call(): pl.pallas_call(body, name=name, in_specs=specs, out_specs=tuple(out_specs...]
    all_gather x2 -> x0, blocking collectives: 64 us -> none  [the longest x1 35.6 us: local(): lax.all_gather(attn_gain, 'seq', axis=0, tiled=True)]
  transfers between devices with their start and end apart: 16 -> 143, of which waited for: 12 -> 56; matrix products, arithmetic and copies ran while one was open for 18% -> 20% of each run, Pallas kernels for 0% -> 10%
where the time goes in v1:
time: 885 us; the launch traced here: 876 us
  waiting for transfers between devices  399 us (45%)
  starting transfers between devices  183 us (21%)
  matrix products  111 us (13%)
  Pallas kernels  94.7 us (11%)
  local copies, waits for them, and re-layouts  46 us (5%)
  other arithmetic  39 us (4%)
    ppermute x32, waiting for transfers between devices, to_right(): return lax.ppermute(x, 'seq', self.right)  184 us
    ppermute x79, waiting for transfers between devices, swap(): return lax.ppermute(x, axis, [(k, k ^ r) for k in range(count)])  119 us
    ppermute x79, starting transfers between devices, swap(): return lax.ppermute(x, axis, [(k, k ^ r) for k in range(count)])  115 us
    ppermute x32, waiting for transfers between devices, to_left(): return lax.ppermute(x, 'seq', self.left)  95.1 us
    pallas_call x10, Pallas kernels, call(): pl.pallas_call(body, name=name, in_specs=specs, out_specs=tuple(out_specs...  94.7 us
    dot_general x27, matrix products, outer_cols(): lax.dot_general(left_side, right_side, (((1,), (1,)), ((), ())), preferre...  45.5 us
    ppermute x32, starting transfers between devices, to_right(): return lax.ppermute(x, 'seq', self.right)  41.3 us
    dot_general x5, matrix products, inner_rows(): lax.dot_general(left_side, right_side, (((0,), (0,)), ((), ())), preferre...  36.3 us
  transfers between devices with their start and end apart: 143, of which 56 were waited for; matrix products, arithmetic and copies ran while one was open for 20% of the time, Pallas kernels for 10%

profile of v1, /device:TPU:0, one launch (start us, length us, event | category | flops | bytes accessed | tf_op | source)
XLA Modules:
  0.0 875.9 jit_solution(6380542783560077584)
XLA Ops:
  5.8 13.3 %collective-permute-done.refs_1_ = bf16[288,1024]{1,0:T(8,128)(2,1)S(1)} collective-permute-done((bf16[288,1024]{1,0:T(8,128)(2,1)S(1)}, bf16[288,1024]{1,0:T(8,128)(2,1)S(1)}, u32[]{:S(2)}, u32[]{:S(2)}) %collective-permute-start) | collective-permute-done | bytes 589856 | tf_op jit(solution)/shard_map/ppermute | solution.py:85
  21.7 12.2 %collective-permute-done.2.refs_3_ = bf16[288,1024]{1,0:T(8,128)(2,1)} collective-permute-done((bf16[288,1024]{1,0:T(8,128)(2,1)S(1)}, bf16[288,1024]{1,0:T(8,128)(2,1)}, u32[]{:S(2)}, u32[]{:S(2)}) %collective-permute-start.2) | collective-permute-done | bytes 589856 | tf_op jit(solution)/shard_map/ppermute | solution.py:85
  35.9 3.7 pack_keys_values.1
  43.2 10.0 %collective-permute-done.24.refs_9_ = bf16[256,512]{1,0:T(8,128)(2,1)S(1)} collective-permute-done((bf16[256,512]{1,0:T(8,128)(2,1)}, bf16[256,512]{1,0:T(8,128)(2,1)S(1)}, u32[]{:S(2)}, u32[]{:S(2)}) %collective-permute-start.24) | collective-permute-done | bytes 262176 | tf_op jit(solution)/shard_map/ppermute | solution.py:92
  53.2 6.5 collective-permute-done.25.refs_10_
  60.2 3.2 collective-permute-done.27.refs_12_
  66.5 9.2 %collective-permute-done.5.refs_6_ = bf16[288,1024]{1,0:T(8,128)(2,1)} collective-permute-done((bf16[288,1024]{1,0:T(8,128)(2,1)}, bf16[288,1024]{1,0:T(8,128)(2,1)}, u32[]{:S(2)}, u32[]{:S(2)}) %collective-permute-start.5) | collective-permute-done | bytes 589856 | tf_op jit(solution)/shard_map/ppermute | solution.py:88
  79.3 5.1 collective-permute-done.6.refs_7_
  87.2 3.7 collective-permute-start.28
  97.3 9.6 %project_queries.1 = (bf16[256,256]{1,0:T(8,128)(2,1)}, bf16[256,256]{1,0:T(8,128)(2,1)}, bf16[256,256]{1,0:T(8,128)(2,1)}, bf16[256,256]{1,0:T(8,128)(2,1)}, bf...) custom-call(s32[11]{0:T(128)} %stack.51.info, ...), custom_call_target="tpu_custom_call" | custom-call | flops 2147483648 | bytes 25165824 | tf_op jit(solution)/shard_map/project_queries/pallas_call | solution.py:140
  106.9 8.0 collective-permute-done.28.refs_13_
  114.9 3.8 collective-permute-start.23
  118.7 10.8 %collective-permute-start.18 = (bf16[256,256]{1,0:T(8,128)(2,1)}, bf16[256,256]{1,0:T(8,128)(2,1)S(1)}, u32[]{:S(2)}, u32[]{:S(2)}) collective-permute-start(bf16[256,256]{1,0:T(8,128)(2,1)} %get-tuple-element.105), channel_id=1, source_target_pairs={{0,2},{1,3},{2,0},{3,1},{4,6},{5,7},{6,4},{7,5},{8,10},{9,11},{10,... | collective-permute-start | bytes 393224 | tf_op jit(solution)/shard_map/ppermute | solution.py:92
  129.5 4.4 collective-permute-start.19
  148.1 6.6 collective-permute-done.21.refs_5_
  156.7 17.8 %attention_forward.1 = (bf16[256,256]{1,0:T(8,128)(2,1)}, bf16[256,256]{1,0:T(8,128)(2,1)}, bf16[256,256]{1,0:T(8,128)(2,1)}, bf16[256,256]{1,0:T(8,128)(2,1)}, ...) custom-call(s32[2]{0:T(128)} %pad_add_fusion.info, ...), custom_call_target="tpu_custom_call" | custom-call | flops 17179869184 | bytes 5242880 | tf_op jit(solution)/shard_map/attention_forward/pallas_call | solution.py:140
  178.5 6.3 collective-permute-done.42.refs_5_
  184.9 4.5 collective-permute-start.45
  194.1 3.6 stack_ring.1.refs_8_
  199.2 3.2 pad_maximum_fusion
  215.3 12.9 %collective-permute-done.51 = bf16[256,2048]{1,0:T(8,128)(2,1)S(1)} collective-permute-done((bf16[256,2048]{1,0:T(8,128)(2,1)}, bf16[256,2048]{1,0:T(8,128)(2,1)S(1)}, u32[]{:S(2)}, u32[]{:S(2)}) %collective-permute-start.51) | collective-permute-done | bytes 1048608 | tf_op jit(solution)/shard_map/ppermute | solution.py:85
  236.1 8.6 collective-permute-done.47.refs_10_
  244.7 8.3 collective-permute-done.53
  260.9 4.8 collective-permute-done.67
  277.6 9.5 %collective-permute-done.34.refs_4_ = bf16[256,256]{1,0:T(8,128)(2,1)S(1)} collective-permute-done((bf16[256,256]{1,0:T(8,128)(2,1)S(1)}, bf16[256,256]{1,0:T(8,128)(2,1)S(1)}, u32[]{:S(2)}, u32[]{:S(2)}) %collective-permute-start.34) | collective-permute-done | bytes 131104 | tf_op jit(solution)/shard_map/ppermute | solution.py:92
  290.5 4.4 collective-permute-done.37.refs_7_
  297.5 10.4 %project_mixed.1 = (f32[256,2048]{1,0:T(8,128)}, bf16[256,2048]{1,0:T(8,128)(2,1)}, bf16[256,2048]{1,0:T(8,128)(2,1)}, bf16[2048,2048]{1,0:T(8,128)(2,1)}) custom-call(s32[11]{0:T(128)} %stack.51.info, bf16[256,2048]{1,0:T(8,128)(2,1)} %x.7, f32[8,2048]{1,0:T(8,128)} %get-tuple-element.102.gains, bf16[256,256]{1,0:T(8,128)(2,1)} %get-tuple-element.119.refs_0_, ...), custom_call_target="tpu_custom_call" | custom-call | flops 2147483648 | bytes 25165824 | tf_op jit(solution)/shard_map/project_mixed/pallas_call | solution.py:140
  316.2 13.2 %collective-permute-done.50 = bf16[256,2048]{1,0:T(8,128)(2,1)S(1)} collective-permute-done((bf16[256,2048]{1,0:T(8,128)(2,1)}, bf16[256,2048]{1,0:T(8,128)(2,1)S(1)}, u32[]{:S(2)}, u32[]{:S(2)}) %collective-permute-start.50) | collective-permute-done | bytes 1048608 | tf_op jit(solution)/shard_map/ppermute | solution.py:85
  342.6 16.3 %collective-permute-done.52 = bf16[256,2048]{1,0:T(8,128)(2,1)S(1)} collective-permute-done((bf16[256,2048]{1,0:T(8,128)(2,1)S(1)}, bf16[256,2048]{1,0:T(8,128)(2,1)S(1)}, u32[]{:S(2)}, u32[]{:S(2)}) %collective-permute-start.52) | collective-permute-done | bytes 1048608 | tf_op jit(solution)/shard_map/ppermute | solution.py:85
  374.6 19.0 %collective-permute-done.54 = bf16[256,2048]{1,0:T(8,128)(2,1)S(1)} collective-permute-done((bf16[256,2048]{1,0:T(8,128)(2,1)S(1)}, bf16[256,2048]{1,0:T(8,128)(2,1)S(1)}, u32[]{:S(2)}, u32[]{:S(2)}) %collective-permute-start.54) | collective-permute-done | bytes 1048608 | tf_op jit(solution)/shard_map/ppermute | solution.py:85
  415.2 9.5 %convolution_convert_fusion = bf16[688,2048]{1,0:T(8,128)(2,1)S(1)} fusion(bf16[2048,688]{0,1:T(8,128)(2,1)} %get-tuple-element.195, bf16[2048,2048]{1,0:T(8,128)(2,1)} %constant_dynamic-update-slice_fusion.38), kind=kOutput, calls=%fused_computation.12 | convolution fusion | flops 5772771328 | bytes 14024704 | tf_op jit(solution)/shard_map/dot_general | solution.py:22
  426.6 9.3 %convolution_convert_fusion.1 = bf16[688,2048]{1,0:T(8,128)(2,1)S(1)} fusion(bf16[2048,688]{0,1:T(8,128)(2,1)} %get-tuple-element.309, bf16[2048,2048]{1,0:T(8,128)(2,1)} %constant_dynamic-update-slice_fusion.11), kind=kOutput, calls=%fused_computation.13 | convolution fusion | flops 5772771328 | bytes 14024704 | tf_op jit(solution)/shard_map/dot_general | solution.py:22
  441.2 10.5 %collective-permute-done.69 = bf16[128,2048]{1,0:T(8,128)(2,1)S(1)} collective-permute-done((bf16[128,2048]{1,0:T(8,128)(2,1)S(1)}, bf16[128,2048]{1,0:T(8,128)(2,1)S(1)}, u32[]{:S(2)}, u32[]{:S(2)}) %collective-permute-start.69) | collective-permute-done | bytes 524320 | tf_op jit(solution)/shard_map/ppermute | solution.py:85
  455.0 9.3 %convolution_convert_fusion.2 = bf16[688,2048]{1,0:T(8,128)(2,1)S(1)} fusion(bf16[2048,688]{0,1:T(8,128)(2,1)} %get-tuple-element.307, bf16[2048,2048]{1,0:T(8,128)(2,1)} %constant_dynamic-update-slice_fusion.11), kind=kOutput, calls=%fused_computation.14 | convolution fusion | flops 5772771328 | bytes 14024704 | tf_op jit(solution)/shard_map/dot_general | solution.py:22
  464.4 11.8 %collective-permute-done.70 = bf16[256,2048]{1,0:T(8,128)(2,1)S(1)} collective-permute-done((bf16[256,2048]{1,0:T(8,128)(2,1)S(1)}, bf16[256,2048]{1,0:T(8,128)(2,1)S(1)}, u32[]{:S(2)}, u32[]{:S(2)}) %collective-permute-start.70) | collective-permute-done | bytes 1048608 | tf_op jit(solution)/shard_map/ppermute | solution.py:85
  482.9 19.2 %collective-permute-done.71 = bf16[256,2048]{1,0:T(8,128)(2,1)S(1)} collective-permute-done((bf16[256,2048]{1,0:T(8,128)(2,1)S(1)}, bf16[256,2048]{1,0:T(8,128)(2,1)S(1)}, u32[]{:S(2)}, u32[]{:S(2)}) %collective-permute-start.71) | collective-permute-done | bytes 1048608 | tf_op jit(solution)/shard_map/ppermute | solution.py:85
  517.4 10.5 %collective-permute-done.72.second = bf16[256,2048]{1,0:T(8,128)(2,1)S(1)} collective-permute-done((bf16[256,2048]{1,0:T(8,128)(2,1)S(1)}, bf16[256,2048]{1,0:T(8,128)(2,1)S(1)}, u32[]{:S(2)}, u32[]{:S(2)}) %collective-permute-start.72) | collective-permute-done | bytes 1048608 | tf_op jit(solution)/shard_map/ppermute | solution.py:85
  528.8 10.1 %branch_gradient.1 = (bf16[256,256]{1,0:T(8,128)(2,1)}, bf16[256,256]{1,0:T(8,128)(2,1)}, bf16[256,256]{1,0:T(8,128)(2,1)}, bf16[256,256]{1,0:T(8,128)(2,1)}, bf...) custom-call(s32[11]{0:T(128)} %stack.51.info, ...), custom_call_target="tpu_custom_call" | custom-call | flops 2147483648 | bytes 25165824 | tf_op jit(solution)/shard_map/branch_gradient/pallas_call | solution.py:140
  541.9 4.1 collective-permute-done.138
  550.8 22.4 %collective-permute-done.135 = bf16[688,1024]{1,0:T(8,128)(2,1)S(1)} collective-permute-done((bf16[688,1024]{1,0:T(8,128)(2,1)S(1)}, bf16[688,1024]{1,0:T(8,128)(2,1)S(1)}, u32[]{:S(2)}, u32[]{:S(2)}) %collective-permute-start.135) | collective-permute-done | bytes 1409056 | tf_op jit(solution)/shard_map/ppermute | solution.py:92
  581.7 4.8 collective-permute-done.85.refs_20_
  587.1 4.0 collective-permute-done.86.refs_21_
  591.7 22.2 %attention_backward.1 = (bf16[256,256]{1,0:T(8,128)(2,1)}, bf16[256,256]{1,0:T(8,128)(2,1)}, bf16[256,256]{1,0:T(8,128)(2,1)}, bf16[256,256]{1,0:T(8,128)(2,1)},...) custom-call(s32[2]{0:T(128)} %pad_add_fusion.info, ...), custom_call_target="tpu_custom_call" | custom-call | flops 42949672960 | bytes 10485760 | tf_op jit(solution)/shard_map/attention_backward/pallas_call | solution.py:140
  632.7 3.8 fusion.6
  639.3 3.5 collective-permute-done.91.refs_4_
  648.0 3.3 sort_columns.1
  651.5 10.3 %input_gradient.1 = (bf16[256,2048]{1,0:T(8,128)(2,1)}, f32[8,2048]{1,0:T(8,128)}) custom-call(bf16[256,2048]{1,0:T(8,128)(2,1)} %x.7, f32[8,2048]{1,0:T(8,128)} %get-tuple-element.102.gains, bf16[256,2048]{1,0:T(8,128)(2,1)} %get-tuple-element.159.grad_query, f32[256,2048]{1,0:T(8,128)} %get-tuple-element.160.grad_hidden, ...), custom_call_target="tpu_custom_call" | custom-call | flops 2147483648 | bytes 25165824 | tf_op jit(solution)/shard_map/input_gradient/pallas_call | solution.py:140
  668.3 4.9 collective-permute-start.99
  677.3 4.0 collective-permute-done.100.refs_6_
  681.3 23.5 %collective-permute-start.97 = (bf16[256,512]{1,0:T(8,128)(2,1)}, bf16[256,512]{1,0:T(8,128)(2,1)S(1)}, u32[]{:S(2)}, u32[]{:S(2)}) collective-permute-start(bf16[256,512]{1,0:T(8,128)(2,1)} %get-tuple-element.170), channel_id=1, source_target_pairs={{0,3},{1,2},{2,1},{3,0},{4,7},{5,6},{6,5},{7,4},{8,11},{9,10},{10,... | collective-permute-start | bytes 786440 | tf_op jit(solution)/shard_map/ppermute | solution.py:92
  704.9 5.1 collective-permute-done.99.refs_5_
  710.0 4.1 collective-permute-done.98.refs_4_
  716.1 4.5 fusion
  727.4 3.7 split_keys_values.1
  736.8 3.2 maximum_convert_fusion.2
  740.4 3.2 maximum_convert_fusion.1
  747.3 3.6 maximum_convert_fusion
  759.4 3.9 collective-permute-done.125
  763.6 6.1 collective-permute-done.108
  775.3 23.1 %collective-permute-done.109 = bf16[288,512]{1,0:T(8,128)(2,1)S(1)} collective-permute-done((bf16[288,512]{1,0:T(8,128)(2,1)S(1)}, bf16[288,512]{1,0:T(8,128)(2,1)S(1)}, u32[]{:S(2)}, u32[]{:S(2)}) %collective-permute-start.109) | collective-permute-done | bytes 294944 | tf_op jit(solution)/shard_map/ppermute | solution.py:88
  800.8 3.2 collective-permute-done.126
  810.7 17.1 %collective-permute-done.79 = bf16[256,2048]{1,0:T(8,128)(2,1)S(1)} collective-permute-done((bf16[256,2048]{1,0:T(8,128)(2,1)S(1)}, bf16[256,2048]{1,0:T(8,128)(2,1)S(1)}, u32[]{:S(2)}, u32[]{:S(2)}) %collective-permute-start.79) | collective-permute-done | bytes 1048608 | tf_op jit(solution)/shard_map/ppermute | solution.py:85
  831.9 18.2 %collective-permute-done.76 = bf16[256,2048]{1,0:T(8,128)(2,1)S(1)} collective-permute-done((bf16[256,2048]{1,0:T(8,128)(2,1)S(1)}, bf16[256,2048]{1,0:T(8,128)(2,1)S(1)}, u32[]{:S(2)}, u32[]{:S(2)}) %collective-permute-start.76) | collective-permute-done | bytes 1048608 | tf_op jit(solution)/shard_map/ppermute | solution.py:88
  855.1 17.0 %collective-permute-done.77 = bf16[256,2048]{1,0:T(8,128)(2,1)S(1)} collective-permute-done((bf16[256,2048]{1,0:T(8,128)(2,1)S(1)}, bf16[256,2048]{1,0:T(8,128)(2,1)S(1)}, u32[]{:S(2)}, u32[]{:S(2)}) %collective-permute-start.77) | collective-permute-done | bytes 1048608 | tf_op jit(solution)/shard_map/ppermute | solution.py:88
  (646 shorter events, 302.3 us)
Async XLA Ops:
  20.8 38.8 %collective-permute-start.3 = (bf16[288,1024]{1,0:T(8,128)(2,1)}, bf16[288,1024]{1,0:T(8,128)(2,1)}, u32[]{:S(2)}, u32[]{:S(2)}) collective-permute-start(bf16[288,1024]{1,0:T(8,128)(2,1)} %collective-permute-done.1.refs_2_), channel_id=1, source_target_pairs={{3,1},{5,3},{7,5},{6,7},{4,6},{2,4},{0,2},{1,0},{11,9},{13,11},{15... | collective-permute-start | bytes 1769480 | tf_op jit(solution)/shard_map/ppermute | solution.py:88
  33.8 29.6 %collective-permute-start.4 = (bf16[288,1024]{1,0:T(8,128)(2,1)}, bf16[288,1024]{1,0:T(8,128)(2,1)}, u32[]{:S(2)}, u32[]{:S(2)}) collective-permute-start(bf16[288,1024]{1,0:T(8,128)(2,1)} %collective-permute-done.2.refs_3_), channel_id=1, source_target_pairs={{1,3},{3,5},{5,7},{7,6},{6,4},{4,2},{2,0},{0,1},{9,11},{11,13},{13... | collective-permute-start | bytes 1769480 | tf_op jit(solution)/shard_map/ppermute | solution.py:85
  87.2 27.7 %collective-permute-start.28 = (bf16[256,512]{1,0:T(8,128)(2,1)}, bf16[256,512]{1,0:T(8,128)(2,1)S(1)}, u32[]{:S(2)}, u32[]{:S(2)}) collective-permute-start(bf16[256,512]{1,0:T(8,128)(2,1)} %get-tuple-element.116), channel_id=1, source_target_pairs={{0,5},{1,4},{2,7},{3,6},{4,1},{5,0},{6,3},{7,2},{8,13},{9,12},{10,... | collective-permute-start | bytes 786440 | tf_op jit(solution)/shard_map/ppermute | solution.py:92
  90.9 27.7 %collective-permute-start.29 = (bf16[256,512]{1,0:T(8,128)(2,1)}, bf16[256,512]{1,0:T(8,128)(2,1)S(1)}, u32[]{:S(2)}, u32[]{:S(2)}) collective-permute-start(bf16[256,512]{1,0:T(8,128)(2,1)} %get-tuple-element.117), channel_id=1, source_target_pairs={{0,6},{1,7},{2,4},{3,5},{4,2},{5,3},{6,0},{7,1},{8,14},{9,15},{10,... | collective-permute-start | bytes 786440 | tf_op jit(solution)/shard_map/ppermute | solution.py:92
  93.3 25.4 %collective-permute-start.30 = (bf16[256,512]{1,0:T(8,128)(2,1)}, bf16[256,512]{1,0:T(8,128)(2,1)S(1)}, u32[]{:S(2)}, u32[]{:S(2)}) collective-permute-start(bf16[256,512]{1,0:T(8,128)(2,1)} %get-tuple-element.118), channel_id=1, source_target_pairs={{0,7},{1,6},{2,5},{3,4},{4,3},{5,2},{6,1},{7,0},{8,15},{9,14},{10,... | collective-permute-start | bytes 786440 | tf_op jit(solution)/shard_map/ppermute | solution.py:92
  94.2 35.3 %collective-permute-start.38 = (bf16[256,512]{1,0:T(8,128)(2,1)S(1)}, bf16[256,512]{1,0:T(8,128)(2,1)S(1)}, u32[]{:S(2)}, u32[]{:S(2)}) collective-permute-start(bf16[256,512]{1,0:T(8,128)(2,1)S(1)} %constant_dynamic-slice_fusion.22.refs_0_), channel_id=1, source_target_pairs={{1,3},{3,5},{5,7},{7,6},{6,4},{4,2},{2,0},{0,1},{9,11},{11,13},{13... | collective-permute-start | bytes 786440 | tf_op jit(solution)/shard_map/ppermute | solution.py:85
  97.3 36.6 %collective-permute-start.39 = (bf16[256,512]{1,0:T(8,128)(2,1)S(1)}, bf16[256,512]{1,0:T(8,128)(2,1)S(1)}, u32[]{:S(2)}, u32[]{:S(2)}) collective-permute-start(bf16[256,512]{1,0:T(8,128)(2,1)S(1)} %constant_dynamic-slice_fusion.22.refs_0_), channel_id=1, source_target_pairs={{3,1},{5,3},{7,5},{6,7},{4,6},{2,4},{0,2},{1,0},{11,9},{13,11},{15... | collective-permute-start | bytes 786440 | tf_op jit(solution)/shard_map/ppermute | solution.py:88
  114.9 22.4 %collective-permute-start.23 = (bf16[256,256]{1,0:T(8,128)(2,1)}, bf16[256,256]{1,0:T(8,128)(2,1)S(1)}, u32[]{:S(2)}, u32[]{:S(2)}) collective-permute-start(bf16[256,256]{1,0:T(8,128)(2,1)} %get-tuple-element.110), channel_id=1, source_target_pairs={{0,7},{1,6},{2,5},{3,4},{4,3},{5,2},{6,1},{7,0},{8,15},{9,14},{10,... | collective-permute-start | bytes 393224 | tf_op jit(solution)/shard_map/ppermute | solution.py:92
  118.7 25.9 %collective-permute-start.18 = (bf16[256,256]{1,0:T(8,128)(2,1)}, bf16[256,256]{1,0:T(8,128)(2,1)S(1)}, u32[]{:S(2)}, u32[]{:S(2)}) collective-permute-start(bf16[256,256]{1,0:T(8,128)(2,1)} %get-tuple-element.105), channel_id=1, source_target_pairs={{0,2},{1,3},{2,0},{3,1},{4,6},{5,7},{6,4},{7,5},{8,10},{9,11},{10,... | collective-permute-start | bytes 393224 | tf_op jit(solution)/shard_map/ppermute | solution.py:92
  144.6 30.0 %collective-permute-start.40 = (bf16[256,512]{1,0:T(8,128)(2,1)}, bf16[256,512]{1,0:T(8,128)(2,1)S(1)}, u32[]{:S(2)}, u32[]{:S(2)}) collective-permute-start(bf16[256,512]{1,0:T(8,128)(2,1)} %copy-done.43), channel_id=1, source_target_pairs={{1,3},{3,5},{5,7},{7,6},{6,4},{4,2},{2,0},{0,1},{9,11},{11,13},{13... | collective-permute-start | bytes 786440 | tf_op jit(solution)/shard_map/ppermute | solution.py:85
  144.6 30.1 %collective-permute-start.41 = (bf16[256,512]{1,0:T(8,128)(2,1)}, bf16[256,512]{1,0:T(8,128)(2,1)S(1)}, u32[]{:S(2)}, u32[]{:S(2)}) collective-permute-start(bf16[256,512]{1,0:T(8,128)(2,1)} %copy-done.44), channel_id=1, source_target_pairs={{3,1},{5,3},{7,5},{6,7},{4,6},{2,4},{0,2},{1,0},{11,9},{13,11},{15... | collective-permute-start | bytes 786440 | tf_op jit(solution)/shard_map/ppermute | solution.py:88
  146.6 52.6 %collective-permute-start.102 = (bf16[256,2048]{1,0:T(8,128)(2,1)}, bf16[256,2048]{1,0:T(8,128)(2,1)}, u32[]{:S(2)}, u32[]{:S(2)}) collective-permute-start(bf16[256,2048]{1,0:T(8,128)(2,1)} %get-tuple-element.181), channel_id=1, source_target_pairs={{0,16},{8,24},{16,0},{24,8},{1,17},{9,25},{17,1},{25,9},{2,18},{10... | collective-permute-start | bytes 3145736 | tf_op jit(solution)/shard_map/ppermute | solution.py:92
  154.7 47.7 %collective-permute-start.49 = (bf16[256,2048]{1,0:T(8,128)(2,1)}, bf16[256,2048]{1,0:T(8,128)(2,1)}, u32[]{:S(2)}, u32[]{:S(2)}) collective-permute-start(bf16[256,2048]{1,0:T(8,128)(2,1)} %cotangent.1), channel_id=1, source_target_pairs={{1,3},{3,5},{5,7},{7,6},{6,4},{4,2},{2,0},{0,1},{9,11},{11,13},{13... | collective-permute-start | bytes 3145736 | tf_op jit(solution)/shard_map/ppermute | solution.py:85
  154.7 49.1 %collective-permute-start.55 = (bf16[256,2048]{1,0:T(8,128)(2,1)}, bf16[256,2048]{1,0:T(8,128)(2,1)}, u32[]{:S(2)}, u32[]{:S(2)}) collective-permute-start(bf16[256,2048]{1,0:T(8,128)(2,1)} %cotangent.1), channel_id=1, source_target_pairs={{3,1},{5,3},{7,5},{6,7},{4,6},{2,4},{0,2},{1,0},{11,9},{13,11},{15... | collective-permute-start | bytes 3145736 | tf_op jit(solution)/shard_map/ppermute | solution.py:88
  192.8 78.4 %collective-permute-start.31 = (bf16[256,256]{1,0:T(8,128)(2,1)}, bf16[256,256]{1,0:T(8,128)(2,1)S(1)}, u32[]{:S(2)}, u32[]{:S(2)}) collective-permute-start(bf16[256,256]{1,0:T(8,128)(2,1)} %get-tuple-element.120), channel_id=1, source_target_pairs={{0,1},{1,0},{2,3},{3,2},{4,5},{5,4},{6,7},{7,6},{8,9},{9,8},{10,11... | collective-permute-start | bytes 393224 | tf_op jit(solution)/shard_map/ppermute | solution.py:92
  197.6 47.0 %collective-permute-start.47 = (bf16[2048,512]{1,0:T(8,128)(2,1)}, bf16[2048,512]{1,0:T(8,128)(2,1)S(1)}, u32[]{:S(2)}, u32[]{:S(2)}) collective-permute-start(bf16[2048,512]{1,0:T(8,128)(2,1)} %stack_ring.1.refs_8_), channel_id=1, source_target_pairs={{0,16},{8,24},{16,0},{24,8},{1,17},{9,25},{17,1},{25,9},{2,18},{10... | collective-permute-start | bytes 6291464 | tf_op jit(solution)/shard_map/ppermute | solution.py:92
  199.2 95.6 %collective-permute-start.46 = (bf16[2048,512]{1,0:T(8,128)(2,1)}, bf16[2048,512]{1,0:T(8,128)(2,1)S(1)}, u32[]{:S(2)}, u32[]{:S(2)}) collective-permute-start(bf16[2048,512]{1,0:T(8,128)(2,1)} %stack_ring.1.refs_8_), channel_id=1, source_target_pairs={{0,8},{8,0},{16,24},{24,16},{1,9},{9,1},{17,25},{25,17},{2,10},{10... | collective-permute-start | bytes 6291464 | tf_op jit(solution)/shard_map/ppermute | solution.py:92
  202.4 25.8 %collective-permute-start.51 = (bf16[256,2048]{1,0:T(8,128)(2,1)}, bf16[256,2048]{1,0:T(8,128)(2,1)S(1)}, u32[]{:S(2)}, u32[]{:S(2)}) collective-permute-start(bf16[256,2048]{1,0:T(8,128)(2,1)} %collective-permute-done.49), channel_id=1, source_target_pairs={{1,3},{3,5},{5,7},{7,6},{6,4},{4,2},{2,0},{0,1},{9,11},{11,13},{13... | collective-permute-start | bytes 3145736 | tf_op jit(solution)/shard_map/ppermute | solution.py:85
  203.8 25.8 %collective-permute-start.56 = (bf16[256,2048]{1,0:T(8,128)(2,1)}, bf16[256,2048]{1,0:T(8,128)(2,1)S(1)}, u32[]{:S(2)}, u32[]{:S(2)}) collective-permute-start(bf16[256,2048]{1,0:T(8,128)(2,1)} %collective-permute-done.55), channel_id=1, source_target_pairs={{3,1},{5,3},{7,5},{6,7},{4,6},{2,4},{0,2},{1,0},{11,9},{13,11},{15... | collective-permute-start | bytes 3145736 | tf_op jit(solution)/shard_map/ppermute | solution.py:88
  228.1 24.8 %collective-permute-start.53 = (bf16[256,2048]{1,0:T(8,128)(2,1)S(1)}, bf16[256,2048]{1,0:T(8,128)(2,1)S(1)}, u32[]{:S(2)}, u32[]{:S(2)}) collective-permute-start(bf16[256,2048]{1,0:T(8,128)(2,1)S(1)} %collective-permute-done.51), channel_id=1, source_target_pairs={{1,3},{3,5},{5,7},{7,6},{6,4},{4,2},{2,0},{0,1},{9,11},{11,13},{13... | collective-permute-start | bytes 3145736 | tf_op jit(solution)/shard_map/ppermute | solution.py:85
  229.6 24.9 %collective-permute-start.57 = (bf16[256,2048]{1,0:T(8,128)(2,1)S(1)}, bf16[256,2048]{1,0:T(8,128)(2,1)S(1)}, u32[]{:S(2)}, u32[]{:S(2)}) collective-permute-start(bf16[256,2048]{1,0:T(8,128)(2,1)S(1)} %collective-permute-done.56), channel_id=1, source_target_pairs={{3,1},{5,3},{7,5},{6,7},{4,6},{2,4},{0,2},{1,0},{11,9},{13,11},{15... | collective-permute-start | bytes 3145736 | tf_op jit(solution)/shard_map/ppermute | solution.py:88
  244.7 50.2 %collective-permute-start.48 = (bf16[2048,512]{1,0:T(8,128)(2,1)S(1)}, bf16[2048,512]{1,0:T(8,128)(2,1)S(1)}, u32[]{:S(2)}, u32[]{:S(2)}) collective-permute-start(bf16[2048,512]{1,0:T(8,128)(2,1)S(1)} %collective-permute-done.47.refs_10_), channel_id=1, source_target_pairs={{0,8},{8,0},{16,24},{24,16},{1,9},{9,1},{17,25},{25,17},{2,10},{10... | collective-permute-start | bytes 6291464 | tf_op jit(solution)/shard_map/ppermute | solution.py:92
  312.5 194.6 %collective-permute-start.118 = (bf16[256,2048]{1,0:T(8,128)(2,1)S(1)}, bf16[256,2048]{1,0:T(8,128)(2,1)}, u32[]{:S(2)}, u32[]{:S(2)}) collective-permute-start(bf16[256,2048]{1,0:T(8,128)(2,1)S(1)} %copy-done.27), channel_id=1, source_target_pairs={{0,16},{8,24},{16,0},{24,8},{1,17},{9,25},{17,1},{25,9},{2,18},{10... | collective-permute-start | bytes 3145736 | tf_op jit(solution)/shard_map/ppermute | solution.py:92
  370.3 23.3 %collective-permute-start.54 = (bf16[256,2048]{1,0:T(8,128)(2,1)S(1)}, bf16[256,2048]{1,0:T(8,128)(2,1)S(1)}, u32[]{:S(2)}, u32[]{:S(2)}) collective-permute-start(bf16[256,2048]{1,0:T(8,128)(2,1)S(1)} %collective-permute-done.52), channel_id=1, source_target_pairs={{1,3},{3,5},{5,7},{7,6},{6,4},{4,2},{2,0},{0,1},{9,11},{11,13},{13... | collective-permute-start | bytes 3145736 | tf_op jit(solution)/shard_map/ppermute | solution.py:85
  371.8 23.3 %collective-permute-start.61 = (bf16[256,2048]{1,0:T(8,128)(2,1)S(1)}, bf16[256,2048]{1,0:T(8,128)(2,1)S(1)}, u32[]{:S(2)}, u32[]{:S(2)}) collective-permute-start(bf16[256,2048]{1,0:T(8,128)(2,1)S(1)} %collective-permute-done.60), channel_id=1, source_target_pairs={{3,1},{5,3},{7,5},{6,7},{4,6},{2,4},{0,2},{1,0},{11,9},{13,11},{15... | collective-permute-start | bytes 3145736 | tf_op jit(solution)/shard_map/ppermute | solution.py:88
  424.8 54.2 %collective-permute-start.140 = (bf16[688,1024]{1,0:T(8,128)(2,1)S(1)}, bf16[688,1024]{1,0:T(8,128)(2,1)S(1)}, u32[]{:S(2)}, u32[]{:S(2)}) collective-permute-start(bf16[688,1024]{1,0:T(8,128)(2,1)S(1)} %constant_dynamic-slice_fusion.5), channel_id=1, source_target_pairs={{0,8},{8,0},{16,24},{24,16},{1,9},{9,1},{17,25},{25,17},{2,10},{10... | collective-permute-start | bytes 4227080 | tf_op jit(solution)/shard_map/ppermute | solution.py:92
  436.1 45.7 %collective-permute-start.137 = (bf16[688,1024]{1,0:T(8,128)(2,1)S(1)}, bf16[688,1024]{1,0:T(8,128)(2,1)S(1)}, u32[]{:S(2)}, u32[]{:S(2)}) collective-permute-start(bf16[688,1024]{1,0:T(8,128)(2,1)S(1)} %constant_dynamic-slice_fusion.6), channel_id=1, source_target_pairs={{0,8},{8,0},{16,24},{24,16},{1,9},{9,1},{17,25},{25,17},{2,10},{10... | collective-permute-start | bytes 4227080 | tf_op jit(solution)/shard_map/ppermute | solution.py:92
  452.0 24.3 %collective-permute-start.70 = (bf16[256,2048]{1,0:T(8,128)(2,1)S(1)}, bf16[256,2048]{1,0:T(8,128)(2,1)S(1)}, u32[]{:S(2)}, u32[]{:S(2)}) collective-permute-start(bf16[256,2048]{1,0:T(8,128)(2,1)S(1)} %pad_maximum_fusion.3), channel_id=1, source_target_pairs={{1,3},{3,5},{5,7},{7,6},{6,4},{4,2},{2,0},{0,1},{9,11},{11,13},{13... | collective-permute-start | bytes 3145736 | tf_op jit(solution)/shard_map/ppermute | solution.py:85
  454.4 24.0 %collective-permute-start.64 = (bf16[256,2048]{1,0:T(8,128)(2,1)S(1)}, bf16[256,2048]{1,0:T(8,128)(2,1)S(1)}, u32[]{:S(2)}, u32[]{:S(2)}) collective-permute-start(bf16[256,2048]{1,0:T(8,128)(2,1)S(1)} %pad_maximum_fusion.2), channel_id=1, source_target_pairs={{3,1},{5,3},{7,5},{6,7},{4,6},{2,4},{0,2},{1,0},{11,9},{13,11},{15... | collective-permute-start | bytes 3145736 | tf_op jit(solution)/shard_map/ppermute | solution.py:88
  476.2 28.6 %collective-permute-start.134 = (bf16[688,1024]{1,0:T(8,128)(2,1)S(1)}, bf16[688,1024]{1,0:T(8,128)(2,1)S(1)}, u32[]{:S(2)}, u32[]{:S(2)}) collective-permute-start(bf16[688,1024]{1,0:T(8,128)(2,1)S(1)} %constant_dynamic-slice_fusion.7), channel_id=1, source_target_pairs={{0,8},{8,0},{16,24},{24,16},{1,9},{9,1},{17,25},{25,17},{2,10},{10... | collective-permute-start | bytes 4227080 | tf_op jit(solution)/shard_map/ppermute | solution.py:92
  478.4 23.8 %collective-permute-start.71 = (bf16[256,2048]{1,0:T(8,128)(2,1)S(1)}, bf16[256,2048]{1,0:T(8,128)(2,1)S(1)}, u32[]{:S(2)}, u32[]{:S(2)}) collective-permute-start(bf16[256,2048]{1,0:T(8,128)(2,1)S(1)} %add_convert_fusion.7), channel_id=1, source_target_pairs={{1,3},{3,5},{5,7},{7,6},{6,4},{4,2},{2,0},{0,1},{9,11},{11,13},{13... | collective-permute-start | bytes 3145736 | tf_op jit(solution)/shard_map/ppermute | solution.py:85
  479.0 25.1 %collective-permute-start.65 = (bf16[256,2048]{1,0:T(8,128)(2,1)S(1)}, bf16[256,2048]{1,0:T(8,128)(2,1)S(1)}, u32[]{:S(2)}, u32[]{:S(2)}) collective-permute-start(bf16[256,2048]{1,0:T(8,128)(2,1)S(1)} %add_convert_fusion.9), channel_id=1, source_target_pairs={{3,1},{5,3},{7,5},{6,7},{4,6},{2,4},{0,2},{1,0},{11,9},{13,11},{15... | collective-permute-start | bytes 3145736 | tf_op jit(solution)/shard_map/ppermute | solution.py:88
  481.7 33.9 %collective-permute-start.141 = (bf16[688,1024]{1,0:T(8,128)(2,1)S(1)}, bf16[688,1024]{1,0:T(8,128)(2,1)S(1)}, u32[]{:S(2)}, u32[]{:S(2)}) collective-permute-start(bf16[688,1024]{1,0:T(8,128)(2,1)S(1)} %add_convert_fusion.1), channel_id=1, source_target_pairs={{0,16},{8,24},{16,0},{24,8},{1,17},{9,25},{17,1},{25,9},{2,18},{10... | collective-permute-start | bytes 4227080 | tf_op jit(solution)/shard_map/ppermute | solution.py:92
  502.2 43.8 %collective-permute-start.138 = (bf16[688,1024]{1,0:T(8,128)(2,1)S(1)}, bf16[688,1024]{1,0:T(8,128)(2,1)}, u32[]{:S(2)}, u32[]{:S(2)}) collective-permute-start(bf16[688,1024]{1,0:T(8,128)(2,1)S(1)} %add_convert_fusion.3), channel_id=1, source_target_pairs={{0,16},{8,24},{16,0},{24,8},{1,17},{9,25},{17,1},{25,9},{2,18},{10... | collective-permute-start | bytes 4227080 | tf_op jit(solution)/shard_map/ppermute | solution.py:92
  504.1 23.8 %collective-permute-start.72 = (bf16[256,2048]{1,0:T(8,128)(2,1)S(1)}, bf16[256,2048]{1,0:T(8,128)(2,1)S(1)}, u32[]{:S(2)}, u32[]{:S(2)}) collective-permute-start(bf16[256,2048]{1,0:T(8,128)(2,1)S(1)} %add_convert_fusion.6), channel_id=1, source_target_pairs={{1,3},{3,5},{5,7},{7,6},{6,4},{4,2},{2,0},{0,1},{9,11},{11,13},{13... | collective-permute-start | bytes 3145736 | tf_op jit(solution)/shard_map/ppermute | solution.py:85
  504.9 23.7 %collective-permute-start.66 = (bf16[256,2048]{1,0:T(8,128)(2,1)S(1)}, bf16[256,2048]{1,0:T(8,128)(2,1)}, u32[]{:S(2)}, u32[]{:S(2)}) collective-permute-start(bf16[256,2048]{1,0:T(8,128)(2,1)S(1)} %add_convert_fusion.8), channel_id=1, source_target_pairs={{3,1},{5,3},{7,5},{6,7},{4,6},{2,4},{0,2},{1,0},{11,9},{13,11},{15... | collective-permute-start | bytes 3145736 | tf_op jit(solution)/shard_map/ppermute | solution.py:88
  507.1 66.1 %collective-permute-start.135 = (bf16[688,1024]{1,0:T(8,128)(2,1)S(1)}, bf16[688,1024]{1,0:T(8,128)(2,1)S(1)}, u32[]{:S(2)}, u32[]{:S(2)}) collective-permute-start(bf16[688,1024]{1,0:T(8,128)(2,1)S(1)} %add_convert_fusion.5), channel_id=1, source_target_pairs={{0,16},{8,24},{16,0},{24,8},{1,17},{9,25},{17,1},{25,9},{2,18},{10... | collective-permute-start | bytes 4227080 | tf_op jit(solution)/shard_map/ppermute | solution.py:92
  538.9 35.5 %collective-permute-start.73 = (bf16[256,256]{1,0:T(8,128)(2,1)}, bf16[256,256]{1,0:T(8,128)(2,1)S(1)}, u32[]{:S(2)}, u32[]{:S(2)}) collective-permute-start(bf16[256,256]{1,0:T(8,128)(2,1)} %get-tuple-element.132), channel_id=1, source_target_pairs={{0,7},{1,6},{2,5},{3,4},{4,3},{5,2},{6,1},{7,0},{8,15},{9,14},{10,... | collective-permute-start | bytes 393224 | tf_op jit(solution)/shard_map/ppermute | solution.py:92
  541.4 35.6 %collective-permute-start.82 = (bf16[256,256]{1,0:T(8,128)(2,1)}, bf16[256,256]{1,0:T(8,128)(2,1)S(1)}, u32[]{:S(2)}, u32[]{:S(2)}) collective-permute-start(bf16[256,256]{1,0:T(8,128)(2,1)} %get-tuple-element.143), channel_id=1, source_target_pairs={{0,1},{1,0},{2,3},{3,2},{4,5},{5,4},{6,7},{7,6},{8,9},{9,8},{10,11... | collective-permute-start | bytes 393224 | tf_op jit(solution)/shard_map/ppermute | solution.py:92
  549.0 32.1 %collective-permute-start.83 = (bf16[256,256]{1,0:T(8,128)(2,1)S(1)}, bf16[256,256]{1,0:T(8,128)(2,1)S(1)}, u32[]{:S(2)}, u32[]{:S(2)}) collective-permute-start(bf16[256,256]{1,0:T(8,128)(2,1)S(1)} %copy-done.106), channel_id=1, source_target_pairs={{0,2},{1,3},{2,0},{3,1},{4,6},{5,7},{6,4},{7,5},{8,10},{9,11},{10,... | collective-permute-start | bytes 393224 | tf_op jit(solution)/shard_map/ppermute | solution.py:92
  549.5 32.2 %collective-permute-start.84 = (bf16[256,256]{1,0:T(8,128)(2,1)S(1)}, bf16[256,256]{1,0:T(8,128)(2,1)}, u32[]{:S(2)}, u32[]{:S(2)}) collective-permute-start(bf16[256,256]{1,0:T(8,128)(2,1)S(1)} %copy-done.105), channel_id=1, source_target_pairs={{0,3},{1,2},{2,1},{3,0},{4,7},{5,6},{6,5},{7,4},{8,11},{9,10},{10,... | collective-permute-start | bytes 393224 | tf_op jit(solution)/shard_map/ppermute | solution.py:92
  581.1 81.7 %collective-permute-start.103 = (bf16[512,2048]{1,0:T(8,128)(2,1)}, bf16[512,2048]{1,0:T(8,128)(2,1)}, u32[]{:S(2)}, u32[]{:S(2)}) collective-permute-start(bf16[512,2048]{1,0:T(8,128)(2,1)} %pad_maximum_fusion), channel_id=1, source_target_pairs={{0,8},{8,0},{16,24},{24,16},{1,9},{9,1},{17,25},{25,17},{2,10},{10... | collective-permute-start | bytes 6291464 | tf_op jit(solution)/shard_map/ppermute | solution.py:92
  581.7 35.8 %collective-permute-start.119 = (bf16[512,2048]{1,0:T(8,128)(2,1)}, bf16[512,2048]{1,0:T(8,128)(2,1)S(1)}, u32[]{:S(2)}, u32[]{:S(2)}) collective-permute-start(bf16[512,2048]{1,0:T(8,128)(2,1)} %pad_maximum_fusion.1), channel_id=1, source_target_pairs={{0,8},{8,0},{16,24},{24,16},{1,9},{9,1},{17,25},{25,17},{2,10},{10... | collective-permute-start | bytes 6291464 | tf_op jit(solution)/shard_map/ppermute | solution.py:92
  586.5 32.3 %collective-permute-start.120 = (bf16[256,512]{1,0:T(8,128)(2,1)}, bf16[256,512]{1,0:T(8,128)(2,1)}, u32[]{:S(2)}, u32[]{:S(2)}) collective-permute-start(bf16[256,512]{1,0:T(8,128)(2,1)} %get-tuple-element.190), channel_id=1, source_target_pairs={{0,16},{8,24},{16,0},{24,8},{1,17},{9,25},{17,1},{25,9},{2,18},{10... | collective-permute-start | bytes 786440 | tf_op jit(solution)/shard_map/ppermute | solution.py:92
  591.0 29.8 %collective-permute-start.121 = (bf16[256,512]{1,0:T(8,128)(2,1)}, bf16[256,512]{1,0:T(8,128)(2,1)}, u32[]{:S(2)}, u32[]{:S(2)}) collective-permute-start(bf16[256,512]{1,0:T(8,128)(2,1)} %get-tuple-element.191), channel_id=1, source_target_pairs={{0,8},{8,0},{16,24},{24,16},{1,9},{9,1},{17,25},{25,17},{2,10},{10... | collective-permute-start | bytes 786440 | tf_op jit(solution)/shard_map/ppermute | solution.py:92
  591.0 33.8 %collective-permute-start.122 = (bf16[256,512]{1,0:T(8,128)(2,1)}, bf16[256,512]{1,0:T(8,128)(2,1)}, u32[]{:S(2)}, u32[]{:S(2)}) collective-permute-start(bf16[256,512]{1,0:T(8,128)(2,1)} %get-tuple-element.192), channel_id=1, source_target_pairs={{0,24},{8,16},{16,8},{24,0},{1,25},{9,17},{17,9},{25,1},{2,26},{10... | collective-permute-start | bytes 786440 | tf_op jit(solution)/shard_map/ppermute | solution.py:92
  668.3 41.7 %collective-permute-start.99 = (bf16[256,512]{1,0:T(8,128)(2,1)}, bf16[256,512]{1,0:T(8,128)(2,1)S(1)}, u32[]{:S(2)}, u32[]{:S(2)}) collective-permute-start(bf16[256,512]{1,0:T(8,128)(2,1)} %get-tuple-element.174), channel_id=1, source_target_pairs={{0,5},{1,4},{2,7},{3,6},{4,1},{5,0},{6,3},{7,2},{8,13},{9,12},{10,... | collective-permute-start | bytes 786440 | tf_op jit(solution)/shard_map/ppermute | solution.py:92
  673.2 40.9 %collective-permute-start.98 = (bf16[256,512]{1,0:T(8,128)(2,1)}, bf16[256,512]{1,0:T(8,128)(2,1)S(1)}, u32[]{:S(2)}, u32[]{:S(2)}) collective-permute-start(bf16[256,512]{1,0:T(8,128)(2,1)} %get-tuple-element.172), channel_id=1, source_target_pairs={{0,4},{1,5},{2,6},{3,7},{4,0},{5,1},{6,2},{7,3},{8,12},{9,13},{10,... | collective-permute-start | bytes 786440 | tf_op jit(solution)/shard_map/ppermute | solution.py:92
  674.4 60.1 %collective-permute-start.142 = (bf16[688,1024]{1,0:T(8,128)(2,1)}, bf16[688,1024]{1,0:T(8,128)(2,1)S(1)}, u32[]{:S(2)}, u32[]{:S(2)}) collective-permute-start(bf16[688,1024]{1,0:T(8,128)(2,1)} %add_convert_fusion), channel_id=1, source_target_pairs={{0,8},{8,0},{16,24},{24,16},{1,9},{9,1},{17,25},{25,17},{2,10},{10... | collective-permute-start | bytes 4227080 | tf_op jit(solution)/shard_map/ppermute | solution.py:92
  677.2 62.9 %collective-permute-start.139 = (bf16[688,1024]{1,0:T(8,128)(2,1)}, bf16[688,1024]{1,0:T(8,128)(2,1)S(1)}, u32[]{:S(2)}, u32[]{:S(2)}) collective-permute-start(bf16[688,1024]{1,0:T(8,128)(2,1)} %add_convert_fusion.2), channel_id=1, source_target_pairs={{0,8},{8,0},{16,24},{24,16},{1,9},{9,1},{17,25},{25,17},{2,10},{10... | collective-permute-start | bytes 4227080 | tf_op jit(solution)/shard_map/ppermute | solution.py:92
  681.3 41.3 %collective-permute-start.97 = (bf16[256,512]{1,0:T(8,128)(2,1)}, bf16[256,512]{1,0:T(8,128)(2,1)S(1)}, u32[]{:S(2)}, u32[]{:S(2)}) collective-permute-start(bf16[256,512]{1,0:T(8,128)(2,1)} %get-tuple-element.170), channel_id=1, source_target_pairs={{0,3},{1,2},{2,1},{3,0},{4,7},{5,6},{6,5},{7,4},{8,11},{9,10},{10,... | collective-permute-start | bytes 786440 | tf_op jit(solution)/shard_map/ppermute | solution.py:92
  725.4 25.6 %collective-permute-start.74 = (bf16[128,2048]{1,0:T(8,128)(2,1)}, bf16[128,2048]{1,0:T(8,128)(2,1)}, u32[]{:S(2)}, u32[]{:S(2)}) collective-permute-start(bf16[128,2048]{1,0:T(8,128)(2,1)} %convolution_convert_fusion.4), channel_id=1, source_target_pairs={{3,1},{5,3},{7,5},{6,7},{4,6},{2,4},{0,2},{1,0},{11,9},{13,11},{15... | collective-permute-start | bytes 1572872 | tf_op jit(solution)/shard_map/ppermute | solution.py:88
  726.8 45.1 %collective-permute-start.78 = (bf16[128,2048]{1,0:T(8,128)(2,1)}, bf16[128,2048]{1,0:T(8,128)(2,1)}, u32[]{:S(2)}, u32[]{:S(2)}) collective-permute-start(bf16[128,2048]{1,0:T(8,128)(2,1)} %convolution_convert_fusion.3), channel_id=1, source_target_pairs={{1,3},{3,5},{5,7},{7,6},{6,4},{4,2},{2,0},{0,1},{9,11},{11,13},{13... | collective-permute-start | bytes 1572872 | tf_op jit(solution)/shard_map/ppermute | solution.py:85
  734.5 23.4 %collective-permute-start.128 = (bf16[256,512]{1,0:T(8,128)(2,1)S(1)}, bf16[256,512]{1,0:T(8,128)(2,1)S(1)}, u32[]{:S(2)}, u32[]{:S(2)}) collective-permute-start(bf16[256,512]{1,0:T(8,128)(2,1)S(1)} %copy-done.52), channel_id=1, source_target_pairs={{1,3},{3,5},{5,7},{7,6},{6,4},{4,2},{2,0},{0,1},{9,11},{11,13},{13... | collective-permute-start | bytes 786440 | tf_op jit(solution)/shard_map/ppermute | solution.py:85
  757.9 51.7 %collective-permute-start.75 = (bf16[256,2048]{1,0:T(8,128)(2,1)S(1)}, bf16[256,2048]{1,0:T(8,128)(2,1)S(1)}, u32[]{:S(2)}, u32[]{:S(2)}) collective-permute-start(bf16[256,2048]{1,0:T(8,128)(2,1)S(1)} %pad_maximum_fusion.4), channel_id=1, source_target_pairs={{3,1},{5,3},{7,5},{6,7},{4,6},{2,4},{0,2},{1,0},{11,9},{13,11},{15... | collective-permute-start | bytes 3145736 | tf_op jit(solution)/shard_map/ppermute | solution.py:88
  769.8 28.6 %collective-permute-start.109 = (bf16[288,512]{1,0:T(8,128)(2,1)S(1)}, bf16[288,512]{1,0:T(8,128)(2,1)S(1)}, u32[]{:S(2)}, u32[]{:S(2)}) collective-permute-start(bf16[288,512]{1,0:T(8,128)(2,1)S(1)} %get-tuple-element.333), channel_id=1, source_target_pairs={{3,1},{5,3},{7,5},{6,7},{4,6},{2,4},{0,2},{1,0},{11,9},{13,11},{15... | collective-permute-start | bytes 884744 | tf_op jit(solution)/shard_map/ppermute | solution.py:88
  769.9 28.5 %collective-permute-start.113 = (bf16[288,512]{1,0:T(8,128)(2,1)S(1)}, bf16[288,512]{1,0:T(8,128)(2,1)S(1)}, u32[]{:S(2)}, u32[]{:S(2)}) collective-permute-start(bf16[288,512]{1,0:T(8,128)(2,1)S(1)} %get-tuple-element.334), channel_id=1, source_target_pairs={{1,3},{3,5},{5,7},{7,6},{6,4},{4,2},{2,0},{0,1},{9,11},{11,13},{13... | collective-permute-start | bytes 884744 | tf_op jit(solution)/shard_map/ppermute | solution.py:85
  773.1 30.9 %collective-permute-start.126 = (bf16[256,512]{1,0:T(8,128)(2,1)S(1)}, bf16[256,512]{1,0:T(8,128)(2,1)S(1)}, u32[]{:S(2)}, u32[]{:S(2)}) collective-permute-start(bf16[256,512]{1,0:T(8,128)(2,1)S(1)} %get-tuple-element.251), channel_id=1, source_target_pairs={{3,1},{5,3},{7,5},{6,7},{4,6},{2,4},{0,2},{1,0},{11,9},{13,11},{15... | collective-permute-start | bytes 786440 | tf_op jit(solution)/shard_map/ppermute | solution.py:88
  773.3 31.0 %collective-permute-start.130 = (bf16[256,512]{1,0:T(8,128)(2,1)S(1)}, bf16[256,512]{1,0:T(8,128)(2,1)S(1)}, u32[]{:S(2)}, u32[]{:S(2)}) collective-permute-start(bf16[256,512]{1,0:T(8,128)(2,1)S(1)} %add_convert_fusion.11), channel_id=1, source_target_pairs={{1,3},{3,5},{5,7},{7,6},{6,4},{4,2},{2,0},{0,1},{9,11},{11,13},{13... | collective-permute-start | bytes 786440 | tf_op jit(solution)/shard_map/ppermute | solution.py:85
  804.0 23.8 %collective-permute-start.79 = (bf16[256,2048]{1,0:T(8,128)(2,1)S(1)}, bf16[256,2048]{1,0:T(8,128)(2,1)S(1)}, u32[]{:S(2)}, u32[]{:S(2)}) collective-permute-start(bf16[256,2048]{1,0:T(8,128)(2,1)S(1)} %pad_maximum_fusion.5), channel_id=1, source_target_pairs={{1,3},{3,5},{5,7},{7,6},{6,4},{4,2},{2,0},{0,1},{9,11},{11,13},{13... | collective-permute-start | bytes 3145736 | tf_op jit(solution)/shard_map/ppermute | solution.py:85
  804.7 24.7 %collective-permute-start.131 = (bf16[256,512]{1,0:T(8,128)(2,1)S(1)}, bf16[256,512]{1,0:T(8,128)(2,1)S(1)}, u32[]{:S(2)}, u32[]{:S(2)}) collective-permute-start(bf16[256,512]{1,0:T(8,128)(2,1)S(1)} %get-tuple-element.250), channel_id=1, source_target_pairs={{0,16},{8,24},{16,0},{24,8},{1,17},{9,25},{17,1},{25,9},{2,18},{10... | collective-permute-start | bytes 786440 | tf_op jit(solution)/shard_map/ppermute | solution.py:92
  807.9 23.0 %collective-permute-start.132 = (bf16[256,512]{1,0:T(8,128)(2,1)S(1)}, bf16[256,512]{1,0:T(8,128)(2,1)S(1)}, u32[]{:S(2)}, u32[]{:S(2)}) collective-permute-start(bf16[256,512]{1,0:T(8,128)(2,1)S(1)} %get-tuple-element.250), channel_id=1, source_target_pairs={{0,8},{8,0},{16,24},{24,16},{1,9},{9,1},{17,25},{25,17},{2,10},{10... | collective-permute-start | bytes 786440 | tf_op jit(solution)/shard_map/ppermute | solution.py:92
  831.0 23.2 %collective-permute-start.133 = (bf16[256,512]{1,0:T(8,128)(2,1)S(1)}, bf16[256,512]{1,0:T(8,128)(2,1)S(1)}, u32[]{:S(2)}, u32[]{:S(2)}) collective-permute-start(bf16[256,512]{1,0:T(8,128)(2,1)S(1)} %collective-permute-done.131), channel_id=1, source_target_pairs={{0,8},{8,0},{16,24},{24,16},{1,9},{9,1},{17,25},{25,17},{2,10},{10... | collective-permute-start | bytes 786440 | tf_op jit(solution)/shard_map/ppermute | solution.py:92
  831.1 23.2 %collective-permute-start.117 = (bf16[288,512]{1,0:T(8,128)(2,1)S(1)}, bf16[288,512]{1,0:T(8,128)(2,1)S(1)}, u32[]{:S(2)}, u32[]{:S(2)}) collective-permute-start(bf16[288,512]{1,0:T(8,128)(2,1)S(1)} %collective-permute-done.116), channel_id=1, source_target_pairs={{0,8},{8,0},{16,24},{24,16},{1,9},{9,1},{17,25},{25,17},{2,10},{10... | collective-permute-start | bytes 884744 | tf_op jit(solution)/shard_map/ppermute | solution.py:92
  (196 other events, 2565.2 us)

commit v2 on v1

v2 whole, which is shorter than its diff:
```python
import functools

import jax
import jax.numpy as jnp
from jax import lax
from jax.experimental import pallas as pl
from jax.experimental.pallas import tpu as pltpu
from jax.sharding import PartitionSpec as P

HEAD_DIM = 128
ATT_BLOCK = 512


EPSILON = 1e-05


def product(left_side, right_side):
    return jnp.dot(left_side, right_side, preferred_element_type=jnp.float32)


def inner_rows(left_side, right_side):
    return lax.dot_general(
        left_side, right_side, (((0,), (0,)), ((), ())), preferred_element_type=jnp.float32
    )


def outer_cols(left_side, right_side):
    return lax.dot_general(
        left_side, right_side, (((1,), (1,)), ((), ())), preferred_element_type=jnp.float32
    )


def snake(count):
    deep = 4 if count % 4 == 0 else 1
    wide = count // deep
    if deep == 1 or wide == 1:
        return list(range(count))
    order = []
    for z in range(deep):
        across = range(1, wide) if z % 2 == 0 else range(wide - 1, 0, -1)
        order += [z * wide + y for y in across]
    return order + [z * wide for z in range(deep - 1, -1, -1)]


def after(value, *others):
    return lax.optimization_barrier((value, *others))[0] if others else value


def tie(values, *others):
    return list(lax.optimization_barrier((*values, *others))[: len(values)])


def low(value):
    return value.astype(jnp.bfloat16)


def wide(value):
    return value.astype(jnp.float32)


class Links:
    def __init__(self, mesh):
        self.n = mesh.shape["seq"]
        self.nd = mesh.shape["dp"]
        self.order = snake(self.n)
        n = self.n
        self.right = [(self.order[k], self.order[(k + 1) % n]) for k in range(n)]
        self.left = [(b, a) for a, b in self.right]

    def group(self, d):
        return d % 2 * (self.nd // 2) + d // 2

    def place(self):
        me = lax.axis_index("seq")
        table = [0] * self.n
        for k, i in enumerate(self.order):
            table[i] = k
        return sum(jnp.where(me == i, table[i], 0) for i in range(self.n))

    def owner(self, place, distance):
        spot = (place + distance) % self.n
        return sum(jnp.where(spot == k, self.order[k], 0) for k in range(self.n))

    def to_right(self, x):
        return lax.ppermute(x, "seq", self.right)

    def to_left(self, x):
        return lax.ppermute(x, "seq", self.left)

    def to_heads(self, x, m):
        per, nx = self.n // self.nd, self.nd // 2
        pairs = []
        for d in range(self.nd):
            for s in range(self.n):
                j = s ^ m
                group = j // per
                to = group % nx * 2 + group // nx
                pairs.append((d * self.n + s, to * self.n + self.group(d) * per + j % per))
        return lax.ppermute(x, ("dp", "seq"), pairs)

    def swap(self, x, axis, r):
        count = self.n if axis == "seq" else self.nd
        return lax.ppermute(x, axis, [(k, k ^ r) for k in range(count)])


class RingGather:
    def __init__(self, net, x):
        self.net, self.got, self.at = net, {0: x}, 0
        self.from_left = self.from_right = x

    def step(self, *deps):
        net, half = self.net, self.net.n // 2
        self.at += 1
        left, right = self.from_left, self.from_right
        if self.at == half:
            rows = left.shape[0] // 2
            left, right = left[:rows], right[rows:]
        if self.at == 1 and half > 1:
            left = right = after(left, *deps)
        else:
            left, right = tie([left, right], *deps)
        self.from_left, self.from_right = net.to_right(left), net.to_left(right)
        keys = ("a", "b") if self.at == half else (-self.at, self.at)
        self.got[keys[0]], self.got[keys[1]] = self.from_left, self.from_right
        return self.from_left, self.from_right

    def rest(self):
        while self.at < self.net.n // 2:
            self.step()
        return self.got


class RowSum:
    def __init__(self, net, part):
        self.net, self.part, self.at = net, part, net.n // 2
        self.going_left = self.going_right = None

    def step(self, *deps):
        net, half, s = self.net, self.net.n // 2, self.at
        if s == half:
            left, right = self.part("b"), self.part("a")
        else:
            left, right = self.part(-s), self.part(s)
            if s == half - 1:
                rows = left.shape[0] // 2
                left = jnp.concatenate([left[:rows], left[rows:] + wide(self.going_left)])
                right = jnp.concatenate([right[:rows] + wide(self.going_right), right[rows:]])
            else:
                left = left + wide(self.going_left)
                right = right + wide(self.going_right)
        left, right = tie([low(left), low(right)], *deps)
        self.going_left, self.going_right = net.to_left(left), net.to_right(right)
        self.at -= 1
        return self.going_left, self.going_right

    def rest(self):
        while self.at:
            self.step()
        return self.part(0), self.going_left, self.going_right


VMEM_LIMIT = 56 * 1024 * 1024
COST_SHARE = 4
ANYWHERE = pl.BlockSpec(memory_space=pl.ANY)
IN_VMEM = pl.BlockSpec(memory_space=pltpu.VMEM)
IN_SMEM = pl.BlockSpec(memory_space=pltpu.SMEM)
LOG2_E = 1.4426950408889634
DEAD = 1e30


def nt_dot(a, b):
    return lax.dot_general(a, b, (((1,), (1,)), ((), ())), preferred_element_type=jnp.float32)


def tn_dot(a, b):
    return lax.dot_general(a, b, (((0,), (0,)), ((), ())), preferred_element_type=jnp.float32)


def call(body, operands, specs, outs, out_specs, scratch, flops, moved, name):
    return pl.pallas_call(
        body,
        name=name,
        in_specs=specs,
        out_specs=tuple(out_specs),
        out_shape=tuple(jax.ShapeDtypeStruct(s, t) for s, t in outs),
        scratch_shapes=scratch,
        compiler_params=pltpu.CompilerParams(vmem_limit_bytes=VMEM_LIMIT),
        cost_estimate=pl.CostEstimate(
            flops=flops // COST_SHARE, bytes_accessed=moved // COST_SHARE, transcendentals=0
        ),
    )(*operands)


def aligned(index, unit):
    return pl.multiple_of(index * unit, unit)


def start_all(copies):
    for copy in copies:
        copy.start()
    return copies


def wait_all(copies):
    for copy in copies:
        copy.wait()


def causal_mask(block):
    key_at = lax.broadcasted_iota(jnp.int32, (block, block), 0)
    query_at = lax.broadcasted_iota(jnp.int32, (block, block), 1)
    return key_at <= query_at


def forward_body(n, info, *refs):
    q_in, kv_in = refs[:n], refs[n : 2 * n]
    outs, stats, ot = refs[2 * n : 3 * n], refs[3 * n], refs[3 * n + 1]
    qs, ks, vs, vt, mixed, sems = refs[3 * n + 2 :]
    me, length, spot = info[0], info[1], info[2]
    count, width = q_in[0].shape
    heads = width // HEAD_DIM
    total = n * count
    blocks = total // ATT_BLOCK
    copies = []
    for r in range(n):
        rows = pl.ds(aligned(me ^ r, count), count)
        query_rows = pl.ds(aligned(spot ^ r, count), count)
        for k, (src, dst) in enumerate(
            (
                (kv_in[r].at[:, pl.ds(0, width)], ks.at[rows]),
                (kv_in[r].at[:, pl.ds(width, width)], vs.at[rows]),
                (q_in[r], qs.at[query_rows]),
            )
        ):
            copies.append(pltpu.make_async_copy(src, dst, sems.at[3 * r + k]))
    wait_all(start_all(copies))
    factor = HEAD_DIM ** (-0.5) * LOG2_E

    def transpose_values(b, _):
        at = pl.ds(pl.multiple_of(b * ATT_BLOCK, ATT_BLOCK), ATT_BLOCK)
        vt[:, at] = vs[at, :].T
        return 0

    lax.fori_loop(0, blocks, transpose_values, 0)
    live = jnp.minimum((length + ATT_BLOCK - 1) // ATT_BLOCK, blocks)

    def tile(qi, kj, state, masked):
        new = []
        q_at = pl.ds(pl.multiple_of(qi * ATT_BLOCK, ATT_BLOCK), ATT_BLOCK)
        k_at = pl.ds(pl.multiple_of(kj * ATT_BLOCK, ATT_BLOCK), ATT_BLOCK)
        for h in range(heads):
            cols = slice(h * HEAD_DIM, (h + 1) * HEAD_DIM)
            top, total_sum, acc = state[h]
            scores = nt_dot(ks[k_at, cols], qs[q_at, cols]) * factor
            if masked:
                scores = jnp.where(causal_mask(ATT_BLOCK), scores, -DEAD)
            higher = jnp.maximum(top, jnp.max(scores, axis=0, keepdims=True))
            weights = jnp.exp2(scores - higher)
            shrink = jnp.exp2(top - higher)
            total_sum = total_sum * shrink + jnp.sum(weights, axis=0, keepdims=True)
            acc = acc * shrink + jnp.dot(
                vt[cols, k_at], weights.astype(jnp.bfloat16), preferred_element_type=jnp.float32
            )
            new.append((higher, total_sum, acc))
        return tuple(new)

    stats[...] = jnp.full(stats.shape, DEAD, jnp.float32)

    def query_block(qi, _):
        first = tuple(
            (
                jnp.full((1, ATT_BLOCK), -DEAD, jnp.float32),
                jnp.zeros((1, ATT_BLOCK), jnp.float32),
                jnp.zeros((HEAD_DIM, ATT_BLOCK), jnp.float32),
            )
            for _ in range(heads)
        )
        state = lax.fori_loop(0, qi, lambda kj, s: tile(qi, kj, s, False), first)
        state = tile(qi, qi, state, True)
        q_at = pl.ds(pl.multiple_of(qi * ATT_BLOCK, ATT_BLOCK), ATT_BLOCK)
        query_at = qi * ATT_BLOCK + lax.broadcasted_iota(jnp.int32, (1, ATT_BLOCK), 1)
        alive = query_at < length
        for h in range(heads):
            cols = slice(h * HEAD_DIM, (h + 1) * HEAD_DIM)
            top, total_sum, acc = state[h]
            scaled = acc * jnp.where(alive, 1.0 / total_sum, 0.0)
            ot[cols, q_at] = scaled
            mixed[q_at, cols] = scaled.T.astype(jnp.bfloat16)
            stats[h : h + 1, q_at] = jnp.where(alive, top + jnp.log2(total_sum), DEAD)
        return 0

    lax.fori_loop(0, live, query_block, 0)

    def dead_block(qi, _):
        q_at = pl.ds(pl.multiple_of(qi * ATT_BLOCK, ATT_BLOCK), ATT_BLOCK)
        mixed[q_at, :] = jnp.zeros((ATT_BLOCK, width), jnp.bfloat16)
        ot[:, q_at] = jnp.zeros((width, ATT_BLOCK), jnp.float32)
        return 0

    lax.fori_loop(live, blocks, dead_block, 0)
    copies = []
    for r in range(n):
        rows = pl.ds(pl.multiple_of((me ^ r) * count, count), count)
        copies.append(pltpu.make_async_copy(mixed.at[rows], outs[r], sems.at[r]))
    wait_all(start_all(copies))


def attention_forward(info, q_blocks, kv_blocks):
    n = len(q_blocks)
    count, width = q_blocks[0].shape
    total = n * count
    got = call(
        functools.partial(forward_body, n),
        [info, *q_blocks, *kv_blocks],
        [IN_SMEM] + [ANYWHERE] * (2 * n),
        [((count, width), jnp.bfloat16)] * n
        + [((8, total), jnp.float32), ((width, total), jnp.float32)],
        [ANYWHERE] * n + [IN_VMEM] * 2,
        [pltpu.VMEM((total, width), jnp.bfloat16)] * 3
        + [pltpu.VMEM((width, total), jnp.bfloat16), pltpu.VMEM((total, width), jnp.bfloat16)]
        + [pltpu.SemaphoreType.DMA((3 * n,))],
        16 * 2 * total * total * width // 2,
        10 * total * width,
        "attention_forward",
    )
    return got[:n], got[n], got[n + 1]


def backward_body(n, info, *refs):
    q_in, kv_in, g_in = refs[:n], refs[n : 2 * n], refs[2 * n : 3 * n]
    stats, ot = refs[3 * n], refs[3 * n + 1]
    refs = refs[3 * n + 2 :]
    dq_out, dkv_out = refs[:n], refs[n : 2 * n]
    qs, ks, vs, gs, kt, delta, dqt, dk, dv, dq_low, dkv_low, sems = refs[2 * n :]
    me, length, spot = info[0], info[1], info[2]
    count, width = q_in[0].shape
    heads = width // HEAD_DIM
    total = n * count
    blocks = total // ATT_BLOCK
    copies = []
    for r in range(n):
        rows = pl.ds(aligned(me ^ r, count), count)
        query_rows = pl.ds(aligned(spot ^ r, count), count)
        for k, (src, dst) in enumerate(
            (
                (kv_in[r].at[:, pl.ds(0, width)], ks.at[rows]),
                (kv_in[r].at[:, pl.ds(width, width)], vs.at[rows]),
                (q_in[r], qs.at[query_rows]),
                (g_in[r], gs.at[rows]),
            )
        ):
            copies.append(pltpu.make_async_copy(src, dst, sems.at[4 * r + k]))
    start_all(copies)
    live = jnp.minimum((length + ATT_BLOCK - 1) // ATT_BLOCK, blocks)
    scale = HEAD_DIM ** (-0.5)
    factor = scale * LOG2_E

    def clear(b, _):
        at = pl.ds(pl.multiple_of(b * ATT_BLOCK, ATT_BLOCK), ATT_BLOCK)
        dqt[:, at] = jnp.zeros((width, ATT_BLOCK), jnp.float32)
        dk[at, :] = jnp.zeros((ATT_BLOCK, width), jnp.float32)
        dv[at, :] = jnp.zeros((ATT_BLOCK, width), jnp.float32)
        return 0

    lax.fori_loop(0, blocks, clear, 0)
    wait_all(copies)

    def prepare(b, _):
        at = pl.ds(pl.multiple_of(b * ATT_BLOCK, ATT_BLOCK), ATT_BLOCK)
        kt[:, at] = ks[at, :].T
        both = gs[at, :].astype(jnp.float32).T * ot[:, at]
        for h in range(heads):
            cols = slice(h * HEAD_DIM, (h + 1) * HEAD_DIM)
            delta[h : h + 1, at] = jnp.sum(both[cols], axis=0, keepdims=True)
        return 0

    lax.fori_loop(0, blocks, prepare, 0)

    def tile(qi, kj, masked):
        q_at = pl.ds(pl.multiple_of(qi * ATT_BLOCK, ATT_BLOCK), ATT_BLOCK)
        k_at = pl.ds(pl.multiple_of(kj * ATT_BLOCK, ATT_BLOCK), ATT_BLOCK)
        for h in range(heads):
            cols = slice(h * HEAD_DIM, (h + 1) * HEAD_DIM)
            q, g = qs[q_at, cols], gs[q_at, cols]
            scores = nt_dot(ks[k_at, cols], q) * factor - stats[h : h + 1, q_at]
            if masked:
                scores = jnp.where(causal_mask(ATT_BLOCK), scores, -DEAD)
            weights = jnp.exp2(scores)
            grad_weights = nt_dot(vs[k_at, cols], g)
            grad_scores = (weights * (grad_weights - delta[h : h + 1, q_at])).astype(jnp.bfloat16)
            dv[k_at, cols] += jnp.dot(
                weights.astype(jnp.bfloat16), g, preferred_element_type=jnp.float32
            )
            dk[k_at, cols] += jnp.dot(grad_scores, q, preferred_element_type=jnp.float32)
            dqt[cols, q_at] += jnp.dot(
                kt[cols, k_at], grad_scores, preferred_element_type=jnp.float32
            )

    def query_block(qi, _):
        def step(kj, _):
            tile(qi, kj, False)
            return 0

        lax.fori_loop(0, qi, step, 0)
        tile(qi, qi, True)
        return 0

    lax.fori_loop(0, live, query_block, 0)

    def finish(b, _):
        at = pl.ds(pl.multiple_of(b * ATT_BLOCK, ATT_BLOCK), ATT_BLOCK)
        dq_low[at, :] = (dqt[:, at] * scale).T.astype(jnp.bfloat16)
        dkv_low[at, :width] = (dk[at, :] * scale).astype(jnp.bfloat16)
        dkv_low[at, width:] = dv[at, :].astype(jnp.bfloat16)
        return 0

    lax.fori_loop(0, blocks, finish, 0)
    copies = []
    for r in range(n):
        rows = pl.ds(pl.multiple_of((me ^ r) * count, count), count)
        copies.append(pltpu.make_async_copy(dq_low.at[rows], dq_out[r], sems.at[2 * r]))
        copies.append(pltpu.make_async_copy(dkv_low.at[rows], dkv_out[r], sems.at[2 * r + 1]))
    wait_all(start_all(copies))


def attention_backward(info, q_blocks, kv_blocks, g_blocks, stats, ot):
    n = len(q_blocks)
    count, width = q_blocks[0].shape
    total = n * count
    low_all = pltpu.VMEM((total, width), jnp.bfloat16)
    got = call(
        functools.partial(backward_body, n),
        [info, *q_blocks, *kv_blocks, *g_blocks, stats, ot],
        [IN_SMEM] + [ANYWHERE] * (3 * n) + [IN_VMEM] * 2,
        [((count, width), jnp.bfloat16)] * n + [((count, 2 * width), jnp.bfloat16)] * n,
        [ANYWHERE] * (2 * n),
        [low_all] * 4
        + [
            pltpu.VMEM((width, total), jnp.bfloat16),
            pltpu.VMEM((8, total), jnp.float32),
            pltpu.VMEM((width, total), jnp.float32),
            pltpu.VMEM((total, width), jnp.float32),
            pltpu.VMEM((total, width), jnp.float32),
            low_all,
            pltpu.VMEM((total, 2 * width), jnp.bfloat16),
            pltpu.SemaphoreType.DMA((4 * n,)),
        ],
        40 * 2 * total * total * width // 2,
        20 * total * width,
        "attention_backward",
    )
    return got[:n], got[n:]


def pack_body(n, info, keys, values, *refs):
    outs, sems = refs[:n], refs[n]
    me = info[0]
    width = outs[0].shape[1] // 2
    copies = []
    for r in range(n):
        cols = pl.ds(aligned(me ^ r, width), width)
        copies.append(
            pltpu.make_async_copy(keys.at[:, cols], outs[r].at[:, pl.ds(0, width)], sems.at[2 * r])
        )
        copies.append(
            pltpu.make_async_copy(
                values.at[:, cols], outs[r].at[:, pl.ds(width, width)], sems.at[2 * r + 1]
            )
        )
    wait_all(start_all(copies))


def pack_keys_values(n, info, keys, values):
    count, depth = keys.shape
    return call(
        functools.partial(pack_body, n),
        [info, keys, values],
        [IN_SMEM, ANYWHERE, ANYWHERE],
        [((count, 2 * depth // n), jnp.bfloat16)] * n,
        [IN_VMEM] * n,
        [pltpu.SemaphoreType.DMA((2 * n,))],
        0,
        8 * count * depth,
        "pack_keys_values",
    )


GAIN_ROWS = 32


def norm_parts(v):
    return lax.rsqrt(jnp.mean(v * v, axis=-1, keepdims=True) + EPSILON)


def query_body(n, nd, info, *refs):
    xs, pieces = refs[:nd], refs[nd : nd + n + 1]
    q_out = refs[nd + n + 1 : nd + 2 * n + 1]
    normed, gains, weight, out_weight = refs[nd + 2 * n + 1 : nd + 2 * n + 5]
    queries, gain_rows, sems = refs[nd + 2 * n + 5 :]
    me, dp = info[0], info[1]
    count, depth = xs[0].shape
    wrows = (pieces[0].shape[0] - GAIN_ROWS) // 2
    cut = wrows - GAIN_ROWS // 2
    copies, later = [], []

    def fetch(into, k, src, dst, j):
        into.append(pltpu.make_async_copy(src, dst, sems.at[3 * k + j]))

    for k in range(n):
        first = info[3 + k] * wrows
        gain_at = gain_rows.at[pl.ds(aligned(info[3 + k], 16), 16)]
        fetch(copies, k, pieces[k].at[pl.ds(0, 16)], gain_at, 0)
        at = pl.multiple_of(first, 16)
        if k < n - 1:
            rows = pl.ds(at, wrows)
            fetch(copies, k, pieces[k].at[pl.ds(GAIN_ROWS, wrows)], weight.at[rows], 1)
            fetch(later, k, pieces[k].at[pl.ds(GAIN_ROWS + wrows, wrows)], out_weight.at[rows], 2)
        else:
            below = pl.multiple_of(first + cut, 16)
            fetch(copies, k, pieces[k].at[pl.ds(GAIN_ROWS, cut)], weight.at[pl.ds(at, cut)], 1)
            rest = pl.ds(below, wrows - cut)
            fetch(copies, k, pieces[n].at[pl.ds(0, wrows - cut)], weight.at[rest], 2)
            tail = pieces[n].at[pl.ds(wrows - cut, wrows)]
            fetch(later, n, tail, out_weight.at[pl.ds(at, wrows)], 0)
    start_all(copies)
    start_all(later)
    wait_all(copies)
    share = depth // n
    for o in range(n):
        row = gain_rows[o * 16 : o * 16 + 16, : 2 * share].astype(jnp.float32)
        gains[0:1, o * share : (o + 1) * share] = row[0:1, :share]
        gains[1:2, o * share : (o + 1) * share] = row[0:1, share:]
    for k in range(nd):
        v = xs[k][...].astype(jnp.float32)
        rows = slice(k * count, (k + 1) * count)
        normed[rows, :] = (v * norm_parts(v) * gains[0:1, :]).astype(jnp.bfloat16)
        queries[rows, :] = jnp.dot(
            normed[rows, :], weight[...], preferred_element_type=jnp.float32
        ).astype(jnp.bfloat16)
    per = n // nd
    copies = []
    for m in range(n):
        j = me ^ m
        slot = dp ^ (j // per)
        copies.append(
            pltpu.make_async_copy(
                queries.at[
                    pl.ds(aligned(slot, count), count), pl.ds(aligned(j % per, share), share)
                ],
                q_out[m],
                sems.at[3 * n + 3 + m],
            )
        )
    wait_all(start_all(copies))
    wait_all(later)


def project_queries(n, nd, info, xs, pieces):
    count, depth = xs[0].shape
    quarter = pieces[0].shape[1]
    got = call(
        functools.partial(query_body, n, nd),
        [info, *xs, *pieces],
        [IN_SMEM] + [IN_VMEM] * nd + [ANYWHERE] * (n + 1),
        [((count, depth // n), jnp.bfloat16)] * n
        + [
            ((nd * count, depth), jnp.bfloat16),
            ((8, depth), jnp.float32),
            ((depth, quarter), jnp.bfloat16),
            ((depth, quarter), jnp.bfloat16),
        ],
        [ANYWHERE] * n + [IN_VMEM] * 4,
        [
            pltpu.VMEM((nd * count, quarter), jnp.bfloat16),
            pltpu.VMEM((n * 16, quarter), jnp.bfloat16),
            pltpu.SemaphoreType.DMA((4 * n + 3,)),
        ],
        2 * count * depth * depth,
        6 * depth * depth,
        "project_queries",
    )
    return got[:n], *got[n:]


def padded(width):
    return (width + 127) // 128 * 128


def ffn_body(m, *refs):
    nf_in, cot_in, weights_in = refs[:m], refs[m : 2 * m], refs[2 * m : 2 * m + 3]
    outs = refs[2 * m + 3 : 7 * m + 3]
    nf, cot, gate_w, up_w, down_w, acts, shares, sems, out_sems = refs[7 * m + 3 :]
    weights = (gate_w, up_w, down_w)
    rows = nf_in[0].shape[0]
    hidden_units = gate_w.shape[0]

    def load(src, dst, k):
        return pltpu.make_async_copy(src, dst, sems.at[k])

    loads = [load(weights_in[k], weights[k], k) for k in range(3)]
    nf_loads = [load(nf_in[b], nf.at[b], 3 + b) for b in range(m)]
    cot_loads = [load(cot_in[b], cot.at[b], 3 + m + b) for b in range(m)]
    start_all([nf_loads[0], loads[0], loads[1], cot_loads[0], loads[2]])
    start_all([*nf_loads[1:], *cot_loads[1:]])
    copies = []

    def store(b, k, src):
        copy = pltpu.make_async_copy(src, outs[5 * b + k], out_sems.at[5 * b + k])
        copy.start()
        copies.append(copy)

    for b in range(m):
        nf_loads[b].wait()
        if b == 0:
            loads[0].wait()
        gate_value = nt_dot(nf[b], gate_w[...])
        if b == 0:
            loads[1].wait()
        up_value = nt_dot(nf[b], up_w[...])
        cot_loads[b].wait()
        if b == 0:
            loads[2].wait()
        grad_inner = nt_dot(cot[b], down_w[...])
        sigmoid = 1.0 / (1.0 + jnp.exp(-gate_value))
        act = gate_value * sigmoid
        inner = (act * up_value).astype(jnp.bfloat16)
        grad_gate = (
            grad_inner * up_value * sigmoid * (1.0 + gate_value * (1.0 - sigmoid))
        ).astype(jnp.bfloat16)
        grad_up = (grad_inner * act).astype(jnp.bfloat16)
        for k, value in enumerate((inner, grad_gate, grad_up)):
            acts[3 * b + k, :, :hidden_units] = value
            store(b, k, acts.at[3 * b + k])
        shares[2 * b] = jnp.dot(
            grad_gate, gate_w[...], preferred_element_type=jnp.float32
        ) + jnp.dot(grad_up, up_w[...], preferred_element_type=jnp.float32)
        store(b, 3, shares.at[2 * b])
        shares[2 * b + 1] = jnp.dot(inner, down_w[...], preferred_element_type=jnp.float32)
        store(b, 4, shares.at[2 * b + 1])
    wait_all(copies)


def ffn_blocks(nf, cot, weights):
    m = len(nf)
    rows, depth = nf[0].shape
    units = weights[0].shape[0]
    act = ((rows, padded(units)), jnp.bfloat16)
    share = ((rows, depth), jnp.float32)
    got = call(
        functools.partial(ffn_body, m),
        [*nf, *cot, *weights],
        [ANYWHERE] * (2 * m + 3),
        [act, act, act, share, share] * m,
        [ANYWHERE] * (5 * m),
        [pltpu.VMEM((m, rows, depth), jnp.bfloat16)] * 2
        + [pltpu.VMEM((units, depth), jnp.bfloat16)] * 3
        + [
            pltpu.VMEM((3 * m, rows, padded(units)), jnp.bfloat16),
            pltpu.VMEM((2 * m, rows, depth), jnp.float32),
            pltpu.SemaphoreType.DMA((3 + 2 * m,)),
            pltpu.SemaphoreType.DMA((5 * m,)),
        ],
        12 * m * rows * units * depth,
        6 * units * depth + 12 * m * rows * depth,
        "ffn_blocks",
    )
    return [got[5 * b : 5 * b + 5] for b in range(m)]


def weight_gradient_body(count, units, info, *refs):
    lhs_in, rhs_in = refs[:count], refs[count : 2 * count]
    kept, sent, lhs, turned, rhs, sems = refs[2 * count :]
    core = info[2]
    copies, first = [], 0
    for k in range(count):
        rows = lhs_in[k].shape[0]
        at = pl.ds(first, rows)
        copies.append(pltpu.make_async_copy(lhs_in[k], lhs.at[at], sems.at[2 * k]))
        copies.append(pltpu.make_async_copy(rhs_in[k], rhs.at[at], sems.at[2 * k + 1]))
        first += rows
    start_all(copies)
    wait_all(copies[::2])
    block = 256

    def turn(b, _):
        at = pl.ds(aligned(b, block), block)
        turned[:, at] = lhs[at, :].T
        return 0

    lax.fori_loop(0, first // block, turn, 0)
    wait_all(copies[1::2])
    half = kept.shape[1]
    piece = 256

    def step(c, _):
        to = pl.ds(aligned(c, piece), piece)
        for out, side in ((kept, core), (sent, 1 - core)):
            cols = pl.ds(pl.multiple_of(side * half + c * piece, piece), piece)
            out[:, to] = jnp.dot(
                turned[...], rhs[:, cols], preferred_element_type=jnp.float32
            )[:units].astype(jnp.bfloat16)
        return 0

    lax.fori_loop(0, half // piece, step, 0)


def weight_gradient(info, lhs, rhs, units):
    count = len(lhs)
    rows = sum(b.shape[0] for b in rhs)
    width, depth = lhs[0].shape[1], rhs[0].shape[1]
    return call(
        functools.partial(weight_gradient_body, count, units),
        [info, *lhs, *rhs],
        [IN_SMEM] + [ANYWHERE] * (2 * count),
        [((units, depth // 2), jnp.bfloat16)] * 2,
        [IN_VMEM] * 2,
        [
            pltpu.VMEM((rows, width), jnp.bfloat16),
            pltpu.VMEM((width, rows), jnp.bfloat16),
            pltpu.VMEM((rows, depth), jnp.bfloat16),
            pltpu.SemaphoreType.DMA((2 * count,)),
        ],
        2 * rows * units * depth,
        2 * rows * depth,
        "weight_gradient",
    )


def hidden_body(n, nd, info, x, gains, *refs):
    blocks, parts = refs[:n], refs[n : n + nd]
    hidden, normed, mixed = refs[n + nd : n + nd + 3]
    weight, sems = refs[n + nd + 3 :]
    me, dp = info[0], info[1]
    share, quarter = blocks[0].shape[1], parts[0].shape[1]
    copies = []
    for r in range(nd):
        cols = pl.ds(aligned(dp ^ r, quarter), quarter)
        copies.append(pltpu.make_async_copy(parts[r], weight.at[:, cols], sems.at[r]))
    for r in range(n):
        cols = pl.ds(aligned(me ^ r, share), share)
        copies.append(pltpu.make_async_copy(blocks[r], mixed.at[:, cols], sems.at[nd + r]))
    wait_all(start_all(copies))
    depth = x.shape[1]
    piece = 512

    def step(c, total):
        cols = pl.ds(aligned(c, piece), piece)
        v = x[:, cols].astype(jnp.float32) + jnp.dot(
            mixed[...], weight[:, cols], preferred_element_type=jnp.float32
        )
        hidden[:, cols] = v
        return total + jnp.sum(v * v, axis=-1, keepdims=True)

    total = lax.fori_loop(0, depth // piece, step, jnp.zeros((x.shape[0], 1), jnp.float32))
    normed[...] = (
        hidden[...] * lax.rsqrt(total / depth + EPSILON) * gains[1:2, :]
    ).astype(jnp.bfloat16)


def project_mixed(n, nd, info, x, gains, blocks, parts):
    count, depth = x.shape
    return call(
        functools.partial(hidden_body, n, nd),
        [info, x, gains, *blocks, *parts],
        [IN_SMEM, IN_VMEM, IN_VMEM] + [ANYWHERE] * (n + nd),
        [
            ((count, depth), jnp.float32),
            ((count, depth), jnp.bfloat16),
            ((count, depth), jnp.bfloat16),
        ],
        [IN_VMEM] * 3,
        [pltpu.VMEM((depth, depth), jnp.bfloat16), pltpu.SemaphoreType.DMA((n + nd,))],
        2 * count * depth * depth,
        6 * depth * depth,
        "project_mixed",
    )


def norm_grad(v, gain, upstream):
    scale = norm_parts(v)
    weighted = upstream * gain
    through = weighted * scale - v * (scale**3) * jnp.mean(weighted * v, axis=-1, keepdims=True)
    return through, jnp.sum(upstream * v * scale, axis=0, keepdims=True)


def branch_body(n, nd, info, hidden, gains, cotangent, own, first, second, *refs):
    parts, refs = refs[:nd], refs[nd:]
    gm_out, cols_out = refs[:n], refs[n : n + nd]
    grad_hidden, gain_part, branch, weight, sems = refs[n + nd :]
    me, dp = info[0], info[1]
    quarter = parts[0].shape[1]
    copies = []
    for r in range(nd):
        cols = pl.ds(aligned(dp ^ r, quarter), quarter)
        copies.append(pltpu.make_async_copy(parts[r], weight.at[:, cols], sems.at[r]))
    start_all(copies)
    upstream = own[...] + first[...].astype(jnp.float32) + second[...].astype(jnp.float32)
    through, gain = norm_grad(hidden[...], gains[1:2, :], upstream)
    gain_part[...] = jnp.broadcast_to(gain, gain_part.shape)
    total = cotangent[...].astype(jnp.float32) + through
    grad_hidden[...] = total
    branch[...] = total.astype(jnp.bfloat16)
    for r in range(nd):
        cols_out[r][...] = branch[:, pl.ds(aligned(dp ^ r, quarter), quarter)]
    wait_all(copies)
    share = gm_out[0].shape[1]
    for r in range(n):
        rows = pl.ds(aligned(me ^ r, share), share)
        gm_out[r][...] = nt_dot(branch[...], weight[rows, :]).astype(jnp.bfloat16)


def branch_gradient(n, nd, info, hidden, gains, cotangent, sums, parts):
    count, depth = cotangent.shape
    got = call(
        functools.partial(branch_body, n, nd),
        [info, hidden, gains, cotangent, *sums, *parts],
        [IN_SMEM] + [IN_VMEM] * 6 + [ANYWHERE] * nd,
        [((count, depth // n), jnp.bfloat16)] * n
        + [((count, depth // nd), jnp.bfloat16)] * nd
        + [((count, depth), jnp.float32), ((8, depth), jnp.float32)],
        [IN_VMEM] * (n + nd + 2),
        [
            pltpu.VMEM((count, depth), jnp.bfloat16),
            pltpu.VMEM((depth, depth), jnp.bfloat16),
            pltpu.SemaphoreType.DMA((nd,)),
        ],
        2 * count * depth * depth,
        6 * depth * depth,
        "branch_gradient",
    )
    return got[:n], got[n : n + nd], got[n + nd], got[n + nd + 1]


def sort_body(n, nd, info, *refs):
    blocks, cols_out = refs[:n], refs[n : n + nd]
    rows, sems = refs[n + nd :]
    me, dp = info[0], info[1]
    share, quarter = blocks[0].shape[1], cols_out[0].shape[1]
    copies = []
    for r in range(n):
        cols = pl.ds(aligned(me ^ r, share), share)
        copies.append(pltpu.make_async_copy(blocks[r], rows.at[:, cols], sems.at[r]))
    wait_all(start_all(copies))
    copies = []
    for r in range(nd):
        cols = pl.ds(aligned(dp ^ r, quarter), quarter)
        copies.append(pltpu.make_async_copy(rows.at[:, cols], cols_out[r], sems.at[r]))
    wait_all(start_all(copies))


def sort_columns(n, nd, info, blocks):
    count, share = blocks[0].shape
    depth = n * share
    return call(
        functools.partial(sort_body, n, nd),
        [info, *blocks],
        [IN_SMEM] + [ANYWHERE] * n,
        [((count, depth // nd), jnp.bfloat16)] * nd,
        [ANYWHERE] * nd,
        [pltpu.VMEM((count, depth), jnp.bfloat16), pltpu.SemaphoreType.DMA((max(n, nd),))],
        0,
        6 * count * depth,
        "sort_columns",
    )


def split_body(n, info, *refs):
    blocks, keys, values, sems = refs[:n], refs[n], refs[n + 1], refs[n + 2]
    me = info[0]
    share = blocks[0].shape[1] // 2
    copies = []
    for r in range(n):
        cols = pl.ds(aligned(me ^ r, share), share)
        copies.append(
            pltpu.make_async_copy(blocks[r].at[:, pl.ds(0, share)], keys.at[:, cols], sems.at[2 * r])
        )
        copies.append(
            pltpu.make_async_copy(
                blocks[r].at[:, pl.ds(share, share)], values.at[:, cols], sems.at[2 * r + 1]
            )
        )
    wait_all(start_all(copies))


def split_keys_values(n, info, blocks):
    count, share = blocks[0].shape
    depth = n * share // 2
    return call(
        functools.partial(split_body, n),
        [info, *blocks],
        [IN_SMEM] + [ANYWHERE] * n,
        [((count, depth), jnp.bfloat16)] * 2,
        [IN_VMEM] * 2,
        [pltpu.SemaphoreType.DMA((2 * n,))],
        0,
        8 * count * depth,
        "split_keys_values",
    )


def input_body(nd, x, gains, grad_hidden, *refs):
    cols, parts = refs[:nd], refs[nd : 2 * nd]
    out, gain_part, upstream = refs[2 * nd :]
    piece = 512

    def step(c, _):
        rows = pl.ds(aligned(c, piece), piece)
        upstream[:, rows] = sum(nt_dot(cols[r][...], parts[r][rows, :]) for r in range(nd))
        return 0

    lax.fori_loop(0, x.shape[1] // piece, step, 0)
    through, gain = norm_grad(x[...].astype(jnp.float32), gains[0:1, :], upstream[...])
    gain_part[...] = jnp.broadcast_to(gain, gain_part.shape)
    out[...] = (grad_hidden[...] + through).astype(jnp.bfloat16)


def input_gradient(nd, x, gains, grad_hidden, cols, parts):
    count, depth = x.shape
    return call(
        functools.partial(input_body, nd),
        [x, gains, grad_hidden, *cols, *parts],
        [IN_VMEM] * (3 + 2 * nd),
        [((count, depth), jnp.bfloat16), ((8, depth), jnp.float32)],
        [IN_VMEM] * 2,
        [pltpu.VMEM((count, depth), jnp.float32)],
        2 * count * depth * depth,
        6 * depth * depth,
        "input_gradient",
    )


def projections_body(n, nd, info, normed, attn_part, ffn_part, *refs):
    branch_cols, query_cols, mixed_in = refs[:nd], refs[nd : 2 * nd], refs[2 * nd : 3 * nd]
    outs = refs[3 * nd : 3 * nd + n]
    branch, query, mixed = refs[3 * nd + n :]
    count = branch_cols[0].shape[0]
    share = mixed.shape[1] // n
    for k in range(nd):
        rows = slice(k * count, (k + 1) * count)
        mixed[rows, :] = mixed_in[k][...]
        branch[rows, :] = branch_cols[k][...]
        query[rows, :] = query_cols[k][...]
    for k in range(n):
        cols = pl.ds(aligned(info[3 + k], share), share)
        outs[k][:share, :] = tn_dot(mixed[:, cols], branch[...])
        outs[k][share : 2 * share, :] = tn_dot(normed[:, cols], query[...])
        outs[k][2 * share :, :] = jnp.zeros((GAIN_ROWS, branch.shape[1]), jnp.float32)
        outs[k][2 * share : 2 * share + 8, :share] = attn_part[:, cols]
        outs[k][2 * share : 2 * share + 8, share : 2 * share] = ffn_part[:, cols]


def projection_gradients(n, nd, info, mixed, normed, attn_part, ffn_part, branch_cols, query_cols):
    rows, depth = normed.shape
    count, quarter = branch_cols[0].shape
    return call(
        functools.partial(projections_body, n, nd),
        [info, normed, attn_part, ffn_part, *branch_cols, *query_cols, *mixed],
        [IN_SMEM] + [IN_VMEM] * (3 + 3 * nd),
        [((2 * depth // n + GAIN_ROWS, quarter), jnp.float32)] * n,
        [IN_VMEM] * n,
        [pltpu.VMEM((rows, quarter), jnp.bfloat16)] * 2
        + [pltpu.VMEM((rows, depth), jnp.bfloat16)],
        4 * rows * depth * quarter,
        4 * rows * depth,
        "projection_gradients",
    )


def join_body(nd, info, *refs):
    parts, (out_grad, query_grad, gain_sum) = refs[:nd], refs[nd:]
    share = out_grad.shape[0]
    quarter = parts[0].shape[1]
    dp = info[1]
    for r in range(nd):
        cols = pl.ds(aligned(dp ^ r, quarter), quarter)
        part = parts[r][...].astype(jnp.float32)
        out_grad[:, cols] = part[:share]
        query_grad[:, cols] = part[share : 2 * share]
    tops = [parts[r][2 * share : 2 * share + 16, :].astype(jnp.float32)[:8] for r in range(nd)]
    gain_sum[...] = tree_sum(tops)


def join_projections(nd, info, parts):
    rows, quarter = parts[0].shape
    share, depth = (rows - GAIN_ROWS) // 2, quarter * nd
    return call(
        functools.partial(join_body, nd),
        [info, *parts],
        [IN_SMEM] + [IN_VMEM] * nd,
        [((share, depth), jnp.float32)] * 2 + [((8, quarter), jnp.float32)],
        [IN_VMEM] * 3,
        [],
        0,
        10 * share * depth,
        "join_projections",
    )


def chip_sum_body(kept, *refs):
    others, out = refs[:-1], refs[-1]
    half = len(others) // 2
    top = others[0].shape[0]
    for side, first in ((others[:half], 0), (others[half:], top)):
        rows = slice(first, first + side[0].shape[0])
        terms = [kept[rows, :].astype(jnp.float32)] + [v[...].astype(jnp.float32) for v in side]
        out[rows, :] = tree_sum(terms).astype(jnp.bfloat16)


def chip_sum(operands):
    shape = operands[0].shape
    return call(
        chip_sum_body,
        operands,
        [IN_VMEM] * len(operands),
        [(shape, jnp.bfloat16)],
        [IN_VMEM],
        [],
        0,
        6 * shape[0] * shape[1],
        "chip_sum",
    )[0]


def spread_body(info, mine, other, out):
    half = mine.shape[1]
    for ref, side in ((mine, info[2]), (other, 1 - info[2])):
        out[:, pl.ds(aligned(side, half), half)] = ref[...].astype(jnp.float32)


def spread_columns(info, mine, other):
    rows, half = mine.shape
    return call(
        spread_body,
        [info, mine, other],
        [IN_SMEM, IN_VMEM, IN_VMEM],
        [((rows, 2 * half), jnp.float32)],
        [IN_VMEM],
        [],
        0,
        12 * rows * half,
        "spread_columns",
    )[0]


def tree_sum(parts):
    while len(parts) > 1:
        parts = [parts[k] + parts[k + 1] for k in range(0, len(parts), 2)]
    return parts[0]


def columns(x, start, width):
    return lax.dynamic_slice_in_dim(x, start, width, 1)


def make_local(mesh):
    net = Links(mesh)
    n, nd = net.n, net.nd
    dp_order = list(range(0, nd, 2)) + list(range(1, nd, 2))
    half_way = n // 2
    ring_order = [0] + [s for k in range(1, half_way) for s in (-k, k)] + ["a", "b"]

    def exchange(blocks, axis="seq"):
        return [b if r == 0 else net.swap(b, axis, r) for r, b in enumerate(blocks)]

    def chips(x, *deps):
        sent = after(x, *deps)
        return [x] + [net.swap(sent, "dp", r) for r in range(2, nd, 2)]

    def cores(near, *deps):
        return list(near) + [net.swap(v, "dp", 1) for v in tie(near, *deps)]

    def paced(ring, blocks, spare=1):
        out, sent = [], 1
        arrived = ring.step()
        steps = half_way - 1
        for k in range(steps):
            until = 1 + (n - 1) * (k + 1) // steps
            some = tie(blocks[sent:until], *arrived)
            fresh = [net.swap(b, "seq", sent + i) for i, b in enumerate(some)]
            arrived = ring.step(*out[-len(some) :]) if k else ring.step()
            out += fresh
            sent = until
        return out

    def local(
        layer_input,
        global_keys,
        global_values,
        lengths,
        attn_gain,
        query_weight,
        out_weight,
        ffn_gain,
        gate_weight,
        up_weight,
        down_weight,
        cotangent,
    ):
        length = lengths[0]
        me, mine = lax.axis_index("seq"), lax.axis_index("dp")
        core, group = mine % 2, net.group(mine)
        place = net.place()
        depth = layer_input.shape[1]
        quarter = depth // nd
        per = n // nd
        owners = [net.owner(place, key) for key in ring_order[:-2]] + [net.owner(place, half_way)]
        info = jnp.stack([me, group, core, *owners]).astype(jnp.int32)
        heads_info = jnp.stack([me, length, group * per + me % per]).astype(jnp.int32)

        gains = jnp.concatenate([attn_gain, ffn_gain])
        gain_rows = jnp.zeros((GAIN_ROWS, quarter), jnp.bfloat16)
        gain_rows = gain_rows.at[:, : gains.shape[0]].set(gains[None])
        mine_of = [columns(w, group * quarter, quarter) for w in (query_weight, out_weight)]
        ring = RingGather(net, jnp.concatenate([gain_rows, *mine_of], 0))
        kv_sent = list(pack_keys_values(n, info, global_keys, global_values))
        kv_blocks = [kv_sent[0]] + paced(ring, kv_sent)
        got = ring.got
        xs = cores(chips(layer_input), got["a"], got["b"])
        q_sent, normed_all, gains, query_quarter, out_quarter = project_queries(
            n, nd, info, xs, [got[k] for k in ring_order]
        )
        q_sent = tie(q_sent, *kv_blocks)
        q_blocks = [net.to_heads(b, m) for m, b in enumerate(q_sent)]
        out_near = chips(out_quarter, *q_blocks)
        mixed_sent, stats, ot = attention_forward(heads_info, q_blocks, kv_blocks)
        cot_ring = RingGather(net, cotangent)
        cot_1 = cot_ring.step(*q_blocks)
        mixed_blocks = exchange(tie(mixed_sent, *cot_1))
        cot_2 = cot_ring.step(*mixed_blocks)
        out_parts = cores(out_near, *mixed_blocks[1:])
        hidden, normed_ffn, mixed = project_mixed(
            n, nd, info, layer_input, gains, mixed_blocks, out_parts
        )

        nf_ring = RingGather(net, normed_ffn)
        weights = (gate_weight, up_weight, down_weight)
        units = gate_weight.shape[0]
        made = {0: ffn_blocks([normed_ffn], [cotangent], weights)[0]}

        def ffn(*keys, deps=()):
            nf, cot = ([ring.got[k] for k in keys] for ring in (nf_ring, cot_ring))
            nf = tie(nf, *deps)
            made.update(zip(keys, ffn_blocks(nf, cot, weights)))

        fresh = nf_ring.step()
        query_near = chips(query_quarter, normed_ffn)
        cot_fresh, before = cot_2, (made[0][3],)
        for k in range(1, half_way):
            later = cot_ring.step(*fresh) if cot_ring.at < half_way else cot_fresh
            fresh = nf_ring.step(*cot_fresh, *before, *(query_near if k == half_way - 1 else ()))
            ffn(-k, k)
            before = (made[k][3], made[-k][3])
            cot_fresh = later
        query_parts = cores(query_near, *fresh)
        mixed_near = chips(mixed, *query_near)
        ffn("a", "b", deps=before)
        nf, cot = nf_ring.got, cot_ring.got

        def exchange_x(kept, *deps):
            sent = after(kept, *deps)
            return [net.swap(sent, "dp", r) for r in range(2, nd, 2)]

        grad_sum = RowSum(net, lambda key: made[key][3])
        arrived = grad_sum.step(*query_parts, *mixed_near)
        mixed_parts = cores(mixed_near, *arrived)
        kept, deps, swapped = [], (), None
        for k in range(3):
            upcoming = grad_sum.step(*deps, *(mixed_parts if k else ()))
            lhs = tie([made[key][(1, 2, 0)[k]] for key in ring_order], *arrived)
            rhs = [(nf, nf, cot)[k][key] for key in ring_order]
            if swapped:
                kept.append(low(wide(mine_half) + wide(swapped[0])))
            deps = (*swapped,) if swapped else ()
            mine_half, sent_half = weight_gradient(info, lhs, rhs, units)
            swapped = (net.swap(sent_half, "dp", 1),)
            deps = (*deps, mine_half)
            last, arrived = arrived, upcoming
        top = units // 2
        others = [exchange_x(kept[0][:top], *last)]
        grad_sums = tie(grad_sum.rest(), *deps, *others[0])
        kept.append(low(wide(mine_half) + wide(swapped[0])))
        others.append(exchange_x(kept[0][top:], *grad_sums[1:]))

        def dp_cols(cols, *deps):
            sent = tie(cols, *deps)
            return [b if r == 0 else net.swap(b, "dp", r) for r, b in zip(dp_order, sent)]

        out_sum = RowSum(net, lambda key: made[key][4])
        out_1 = out_sum.step(*grad_sums[1:])
        gm_sent, branch_cols, grad_hidden, ffn_gain_part = branch_gradient(
            n, nd, info, hidden, gains, cotangent, grad_sums, out_parts
        )
        gm_blocks = exchange(tie(gm_sent, *out_1, *others[1]))
        branch_got = dp_cols(branch_cols, *gm_sent)
        gm_blocks = tie(gm_blocks, *branch_got)
        others.append(exchange_x(kept[1][:top], *gm_blocks))
        out_2 = out_sum.step(*gm_blocks)
        dq_sent, dkv_sent = attention_backward(
            heads_info, q_blocks, kv_blocks, gm_blocks, stats, ot
        )


        dq_sent = tie(dq_sent, *out_2, *others[2])
        others.append(exchange_x(kept[1][top:], *dq_sent))
        dq_blocks = tie(exchange(dq_sent), *others[3])

        def dp_total(k, *deps):
            total = chip_sum(tie([kept[k], *others[2 * k], *others[2 * k + 1]], *deps))
            return total, net.swap(total, "dp", 1)

        query_cols = sort_columns(n, nd, info, dq_blocks)

        query_got = dp_cols(query_cols)
        out_3 = out_sum.step(*query_cols)
        gate_total = dp_total(0, *dq_blocks)
        up_total = dp_total(1, *query_cols)
        others.append(exchange_x(kept[2][:top], *query_got))
        early = (n - 1) * 4 // 7
        dkv_early = [
            net.swap(b, "seq", r + 1) for r, b in enumerate(tie(dkv_sent[1 : early + 1], *query_cols))
        ]
        input_grad, attn_gain_part = input_gradient(
            nd, layer_input, gains, grad_hidden, query_cols, query_parts
        )
        shares = projection_gradients(
            n,
            nd,
            info,
            mixed_parts,
            normed_all,
            attn_gain_part,
            ffn_gain_part,
            branch_got,
            tie(query_got, *out_3, *dkv_early, gate_total[1], up_total[1]),
        )

        def share_of(key):
            if key in ("a", "b"):
                rows = shares[-1].shape[0] // 2
                return shares[-1][:rows] if key == "a" else shares[-1][rows:]
            return shares[ring_order.index(key)]

        share_sum = RowSum(net, share_of)
        shared = share_sum.step()
        others.append(exchange_x(kept[2][top:], *shared))
        for _ in range(half_way - 3):
            shared = share_sum.step()
        dkv_more = [
            net.swap(b, "seq", early + 1 + i)
            for i, b in enumerate(tie(dkv_sent[early + 1 :], *shared))
        ]
        dkv_blocks = [dkv_sent[0], *dkv_early, *dkv_more]
        shared = share_sum.step()
        out_sum.step(*shared)
        share_sum.step(*others[4])
        own, first, second = share_sum.rest()
        down_total = dp_total(2, first, second)
        gate_grad, up_grad, down_grad = [
            spread_columns(info, *t) for t in (gate_total, up_total, down_total)
        ]
        projections = low(own + wide(first) + wide(second))
        out_grad, query_grad, gain_sum = join_projections(
            nd, info, cores(chips(projections))
        )
        own, first, second = out_sum.rest()
        layer_output = low(hidden + (own + wide(first) + wide(second)))
        key_grad, value_grad = split_keys_values(n, info, dkv_blocks)
        attn_count = attn_gain.shape[0]
        return (
            layer_output,
            input_grad,
            key_grad,
            value_grad,
            gain_sum[0, :attn_count],
            query_grad,
            out_grad,
            gain_sum[0, attn_count : 2 * attn_count],
            gate_grad,
            up_grad,
            down_grad,
        )

    return local


def solution(mesh):
    placed = (
        P(("dp", "seq"), None),
        P(("dp", "seq"), None),
        P(("dp", "seq"), None),
        P("dp"),
        P("seq"),
        P("seq", None),
        P("seq", None),
        P("seq"),
        P("seq", None),
        P("seq", None),
        P("seq", None),
        P(("dp", "seq"), None),
    )
    return jax.shard_map(
        make_local(mesh),
        mesh=mesh,
        in_specs=placed,
        out_specs=(
            P(("dp", "seq"), None),
            P(("dp", "seq"), None),
            P(("dp", "seq"), None),
            P(("dp", "seq"), None),
            P("seq"),
            P("seq", None),
            P("seq", None),
            P("seq"),
            P("seq", None),
            P("seq", None),
            P("seq", None),
        ),
        check_vma=False,
    )
```

time: 885 us -> 808 us (0.913)
  Pallas kernels: 94.7 us -> 235 us
  matrix products: 111 us -> 0 us
  waiting for transfers between devices: 399 us -> 351 us
  local copies, waits for them, and re-layouts: 46 us -> 15.1 us
  other arithmetic: 39 us -> 24.6 us
  starting transfers between devices: 183 us -> 171 us
    pallas_call x10 -> x25, Pallas kernels: 94.7 us -> 235 us  [call(): pl.pallas_call(body, name=name, in_specs=specs, out_specs=tuple(out_specs...]
    dot_general x59 -> x0, matrix products: 111 us -> none  [the longest x27 45.5 us: outer_cols(): lax.dot_general(left_side, right_side, (((1,), (1,)), ((), ())), preferre...]
    ppermute x32 -> x24, waiting for transfers between devices: 184 us -> 121 us  [to_right(): return lax.ppermute(x, 'seq', self.right)]
    ppermute x32 -> x24, waiting for transfers between devices: 95.1 us -> 60.2 us  [to_left(): return lax.ppermute(x, 'seq', self.left)]
    ppermute x79 -> x68, starting transfers between devices: 115 us -> 81.9 us  [swap(): return lax.ppermute(x, axis, [(k, k ^ r) for k in range(count)])]
    ppermute x79 -> x68, waiting for transfers between devices: 119 us -> 149 us  [swap(): return lax.ppermute(x, axis, [(k, k ^ r) for k in range(count)])]
    ppermute x0 -> x8, starting transfers between devices: none -> 24 us  [to_heads(): return lax.ppermute(x, ('dp', 'seq'), pairs)]
    unnamed x253 -> x250, local copies, waits for them, and re-layouts: 30.4 us -> 7.99 us
  transfers between devices with their start and end apart: 143 -> 124, of which waited for: 56 -> 58; matrix products, arithmetic and copies ran while one was open for 20% -> 4% of each run, Pallas kernels for 10% -> 28%
where the time goes in v2:
time: 808 us; the launch traced here: 799 us
  waiting for transfers between devices  351 us (43%)
  Pallas kernels  235 us (29%)
  starting transfers between devices  171 us (21%)
  other arithmetic  24.6 us (3%)
  local copies, waits for them, and re-layouts  15.1 us (2%)
    pallas_call x25, Pallas kernels, call(): pl.pallas_call(body, name=name, in_specs=specs, out_specs=tuple(out_specs...  235 us
    ppermute x68, waiting for transfers between devices, swap(): return lax.ppermute(x, axis, [(k, k ^ r) for k in range(count)])  149 us
    ppermute x24, waiting for transfers between devices, to_right(): return lax.ppermute(x, 'seq', self.right)  121 us
    ppermute x68, starting transfers between devices, swap(): return lax.ppermute(x, axis, [(k, k ^ r) for k in range(count)])  81.9 us
    ppermute x24, waiting for transfers between devices, to_left(): return lax.ppermute(x, 'seq', self.left)  60.2 us
    ppermute x24, starting transfers between devices, to_left(): return lax.ppermute(x, 'seq', self.left)  37.8 us
    ppermute x24, starting transfers between devices, to_right(): return lax.ppermute(x, 'seq', self.right)  26.8 us
    ppermute x8, starting transfers between devices, to_heads(): return lax.ppermute(x, ('dp', 'seq'), pairs)  24 us
  transfers between devices with their start and end apart: 124, of which 58 were waited for; matrix products, arithmetic and copies ran while one was open for 4% of the time, Pallas kernels for 28%

profile of v2, /device:TPU:0, one launch (start us, length us, event | category | flops | bytes accessed | tf_op | source)
XLA Modules:
  0.0 799.1 jit_solution(5864333476116182208)
XLA Ops:
  5.6 12.6 %collective-permute-done.1.refs_5_ = bf16[544,512]{1,0:T(8,128)(2,1)S(1)} collective-permute-done((bf16[544,512]{1,0:T(8,128)(2,1)S(1)}, bf16[544,512]{1,0:T(8,128)(2,1)S(1)}, u32[]{:S(2)}, u32[]{:S(2)}) %collective-permute-start.1) | collective-permute-done | bytes 557088 | tf_op jit(solution)/shard_map/ppermute | solution.py:85
  22.3 3.7 pack_keys_values.1
  30.7 9.0 %collective-permute-done.5.refs_9_ = bf16[256,512]{1,0:T(8,128)(2,1)S(1)} collective-permute-done((bf16[256,512]{1,0:T(8,128)(2,1)}, bf16[256,512]{1,0:T(8,128)(2,1)S(1)}, u32[]{:S(2)}, u32[]{:S(2)}) %collective-permute-start.5) | collective-permute-done | bytes 262176 | tf_op jit(solution)/shard_map/ppermute | solution.py:103
  45.0 15.4 %collective-permute-done.7.refs_9_ = bf16[544,512]{1,0:T(8,128)(2,1)S(1)} collective-permute-done((bf16[544,512]{1,0:T(8,128)(2,1)}, bf16[544,512]{1,0:T(8,128)(2,1)S(1)}, u32[]{:S(2)}, u32[]{:S(2)}) %collective-permute-start.7) | collective-permute-done | bytes 557088 | tf_op jit(solution)/shard_map/ppermute | solution.py:85
  60.5 4.2 collective-permute-done.9.refs_11_
  66.7 4.5 collective-permute-done.11.refs_11_
  80.9 11.5 %project_queries.1 = (bf16[256,256]{1,0:T(8,128)(2,1)}, bf16[256,256]{1,0:T(8,128)(2,1)}, bf16[256,256]{1,0:T(8,128)(2,1)}, bf16[256,256]{1,0:T(8,128)(2,1)}, bf...) custom-call(s32[11]{0:T(128)} %stack.54.info, ...), custom_call_target="tpu_custom_call" | custom-call | flops 536870912 | bytes 6291456 | tf_op jit(solution)/shard_map/project_queries/pallas_call | solution.py:180
  92.3 8.2 %collective-permute-done.15.refs_13_ = bf16[256,512]{1,0:T(8,128)(2,1)} collective-permute-done((bf16[256,512]{1,0:T(8,128)(2,1)}, bf16[256,512]{1,0:T(8,128)(2,1)}, u32[]{:S(2)}, u32[]{:S(2)}) %collective-permute-start.15) | collective-permute-done | bytes 262176 | tf_op jit(solution)/shard_map/ppermute | solution.py:103
  103.7 15.8 %collective-permute-start.20 = (bf16[256,256]{1,0:T(8,128)(2,1)}, bf16[256,256]{1,0:T(8,128)(2,1)S(1)}, u32[]{:S(2)}, u32[]{:S(2)}) collective-permute-start(bf16[256,256]{1,0:T(8,128)(2,1)} %get-tuple-element.381), channel_id=1, source_target_pairs={{0,16},{1,17},{2,0},{3,1},{4,24},{5,25},{6,8},{7,9},{8,20},{9,21},... | collective-permute-start | bytes 393224 | tf_op jit(solution)/shard_map/ppermute | solution.py:99
  124.5 13.0 %collective-permute-done.20.refs_2_ = bf16[256,256]{1,0:T(8,128)(2,1)S(1)} collective-permute-done((bf16[256,256]{1,0:T(8,128)(2,1)}, bf16[256,256]{1,0:T(8,128)(2,1)S(1)}, u32[]{:S(2)}, u32[]{:S(2)}) %collective-permute-start.20) | collective-permute-done | bytes 131104 | tf_op jit(solution)/shard_map/ppermute | solution.py:99
  137.7 8.0 collective-permute-done.25.refs_7_
  152.5 9.3 %attention_forward.1 = (bf16[256,256]{1,0:T(8,128)(2,1)}, bf16[256,256]{1,0:T(8,128)(2,1)}, bf16[256,256]{1,0:T(8,128)(2,1)}, bf16[256,256]{1,0:T(8,128)(2,1)}, ...) custom-call(s32[3]{0:T(128)} %pad_add_fusion.info, ...), custom_call_target="tpu_custom_call" | custom-call | flops 4294967296 | bytes 1310720 | tf_op jit(solution)/shard_map/attention_forward/pallas_call | solution.py:180
  161.8 13.5 %collective-permute-done.26.refs_2_.refs_10_ = bf16[256,2048]{1,0:T(8,128)(2,1)} collective-permute-done((bf16[256,2048]{1,0:T(8,128)(2,1)S(1)}, bf16[256,2048]{1,0:T(8,128)(2,1)}, u32[]{:S(2)}, u32[]{:S(2)}) %collective-permute-start.26) | collective-permute-done | bytes 1048608 | tf_op jit(solution)/shard_map/ppermute | solution.py:85
  184.6 4.2 collective-permute-done.30.refs_3_
  190.7 6.8 collective-permute-done.31.refs_4_
  202.4 3.4 collective-permute-start.41
  208.3 10.2 %project_mixed.1 = (f32[256,2048]{1,0:T(8,128)}, bf16[256,2048]{1,0:T(8,128)(2,1)}, bf16[256,2048]{1,0:T(8,128)(2,1)}) custom-call(s32[11]{0:T(128)} %stack.54.info, bf16[256,2048]{1,0:T(8,128)(2,1)} %x.3, f32[8,2048]{1,0:T(8,128)} %get-tuple-element.363.gains, bf16[256,256]{1,0:T(8,128)(2,1)} %get-tuple-element.396.refs_0_, bf16[256,256]{1,0:T(8,128)(2,1)} %copy-done.81, ...), custom_call_target="tpu_custom_call" | custom-call | flops 536870912 | bytes 6291456 | tf_op jit(solution)/shard_map/project_mixed/pallas_call | solution.py:180
  220.7 3.8 collective-permute-start.39
  224.5 10.4 %ffn_blocks.5 = (bf16[256,768]{1,0:T(8,128)(2,1)}, bf16[256,768]{1,0:T(8,128)(2,1)}, bf16[256,768]{1,0:T(8,128)(2,1)}, f32[256,2048]{1,0:T(8,128)}, f32[256,2048]{1,0:T(8,128)}) custom-call(bf16[256,2048]{1,0:T(8,128)(2,1)} %get-tuple-element.409.refs_0_.refs_9_, bf16[256,2048]{1,0:T(8,128)(2,1)} %cotangent.1, bf16[688,2048]{1,0:T(8,128)(2,1)} %refs_4_.9, ...), custom_call_target="tpu_custom_call" | custom-call | flops 1082130432 | bytes 3686400 | tf_op jit(solution)/shard_map/ffn_blocks/pallas_call | solution.py:180
  234.9 17.0 %collective-permute-done.38.refs_0_.refs_10_ = bf16[256,2048]{1,0:T(8,128)(2,1)S(1)} collective-permute-done((bf16[256,2048]{1,0:T(8,128)(2,1)}, bf16[256,2048]{1,0:T(8,128)(2,1)S(1)}, u32[]{:S(2)}, u32[]{:S(2)}) %collective-permute-start.38) | collective-permute-done | bytes 1048608 | tf_op jit(solution)/shard_map/ppermute | solution.py:85
  258.0 16.7 %ffn_blocks.6 = (bf16[256,768]{1,0:T(8,128)(2,1)}, bf16[256,768]{1,0:T(8,128)(2,1)}, bf16[256,768]{1,0:T(8,128)(2,1)}, f32[256,2048]{1,0:T(8,128)}, f32[256,2048...) custom-call(bf16[256,2048]{1,0:T(8,128)(2,1)} %copy-done.6, ...), custom_call_target="tpu_custom_call" | custom-call | flops 2164260864 | bytes 5259264 | tf_op jit(solution)/shard_map/ffn_blocks/pallas_call | solution.py:180
  274.7 4.1 collective-permute-done.42.refs_0_.refs_12_
  280.7 18.9 %collective-permute-done.44.refs_2_.refs_14_ = bf16[256,2048]{1,0:T(8,128)(2,1)S(1)} collective-permute-done((bf16[256,2048]{1,0:T(8,128)(2,1)}, bf16[256,2048]{1,0:T(8,128)(2,1)S(1)}, u32[]{:S(2)}, u32[]{:S(2)}) %collective-permute-start.44) | collective-permute-done | bytes 1048608 | tf_op jit(solution)/shard_map/ppermute | solution.py:85
  306.2 16.8 %ffn_blocks.7 = (bf16[256,768]{1,0:T(8,128)(2,1)}, bf16[256,768]{1,0:T(8,128)(2,1)}, bf16[256,768]{1,0:T(8,128)(2,1)}, f32[256,2048]{1,0:T(8,128)}, f32[256,2048...) custom-call(bf16[256,2048]{1,0:T(8,128)(2,1)} %copy-done.8, ...), custom_call_target="tpu_custom_call" | custom-call | flops 2164260864 | bytes 5259264 | tf_op jit(solution)/shard_map/ffn_blocks/pallas_call | solution.py:180
  323.0 3.9 collective-permute-done.46.refs_0_.refs_14_
  327.6 7.2 collective-permute-done.48.refs_2_.refs_16_
  337.6 8.4 %collective-permute-done.51.refs_0_.refs_16_ = bf16[128,2048]{1,0:T(8,128)(2,1)S(1)} collective-permute-done((bf16[128,2048]{1,0:T(8,128)(2,1)S(1)}, bf16[128,2048]{1,0:T(8,128)(2,1)S(1)}, u32[]{:S(2)}, u32[]{:S(2)}) %collective-permute-start.51) | collective-permute-done | bytes 524320 | tf_op jit(solution)/shard_map/ppermute | solution.py:85
  348.6 16.7 %ffn_blocks.8 = (bf16[256,768]{1,0:T(8,128)(2,1)}, bf16[256,768]{1,0:T(8,128)(2,1)}, bf16[256,768]{1,0:T(8,128)(2,1)}, f32[256,2048]{1,0:T(8,128)}, f32[256,2048...) custom-call(bf16[256,2048]{1,0:T(8,128)(2,1)} %copy-done, ...), custom_call_target="tpu_custom_call" | custom-call | flops 2164260864 | bytes 5259264 | tf_op jit(solution)/shard_map/ffn_blocks/pallas_call | solution.py:180
  365.3 13.6 %ffn_blocks.9 = (bf16[128,768]{1,0:T(8,128)(2,1)}, bf16[128,768]{1,0:T(8,128)(2,1)}, bf16[128,768]{1,0:T(8,128)(2,1)}, f32[128,2048]{1,0:T(8,128)}, f32[128,2048...) custom-call(bf16[128,2048]{1,0:T(8,128)(2,1)} %copy-done.17, ...), custom_call_target="tpu_custom_call" | custom-call | flops 1082130432 | bytes 3686400 | tf_op jit(solution)/shard_map/ffn_blocks/pallas_call | solution.py:180
  384.1 11.3 %collective-permute-done.56 = bf16[128,2048]{1,0:T(8,128)(2,1)S(1)} collective-permute-done((bf16[128,2048]{1,0:T(8,128)(2,1)S(1)}, bf16[128,2048]{1,0:T(8,128)(2,1)S(1)}, u32[]{:S(2)}, u32[]{:S(2)}) %collective-permute-start.56) | collective-permute-done | bytes 524320 | tf_op jit(solution)/shard_map/ppermute | solution.py:88
  399.1 15.1 %weight_gradient.3 = (bf16[688,1024]{1,0:T(8,128)(2,1)}, bf16[688,1024]{1,0:T(8,128)(2,1)}) custom-call(s32[11]{0:T(128)} %stack.54.info, bf16[256,768]{1,0:T(8,128)(2,1)} %get-tuple-element.464.refs_0_, bf16[256,768]{1,0:T(8,128)(2,1)} %get-tuple-element.465.refs_1_, bf16[256,768]{1,0:T(8,128)(2,1)} %get-tuple-element.466.refs_2_, ...), custom_call_target="tpu_custom_call" | custom-call | flops 1442840576 | bytes 2097152 | tf_op jit(solution)/shard_map/weight_gradient/pallas_call | solution.py:180
  414.3 5.9 collective-permute-done.58
  423.3 15.3 %weight_gradient.4 = (bf16[688,1024]{1,0:T(8,128)(2,1)}, bf16[688,1024]{1,0:T(8,128)(2,1)}) custom-call(s32[11]{0:T(128)} %stack.54.info, bf16[256,768]{1,0:T(8,128)(2,1)} %get-tuple-element.488.refs_0_, bf16[256,768]{1,0:T(8,128)(2,1)} %get-tuple-element.489.refs_1_, bf16[256,768]{1,0:T(8,128)(2,1)} %get-tuple-element.490.refs_2_, ...), custom_call_target="tpu_custom_call" | custom-call | flops 1442840576 | bytes 2097152 | tf_op jit(solution)/shard_map/weight_gradient/pallas_call | solution.py:180
  439.2 4.6 collective-permute-done.62
  455.5 15.5 %weight_gradient.5 = (bf16[688,1024]{1,0:T(8,128)(2,1)}, bf16[688,1024]{1,0:T(8,128)(2,1)}) custom-call(s32[11]{0:T(128)} %stack.54.info, bf16[256,768]{1,0:T(8,128)(2,1)} %get-tuple-element.510.refs_0_, bf16[256,768]{1,0:T(8,128)(2,1)} %get-tuple-element.511.refs_1_, bf16[256,768]{1,0:T(8,128)(2,1)} %get-tuple-element.512.refs_2_, ...), custom_call_target="tpu_custom_call" | custom-call | flops 1442840576 | bytes 2097152 | tf_op jit(solution)/shard_map/weight_gradient/pallas_call | solution.py:180
  475.8 10.4 %branch_gradient.1 = (bf16[256,256]{1,0:T(8,128)(2,1)}, bf16[256,256]{1,0:T(8,128)(2,1)}, bf16[256,256]{1,0:T(8,128)(2,1)}, bf16[256,256]{1,0:T(8,128)(2,1)}, bf...) custom-call(s32[11]{0:T(128)} %stack.54.info, ...), custom_call_target="tpu_custom_call" | custom-call | flops 536870912 | bytes 6291456 | tf_op jit(solution)/shard_map/branch_gradient/pallas_call | solution.py:180
  506.6 8.6 %collective-permute-done.75.refs_20_ = bf16[256,256]{1,0:T(8,128)(2,1)S(1)} collective-permute-done((bf16[256,256]{1,0:T(8,128)(2,1)S(1)}, bf16[256,256]{1,0:T(8,128)(2,1)S(1)}, u32[]{:S(2)}, u32[]{:S(2)}) %collective-permute-start.75) | collective-permute-done | bytes 131104 | tf_op jit(solution)/shard_map/ppermute | solution.py:103
  516.8 5.9 collective-permute-start.82
  525.3 12.0 %attention_backward.1 = (bf16[256,256]{1,0:T(8,128)(2,1)}, bf16[256,256]{1,0:T(8,128)(2,1)}, bf16[256,256]{1,0:T(8,128)(2,1)}, bf16[256,256]{1,0:T(8,128)(2,1)},...) custom-call(s32[3]{0:T(128)} %pad_add_fusion.info, ...), custom_call_target="tpu_custom_call" | custom-call | flops 10737418240 | bytes 2621440 | tf_op jit(solution)/shard_map/attention_backward/pallas_call | solution.py:180
  537.3 4.2 collective-permute-done.84.refs_0_
  541.4 3.7 collective-permute-done.82
  554.8 3.7 collective-permute-start.89
  563.8 6.3 collective-permute-done.88.refs_4_
  570.1 3.8 collective-permute-done.89.refs_5_
  581.6 3.1 chip_sum.3.mine
  584.8 3.3 chip_sum.4.mine
  589.7 4.4 collective-permute-start.93
  596.4 28.7 %collective-permute-done.99.refs_2_ = bf16[256,512]{1,0:T(8,128)(2,1)S(1)} collective-permute-done((bf16[256,512]{1,0:T(8,128)(2,1)S(1)}, bf16[256,512]{1,0:T(8,128)(2,1)S(1)}, u32[]{:S(2)}, u32[]{:S(2)}) %collective-permute-start.99) | collective-permute-done | bytes 262176 | tf_op jit(solution)/shard_map/ppermute | solution.py:103
  626.3 7.0 collective-permute-done.100.refs_3_
  634.6 10.3 %input_gradient.1 = (bf16[256,2048]{1,0:T(8,128)(2,1)}, f32[8,2048]{1,0:T(8,128)}) custom-call(bf16[256,2048]{1,0:T(8,128)(2,1)} %x.3, f32[8,2048]{1,0:T(8,128)} %get-tuple-element.363.gains, f32[256,2048]{1,0:T(8,128)} %get-tuple-element.599.grad_hidden, bf16[256,512]{1,0:T(8,128)(2,1)} %get-tuple-element.591.refs_0_, ...), custom_call_target="tpu_custom_call" | custom-call | flops 536870912 | bytes 6291456 | tf_op jit(solution)/shard_map/input_gradient/pallas_call | solution.py:180
  646.2 13.2 %projection_gradients.1 = (f32[544,512]{1,0:T(8,128)}, f32[544,512]{1,0:T(8,128)}, f32[544,512]{1,0:T(8,128)}, f32[544,512]{1,0:T(8,128)}, f32[544,512]{1,0:T(8,...) custom-call(s32[11]{0:T(128)} %stack.54.info, bf16[1024,2048]{1,0:T(8,128)(2,1)} %get-tuple-element.598.normed, ...), custom_call_target="tpu_custom_call" | custom-call | flops 1073741824 | bytes 2097152 | tf_op jit(solution)/shard_map/projection_gradients/pallas_call | solution.py:180
  663.2 6.8 collective-permute-done.104
  673.3 11.5 %collective-permute-done.106 = bf16[544,512]{1,0:T(8,128)(2,1)S(1)} collective-permute-done((bf16[544,512]{1,0:T(8,128)(2,1)S(1)}, bf16[544,512]{1,0:T(8,128)(2,1)S(1)}, u32[]{:S(2)}, u32[]{:S(2)}) %collective-permute-start.106) | collective-permute-done | bytes 557088 | tf_op jit(solution)/shard_map/ppermute | solution.py:88
  690.8 7.7 collective-permute-done.108
  699.7 5.9 collective-permute-done.116.refs_0_
  711.2 10.0 %collective-permute-done.118 = bf16[544,512]{1,0:T(8,128)(2,1)S(1)} collective-permute-done((bf16[544,512]{1,0:T(8,128)(2,1)S(1)}, bf16[544,512]{1,0:T(8,128)(2,1)S(1)}, u32[]{:S(2)}, u32[]{:S(2)}) %collective-permute-start.118) | collective-permute-done | bytes 557088 | tf_op jit(solution)/shard_map/ppermute | solution.py:85
  725.0 3.2 chip_sum.5.mine
  728.2 32.5 %collective-permute-done.112.refs_5_ = bf16[256,512]{1,0:T(8,128)(2,1)S(1)} collective-permute-done((bf16[256,512]{1,0:T(8,128)(2,1)}, bf16[256,512]{1,0:T(8,128)(2,1)S(1)}, u32[]{:S(2)}, u32[]{:S(2)}) %collective-permute-start.112) | collective-permute-done | bytes 262176 | tf_op jit(solution)/shard_map/ppermute | solution.py:103
  761.2 7.7 collective-permute-done.113.refs_6_
  771.3 4.6 spread_columns.3
  776.0 4.8 spread_columns.4
  780.8 3.9 split_keys_values.1
  787.8 3.8 join_projections.1
  794.0 4.6 spread_columns.5
  (516 shorter events, 201.7 us)
Async XLA Ops:
  19.6 20.1 %collective-permute-start.3 = (bf16[544,512]{1,0:T(8,128)(2,1)S(1)}, bf16[544,512]{1,0:T(8,128)(2,1)}, u32[]{:S(2)}, u32[]{:S(2)}) collective-permute-start(bf16[544,512]{1,0:T(8,128)(2,1)S(1)} %collective-permute-done.1.refs_5_), channel_id=1, source_target_pairs={{1,3},{3,5},{5,7},{7,6},{6,4},{4,2},{2,0},{0,1},{9,11},{11,13},{13... | collective-permute-start | bytes 1671176 | tf_op jit(solution)/shard_map/ppermute | solution.py:85
  21.2 18.5 %collective-permute-start.4 = (bf16[544,512]{1,0:T(8,128)(2,1)S(1)}, bf16[544,512]{1,0:T(8,128)(2,1)}, u32[]{:S(2)}, u32[]{:S(2)}) collective-permute-start(bf16[544,512]{1,0:T(8,128)(2,1)S(1)} %collective-permute-done.2.refs_6_), channel_id=1, source_target_pairs={{3,1},{5,3},{7,5},{6,7},{4,6},{2,4},{0,2},{1,0},{11,9},{13,11},{15... | collective-permute-start | bytes 1671176 | tf_op jit(solution)/shard_map/ppermute | solution.py:88
  29.2 37.5 %collective-permute-start = (bf16[256,2048]{1,0:T(8,128)(2,1)S(1)}, bf16[256,2048]{1,0:T(8,128)(2,1)S(1)}, u32[]{:S(2)}, u32[]{:S(2)}) collective-permute-start(bf16[256,2048]{1,0:T(8,128)(2,1)S(1)} %copy-done.10), channel_id=1, source_target_pairs={{0,16},{8,24},{16,0},{24,8},{1,17},{9,25},{17,1},{25,9},{2,18},{10... | collective-permute-start | bytes 3145736 | tf_op jit(solution)/shard_map/ppermute | solution.py:103
  39.7 20.7 %collective-permute-start.7 = (bf16[544,512]{1,0:T(8,128)(2,1)}, bf16[544,512]{1,0:T(8,128)(2,1)S(1)}, u32[]{:S(2)}, u32[]{:S(2)}) collective-permute-start(bf16[544,512]{1,0:T(8,128)(2,1)} %collective-permute-done.3.refs_7_), channel_id=1, source_target_pairs={{1,3},{3,5},{5,7},{7,6},{6,4},{4,2},{2,0},{0,1},{9,11},{11,13},{13... | collective-permute-start | bytes 1671176 | tf_op jit(solution)/shard_map/ppermute | solution.py:85
  41.3 19.1 %collective-permute-start.8 = (bf16[544,512]{1,0:T(8,128)(2,1)}, bf16[544,512]{1,0:T(8,128)(2,1)S(1)}, u32[]{:S(2)}, u32[]{:S(2)}) collective-permute-start(bf16[544,512]{1,0:T(8,128)(2,1)} %collective-permute-done.4.refs_8_), channel_id=1, source_target_pairs={{3,1},{5,3},{7,5},{6,7},{4,6},{2,4},{0,2},{1,0},{11,9},{13,11},{15... | collective-permute-start | bytes 1671176 | tf_op jit(solution)/shard_map/ppermute | solution.py:88
  41.8 22.8 %collective-permute-start.9 = (bf16[256,512]{1,0:T(8,128)(2,1)}, bf16[256,512]{1,0:T(8,128)(2,1)S(1)}, u32[]{:S(2)}, u32[]{:S(2)}) collective-permute-start(bf16[256,512]{1,0:T(8,128)(2,1)} %get-tuple-element.357), channel_id=1, source_target_pairs={{0,3},{1,2},{2,1},{3,0},{4,7},{5,6},{6,5},{7,4},{8,11},{9,10},{10,... | collective-permute-start | bytes 786440 | tf_op jit(solution)/shard_map/ppermute | solution.py:103
  43.1 21.5 %collective-permute-start.10 = (bf16[256,512]{1,0:T(8,128)(2,1)}, bf16[256,512]{1,0:T(8,128)(2,1)S(1)}, u32[]{:S(2)}, u32[]{:S(2)}) collective-permute-start(bf16[256,512]{1,0:T(8,128)(2,1)} %get-tuple-element.358), channel_id=1, source_target_pairs={{0,4},{1,5},{2,6},{3,7},{4,0},{5,1},{6,2},{7,3},{8,12},{9,13},{10,... | collective-permute-start | bytes 786440 | tf_op jit(solution)/shard_map/ppermute | solution.py:103
  73.3 27.3 %collective-permute-start.15 = (bf16[256,512]{1,0:T(8,128)(2,1)}, bf16[256,512]{1,0:T(8,128)(2,1)}, u32[]{:S(2)}, u32[]{:S(2)}) collective-permute-start(bf16[256,512]{1,0:T(8,128)(2,1)} %get-tuple-element.376), channel_id=1, source_target_pairs={{0,5},{1,4},{2,7},{3,6},{4,1},{5,0},{6,3},{7,2},{8,13},{9,12},{10,... | collective-permute-start | bytes 786440 | tf_op jit(solution)/shard_map/ppermute | solution.py:103
  74.7 25.8 %collective-permute-start.16 = (bf16[256,512]{1,0:T(8,128)(2,1)}, bf16[256,512]{1,0:T(8,128)(2,1)}, u32[]{:S(2)}, u32[]{:S(2)}) collective-permute-start(bf16[256,512]{1,0:T(8,128)(2,1)} %get-tuple-element.377), channel_id=1, source_target_pairs={{0,6},{1,7},{2,4},{3,5},{4,2},{5,3},{6,0},{7,1},{8,14},{9,15},{10,... | collective-permute-start | bytes 786440 | tf_op jit(solution)/shard_map/ppermute | solution.py:103
  77.2 23.4 %collective-permute-start.17 = (bf16[256,512]{1,0:T(8,128)(2,1)}, bf16[256,512]{1,0:T(8,128)(2,1)}, u32[]{:S(2)}, u32[]{:S(2)}) collective-permute-start(bf16[256,512]{1,0:T(8,128)(2,1)} %get-tuple-element.378), channel_id=1, source_target_pairs={{0,7},{1,6},{2,5},{3,4},{4,3},{5,2},{6,1},{7,0},{8,15},{9,14},{10,... | collective-permute-start | bytes 786440 | tf_op jit(solution)/shard_map/ppermute | solution.py:103
  100.6 21.5 %collective-permute-start.18 = (bf16[256,256]{1,0:T(8,128)(2,1)}, bf16[256,256]{1,0:T(8,128)(2,1)S(1)}, u32[]{:S(2)}, u32[]{:S(2)}) collective-permute-start(bf16[256,256]{1,0:T(8,128)(2,1)} %get-tuple-element.379), channel_id=1, source_target_pairs={{0,0},{1,1},{2,16},{3,17},{4,8},{5,9},{6,24},{7,25},{8,4},{9,5},{1... | collective-permute-start | bytes 393224 | tf_op jit(solution)/shard_map/ppermute | solution.py:99
  102.1 20.7 %collective-permute-start.19 = (bf16[256,256]{1,0:T(8,128)(2,1)}, bf16[256,256]{1,0:T(8,128)(2,1)S(1)}, u32[]{:S(2)}, u32[]{:S(2)}) collective-permute-start(bf16[256,256]{1,0:T(8,128)(2,1)} %get-tuple-element.380), channel_id=1, source_target_pairs={{0,1},{1,0},{2,17},{3,16},{4,9},{5,8},{6,25},{7,24},{8,5},{9,4},{1... | collective-permute-start | bytes 393224 | tf_op jit(solution)/shard_map/ppermute | solution.py:99
  103.7 33.8 %collective-permute-start.20 = (bf16[256,256]{1,0:T(8,128)(2,1)}, bf16[256,256]{1,0:T(8,128)(2,1)S(1)}, u32[]{:S(2)}, u32[]{:S(2)}) collective-permute-start(bf16[256,256]{1,0:T(8,128)(2,1)} %get-tuple-element.381), channel_id=1, source_target_pairs={{0,16},{1,17},{2,0},{3,1},{4,24},{5,25},{6,8},{7,9},{8,20},{9,21},... | collective-permute-start | bytes 393224 | tf_op jit(solution)/shard_map/ppermute | solution.py:99
  119.6 18.0 %collective-permute-start.21 = (bf16[256,256]{1,0:T(8,128)(2,1)}, bf16[256,256]{1,0:T(8,128)(2,1)S(1)}, u32[]{:S(2)}, u32[]{:S(2)}) collective-permute-start(bf16[256,256]{1,0:T(8,128)(2,1)} %get-tuple-element.382), channel_id=1, source_target_pairs={{0,17},{1,16},{2,1},{3,0},{4,25},{5,24},{6,9},{7,8},{8,21},{9,20},... | collective-permute-start | bytes 393224 | tf_op jit(solution)/shard_map/ppermute | solution.py:99
  119.7 17.9 %collective-permute-start.22 = (bf16[256,256]{1,0:T(8,128)(2,1)}, bf16[256,256]{1,0:T(8,128)(2,1)S(1)}, u32[]{:S(2)}, u32[]{:S(2)}) collective-permute-start(bf16[256,256]{1,0:T(8,128)(2,1)} %get-tuple-element.383), channel_id=1, source_target_pairs={{0,8},{1,9},{2,24},{3,25},{4,0},{5,1},{6,16},{7,17},{8,12},{9,13},... | collective-permute-start | bytes 393224 | tf_op jit(solution)/shard_map/ppermute | solution.py:99
  146.3 53.4 %collective-permute-start.35 = (bf16[2048,512]{1,0:T(8,128)(2,1)}, bf16[2048,512]{1,0:T(8,128)(2,1)S(1)}, u32[]{:S(2)}, u32[]{:S(2)}) collective-permute-start(bf16[2048,512]{1,0:T(8,128)(2,1)} %get-tuple-element.406.refs_8_.refs_0_), channel_id=1, source_target_pairs={{0,16},{8,24},{16,0},{24,8},{1,17},{9,25},{17,1},{25,9},{2,18},{10... | collective-permute-start | bytes 6291464 | tf_op jit(solution)/shard_map/ppermute | solution.py:103
  149.3 26.0 %collective-permute-start.26 = (bf16[256,2048]{1,0:T(8,128)(2,1)S(1)}, bf16[256,2048]{1,0:T(8,128)(2,1)}, u32[]{:S(2)}, u32[]{:S(2)}) collective-permute-start(bf16[256,2048]{1,0:T(8,128)(2,1)S(1)} %copy-done.5), channel_id=1, source_target_pairs={{1,3},{3,5},{5,7},{7,6},{6,4},{4,2},{2,0},{0,1},{9,11},{11,13},{13... | collective-permute-start | bytes 3145736 | tf_op jit(solution)/shard_map/ppermute | solution.py:85
  149.3 26.0 %collective-permute-start.27 = (bf16[256,2048]{1,0:T(8,128)(2,1)S(1)}, bf16[256,2048]{1,0:T(8,128)(2,1)}, u32[]{:S(2)}, u32[]{:S(2)}) collective-permute-start(bf16[256,2048]{1,0:T(8,128)(2,1)S(1)} %copy-done.5), channel_id=1, source_target_pairs={{3,1},{5,3},{7,5},{6,7},{4,6},{2,4},{0,2},{1,0},{11,9},{13,11},{15... | collective-permute-start | bytes 3145736 | tf_op jit(solution)/shard_map/ppermute | solution.py:88
  178.8 18.7 %collective-permute-start.31 = (bf16[256,256]{1,0:T(8,128)(2,1)}, bf16[256,256]{1,0:T(8,128)(2,1)S(1)}, u32[]{:S(2)}, u32[]{:S(2)}) collective-permute-start(bf16[256,256]{1,0:T(8,128)(2,1)} %get-tuple-element.400), channel_id=1, source_target_pairs={{0,4},{1,5},{2,6},{3,7},{4,0},{5,1},{6,2},{7,3},{8,12},{9,13},{10,... | collective-permute-start | bytes 393224 | tf_op jit(solution)/shard_map/ppermute | solution.py:103
  181.1 18.6 %collective-permute-start.32 = (bf16[256,256]{1,0:T(8,128)(2,1)}, bf16[256,256]{1,0:T(8,128)(2,1)S(1)}, u32[]{:S(2)}, u32[]{:S(2)}) collective-permute-start(bf16[256,256]{1,0:T(8,128)(2,1)} %get-tuple-element.401), channel_id=1, source_target_pairs={{0,5},{1,4},{2,7},{3,6},{4,1},{5,0},{6,3},{7,2},{8,13},{9,12},{10,... | collective-permute-start | bytes 393224 | tf_op jit(solution)/shard_map/ppermute | solution.py:103
  200.3 34.6 %collective-permute-start.40 = (bf16[256,2048]{1,0:T(8,128)(2,1)}, bf16[256,2048]{1,0:T(8,128)(2,1)}, u32[]{:S(2)}, u32[]{:S(2)}) collective-permute-start(bf16[256,2048]{1,0:T(8,128)(2,1)} %collective-permute-done.26.refs_2_.refs_10_), channel_id=1, source_target_pairs={{1,3},{3,5},{5,7},{7,6},{6,4},{4,2},{2,0},{0,1},{9,11},{11,13},{13... | collective-permute-start | bytes 3145736 | tf_op jit(solution)/shard_map/ppermute | solution.py:85
  202.4 32.5 %collective-permute-start.41 = (bf16[256,2048]{1,0:T(8,128)(2,1)}, bf16[256,2048]{1,0:T(8,128)(2,1)S(1)}, u32[]{:S(2)}, u32[]{:S(2)}) collective-permute-start(bf16[256,2048]{1,0:T(8,128)(2,1)} %collective-permute-done.27.refs_3_.refs_11_), channel_id=1, source_target_pairs={{3,1},{5,3},{7,5},{6,7},{4,6},{2,4},{0,2},{1,0},{11,9},{13,11},{15... | collective-permute-start | bytes 3145736 | tf_op jit(solution)/shard_map/ppermute | solution.py:88
  218.5 33.4 %collective-permute-start.38 = (bf16[256,2048]{1,0:T(8,128)(2,1)}, bf16[256,2048]{1,0:T(8,128)(2,1)S(1)}, u32[]{:S(2)}, u32[]{:S(2)}) collective-permute-start(bf16[256,2048]{1,0:T(8,128)(2,1)} %get-tuple-element.409.refs_0_.refs_9_), channel_id=1, source_target_pairs={{1,3},{3,5},{5,7},{7,6},{6,4},{4,2},{2,0},{0,1},{9,11},{11,13},{13... | collective-permute-start | bytes 3145736 | tf_op jit(solution)/shard_map/ppermute | solution.py:85
  220.7 32.1 %collective-permute-start.39 = (bf16[256,2048]{1,0:T(8,128)(2,1)}, bf16[256,2048]{1,0:T(8,128)(2,1)S(1)}, u32[]{:S(2)}, u32[]{:S(2)}) collective-permute-start(bf16[256,2048]{1,0:T(8,128)(2,1)} %get-tuple-element.409.refs_0_.refs_9_), channel_id=1, source_target_pairs={{3,1},{5,3},{7,5},{6,7},{4,6},{2,4},{0,2},{1,0},{11,9},{13,11},{15... | collective-permute-start | bytes 3145736 | tf_op jit(solution)/shard_map/ppermute | solution.py:88
  252.8 26.1 %collective-permute-start.42 = (bf16[256,2048]{1,0:T(8,128)(2,1)S(1)}, bf16[256,2048]{1,0:T(8,128)(2,1)S(1)}, u32[]{:S(2)}, u32[]{:S(2)}) collective-permute-start(bf16[256,2048]{1,0:T(8,128)(2,1)S(1)} %collective-permute-done.38.refs_0_.refs_10_), channel_id=1, source_target_pairs={{1,3},{3,5},{5,7},{7,6},{6,4},{4,2},{2,0},{0,1},{9,11},{11,13},{13... | collective-permute-start | bytes 3145736 | tf_op jit(solution)/shard_map/ppermute | solution.py:85
  254.6 26.1 %collective-permute-start.43 = (bf16[256,2048]{1,0:T(8,128)(2,1)S(1)}, bf16[256,2048]{1,0:T(8,128)(2,1)S(1)}, u32[]{:S(2)}, u32[]{:S(2)}) collective-permute-start(bf16[256,2048]{1,0:T(8,128)(2,1)S(1)} %collective-permute-done.39.refs_1_.refs_11_), channel_id=1, source_target_pairs={{3,1},{5,3},{7,5},{6,7},{4,6},{2,4},{0,2},{1,0},{11,9},{13,11},{15... | collective-permute-start | bytes 3145736 | tf_op jit(solution)/shard_map/ppermute | solution.py:88
  254.8 44.7 %collective-permute-start.44 = (bf16[256,2048]{1,0:T(8,128)(2,1)}, bf16[256,2048]{1,0:T(8,128)(2,1)S(1)}, u32[]{:S(2)}, u32[]{:S(2)}) collective-permute-start(bf16[256,2048]{1,0:T(8,128)(2,1)} %collective-permute-done.40.refs_2_.refs_12_), channel_id=1, source_target_pairs={{1,3},{3,5},{5,7},{7,6},{6,4},{4,2},{2,0},{0,1},{9,11},{11,13},{13... | collective-permute-start | bytes 3145736 | tf_op jit(solution)/shard_map/ppermute | solution.py:85
  256.6 44.2 %collective-permute-start.45 = (bf16[256,2048]{1,0:T(8,128)(2,1)}, bf16[256,2048]{1,0:T(8,128)(2,1)}, u32[]{:S(2)}, u32[]{:S(2)}) collective-permute-start(bf16[256,2048]{1,0:T(8,128)(2,1)} %copy-done.19), channel_id=1, source_target_pairs={{3,1},{5,3},{7,5},{6,7},{4,6},{2,4},{0,2},{1,0},{11,9},{13,11},{15... | collective-permute-start | bytes 3145736 | tf_op jit(solution)/shard_map/ppermute | solution.py:88
  256.8 70.8 %collective-permute-start.50 = (bf16[2048,512]{1,0:T(8,128)(2,1)}, bf16[2048,512]{1,0:T(8,128)(2,1)}, u32[]{:S(2)}, u32[]{:S(2)}) collective-permute-start(bf16[2048,512]{1,0:T(8,128)(2,1)} %get-tuple-element.447.refs_4_), channel_id=1, source_target_pairs={{0,16},{8,24},{16,0},{24,8},{1,17},{9,25},{17,1},{25,9},{2,18},{10... | collective-permute-start | bytes 6291464 | tf_op jit(solution)/shard_map/ppermute | solution.py:103
  300.8 26.1 %collective-permute-start.46 = (bf16[256,2048]{1,0:T(8,128)(2,1)S(1)}, bf16[256,2048]{1,0:T(8,128)(2,1)S(1)}, u32[]{:S(2)}, u32[]{:S(2)}) collective-permute-start(bf16[256,2048]{1,0:T(8,128)(2,1)S(1)} %collective-permute-done.42.refs_0_.refs_12_), channel_id=1, source_target_pairs={{1,3},{3,5},{5,7},{7,6},{6,4},{4,2},{2,0},{0,1},{9,11},{11,13},{13... | collective-permute-start | bytes 3145736 | tf_op jit(solution)/shard_map/ppermute | solution.py:85
  301.5 26.1 %collective-permute-start.47 = (bf16[256,2048]{1,0:T(8,128)(2,1)S(1)}, bf16[256,2048]{1,0:T(8,128)(2,1)S(1)}, u32[]{:S(2)}, u32[]{:S(2)}) collective-permute-start(bf16[256,2048]{1,0:T(8,128)(2,1)S(1)} %collective-permute-done.43.refs_1_.refs_13_), channel_id=1, source_target_pairs={{3,1},{5,3},{7,5},{6,7},{4,6},{2,4},{0,2},{1,0},{11,9},{13,11},{15... | collective-permute-start | bytes 3145736 | tf_op jit(solution)/shard_map/ppermute | solution.py:88
  304.0 30.8 %collective-permute-start.48 = (bf16[128,2048]{1,0:T(8,128)(2,1)S(1)}, bf16[128,2048]{1,0:T(8,128)(2,1)S(1)}, u32[]{:S(2)}, u32[]{:S(2)}) collective-permute-start(bf16[128,2048]{1,0:T(8,128)(2,1)S(1)} %slice.139), channel_id=1, source_target_pairs={{1,3},{3,5},{5,7},{7,6},{6,4},{4,2},{2,0},{0,1},{9,11},{11,13},{13... | collective-permute-start | bytes 1572872 | tf_op jit(solution)/shard_map/ppermute | solution.py:85
  304.7 30.7 %collective-permute-start.49 = (bf16[128,2048]{1,0:T(8,128)(2,1)S(1)}, bf16[128,2048]{1,0:T(8,128)(2,1)S(1)}, u32[]{:S(2)}, u32[]{:S(2)}) collective-permute-start(bf16[128,2048]{1,0:T(8,128)(2,1)S(1)} %slice.140), channel_id=1, source_target_pairs={{3,1},{5,3},{7,5},{6,7},{4,6},{2,4},{0,2},{1,0},{11,9},{13,11},{15... | collective-permute-start | bytes 1572872 | tf_op jit(solution)/shard_map/ppermute | solution.py:88
  346.6 35.2 %collective-permute-start.53 = (bf16[2048,512]{1,0:T(8,128)(2,1)}, bf16[2048,512]{1,0:T(8,128)(2,1)S(1)}, u32[]{:S(2)}, u32[]{:S(2)}) collective-permute-start(bf16[2048,512]{1,0:T(8,128)(2,1)} %get-tuple-element.447.refs_4_), channel_id=1, source_target_pairs={{0,8},{8,0},{16,24},{24,16},{1,9},{9,1},{17,25},{25,17},{2,10},{10... | collective-permute-start | bytes 6291464 | tf_op jit(solution)/shard_map/ppermute | solution.py:103
  346.6 35.2 %collective-permute-start.54 = (bf16[2048,512]{1,0:T(8,128)(2,1)}, bf16[2048,512]{1,0:T(8,128)(2,1)}, u32[]{:S(2)}, u32[]{:S(2)}) collective-permute-start(bf16[2048,512]{1,0:T(8,128)(2,1)} %collective-permute-done.50.refs_5_), channel_id=1, source_target_pairs={{0,8},{8,0},{16,24},{24,16},{1,9},{9,1},{17,25},{25,17},{2,10},{10... | collective-permute-start | bytes 6291464 | tf_op jit(solution)/shard_map/ppermute | solution.py:103
  347.2 34.6 %collective-permute-start.55 = (bf16[256,2048]{1,0:T(8,128)(2,1)}, bf16[256,2048]{1,0:T(8,128)(2,1)S(1)}, u32[]{:S(2)}, u32[]{:S(2)}) collective-permute-start(bf16[256,2048]{1,0:T(8,128)(2,1)} %get-tuple-element.474.refs_8_), channel_id=1, source_target_pairs={{0,16},{8,24},{16,0},{24,8},{1,17},{9,25},{17,1},{25,9},{2,18},{10... | collective-permute-start | bytes 3145736 | tf_op jit(solution)/shard_map/ppermute | solution.py:103
  396.5 23.6 %collective-permute-start.58 = (bf16[256,2048]{1,0:T(8,128)(2,1)S(1)}, bf16[256,2048]{1,0:T(8,128)(2,1)S(1)}, u32[]{:S(2)}, u32[]{:S(2)}) collective-permute-start(bf16[256,2048]{1,0:T(8,128)(2,1)S(1)} %pad_maximum_fusion), channel_id=1, source_target_pairs={{3,1},{5,3},{7,5},{6,7},{4,6},{2,4},{0,2},{1,0},{11,9},{13,11},{15... | collective-permute-start | bytes 3145736 | tf_op jit(solution)/shard_map/ppermute | solution.py:88
  397.6 23.3 %collective-permute-start.59 = (bf16[256,2048]{1,0:T(8,128)(2,1)S(1)}, bf16[256,2048]{1,0:T(8,128)(2,1)S(1)}, u32[]{:S(2)}, u32[]{:S(2)}) collective-permute-start(bf16[256,2048]{1,0:T(8,128)(2,1)S(1)} %pad_maximum_fusion.1), channel_id=1, source_target_pairs={{1,3},{3,5},{5,7},{7,6},{6,4},{4,2},{2,0},{0,1},{9,11},{11,13},{13... | collective-permute-start | bytes 3145736 | tf_op jit(solution)/shard_map/ppermute | solution.py:85
  398.6 22.6 %collective-permute-start.60 = (bf16[256,2048]{1,0:T(8,128)(2,1)}, bf16[256,2048]{1,0:T(8,128)(2,1)}, u32[]{:S(2)}, u32[]{:S(2)}) collective-permute-start(bf16[256,2048]{1,0:T(8,128)(2,1)} %get-tuple-element.474.refs_8_), channel_id=1, source_target_pairs={{0,8},{8,0},{16,24},{24,16},{1,9},{9,1},{17,25},{25,17},{2,10},{10... | collective-permute-start | bytes 3145736 | tf_op jit(solution)/shard_map/ppermute | solution.py:103
  398.6 22.6 %collective-permute-start.61 = (bf16[256,2048]{1,0:T(8,128)(2,1)}, bf16[256,2048]{1,0:T(8,128)(2,1)}, u32[]{:S(2)}, u32[]{:S(2)}) collective-permute-start(bf16[256,2048]{1,0:T(8,128)(2,1)} %copy-done.57), channel_id=1, source_target_pairs={{0,8},{8,0},{16,24},{24,16},{1,9},{9,1},{17,25},{25,17},{2,10},{10... | collective-permute-start | bytes 3145736 | tf_op jit(solution)/shard_map/ppermute | solution.py:103
  421.3 22.5 %collective-permute-start.62 = (bf16[256,2048]{1,0:T(8,128)(2,1)S(1)}, bf16[256,2048]{1,0:T(8,128)(2,1)}, u32[]{:S(2)}, u32[]{:S(2)}) collective-permute-start(bf16[256,2048]{1,0:T(8,128)(2,1)S(1)} %add_convert_fusion.11), channel_id=1, source_target_pairs={{3,1},{5,3},{7,5},{6,7},{4,6},{2,4},{0,2},{1,0},{11,9},{13,11},{15... | collective-permute-start | bytes 3145736 | tf_op jit(solution)/shard_map/ppermute | solution.py:88
  422.7 23.6 %collective-permute-start.63 = (bf16[256,2048]{1,0:T(8,128)(2,1)S(1)}, bf16[256,2048]{1,0:T(8,128)(2,1)}, u32[]{:S(2)}, u32[]{:S(2)}) collective-permute-start(bf16[256,2048]{1,0:T(8,128)(2,1)S(1)} %add_convert_fusion.10), channel_id=1, source_target_pairs={{1,3},{3,5},{5,7},{7,6},{6,4},{4,2},{2,0},{0,1},{9,11},{11,13},{13... | collective-permute-start | bytes 3145736 | tf_op jit(solution)/shard_map/ppermute | solution.py:85
  423.3 25.6 %collective-permute-start.64 = (bf16[688,1024]{1,0:T(8,128)(2,1)}, bf16[688,1024]{1,0:T(8,128)(2,1)S(1)}, u32[]{:S(2)}, u32[]{:S(2)}) collective-permute-start(bf16[688,1024]{1,0:T(8,128)(2,1)} %get-tuple-element.478), channel_id=1, source_target_pairs={{0,8},{8,0},{16,24},{24,16},{1,9},{9,1},{17,25},{25,17},{2,10},{10... | collective-permute-start | bytes 4227080 | tf_op jit(solution)/shard_map/ppermute | solution.py:103
  438.6 32.5 %collective-permute-start.67 = (bf16[688,1024]{1,0:T(8,128)(2,1)}, bf16[688,1024]{1,0:T(8,128)(2,1)S(1)}, u32[]{:S(2)}, u32[]{:S(2)}) collective-permute-start(bf16[688,1024]{1,0:T(8,128)(2,1)} %get-tuple-element.500), channel_id=1, source_target_pairs={{0,8},{8,0},{16,24},{24,16},{1,9},{9,1},{17,25},{25,17},{2,10},{10... | collective-permute-start | bytes 4227080 | tf_op jit(solution)/shard_map/ppermute | solution.py:103
  448.9 22.3 %collective-permute-start.65 = (bf16[256,2048]{1,0:T(8,128)(2,1)}, bf16[256,2048]{1,0:T(8,128)(2,1)S(1)}, u32[]{:S(2)}, u32[]{:S(2)}) collective-permute-start(bf16[256,2048]{1,0:T(8,128)(2,1)} %add_convert_fusion.9), channel_id=1, source_target_pairs={{3,1},{5,3},{7,5},{6,7},{4,6},{2,4},{0,2},{1,0},{11,9},{13,11},{15... | collective-permute-start | bytes 3145736 | tf_op jit(solution)/shard_map/ppermute | solution.py:88
  450.3 21.6 %collective-permute-start.66 = (bf16[256,2048]{1,0:T(8,128)(2,1)}, bf16[256,2048]{1,0:T(8,128)(2,1)}, u32[]{:S(2)}, u32[]{:S(2)}) collective-permute-start(bf16[256,2048]{1,0:T(8,128)(2,1)} %add_convert_fusion.8), channel_id=1, source_target_pairs={{1,3},{3,5},{5,7},{7,6},{6,4},{4,2},{2,0},{0,1},{9,11},{11,13},{13... | collective-permute-start | bytes 3145736 | tf_op jit(solution)/shard_map/ppermute | solution.py:85
  452.9 18.2 %collective-permute-start.68 = (bf16[344,1024]{1,0:T(8,128)(2,1)}, bf16[344,1024]{1,0:T(8,128)(2,1)}, u32[]{:S(2)}, u32[]{:S(2)}) collective-permute-start(bf16[344,1024]{1,0:T(8,128)(2,1)} %get-tuple-element.520), channel_id=1, source_target_pairs={{0,16},{8,24},{16,0},{24,8},{1,17},{9,25},{17,1},{25,9},{2,18},{10... | collective-permute-start | bytes 2113544 | tf_op jit(solution)/shard_map/ppermute | solution.py:103
  516.8 28.3 %collective-permute-start.82 = (bf16[256,2048]{1,0:T(8,128)(2,1)S(1)}, bf16[256,2048]{1,0:T(8,128)(2,1)S(1)}, u32[]{:S(2)}, u32[]{:S(2)}) collective-permute-start(bf16[256,2048]{1,0:T(8,128)(2,1)S(1)} %pad_maximum_fusion.2), channel_id=1, source_target_pairs={{3,1},{5,3},{7,5},{6,7},{4,6},{2,4},{0,2},{1,0},{11,9},{13,11},{15... | collective-permute-start | bytes 3145736 | tf_op jit(solution)/shard_map/ppermute | solution.py:88
  522.7 24.6 %collective-permute-start.83 = (bf16[256,2048]{1,0:T(8,128)(2,1)S(1)}, bf16[256,2048]{1,0:T(8,128)(2,1)S(1)}, u32[]{:S(2)}, u32[]{:S(2)}) collective-permute-start(bf16[256,2048]{1,0:T(8,128)(2,1)S(1)} %pad_maximum_fusion.3), channel_id=1, source_target_pairs={{1,3},{3,5},{5,7},{7,6},{6,4},{4,2},{2,0},{0,1},{9,11},{11,13},{13... | collective-permute-start | bytes 3145736 | tf_op jit(solution)/shard_map/ppermute | solution.py:85
  547.3 26.6 %collective-permute-start.92 = (bf16[344,1024]{1,0:T(8,128)(2,1)}, bf16[344,1024]{1,0:T(8,128)(2,1)S(1)}, u32[]{:S(2)}, u32[]{:S(2)}) collective-permute-start(bf16[344,1024]{1,0:T(8,128)(2,1)} %get-tuple-element.582), channel_id=1, source_target_pairs={{0,16},{8,24},{16,0},{24,8},{1,17},{9,25},{17,1},{25,9},{2,18},{10... | collective-permute-start | bytes 2113544 | tf_op jit(solution)/shard_map/ppermute | solution.py:103
  554.8 19.1 %collective-permute-start.89 = (bf16[256,256]{1,0:T(8,128)(2,1)}, bf16[256,256]{1,0:T(8,128)(2,1)S(1)}, u32[]{:S(2)}, u32[]{:S(2)}) collective-permute-start(bf16[256,256]{1,0:T(8,128)(2,1)} %get-tuple-element.579), channel_id=1, source_target_pairs={{0,5},{1,4},{2,7},{3,6},{4,1},{5,0},{6,3},{7,2},{8,13},{9,12},{10,... | collective-permute-start | bytes 393224 | tf_op jit(solution)/shard_map/ppermute | solution.py:103
  584.8 61.4 %collective-permute-start.102 = (bf16[688,1024]{1,0:T(8,128)(2,1)}, bf16[688,1024]{1,0:T(8,128)(2,1)S(1)}, u32[]{:S(2)}, u32[]{:S(2)}) collective-permute-start(bf16[688,1024]{1,0:T(8,128)(2,1)} %chip_sum.3.mine), channel_id=1, source_target_pairs={{0,8},{8,0},{16,24},{24,16},{1,9},{9,1},{17,25},{25,17},{2,10},{10... | collective-permute-start | bytes 4227080 | tf_op jit(solution)/shard_map/ppermute | solution.py:103
  588.1 58.1 %collective-permute-start.103 = (bf16[688,1024]{1,0:T(8,128)(2,1)}, bf16[688,1024]{1,0:T(8,128)(2,1)S(1)}, u32[]{:S(2)}, u32[]{:S(2)}) collective-permute-start(bf16[688,1024]{1,0:T(8,128)(2,1)} %chip_sum.4.mine), channel_id=1, source_target_pairs={{0,8},{8,0},{16,24},{24,16},{1,9},{9,1},{17,25},{25,17},{2,10},{10... | collective-permute-start | bytes 4227080 | tf_op jit(solution)/shard_map/ppermute | solution.py:103
  589.7 56.4 %collective-permute-start.93 = (bf16[256,2048]{1,0:T(8,128)(2,1)}, bf16[256,2048]{1,0:T(8,128)(2,1)S(1)}, u32[]{:S(2)}, u32[]{:S(2)}) collective-permute-start(bf16[256,2048]{1,0:T(8,128)(2,1)} %add_convert_fusion.7), channel_id=1, source_target_pairs={{3,1},{5,3},{7,5},{6,7},{4,6},{2,4},{0,2},{1,0},{11,9},{13,11},{15... | collective-permute-start | bytes 3145736 | tf_op jit(solution)/shard_map/ppermute | solution.py:88
  594.1 52.0 %collective-permute-start.94 = (bf16[256,2048]{1,0:T(8,128)(2,1)}, bf16[256,2048]{1,0:T(8,128)(2,1)S(1)}, u32[]{:S(2)}, u32[]{:S(2)}) collective-permute-start(bf16[256,2048]{1,0:T(8,128)(2,1)} %add_convert_fusion.6), channel_id=1, source_target_pairs={{1,3},{3,5},{5,7},{7,6},{6,4},{4,2},{2,0},{0,1},{9,11},{11,13},{13... | collective-permute-start | bytes 3145736 | tf_op jit(solution)/shard_map/ppermute | solution.py:85
  594.4 30.7 %collective-permute-start.99 = (bf16[256,512]{1,0:T(8,128)(2,1)S(1)}, bf16[256,512]{1,0:T(8,128)(2,1)S(1)}, u32[]{:S(2)}, u32[]{:S(2)}) collective-permute-start(bf16[256,512]{1,0:T(8,128)(2,1)S(1)} %copy-done.102), channel_id=1, source_target_pairs={{0,2},{1,3},{2,0},{3,1},{4,6},{5,7},{6,4},{7,5},{8,10},{9,11},{10,... | collective-permute-start | bytes 786440 | tf_op jit(solution)/shard_map/ppermute | solution.py:103
  646.1 26.5 %collective-permute-start.115 = (bf16[688,1024]{1,0:T(8,128)(2,1)}, bf16[688,1024]{1,0:T(8,128)(2,1)S(1)}, u32[]{:S(2)}, u32[]{:S(2)}) collective-permute-start(bf16[688,1024]{1,0:T(8,128)(2,1)} %get-tuple-element.650), channel_id=1, source_target_pairs={{0,8},{8,0},{16,24},{24,16},{1,9},{9,1},{17,25},{25,17},{2,10},{10... | collective-permute-start | bytes 4227080 | tf_op jit(solution)/shard_map/ppermute | solution.py:103
  686.8 18.8 %collective-permute-start.116 = (bf16[344,1024]{1,0:T(8,128)(2,1)S(1)}, bf16[344,1024]{1,0:T(8,128)(2,1)S(1)}, u32[]{:S(2)}, u32[]{:S(2)}) collective-permute-start(bf16[344,1024]{1,0:T(8,128)(2,1)S(1)} %get-tuple-element.651), channel_id=1, source_target_pairs={{0,16},{8,24},{16,0},{24,8},{1,17},{9,25},{17,1},{25,9},{2,18},{10... | collective-permute-start | bytes 2113544 | tf_op jit(solution)/shard_map/ppermute | solution.py:103
  689.3 34.9 %collective-permute-start.122 = (bf16[344,1024]{1,0:T(8,128)(2,1)S(1)}, bf16[344,1024]{1,0:T(8,128)(2,1)S(1)}, u32[]{:S(2)}, u32[]{:S(2)}) collective-permute-start(bf16[344,1024]{1,0:T(8,128)(2,1)S(1)} %get-tuple-element.659), channel_id=1, source_target_pairs={{0,16},{8,24},{16,0},{24,8},{1,17},{9,25},{17,1},{25,9},{2,18},{10... | collective-permute-start | bytes 2113544 | tf_op jit(solution)/shard_map/ppermute | solution.py:103
  708.9 76.3 %collective-permute-start.111 = (bf16[256,2048]{1,0:T(8,128)(2,1)}, bf16[256,2048]{1,0:T(8,128)(2,1)S(1)}, u32[]{:S(2)}, u32[]{:S(2)}) collective-permute-start(bf16[256,2048]{1,0:T(8,128)(2,1)} %add_convert_fusion.4), channel_id=1, source_target_pairs={{1,3},{3,5},{5,7},{7,6},{6,4},{4,2},{2,0},{0,1},{9,11},{11,13},{13... | collective-permute-start | bytes 3145736 | tf_op jit(solution)/shard_map/ppermute | solution.py:85
  709.5 75.7 %collective-permute-start.110 = (bf16[256,2048]{1,0:T(8,128)(2,1)}, bf16[256,2048]{1,0:T(8,128)(2,1)S(1)}, u32[]{:S(2)}, u32[]{:S(2)}) collective-permute-start(bf16[256,2048]{1,0:T(8,128)(2,1)} %add_convert_fusion.5), channel_id=1, source_target_pairs={{3,1},{5,3},{7,5},{6,7},{4,6},{2,4},{0,2},{1,0},{11,9},{13,11},{15... | collective-permute-start | bytes 3145736 | tf_op jit(solution)/shard_map/ppermute | solution.py:88
  721.1 39.5 %collective-permute-start.112 = (bf16[256,512]{1,0:T(8,128)(2,1)}, bf16[256,512]{1,0:T(8,128)(2,1)S(1)}, u32[]{:S(2)}, u32[]{:S(2)}) collective-permute-start(bf16[256,512]{1,0:T(8,128)(2,1)} %get-tuple-element.642), channel_id=1, source_target_pairs={{0,5},{1,4},{2,7},{3,6},{4,1},{5,0},{6,3},{7,2},{8,13},{9,12},{10,... | collective-permute-start | bytes 786440 | tf_op jit(solution)/shard_map/ppermute | solution.py:103
  723.6 61.0 %collective-permute-start.119 = (bf16[544,512]{1,0:T(8,128)(2,1)S(1)}, bf16[544,512]{1,0:T(8,128)(2,1)}, u32[]{:S(2)}, u32[]{:S(2)}) collective-permute-start(bf16[544,512]{1,0:T(8,128)(2,1)S(1)} %add_convert_fusion.12.refs_0_), channel_id=1, source_target_pairs={{0,16},{8,24},{16,0},{24,8},{1,17},{9,25},{17,1},{25,9},{2,18},{10... | collective-permute-start | bytes 1671176 | tf_op jit(solution)/shard_map/ppermute | solution.py:103
  728.2 64.7 %collective-permute-start.123 = (bf16[688,1024]{1,0:T(8,128)(2,1)}, bf16[688,1024]{1,0:T(8,128)(2,1)S(1)}, u32[]{:S(2)}, u32[]{:S(2)}) collective-permute-start(bf16[688,1024]{1,0:T(8,128)(2,1)} %chip_sum.5.mine), channel_id=1, source_target_pairs={{0,8},{8,0},{16,24},{24,16},{1,9},{9,1},{17,25},{25,17},{2,10},{10... | collective-permute-start | bytes 4227080 | tf_op jit(solution)/shard_map/ppermute | solution.py:103
  (185 other events, 2781.4 us)

commit v3 on v2

--- a/solution.py
+++ b/solution.py
@@ -1161,11 +1161,12 @@
             return [net.swap(sent, "dp", r) for r in range(2, nd, 2)]
 
         grad_sum = RowSum(net, lambda key: made[key][3])
-        arrived = grad_sum.step(*query_parts, *mixed_near)
-        mixed_parts = cores(mixed_near, *arrived)
-        kept, deps, swapped = [], (), None
+        arrived = grad_sum.step()
+        kept, deps, swapped, mixed_parts = [], (), None, ()
         for k in range(3):
-            upcoming = grad_sum.step(*deps, *(mixed_parts if k else ()))
+            upcoming = grad_sum.step(*deps, *((query_parts, mixed_near, mixed_parts)[k]))
+            if k == 1:
+                mixed_parts = cores(mixed_near, *arrived)
             lhs = tie([made[key][(1, 2, 0)[k]] for key in ring_order], *arrived)
             rhs = [(nf, nf, cot)[k][key] for key in ring_order]
             if swapped:
@@ -1212,16 +1213,23 @@
 
         query_got = dp_cols(query_cols)
         out_3 = out_sum.step(*query_cols)
-        gate_total = dp_total(0, *dq_blocks)
-        up_total = dp_total(1, *query_cols)
-        others.append(exchange_x(kept[2][:top], *query_got))
-        early = (n - 1) * 4 // 7
+        early = (n - 1) // 2
         dkv_early = [
             net.swap(b, "seq", r + 1) for r, b in enumerate(tie(dkv_sent[1 : early + 1], *query_cols))
         ]
         input_grad, attn_gain_part = input_gradient(
             nd, layer_input, gains, grad_hidden, query_cols, query_parts
         )
+        out_4 = out_sum.step(attn_gain_part, *dkv_early)
+        dkv_more = [
+            net.swap(b, "seq", early + 1 + r)
+            for r, b in enumerate(tie(dkv_sent[early + 1 :], *out_3, attn_gain_part))
+        ]
+        dkv_blocks = [dkv_sent[0], *dkv_early, *dkv_more]
+        for rows in (slice(top), slice(top, units)):
+            others.append(exchange_x(kept[2][rows], *query_got))
+        gate_total = dp_total(0, *dq_blocks)
+        up_total = dp_total(1, *query_cols)
         shares = projection_gradients(
             n,
             nd,
@@ -1231,7 +1239,7 @@
             attn_gain_part,
             ffn_gain_part,
             branch_got,
-            tie(query_got, *out_3, *dkv_early, gate_total[1], up_total[1]),
+            query_got,
         )
 
         def share_of(key):
@@ -1241,30 +1249,24 @@
             return shares[ring_order.index(key)]
 
         share_sum = RowSum(net, share_of)
-        shared = share_sum.step()
-        others.append(exchange_x(kept[2][top:], *shared))
+        shared = share_sum.step(*out_3, *dkv_early)
+        gate_grad = spread_columns(info, *tie(gate_total, *shared))
+        share_sum.step(*out_4, *dkv_more[: len(dkv_more) // 2])
+        up_grad = spread_columns(info, *tie(up_total, *shared))
         for _ in range(half_way - 3):
-            shared = share_sum.step()
-        dkv_more = [
-            net.swap(b, "seq", early + 1 + i)
-            for i, b in enumerate(tie(dkv_sent[early + 1 :], *shared))
-        ]
-        dkv_blocks = [dkv_sent[0], *dkv_early, *dkv_more]
-        shared = share_sum.step()
-        out_sum.step(*shared)
-        share_sum.step(*others[4])
+            share_sum.step(gate_grad, *dkv_more)
+        down_total = dp_total(2, *shared)
+        share_sum.step(up_grad)
+        down_grad = spread_columns(info, *down_total)
+        key_grad, value_grad = split_keys_values(n, info, dkv_blocks)
         own, first, second = share_sum.rest()
-        down_total = dp_total(2, first, second)
-        gate_grad, up_grad, down_grad = [
-            spread_columns(info, *t) for t in (gate_total, up_total, down_total)
-        ]
         projections = low(own + wide(first) + wide(second))
+        projections = after(projections, down_grad, key_grad)
         out_grad, query_grad, gain_sum = join_projections(
             nd, info, cores(chips(projections))
         )
         own, first, second = out_sum.rest()
         layer_output = low(hidden + (own + wide(first) + wide(second)))
-        key_grad, value_grad = split_keys_values(n, info, dkv_blocks)
         attn_count = attn_gain.shape[0]
         return (
             layer_output,

time: 808 us -> 776 us (0.960)
  waiting for transfers between devices: 351 us -> 278 us
  Pallas kernels: 235 us -> 252 us
  local copies, waits for them, and re-layouts: 15.1 us -> 23.5 us
  other arithmetic: 24.6 us -> 33 us
    ppermute x68, waiting for transfers between devices: 149 us -> 101 us  [swap(): return lax.ppermute(x, axis, [(k, k ^ r) for k in range(count)])]
    ppermute x24, waiting for transfers between devices: 60.2 us -> 39.2 us  [to_left(): return lax.ppermute(x, 'seq', self.left)]
    pallas_call x25, Pallas kernels: 235 us -> 252 us  [call(): pl.pallas_call(body, name=name, in_specs=specs, out_specs=tuple(out_specs...]
    ppermute x24, starting transfers between devices: 37.8 us -> 46.9 us  [to_left(): return lax.ppermute(x, 'seq', self.left)]
  transfers between devices with their start and end apart: 124 -> 124, of which waited for: 58 -> 51; matrix products, arithmetic and copies ran while one was open for 4% -> 5% of each run, Pallas kernels for 28% -> 32%
where the time goes in v3:
time: 776 us; the launch traced here: 768 us
  waiting for transfers between devices  278 us (36%)
  Pallas kernels  252 us (32%)
  starting transfers between devices  178 us (23%)
  other arithmetic  33 us (4%)
  local copies, waits for them, and re-layouts  23.5 us (3%)
    pallas_call x25, Pallas kernels, call(): pl.pallas_call(body, name=name, in_specs=specs, out_specs=tuple(out_specs...  252 us
    ppermute x24, waiting for transfers between devices, to_right(): return lax.ppermute(x, 'seq', self.right)  117 us
    ppermute x68, waiting for transfers between devices, swap(): return lax.ppermute(x, axis, [(k, k ^ r) for k in range(count)])  101 us
    ppermute x68, starting transfers between devices, swap(): return lax.ppermute(x, axis, [(k, k ^ r) for k in range(count)])  79.3 us
    ppermute x24, starting transfers between devices, to_left(): return lax.ppermute(x, 'seq', self.left)  46.9 us
    ppermute x24, waiting for transfers between devices, to_left(): return lax.ppermute(x, 'seq', self.left)  39.2 us
    ppermute x24, starting transfers between devices, to_right(): return lax.ppermute(x, 'seq', self.right)  27.8 us
    convert_element_type x21, other arithmetic, low(): return value.astype(jnp.bfloat16)  24.2 us
  transfers between devices with their start and end apart: 124, of which 51 were waited for; matrix products, arithmetic and copies ran while one was open for 5% of the time, Pallas kernels for 32%

profile of v3, /device:TPU:0, one launch (start us, length us, event | category | flops | bytes accessed | tf_op | source)
XLA Modules:
  0.0 767.6 jit_solution(14491803525532858670)
XLA Ops:
  2.5 3.0 collective-permute-start.1
  5.6 12.6 %collective-permute-done.1.refs_5_ = bf16[544,512]{1,0:T(8,128)(2,1)S(1)} collective-permute-done((bf16[544,512]{1,0:T(8,128)(2,1)S(1)}, bf16[544,512]{1,0:T(8,128)(2,1)S(1)}, u32[]{:S(2)}, u32[]{:S(2)}) %collective-permute-start.1) | collective-permute-done | bytes 557088 | tf_op jit(solution)/shard_map/ppermute | solution.py:85
  22.2 3.7 pack_keys_values.1
  30.7 9.0 %collective-permute-done.5.refs_9_ = bf16[256,512]{1,0:T(8,128)(2,1)S(1)} collective-permute-done((bf16[256,512]{1,0:T(8,128)(2,1)}, bf16[256,512]{1,0:T(8,128)(2,1)S(1)}, u32[]{:S(2)}, u32[]{:S(2)}) %collective-permute-start.5) | collective-permute-done | bytes 262176 | tf_op jit(solution)/shard_map/ppermute | solution.py:103
  45.0 15.4 %collective-permute-done.7.refs_9_ = bf16[544,512]{1,0:T(8,128)(2,1)S(1)} collective-permute-done((bf16[544,512]{1,0:T(8,128)(2,1)}, bf16[544,512]{1,0:T(8,128)(2,1)S(1)}, u32[]{:S(2)}, u32[]{:S(2)}) %collective-permute-start.7) | collective-permute-done | bytes 557088 | tf_op jit(solution)/shard_map/ppermute | solution.py:85
  60.5 4.2 collective-permute-done.9.refs_11_
  66.7 4.5 collective-permute-done.11.refs_11_
  80.9 11.5 %project_queries.1 = (bf16[256,256]{1,0:T(8,128)(2,1)}, bf16[256,256]{1,0:T(8,128)(2,1)}, bf16[256,256]{1,0:T(8,128)(2,1)}, bf16[256,256]{1,0:T(8,128)(2,1)}, bf...) custom-call(s32[11]{0:T(128)} %stack.54.info, ...), custom_call_target="tpu_custom_call" | custom-call | flops 536870912 | bytes 6291456 | tf_op jit(solution)/shard_map/project_queries/pallas_call | solution.py:180
  92.3 8.2 %collective-permute-done.15.refs_13_ = bf16[256,512]{1,0:T(8,128)(2,1)} collective-permute-done((bf16[256,512]{1,0:T(8,128)(2,1)}, bf16[256,512]{1,0:T(8,128)(2,1)}, u32[]{:S(2)}, u32[]{:S(2)}) %collective-permute-start.15) | collective-permute-done | bytes 262176 | tf_op jit(solution)/shard_map/ppermute | solution.py:103
  103.7 15.8 %collective-permute-start.20 = (bf16[256,256]{1,0:T(8,128)(2,1)}, bf16[256,256]{1,0:T(8,128)(2,1)S(1)}, u32[]{:S(2)}, u32[]{:S(2)}) collective-permute-start(bf16[256,256]{1,0:T(8,128)(2,1)} %get-tuple-element.382), channel_id=1, source_target_pairs={{0,16},{1,17},{2,0},{3,1},{4,24},{5,25},{6,8},{7,9},{8,20},{9,21},... | collective-permute-start | bytes 393224 | tf_op jit(solution)/shard_map/ppermute | solution.py:99
  124.5 13.0 %collective-permute-done.20.refs_2_ = bf16[256,256]{1,0:T(8,128)(2,1)S(1)} collective-permute-done((bf16[256,256]{1,0:T(8,128)(2,1)}, bf16[256,256]{1,0:T(8,128)(2,1)S(1)}, u32[]{:S(2)}, u32[]{:S(2)}) %collective-permute-start.20) | collective-permute-done | bytes 131104 | tf_op jit(solution)/shard_map/ppermute | solution.py:99
  137.7 8.0 %collective-permute-done.25.refs_7_ = bf16[256,256]{1,0:T(8,128)(2,1)S(1)} collective-permute-done((bf16[256,256]{1,0:T(8,128)(2,1)}, bf16[256,256]{1,0:T(8,128)(2,1)S(1)}, u32[]{:S(2)}, u32[]{:S(2)}) %collective-permute-start.25) | collective-permute-done | bytes 131104 | tf_op jit(solution)/shard_map/ppermute | solution.py:99
  152.6 17.4 %attention_forward.1 = (bf16[256,256]{1,0:T(8,128)(2,1)}, bf16[256,256]{1,0:T(8,128)(2,1)}, bf16[256,256]{1,0:T(8,128)(2,1)}, bf16[256,256]{1,0:T(8,128)(2,1)}, ...) custom-call(s32[3]{0:T(128)} %pad_add_fusion.info, ...), custom_call_target="tpu_custom_call" | custom-call | flops 4294967296 | bytes 1310720 | tf_op jit(solution)/shard_map/attention_forward/pallas_call | solution.py:180
  170.0 5.3 collective-permute-done.26.refs_2_.refs_10_
  184.6 4.2 collective-permute-done.30.refs_3_
  190.7 6.8 collective-permute-done.31.refs_4_
  202.4 3.4 collective-permute-start.41
  208.4 10.1 %project_mixed.1 = (f32[256,2048]{1,0:T(8,128)}, bf16[256,2048]{1,0:T(8,128)(2,1)}, bf16[256,2048]{1,0:T(8,128)(2,1)}) custom-call(s32[11]{0:T(128)} %stack.54.info, bf16[256,2048]{1,0:T(8,128)(2,1)} %x.3, f32[8,2048]{1,0:T(8,128)} %get-tuple-element.364.gains, bf16[256,256]{1,0:T(8,128)(2,1)} %get-tuple-element.397.refs_0_, bf16[256,256]{1,0:T(8,128)(2,1)} %copy-done.87, ...), custom_call_target="tpu_custom_call" | custom-call | flops 536870912 | bytes 6291456 | tf_op jit(solution)/shard_map/project_mixed/pallas_call | solution.py:180
  220.7 3.8 collective-permute-start.39
  224.6 10.4 %ffn_blocks.5 = (bf16[256,768]{1,0:T(8,128)(2,1)}, bf16[256,768]{1,0:T(8,128)(2,1)}, bf16[256,768]{1,0:T(8,128)(2,1)}, f32[256,2048]{1,0:T(8,128)}, f32[256,2048]{1,0:T(8,128)}) custom-call(bf16[256,2048]{1,0:T(8,128)(2,1)} %get-tuple-element.410.refs_0_.refs_9_, bf16[256,2048]{1,0:T(8,128)(2,1)} %cotangent.1, bf16[688,2048]{1,0:T(8,128)(2,1)} %refs_4_.9, ...), custom_call_target="tpu_custom_call" | custom-call | flops 1082130432 | bytes 3686400 | tf_op jit(solution)/shard_map/ffn_blocks/pallas_call | solution.py:180
  235.0 16.9 %collective-permute-done.38.refs_0_.refs_10_ = bf16[256,2048]{1,0:T(8,128)(2,1)S(1)} collective-permute-done((bf16[256,2048]{1,0:T(8,128)(2,1)}, bf16[256,2048]{1,0:T(8,128)(2,1)S(1)}, u32[]{:S(2)}, u32[]{:S(2)}) %collective-permute-start.38) | collective-permute-done | bytes 1048608 | tf_op jit(solution)/shard_map/ppermute | solution.py:85
  258.0 16.7 %ffn_blocks.6 = (bf16[256,768]{1,0:T(8,128)(2,1)}, bf16[256,768]{1,0:T(8,128)(2,1)}, bf16[256,768]{1,0:T(8,128)(2,1)}, f32[256,2048]{1,0:T(8,128)}, f32[256,2048...) custom-call(bf16[256,2048]{1,0:T(8,128)(2,1)} %copy-done.6, ...), custom_call_target="tpu_custom_call" | custom-call | flops 2164260864 | bytes 5259264 | tf_op jit(solution)/shard_map/ffn_blocks/pallas_call | solution.py:180
  274.7 4.2 collective-permute-done.42.refs_0_.refs_12_
  280.7 18.9 %collective-permute-done.44.refs_2_.refs_14_ = bf16[256,2048]{1,0:T(8,128)(2,1)S(1)} collective-permute-done((bf16[256,2048]{1,0:T(8,128)(2,1)}, bf16[256,2048]{1,0:T(8,128)(2,1)S(1)}, u32[]{:S(2)}, u32[]{:S(2)}) %collective-permute-start.44) | collective-permute-done | bytes 1048608 | tf_op jit(solution)/shard_map/ppermute | solution.py:85
  306.2 16.6 %ffn_blocks.7 = (bf16[256,768]{1,0:T(8,128)(2,1)}, bf16[256,768]{1,0:T(8,128)(2,1)}, bf16[256,768]{1,0:T(8,128)(2,1)}, f32[256,2048]{1,0:T(8,128)}, f32[256,2048...) custom-call(bf16[256,2048]{1,0:T(8,128)(2,1)} %copy-done.8, ...), custom_call_target="tpu_custom_call" | custom-call | flops 2164260864 | bytes 5259264 | tf_op jit(solution)/shard_map/ffn_blocks/pallas_call | solution.py:180
  322.8 4.1 collective-permute-done.46.refs_0_.refs_14_
  327.6 7.3 collective-permute-done.48.refs_2_.refs_16_
  337.6 16.6 %ffn_blocks.8 = (bf16[256,768]{1,0:T(8,128)(2,1)}, bf16[256,768]{1,0:T(8,128)(2,1)}, bf16[256,768]{1,0:T(8,128)(2,1)}, f32[256,2048]{1,0:T(8,128)}, f32[256,2048...) custom-call(bf16[256,2048]{1,0:T(8,128)(2,1)} %copy-done, ...), custom_call_target="tpu_custom_call" | custom-call | flops 2164260864 | bytes 5259264 | tf_op jit(solution)/shard_map/ffn_blocks/pallas_call | solution.py:180
  355.2 13.5 %ffn_blocks.9 = (bf16[128,768]{1,0:T(8,128)(2,1)}, bf16[128,768]{1,0:T(8,128)(2,1)}, bf16[128,768]{1,0:T(8,128)(2,1)}, f32[128,2048]{1,0:T(8,128)}, f32[128,2048...) custom-call(bf16[128,2048]{1,0:T(8,128)(2,1)} %copy-done.18, ...), custom_call_target="tpu_custom_call" | custom-call | flops 1082130432 | bytes 3686400 | tf_op jit(solution)/shard_map/ffn_blocks/pallas_call | solution.py:180
  373.9 11.3 %collective-permute-done.53 = bf16[128,2048]{1,0:T(8,128)(2,1)S(1)} collective-permute-done((bf16[128,2048]{1,0:T(8,128)(2,1)S(1)}, bf16[128,2048]{1,0:T(8,128)(2,1)S(1)}, u32[]{:S(2)}, u32[]{:S(2)}) %collective-permute-start.53) | collective-permute-done | bytes 524320 | tf_op jit(solution)/shard_map/ppermute | solution.py:88
  391.0 15.2 %weight_gradient.3 = (bf16[688,1024]{1,0:T(8,128)(2,1)}, bf16[688,1024]{1,0:T(8,128)(2,1)}) custom-call(s32[11]{0:T(128)} %stack.54.info, bf16[256,768]{1,0:T(8,128)(2,1)} %get-tuple-element.463.refs_0_, bf16[256,768]{1,0:T(8,128)(2,1)} %get-tuple-element.464.refs_1_, bf16[256,768]{1,0:T(8,128)(2,1)} %get-tuple-element.465.refs_2_, ...), custom_call_target="tpu_custom_call" | custom-call | flops 1442840576 | bytes 2097152 | tf_op jit(solution)/shard_map/weight_gradient/pallas_call | solution.py:180
  406.2 5.1 collective-permute-done.57
  416.9 15.1 %weight_gradient.4 = (bf16[688,1024]{1,0:T(8,128)(2,1)}, bf16[688,1024]{1,0:T(8,128)(2,1)}) custom-call(s32[11]{0:T(128)} %stack.54.info, bf16[256,768]{1,0:T(8,128)(2,1)} %get-tuple-element.487.refs_0_, bf16[256,768]{1,0:T(8,128)(2,1)} %get-tuple-element.488.refs_1_, bf16[256,768]{1,0:T(8,128)(2,1)} %get-tuple-element.489.refs_2_, ...), custom_call_target="tpu_custom_call" | custom-call | flops 1442840576 | bytes 2097152 | tf_op jit(solution)/shard_map/weight_gradient/pallas_call | solution.py:180
  432.1 5.1 collective-permute-done.60
  448.3 15.5 %weight_gradient.5 = (bf16[688,1024]{1,0:T(8,128)(2,1)}, bf16[688,1024]{1,0:T(8,128)(2,1)}) custom-call(s32[11]{0:T(128)} %stack.54.info, bf16[256,768]{1,0:T(8,128)(2,1)} %get-tuple-element.511.refs_0_, bf16[256,768]{1,0:T(8,128)(2,1)} %get-tuple-element.512.refs_1_, bf16[256,768]{1,0:T(8,128)(2,1)} %get-tuple-element.513.refs_2_, ...), custom_call_target="tpu_custom_call" | custom-call | flops 1442840576 | bytes 2097152 | tf_op jit(solution)/shard_map/weight_gradient/pallas_call | solution.py:180
  471.8 10.4 %branch_gradient.1 = (bf16[256,256]{1,0:T(8,128)(2,1)}, bf16[256,256]{1,0:T(8,128)(2,1)}, bf16[256,256]{1,0:T(8,128)(2,1)}, bf16[256,256]{1,0:T(8,128)(2,1)}, bf...) custom-call(s32[11]{0:T(128)} %stack.54.info, ...), custom_call_target="tpu_custom_call" | custom-call | flops 536870912 | bytes 6291456 | tf_op jit(solution)/shard_map/branch_gradient/pallas_call | solution.py:180
  485.8 3.7 collective-permute-done.71.refs_1_
  491.6 3.6 collective-permute-done.79.refs_1_
  505.1 7.8 %collective-permute-done.75.refs_20_ = bf16[256,256]{1,0:T(8,128)(2,1)S(1)} collective-permute-done((bf16[256,256]{1,0:T(8,128)(2,1)S(1)}, bf16[256,256]{1,0:T(8,128)(2,1)S(1)}, u32[]{:S(2)}, u32[]{:S(2)}) %collective-permute-start.75) | collective-permute-done | bytes 131104 | tf_op jit(solution)/shard_map/ppermute | solution.py:103
  512.9 3.4 collective-permute-done.76.refs_21_
  516.4 5.4 collective-permute-start.82
  524.5 22.2 %attention_backward.1 = (bf16[256,256]{1,0:T(8,128)(2,1)}, bf16[256,256]{1,0:T(8,128)(2,1)}, bf16[256,256]{1,0:T(8,128)(2,1)}, bf16[256,256]{1,0:T(8,128)(2,1)},...) custom-call(s32[3]{0:T(128)} %pad_add_fusion.info, ...), custom_call_target="tpu_custom_call" | custom-call | flops 10737418240 | bytes 2621440 | tf_op jit(solution)/shard_map/attention_backward/pallas_call | solution.py:180
  559.8 7.6 collective-permute-done.88.refs_4_
  570.9 3.0 sort_columns.1
  573.9 5.0 collective-permute-start.93
  581.1 10.4 %input_gradient.1 = (bf16[256,2048]{1,0:T(8,128)(2,1)}, f32[8,2048]{1,0:T(8,128)}) custom-call(bf16[256,2048]{1,0:T(8,128)(2,1)} %x.3, f32[8,2048]{1,0:T(8,128)} %get-tuple-element.364.gains, f32[256,2048]{1,0:T(8,128)} %get-tuple-element.599.grad_hidden, bf16[256,512]{1,0:T(8,128)(2,1)} %get-tuple-element.592.refs_0_, ...), custom_call_target="tpu_custom_call" | custom-call | flops 536870912 | bytes 6291456 | tf_op jit(solution)/shard_map/input_gradient/pallas_call | solution.py:180
  595.6 12.2 %projection_gradients.1 = (f32[544,512]{1,0:T(8,128)}, f32[544,512]{1,0:T(8,128)}, f32[544,512]{1,0:T(8,128)}, f32[544,512]{1,0:T(8,128)}, f32[544,512]{1,0:T(8,...) custom-call(s32[11]{0:T(128)} %stack.54.info, bf16[1024,2048]{1,0:T(8,128)(2,1)} %get-tuple-element.621.normed, ...), custom_call_target="tpu_custom_call" | custom-call | flops 1073741824 | bytes 2097152 | tf_op jit(solution)/shard_map/projection_gradients/pallas_call | solution.py:180
  619.8 3.1 chip_sum.3.mine
  628.3 3.1 chip_sum.4.mine
  635.1 16.9 %collective-permute-done.108 = bf16[272,512]{1,0:T(8,128)(2,1)S(1)} collective-permute-done((bf16[272,512]{1,0:T(8,128)(2,1)S(1)}, bf16[272,512]{1,0:T(8,128)(2,1)S(1)}, u32[]{:S(2)}, u32[]{:S(2)}) %collective-permute-start.108) | collective-permute-done | bytes 278560 | tf_op jit(solution)/shard_map/ppermute | solution.py:85
  652.0 3.4 collective-permute-start.101
  657.1 10.1 %collective-permute-done.101.refs_5_ = bf16[256,512]{1,0:T(8,128)(2,1)} collective-permute-done((bf16[256,512]{1,0:T(8,128)(2,1)S(1)}, bf16[256,512]{1,0:T(8,128)(2,1)}, u32[]{:S(2)}, u32[]{:S(2)}) %collective-permute-start.101) | collective-permute-done | bytes 262176 | tf_op jit(solution)/shard_map/ppermute | solution.py:103
  673.5 4.6 spread_columns.3
  678.1 4.5 collective-permute-done.109
  688.0 5.9 collective-permute-done.102.refs_6_
  693.9 3.4 collective-permute-done.103.refs_7_
  697.3 10.4 %collective-permute-start.112 = (bf16[544,512]{1,0:T(8,128)(2,1)S(1)}, bf16[544,512]{1,0:T(8,128)(2,1)S(1)}, u32[]{:S(2)}, u32[]{:S(2)}) collective-permute-start(bf16[544,512]{1,0:T(8,128)(2,1)S(1)} %add_convert_fusion.16), channel_id=1, source_target_pairs={{3,1},{5,3},{7,5},{6,7},{4,6},{2,4},{0,2},{1,0},{11,9},{13,11},{15... | collective-permute-start | bytes 1671176 | tf_op jit(solution)/shard_map/ppermute | solution.py:88
  707.7 3.1 chip_sum.5.mine
  712.1 4.6 spread_columns.4
  719.3 6.8 collective-permute-done.113
  730.1 3.7 split_keys_values.1
  735.0 4.8 spread_columns.5
  746.1 12.2 %collective-permute-done.121.refs_1_ = bf16[544,512]{1,0:T(8,128)(2,1)S(1)} collective-permute-done((bf16[544,512]{1,0:T(8,128)(2,1)S(1)}, bf16[544,512]{1,0:T(8,128)(2,1)S(1)}, u32[]{:S(2)}, u32[]{:S(2)}) %collective-permute-start.121) | collective-permute-done | bytes 557088 | tf_op jit(solution)/shard_map/ppermute | solution.py:103
  762.0 3.8 join_projections.1
  (538 shorter events, 212.6 us)
Async XLA Ops:
  19.6 20.1 %collective-permute-start.3 = (bf16[544,512]{1,0:T(8,128)(2,1)S(1)}, bf16[544,512]{1,0:T(8,128)(2,1)}, u32[]{:S(2)}, u32[]{:S(2)}) collective-permute-start(bf16[544,512]{1,0:T(8,128)(2,1)S(1)} %collective-permute-done.1.refs_5_), channel_id=1, source_target_pairs={{1,3},{3,5},{5,7},{7,6},{6,4},{4,2},{2,0},{0,1},{9,11},{11,13},{13... | collective-permute-start | bytes 1671176 | tf_op jit(solution)/shard_map/ppermute | solution.py:85
  29.2 37.5 %collective-permute-start = (bf16[256,2048]{1,0:T(8,128)(2,1)S(1)}, bf16[256,2048]{1,0:T(8,128)(2,1)S(1)}, u32[]{:S(2)}, u32[]{:S(2)}) collective-permute-start(bf16[256,2048]{1,0:T(8,128)(2,1)S(1)} %copy-done.10), channel_id=1, source_target_pairs={{0,16},{8,24},{16,0},{24,8},{1,17},{9,25},{17,1},{25,9},{2,18},{10... | collective-permute-start | bytes 3145736 | tf_op jit(solution)/shard_map/ppermute | solution.py:103
  39.7 20.7 %collective-permute-start.7 = (bf16[544,512]{1,0:T(8,128)(2,1)}, bf16[544,512]{1,0:T(8,128)(2,1)S(1)}, u32[]{:S(2)}, u32[]{:S(2)}) collective-permute-start(bf16[544,512]{1,0:T(8,128)(2,1)} %collective-permute-done.3.refs_7_), channel_id=1, source_target_pairs={{1,3},{3,5},{5,7},{7,6},{6,4},{4,2},{2,0},{0,1},{9,11},{11,13},{13... | collective-permute-start | bytes 1671176 | tf_op jit(solution)/shard_map/ppermute | solution.py:85
  41.3 19.1 %collective-permute-start.8 = (bf16[544,512]{1,0:T(8,128)(2,1)}, bf16[544,512]{1,0:T(8,128)(2,1)S(1)}, u32[]{:S(2)}, u32[]{:S(2)}) collective-permute-start(bf16[544,512]{1,0:T(8,128)(2,1)} %collective-permute-done.4.refs_8_), channel_id=1, source_target_pairs={{3,1},{5,3},{7,5},{6,7},{4,6},{2,4},{0,2},{1,0},{11,9},{13,11},{15... | collective-permute-start | bytes 1671176 | tf_op jit(solution)/shard_map/ppermute | solution.py:88
  41.8 22.8 %collective-permute-start.9 = (bf16[256,512]{1,0:T(8,128)(2,1)}, bf16[256,512]{1,0:T(8,128)(2,1)S(1)}, u32[]{:S(2)}, u32[]{:S(2)}) collective-permute-start(bf16[256,512]{1,0:T(8,128)(2,1)} %get-tuple-element.358), channel_id=1, source_target_pairs={{0,3},{1,2},{2,1},{3,0},{4,7},{5,6},{6,5},{7,4},{8,11},{9,10},{10,... | collective-permute-start | bytes 786440 | tf_op jit(solution)/shard_map/ppermute | solution.py:103
  43.1 21.5 %collective-permute-start.10 = (bf16[256,512]{1,0:T(8,128)(2,1)}, bf16[256,512]{1,0:T(8,128)(2,1)S(1)}, u32[]{:S(2)}, u32[]{:S(2)}) collective-permute-start(bf16[256,512]{1,0:T(8,128)(2,1)} %get-tuple-element.359), channel_id=1, source_target_pairs={{0,4},{1,5},{2,6},{3,7},{4,0},{5,1},{6,2},{7,3},{8,12},{9,13},{10,... | collective-permute-start | bytes 786440 | tf_op jit(solution)/shard_map/ppermute | solution.py:103
  73.3 27.3 %collective-permute-start.15 = (bf16[256,512]{1,0:T(8,128)(2,1)}, bf16[256,512]{1,0:T(8,128)(2,1)}, u32[]{:S(2)}, u32[]{:S(2)}) collective-permute-start(bf16[256,512]{1,0:T(8,128)(2,1)} %get-tuple-element.377), channel_id=1, source_target_pairs={{0,5},{1,4},{2,7},{3,6},{4,1},{5,0},{6,3},{7,2},{8,13},{9,12},{10,... | collective-permute-start | bytes 786440 | tf_op jit(solution)/shard_map/ppermute | solution.py:103
  74.7 25.8 %collective-permute-start.16 = (bf16[256,512]{1,0:T(8,128)(2,1)}, bf16[256,512]{1,0:T(8,128)(2,1)}, u32[]{:S(2)}, u32[]{:S(2)}) collective-permute-start(bf16[256,512]{1,0:T(8,128)(2,1)} %get-tuple-element.378), channel_id=1, source_target_pairs={{0,6},{1,7},{2,4},{3,5},{4,2},{5,3},{6,0},{7,1},{8,14},{9,15},{10,... | collective-permute-start | bytes 786440 | tf_op jit(solution)/shard_map/ppermute | solution.py:103
  77.2 23.4 %collective-permute-start.17 = (bf16[256,512]{1,0:T(8,128)(2,1)}, bf16[256,512]{1,0:T(8,128)(2,1)}, u32[]{:S(2)}, u32[]{:S(2)}) collective-permute-start(bf16[256,512]{1,0:T(8,128)(2,1)} %get-tuple-element.379), channel_id=1, source_target_pairs={{0,7},{1,6},{2,5},{3,4},{4,3},{5,2},{6,1},{7,0},{8,15},{9,14},{10,... | collective-permute-start | bytes 786440 | tf_op jit(solution)/shard_map/ppermute | solution.py:103
  100.6 21.5 %collective-permute-start.18 = (bf16[256,256]{1,0:T(8,128)(2,1)}, bf16[256,256]{1,0:T(8,128)(2,1)S(1)}, u32[]{:S(2)}, u32[]{:S(2)}) collective-permute-start(bf16[256,256]{1,0:T(8,128)(2,1)} %get-tuple-element.380), channel_id=1, source_target_pairs={{0,0},{1,1},{2,16},{3,17},{4,8},{5,9},{6,24},{7,25},{8,4},{9,5},{1... | collective-permute-start | bytes 393224 | tf_op jit(solution)/shard_map/ppermute | solution.py:99
  102.1 20.7 %collective-permute-start.19 = (bf16[256,256]{1,0:T(8,128)(2,1)}, bf16[256,256]{1,0:T(8,128)(2,1)S(1)}, u32[]{:S(2)}, u32[]{:S(2)}) collective-permute-start(bf16[256,256]{1,0:T(8,128)(2,1)} %get-tuple-element.381), channel_id=1, source_target_pairs={{0,1},{1,0},{2,17},{3,16},{4,9},{5,8},{6,25},{7,24},{8,5},{9,4},{1... | collective-permute-start | bytes 393224 | tf_op jit(solution)/shard_map/ppermute | solution.py:99
  103.7 33.8 %collective-permute-start.20 = (bf16[256,256]{1,0:T(8,128)(2,1)}, bf16[256,256]{1,0:T(8,128)(2,1)S(1)}, u32[]{:S(2)}, u32[]{:S(2)}) collective-permute-start(bf16[256,256]{1,0:T(8,128)(2,1)} %get-tuple-element.382), channel_id=1, source_target_pairs={{0,16},{1,17},{2,0},{3,1},{4,24},{5,25},{6,8},{7,9},{8,20},{9,21},... | collective-permute-start | bytes 393224 | tf_op jit(solution)/shard_map/ppermute | solution.py:99
  146.3 53.4 %collective-permute-start.35 = (bf16[2048,512]{1,0:T(8,128)(2,1)}, bf16[2048,512]{1,0:T(8,128)(2,1)S(1)}, u32[]{:S(2)}, u32[]{:S(2)}) collective-permute-start(bf16[2048,512]{1,0:T(8,128)(2,1)} %get-tuple-element.407.refs_8_.refs_0_), channel_id=1, source_target_pairs={{0,16},{8,24},{16,0},{24,8},{1,17},{9,25},{17,1},{25,9},{2,18},{10... | collective-permute-start | bytes 6291464 | tf_op jit(solution)/shard_map/ppermute | solution.py:103
  149.3 26.0 %collective-permute-start.26 = (bf16[256,2048]{1,0:T(8,128)(2,1)S(1)}, bf16[256,2048]{1,0:T(8,128)(2,1)}, u32[]{:S(2)}, u32[]{:S(2)}) collective-permute-start(bf16[256,2048]{1,0:T(8,128)(2,1)S(1)} %copy-done.5), channel_id=1, source_target_pairs={{1,3},{3,5},{5,7},{7,6},{6,4},{4,2},{2,0},{0,1},{9,11},{11,13},{13... | collective-permute-start | bytes 3145736 | tf_op jit(solution)/shard_map/ppermute | solution.py:85
  149.3 26.0 %collective-permute-start.27 = (bf16[256,2048]{1,0:T(8,128)(2,1)S(1)}, bf16[256,2048]{1,0:T(8,128)(2,1)}, u32[]{:S(2)}, u32[]{:S(2)}) collective-permute-start(bf16[256,2048]{1,0:T(8,128)(2,1)S(1)} %copy-done.5), channel_id=1, source_target_pairs={{3,1},{5,3},{7,5},{6,7},{4,6},{2,4},{0,2},{1,0},{11,9},{13,11},{15... | collective-permute-start | bytes 3145736 | tf_op jit(solution)/shard_map/ppermute | solution.py:88
  178.8 18.7 %collective-permute-start.31 = (bf16[256,256]{1,0:T(8,128)(2,1)}, bf16[256,256]{1,0:T(8,128)(2,1)S(1)}, u32[]{:S(2)}, u32[]{:S(2)}) collective-permute-start(bf16[256,256]{1,0:T(8,128)(2,1)} %get-tuple-element.401), channel_id=1, source_target_pairs={{0,4},{1,5},{2,6},{3,7},{4,0},{5,1},{6,2},{7,3},{8,12},{9,13},{10,... | collective-permute-start | bytes 393224 | tf_op jit(solution)/shard_map/ppermute | solution.py:103
  181.1 18.6 %collective-permute-start.32 = (bf16[256,256]{1,0:T(8,128)(2,1)}, bf16[256,256]{1,0:T(8,128)(2,1)S(1)}, u32[]{:S(2)}, u32[]{:S(2)}) collective-permute-start(bf16[256,256]{1,0:T(8,128)(2,1)} %get-tuple-element.402), channel_id=1, source_target_pairs={{0,5},{1,4},{2,7},{3,6},{4,1},{5,0},{6,3},{7,2},{8,13},{9,12},{10,... | collective-permute-start | bytes 393224 | tf_op jit(solution)/shard_map/ppermute | solution.py:103
  200.3 34.7 %collective-permute-start.40 = (bf16[256,2048]{1,0:T(8,128)(2,1)}, bf16[256,2048]{1,0:T(8,128)(2,1)}, u32[]{:S(2)}, u32[]{:S(2)}) collective-permute-start(bf16[256,2048]{1,0:T(8,128)(2,1)} %collective-permute-done.26.refs_2_.refs_10_), channel_id=1, source_target_pairs={{1,3},{3,5},{5,7},{7,6},{6,4},{4,2},{2,0},{0,1},{9,11},{11,13},{13... | collective-permute-start | bytes 3145736 | tf_op jit(solution)/shard_map/ppermute | solution.py:85
  202.4 32.6 %collective-permute-start.41 = (bf16[256,2048]{1,0:T(8,128)(2,1)}, bf16[256,2048]{1,0:T(8,128)(2,1)}, u32[]{:S(2)}, u32[]{:S(2)}) collective-permute-start(bf16[256,2048]{1,0:T(8,128)(2,1)} %collective-permute-done.27.refs_3_.refs_11_), channel_id=1, source_target_pairs={{3,1},{5,3},{7,5},{6,7},{4,6},{2,4},{0,2},{1,0},{11,9},{13,11},{15... | collective-permute-start | bytes 3145736 | tf_op jit(solution)/shard_map/ppermute | solution.py:88
  218.6 33.4 %collective-permute-start.38 = (bf16[256,2048]{1,0:T(8,128)(2,1)}, bf16[256,2048]{1,0:T(8,128)(2,1)S(1)}, u32[]{:S(2)}, u32[]{:S(2)}) collective-permute-start(bf16[256,2048]{1,0:T(8,128)(2,1)} %get-tuple-element.410.refs_0_.refs_9_), channel_id=1, source_target_pairs={{1,3},{3,5},{5,7},{7,6},{6,4},{4,2},{2,0},{0,1},{9,11},{11,13},{13... | collective-permute-start | bytes 3145736 | tf_op jit(solution)/shard_map/ppermute | solution.py:85
  220.7 32.1 %collective-permute-start.39 = (bf16[256,2048]{1,0:T(8,128)(2,1)}, bf16[256,2048]{1,0:T(8,128)(2,1)S(1)}, u32[]{:S(2)}, u32[]{:S(2)}) collective-permute-start(bf16[256,2048]{1,0:T(8,128)(2,1)} %get-tuple-element.410.refs_0_.refs_9_), channel_id=1, source_target_pairs={{3,1},{5,3},{7,5},{6,7},{4,6},{2,4},{0,2},{1,0},{11,9},{13,11},{15... | collective-permute-start | bytes 3145736 | tf_op jit(solution)/shard_map/ppermute | solution.py:88
  252.8 26.1 %collective-permute-start.42 = (bf16[256,2048]{1,0:T(8,128)(2,1)S(1)}, bf16[256,2048]{1,0:T(8,128)(2,1)S(1)}, u32[]{:S(2)}, u32[]{:S(2)}) collective-permute-start(bf16[256,2048]{1,0:T(8,128)(2,1)S(1)} %collective-permute-done.38.refs_0_.refs_10_), channel_id=1, source_target_pairs={{1,3},{3,5},{5,7},{7,6},{6,4},{4,2},{2,0},{0,1},{9,11},{11,13},{13... | collective-permute-start | bytes 3145736 | tf_op jit(solution)/shard_map/ppermute | solution.py:85
  254.6 26.1 %collective-permute-start.43 = (bf16[256,2048]{1,0:T(8,128)(2,1)S(1)}, bf16[256,2048]{1,0:T(8,128)(2,1)S(1)}, u32[]{:S(2)}, u32[]{:S(2)}) collective-permute-start(bf16[256,2048]{1,0:T(8,128)(2,1)S(1)} %collective-permute-done.39.refs_1_.refs_11_), channel_id=1, source_target_pairs={{3,1},{5,3},{7,5},{6,7},{4,6},{2,4},{0,2},{1,0},{11,9},{13,11},{15... | collective-permute-start | bytes 3145736 | tf_op jit(solution)/shard_map/ppermute | solution.py:88
  254.8 44.7 %collective-permute-start.44 = (bf16[256,2048]{1,0:T(8,128)(2,1)}, bf16[256,2048]{1,0:T(8,128)(2,1)S(1)}, u32[]{:S(2)}, u32[]{:S(2)}) collective-permute-start(bf16[256,2048]{1,0:T(8,128)(2,1)} %collective-permute-done.40.refs_2_.refs_12_), channel_id=1, source_target_pairs={{1,3},{3,5},{5,7},{7,6},{6,4},{4,2},{2,0},{0,1},{9,11},{11,13},{13... | collective-permute-start | bytes 3145736 | tf_op jit(solution)/shard_map/ppermute | solution.py:85
  256.6 44.2 %collective-permute-start.45 = (bf16[256,2048]{1,0:T(8,128)(2,1)}, bf16[256,2048]{1,0:T(8,128)(2,1)}, u32[]{:S(2)}, u32[]{:S(2)}) collective-permute-start(bf16[256,2048]{1,0:T(8,128)(2,1)} %collective-permute-done.41.refs_3_.refs_13_), channel_id=1, source_target_pairs={{3,1},{5,3},{7,5},{6,7},{4,6},{2,4},{0,2},{1,0},{11,9},{13,11},{15... | collective-permute-start | bytes 3145736 | tf_op jit(solution)/shard_map/ppermute | solution.py:88
  256.8 70.8 %collective-permute-start.50 = (bf16[2048,512]{1,0:T(8,128)(2,1)}, bf16[2048,512]{1,0:T(8,128)(2,1)}, u32[]{:S(2)}, u32[]{:S(2)}) collective-permute-start(bf16[2048,512]{1,0:T(8,128)(2,1)} %get-tuple-element.450.refs_4_), channel_id=1, source_target_pairs={{0,16},{8,24},{16,0},{24,8},{1,17},{9,25},{17,1},{25,9},{2,18},{10... | collective-permute-start | bytes 6291464 | tf_op jit(solution)/shard_map/ppermute | solution.py:103
  300.8 26.1 %collective-permute-start.46 = (bf16[256,2048]{1,0:T(8,128)(2,1)S(1)}, bf16[256,2048]{1,0:T(8,128)(2,1)S(1)}, u32[]{:S(2)}, u32[]{:S(2)}) collective-permute-start(bf16[256,2048]{1,0:T(8,128)(2,1)S(1)} %collective-permute-done.42.refs_0_.refs_12_), channel_id=1, source_target_pairs={{1,3},{3,5},{5,7},{7,6},{6,4},{4,2},{2,0},{0,1},{9,11},{11,13},{13... | collective-permute-start | bytes 3145736 | tf_op jit(solution)/shard_map/ppermute | solution.py:85
  301.5 26.1 %collective-permute-start.47 = (bf16[256,2048]{1,0:T(8,128)(2,1)S(1)}, bf16[256,2048]{1,0:T(8,128)(2,1)S(1)}, u32[]{:S(2)}, u32[]{:S(2)}) collective-permute-start(bf16[256,2048]{1,0:T(8,128)(2,1)S(1)} %collective-permute-done.43.refs_1_.refs_13_), channel_id=1, source_target_pairs={{3,1},{5,3},{7,5},{6,7},{4,6},{2,4},{0,2},{1,0},{11,9},{13,11},{15... | collective-permute-start | bytes 3145736 | tf_op jit(solution)/shard_map/ppermute | solution.py:88
  304.0 30.9 %collective-permute-start.48 = (bf16[128,2048]{1,0:T(8,128)(2,1)S(1)}, bf16[128,2048]{1,0:T(8,128)(2,1)S(1)}, u32[]{:S(2)}, u32[]{:S(2)}) collective-permute-start(bf16[128,2048]{1,0:T(8,128)(2,1)S(1)} %slice.139), channel_id=1, source_target_pairs={{1,3},{3,5},{5,7},{7,6},{6,4},{4,2},{2,0},{0,1},{9,11},{11,13},{13... | collective-permute-start | bytes 1572872 | tf_op jit(solution)/shard_map/ppermute | solution.py:85
  304.7 30.7 %collective-permute-start.49 = (bf16[128,2048]{1,0:T(8,128)(2,1)S(1)}, bf16[128,2048]{1,0:T(8,128)(2,1)S(1)}, u32[]{:S(2)}, u32[]{:S(2)}) collective-permute-start(bf16[128,2048]{1,0:T(8,128)(2,1)S(1)} %slice.140), channel_id=1, source_target_pairs={{3,1},{5,3},{7,5},{6,7},{4,6},{2,4},{0,2},{1,0},{11,9},{13,11},{15... | collective-permute-start | bytes 1572872 | tf_op jit(solution)/shard_map/ppermute | solution.py:88
  335.4 18.9 %collective-permute-start.51 = (bf16[128,2048]{1,0:T(8,128)(2,1)S(1)}, bf16[128,2048]{1,0:T(8,128)(2,1)S(1)}, u32[]{:S(2)}, u32[]{:S(2)}) collective-permute-start(bf16[128,2048]{1,0:T(8,128)(2,1)S(1)} %slice.137), channel_id=1, source_target_pairs={{1,3},{3,5},{5,7},{7,6},{6,4},{4,2},{2,0},{0,1},{9,11},{11,13},{13... | collective-permute-start | bytes 1572872 | tf_op jit(solution)/shard_map/ppermute | solution.py:85
  354.3 33.2 %collective-permute-start.55 = (bf16[2048,512]{1,0:T(8,128)(2,1)}, bf16[2048,512]{1,0:T(8,128)(2,1)S(1)}, u32[]{:S(2)}, u32[]{:S(2)}) collective-permute-start(bf16[2048,512]{1,0:T(8,128)(2,1)} %get-tuple-element.450.refs_4_), channel_id=1, source_target_pairs={{0,8},{8,0},{16,24},{24,16},{1,9},{9,1},{17,25},{25,17},{2,10},{10... | collective-permute-start | bytes 6291464 | tf_op jit(solution)/shard_map/ppermute | solution.py:103
  354.4 33.1 %collective-permute-start.56 = (bf16[2048,512]{1,0:T(8,128)(2,1)}, bf16[2048,512]{1,0:T(8,128)(2,1)S(1)}, u32[]{:S(2)}, u32[]{:S(2)}) collective-permute-start(bf16[2048,512]{1,0:T(8,128)(2,1)} %collective-permute-done.50.refs_5_), channel_id=1, source_target_pairs={{0,8},{8,0},{16,24},{24,16},{1,9},{9,1},{17,25},{25,17},{2,10},{10... | collective-permute-start | bytes 6291464 | tf_op jit(solution)/shard_map/ppermute | solution.py:103
  387.5 23.7 %collective-permute-start.57 = (bf16[256,2048]{1,0:T(8,128)(2,1)S(1)}, bf16[256,2048]{1,0:T(8,128)(2,1)}, u32[]{:S(2)}, u32[]{:S(2)}) collective-permute-start(bf16[256,2048]{1,0:T(8,128)(2,1)S(1)} %pad_maximum_fusion), channel_id=1, source_target_pairs={{3,1},{5,3},{7,5},{6,7},{4,6},{2,4},{0,2},{1,0},{11,9},{13,11},{15... | collective-permute-start | bytes 3145736 | tf_op jit(solution)/shard_map/ppermute | solution.py:88
  388.5 24.2 %collective-permute-start.58 = (bf16[256,2048]{1,0:T(8,128)(2,1)}, bf16[256,2048]{1,0:T(8,128)(2,1)}, u32[]{:S(2)}, u32[]{:S(2)}) collective-permute-start(bf16[256,2048]{1,0:T(8,128)(2,1)} %pad_maximum_fusion.1), channel_id=1, source_target_pairs={{1,3},{3,5},{5,7},{7,6},{6,4},{4,2},{2,0},{0,1},{9,11},{11,13},{13... | collective-permute-start | bytes 3145736 | tf_op jit(solution)/shard_map/ppermute | solution.py:85
  389.6 24.8 %collective-permute-start.59 = (bf16[256,2048]{1,0:T(8,128)(2,1)}, bf16[256,2048]{1,0:T(8,128)(2,1)}, u32[]{:S(2)}, u32[]{:S(2)}) collective-permute-start(bf16[256,2048]{1,0:T(8,128)(2,1)} %get-tuple-element.497.refs_8_), channel_id=1, source_target_pairs={{0,16},{8,24},{16,0},{24,8},{1,17},{9,25},{17,1},{25,9},{2,18},{10... | collective-permute-start | bytes 3145736 | tf_op jit(solution)/shard_map/ppermute | solution.py:103
  414.3 22.8 %collective-permute-start.60 = (bf16[256,2048]{1,0:T(8,128)(2,1)S(1)}, bf16[256,2048]{1,0:T(8,128)(2,1)}, u32[]{:S(2)}, u32[]{:S(2)}) collective-permute-start(bf16[256,2048]{1,0:T(8,128)(2,1)S(1)} %add_convert_fusion.11), channel_id=1, source_target_pairs={{3,1},{5,3},{7,5},{6,7},{4,6},{2,4},{0,2},{1,0},{11,9},{13,11},{15... | collective-permute-start | bytes 3145736 | tf_op jit(solution)/shard_map/ppermute | solution.py:88
  415.3 24.5 %collective-permute-start.61 = (bf16[256,2048]{1,0:T(8,128)(2,1)S(1)}, bf16[256,2048]{1,0:T(8,128)(2,1)S(1)}, u32[]{:S(2)}, u32[]{:S(2)}) collective-permute-start(bf16[256,2048]{1,0:T(8,128)(2,1)S(1)} %add_convert_fusion.10), channel_id=1, source_target_pairs={{1,3},{3,5},{5,7},{7,6},{6,4},{4,2},{2,0},{0,1},{9,11},{11,13},{13... | collective-permute-start | bytes 3145736 | tf_op jit(solution)/shard_map/ppermute | solution.py:85
  416.4 24.7 %collective-permute-start.62 = (bf16[688,1024]{1,0:T(8,128)(2,1)}, bf16[688,1024]{1,0:T(8,128)(2,1)S(1)}, u32[]{:S(2)}, u32[]{:S(2)}) collective-permute-start(bf16[688,1024]{1,0:T(8,128)(2,1)} %get-tuple-element.477), channel_id=1, source_target_pairs={{0,8},{8,0},{16,24},{24,16},{1,9},{9,1},{17,25},{25,17},{2,10},{10... | collective-permute-start | bytes 4227080 | tf_op jit(solution)/shard_map/ppermute | solution.py:103
  416.4 24.7 %collective-permute-start.63 = (bf16[256,2048]{1,0:T(8,128)(2,1)}, bf16[256,2048]{1,0:T(8,128)(2,1)}, u32[]{:S(2)}, u32[]{:S(2)}) collective-permute-start(bf16[256,2048]{1,0:T(8,128)(2,1)} %get-tuple-element.497.refs_8_), channel_id=1, source_target_pairs={{0,8},{8,0},{16,24},{24,16},{1,9},{9,1},{17,25},{25,17},{2,10},{10... | collective-permute-start | bytes 3145736 | tf_op jit(solution)/shard_map/ppermute | solution.py:103
  416.9 24.2 %collective-permute-start.64 = (bf16[256,2048]{1,0:T(8,128)(2,1)}, bf16[256,2048]{1,0:T(8,128)(2,1)}, u32[]{:S(2)}, u32[]{:S(2)}) collective-permute-start(bf16[256,2048]{1,0:T(8,128)(2,1)} %collective-permute-done.59.refs_9_), channel_id=1, source_target_pairs={{0,8},{8,0},{16,24},{24,16},{1,9},{9,1},{17,25},{25,17},{2,10},{10... | collective-permute-start | bytes 3145736 | tf_op jit(solution)/shard_map/ppermute | solution.py:103
  437.1 26.7 %collective-permute-start.67 = (bf16[688,1024]{1,0:T(8,128)(2,1)}, bf16[688,1024]{1,0:T(8,128)(2,1)S(1)}, u32[]{:S(2)}, u32[]{:S(2)}) collective-permute-start(bf16[688,1024]{1,0:T(8,128)(2,1)} %get-tuple-element.501), channel_id=1, source_target_pairs={{0,8},{8,0},{16,24},{24,16},{1,9},{9,1},{17,25},{25,17},{2,10},{10... | collective-permute-start | bytes 4227080 | tf_op jit(solution)/shard_map/ppermute | solution.py:103
  441.1 25.7 %collective-permute-start.65 = (bf16[256,2048]{1,0:T(8,128)(2,1)}, bf16[256,2048]{1,0:T(8,128)(2,1)S(1)}, u32[]{:S(2)}, u32[]{:S(2)}) collective-permute-start(bf16[256,2048]{1,0:T(8,128)(2,1)} %add_convert_fusion.9), channel_id=1, source_target_pairs={{3,1},{5,3},{7,5},{6,7},{4,6},{2,4},{0,2},{1,0},{11,9},{13,11},{15... | collective-permute-start | bytes 3145736 | tf_op jit(solution)/shard_map/ppermute | solution.py:88
  442.1 25.6 %collective-permute-start.66 = (bf16[256,2048]{1,0:T(8,128)(2,1)}, bf16[256,2048]{1,0:T(8,128)(2,1)}, u32[]{:S(2)}, u32[]{:S(2)}) collective-permute-start(bf16[256,2048]{1,0:T(8,128)(2,1)} %add_convert_fusion.8), channel_id=1, source_target_pairs={{1,3},{3,5},{5,7},{7,6},{6,4},{4,2},{2,0},{0,1},{9,11},{11,13},{13... | collective-permute-start | bytes 3145736 | tf_op jit(solution)/shard_map/ppermute | solution.py:85
  445.2 18.7 %collective-permute-start.68 = (bf16[344,1024]{1,0:T(8,128)(2,1)}, bf16[344,1024]{1,0:T(8,128)(2,1)}, u32[]{:S(2)}, u32[]{:S(2)}) collective-permute-start(bf16[344,1024]{1,0:T(8,128)(2,1)} %get-tuple-element.521), channel_id=1, source_target_pairs={{0,16},{8,24},{16,0},{24,8},{1,17},{9,25},{17,1},{25,9},{2,18},{10... | collective-permute-start | bytes 2113544 | tf_op jit(solution)/shard_map/ppermute | solution.py:103
  470.6 18.9 %collective-permute-start.71 = (bf16[344,1024]{1,0:T(8,128)(2,1)}, bf16[344,1024]{1,0:T(8,128)(2,1)S(1)}, u32[]{:S(2)}, u32[]{:S(2)}) collective-permute-start(bf16[344,1024]{1,0:T(8,128)(2,1)} %get-tuple-element.536), channel_id=1, source_target_pairs={{0,16},{8,24},{16,0},{24,8},{1,17},{9,25},{17,1},{25,9},{2,18},{10... | collective-permute-start | bytes 2113544 | tf_op jit(solution)/shard_map/ppermute | solution.py:103
  497.4 18.9 %collective-permute-start.76 = (bf16[256,256]{1,0:T(8,128)(2,1)S(1)}, bf16[256,256]{1,0:T(8,128)(2,1)S(1)}, u32[]{:S(2)}, u32[]{:S(2)}) collective-permute-start(bf16[256,256]{1,0:T(8,128)(2,1)S(1)} %copy-done.127), channel_id=1, source_target_pairs={{0,5},{1,4},{2,7},{3,6},{4,1},{5,0},{6,3},{7,2},{8,13},{9,12},{10,... | collective-permute-start | bytes 393224 | tf_op jit(solution)/shard_map/ppermute | solution.py:103
  516.4 30.4 %collective-permute-start.82 = (bf16[256,2048]{1,0:T(8,128)(2,1)S(1)}, bf16[256,2048]{1,0:T(8,128)(2,1)S(1)}, u32[]{:S(2)}, u32[]{:S(2)}) collective-permute-start(bf16[256,2048]{1,0:T(8,128)(2,1)S(1)} %pad_maximum_fusion.2), channel_id=1, source_target_pairs={{3,1},{5,3},{7,5},{6,7},{4,6},{2,4},{0,2},{1,0},{11,9},{13,11},{15... | collective-permute-start | bytes 3145736 | tf_op jit(solution)/shard_map/ppermute | solution.py:88
  521.7 25.0 %collective-permute-start.83 = (bf16[256,2048]{1,0:T(8,128)(2,1)S(1)}, bf16[256,2048]{1,0:T(8,128)(2,1)S(1)}, u32[]{:S(2)}, u32[]{:S(2)}) collective-permute-start(bf16[256,2048]{1,0:T(8,128)(2,1)S(1)} %pad_maximum_fusion.3), channel_id=1, source_target_pairs={{1,3},{3,5},{5,7},{7,6},{6,4},{4,2},{2,0},{0,1},{9,11},{11,13},{13... | collective-permute-start | bytes 3145736 | tf_op jit(solution)/shard_map/ppermute | solution.py:85
  522.7 24.0 %collective-permute-start.84 = (bf16[344,1024]{1,0:T(8,128)(2,1)}, bf16[344,1024]{1,0:T(8,128)(2,1)S(1)}, u32[]{:S(2)}, u32[]{:S(2)}) collective-permute-start(bf16[344,1024]{1,0:T(8,128)(2,1)} %get-tuple-element.574), channel_id=1, source_target_pairs={{0,16},{8,24},{16,0},{24,8},{1,17},{9,25},{17,1},{25,9},{2,18},{10... | collective-permute-start | bytes 2113544 | tf_op jit(solution)/shard_map/ppermute | solution.py:103
  573.9 36.1 %collective-permute-start.93 = (bf16[256,2048]{1,0:T(8,128)(2,1)S(1)}, bf16[256,2048]{1,0:T(8,128)(2,1)S(1)}, u32[]{:S(2)}, u32[]{:S(2)}) collective-permute-start(bf16[256,2048]{1,0:T(8,128)(2,1)S(1)} %add_convert_fusion.7), channel_id=1, source_target_pairs={{3,1},{5,3},{7,5},{6,7},{4,6},{2,4},{0,2},{1,0},{11,9},{13,11},{15... | collective-permute-start | bytes 3145736 | tf_op jit(solution)/shard_map/ppermute | solution.py:88
  578.9 31.1 %collective-permute-start.94 = (bf16[256,2048]{1,0:T(8,128)(2,1)S(1)}, bf16[256,2048]{1,0:T(8,128)(2,1)S(1)}, u32[]{:S(2)}, u32[]{:S(2)}) collective-permute-start(bf16[256,2048]{1,0:T(8,128)(2,1)S(1)} %add_convert_fusion.6), channel_id=1, source_target_pairs={{1,3},{3,5},{5,7},{7,6},{6,4},{4,2},{2,0},{0,1},{9,11},{11,13},{13... | collective-permute-start | bytes 3145736 | tf_op jit(solution)/shard_map/ppermute | solution.py:85
  591.5 20.7 %collective-permute-start.95 = (bf16[256,512]{1,0:T(8,128)(2,1)S(1)}, bf16[256,512]{1,0:T(8,128)(2,1)S(1)}, u32[]{:S(2)}, u32[]{:S(2)}) collective-permute-start(bf16[256,512]{1,0:T(8,128)(2,1)S(1)} %copy-done.110), channel_id=1, source_target_pairs={{0,1},{1,0},{2,3},{3,2},{4,5},{5,4},{6,7},{7,6},{8,9},{9,8},{10,11... | collective-permute-start | bytes 786440 | tf_op jit(solution)/shard_map/ppermute | solution.py:103
  592.8 19.4 %collective-permute-start.96 = (bf16[256,512]{1,0:T(8,128)(2,1)S(1)}, bf16[256,512]{1,0:T(8,128)(2,1)S(1)}, u32[]{:S(2)}, u32[]{:S(2)}) collective-permute-start(bf16[256,512]{1,0:T(8,128)(2,1)S(1)} %copy-done.109), channel_id=1, source_target_pairs={{0,2},{1,3},{2,0},{3,1},{4,6},{5,7},{6,4},{7,5},{8,10},{9,11},{10,... | collective-permute-start | bytes 786440 | tf_op jit(solution)/shard_map/ppermute | solution.py:103
  610.0 58.2 %collective-permute-start.117 = (bf16[688,1024]{1,0:T(8,128)(2,1)}, bf16[688,1024]{1,0:T(8,128)(2,1)S(1)}, u32[]{:S(2)}, u32[]{:S(2)}) collective-permute-start(bf16[688,1024]{1,0:T(8,128)(2,1)} %get-tuple-element.653), channel_id=1, source_target_pairs={{0,8},{8,0},{16,24},{24,16},{1,9},{9,1},{17,25},{25,17},{2,10},{10... | collective-permute-start | bytes 4227080 | tf_op jit(solution)/shard_map/ppermute | solution.py:103
  617.8 49.4 %collective-permute-start.99 = (bf16[256,2048]{1,0:T(8,128)(2,1)}, bf16[256,2048]{1,0:T(8,128)(2,1)S(1)}, u32[]{:S(2)}, u32[]{:S(2)}) collective-permute-start(bf16[256,2048]{1,0:T(8,128)(2,1)} %add_convert_fusion.4), channel_id=1, source_target_pairs={{1,3},{3,5},{5,7},{7,6},{6,4},{4,2},{2,0},{0,1},{9,11},{11,13},{13... | collective-permute-start | bytes 3145736 | tf_op jit(solution)/shard_map/ppermute | solution.py:85
  618.9 48.3 %collective-permute-start.98 = (bf16[256,2048]{1,0:T(8,128)(2,1)}, bf16[256,2048]{1,0:T(8,128)(2,1)S(1)}, u32[]{:S(2)}, u32[]{:S(2)}) collective-permute-start(bf16[256,2048]{1,0:T(8,128)(2,1)} %add_convert_fusion.5), channel_id=1, source_target_pairs={{3,1},{5,3},{7,5},{6,7},{4,6},{2,4},{0,2},{1,0},{11,9},{13,11},{15... | collective-permute-start | bytes 3145736 | tf_op jit(solution)/shard_map/ppermute | solution.py:88
  625.8 46.6 %collective-permute-start.111 = (bf16[688,1024]{1,0:T(8,128)(2,1)}, bf16[688,1024]{1,0:T(8,128)(2,1)S(1)}, u32[]{:S(2)}, u32[]{:S(2)}) collective-permute-start(bf16[688,1024]{1,0:T(8,128)(2,1)} %chip_sum.3.mine), channel_id=1, source_target_pairs={{0,8},{8,0},{16,24},{24,16},{1,9},{9,1},{17,25},{25,17},{2,10},{10... | collective-permute-start | bytes 4227080 | tf_op jit(solution)/shard_map/ppermute | solution.py:103
  625.8 26.2 %collective-permute-start.108 = (bf16[272,512]{1,0:T(8,128)(2,1)S(1)}, bf16[272,512]{1,0:T(8,128)(2,1)S(1)}, u32[]{:S(2)}, u32[]{:S(2)}) collective-permute-start(bf16[272,512]{1,0:T(8,128)(2,1)S(1)} %get-tuple-element.634), channel_id=1, source_target_pairs={{1,3},{3,5},{5,7},{7,6},{6,4},{4,2},{2,0},{0,1},{9,11},{11,13},{13... | collective-permute-start | bytes 835592 | tf_op jit(solution)/shard_map/ppermute | solution.py:85
  667.2 43.8 %collective-permute-start.114 = (bf16[688,1024]{1,0:T(8,128)(2,1)S(1)}, bf16[688,1024]{1,0:T(8,128)(2,1)S(1)}, u32[]{:S(2)}, u32[]{:S(2)}) collective-permute-start(bf16[688,1024]{1,0:T(8,128)(2,1)S(1)} %copy-done.17), channel_id=1, source_target_pairs={{0,8},{8,0},{16,24},{24,16},{1,9},{9,1},{17,25},{25,17},{2,10},{10... | collective-permute-start | bytes 4227080 | tf_op jit(solution)/shard_map/ppermute | solution.py:103
  671.2 36.5 %collective-permute-start.118 = (bf16[344,1024]{1,0:T(8,128)(2,1)}, bf16[344,1024]{1,0:T(8,128)(2,1)}, u32[]{:S(2)}, u32[]{:S(2)}) collective-permute-start(bf16[344,1024]{1,0:T(8,128)(2,1)} %get-tuple-element.654), channel_id=1, source_target_pairs={{0,16},{8,24},{16,0},{24,8},{1,17},{9,25},{17,1},{25,9},{2,18},{10... | collective-permute-start | bytes 2113544 | tf_op jit(solution)/shard_map/ppermute | solution.py:103
  672.4 35.3 %collective-permute-start.119 = (bf16[344,1024]{1,0:T(8,128)(2,1)}, bf16[344,1024]{1,0:T(8,128)(2,1)}, u32[]{:S(2)}, u32[]{:S(2)}) collective-permute-start(bf16[344,1024]{1,0:T(8,128)(2,1)} %get-tuple-element.655), channel_id=1, source_target_pairs={{0,16},{8,24},{16,0},{24,8},{1,17},{9,25},{17,1},{25,9},{2,18},{10... | collective-permute-start | bytes 2113544 | tf_op jit(solution)/shard_map/ppermute | solution.py:103
  697.3 21.9 %collective-permute-start.112 = (bf16[544,512]{1,0:T(8,128)(2,1)S(1)}, bf16[544,512]{1,0:T(8,128)(2,1)S(1)}, u32[]{:S(2)}, u32[]{:S(2)}) collective-permute-start(bf16[544,512]{1,0:T(8,128)(2,1)S(1)} %add_convert_fusion.16), channel_id=1, source_target_pairs={{3,1},{5,3},{7,5},{6,7},{4,6},{2,4},{0,2},{1,0},{11,9},{13,11},{15... | collective-permute-start | bytes 1671176 | tf_op jit(solution)/shard_map/ppermute | solution.py:88
  710.9 23.0 %collective-permute-start.120 = (bf16[688,1024]{1,0:T(8,128)(2,1)}, bf16[688,1024]{1,0:T(8,128)(2,1)S(1)}, u32[]{:S(2)}, u32[]{:S(2)}) collective-permute-start(bf16[688,1024]{1,0:T(8,128)(2,1)} %chip_sum.5.mine), channel_id=1, source_target_pairs={{0,8},{8,0},{16,24},{24,16},{1,9},{9,1},{17,25},{25,17},{2,10},{10... | collective-permute-start | bytes 4227080 | tf_op jit(solution)/shard_map/ppermute | solution.py:103
  (196 other events, 2581.6 us)

commit v4 on v3

--- a/solution.py
+++ b/solution.py
@@ -597,46 +597,45 @@
     def load(src, dst, k):
         return pltpu.make_async_copy(src, dst, sems.at[k])
 
+    at = [pl.ds(b * rows, rows) for b in range(m)]
     loads = [load(weights_in[k], weights[k], k) for k in range(3)]
-    nf_loads = [load(nf_in[b], nf.at[b], 3 + b) for b in range(m)]
-    cot_loads = [load(cot_in[b], cot.at[b], 3 + m + b) for b in range(m)]
-    start_all([nf_loads[0], loads[0], loads[1], cot_loads[0], loads[2]])
-    start_all([*nf_loads[1:], *cot_loads[1:]])
+    nf_loads = [load(nf_in[b], nf.at[at[b]], 3 + b) for b in range(m)]
+    cot_loads = [load(cot_in[b], cot.at[at[b]], 3 + m + b) for b in range(m)]
+    start_all([*nf_loads, loads[0], loads[1], *cot_loads, loads[2]])
     copies = []
 
-    def store(b, k, src):
-        copy = pltpu.make_async_copy(src, outs[5 * b + k], out_sems.at[5 * b + k])
-        copy.start()
-        copies.append(copy)
-
-    for b in range(m):
-        nf_loads[b].wait()
-        if b == 0:
-            loads[0].wait()
-        gate_value = nt_dot(nf[b], gate_w[...])
-        if b == 0:
-            loads[1].wait()
-        up_value = nt_dot(nf[b], up_w[...])
-        cot_loads[b].wait()
-        if b == 0:
-            loads[2].wait()
-        grad_inner = nt_dot(cot[b], down_w[...])
-        sigmoid = 1.0 / (1.0 + jnp.exp(-gate_value))
-        act = gate_value * sigmoid
-        inner = (act * up_value).astype(jnp.bfloat16)
-        grad_gate = (
-            grad_inner * up_value * sigmoid * (1.0 + gate_value * (1.0 - sigmoid))
-        ).astype(jnp.bfloat16)
-        grad_up = (grad_inner * act).astype(jnp.bfloat16)
-        for k, value in enumerate((inner, grad_gate, grad_up)):
-            acts[3 * b + k, :, :hidden_units] = value
-            store(b, k, acts.at[3 * b + k])
-        shares[2 * b] = jnp.dot(
-            grad_gate, gate_w[...], preferred_element_type=jnp.float32
-        ) + jnp.dot(grad_up, up_w[...], preferred_element_type=jnp.float32)
-        store(b, 3, shares.at[2 * b])
-        shares[2 * b + 1] = jnp.dot(inner, down_w[...], preferred_element_type=jnp.float32)
-        store(b, 4, shares.at[2 * b + 1])
+    def store(k, src):
+        for b in range(m):
+            copy = pltpu.make_async_copy(
+                src.at[at[b]], outs[5 * b + k], out_sems.at[5 * b + k]
+            )
+            copy.start()
+            copies.append(copy)
+
+    wait_all(nf_loads)
+    loads[0].wait()
+    gate_value = nt_dot(nf[...], gate_w[...])
+    loads[1].wait()
+    up_value = nt_dot(nf[...], up_w[...])
+    wait_all(cot_loads)
+    loads[2].wait()
+    grad_inner = nt_dot(cot[...], down_w[...])
+    sigmoid = 1.0 / (1.0 + jnp.exp(-gate_value))
+    act = gate_value * sigmoid
+    inner = (act * up_value).astype(jnp.bfloat16)
+    grad_gate = (
+        grad_inner * up_value * sigmoid * (1.0 + gate_value * (1.0 - sigmoid))
+    ).astype(jnp.bfloat16)
+    grad_up = (grad_inner * act).astype(jnp.bfloat16)
+    for k, value in enumerate((inner, grad_gate, grad_up)):
+        acts[k, :, :hidden_units] = value
+        store(k, acts.at[k])
+    shares[0] = jnp.dot(grad_gate, gate_w[...], preferred_element_type=jnp.float32) + jnp.dot(
+        grad_up, up_w[...], preferred_element_type=jnp.float32
+    )
+    store(3, shares.at[0])
+    shares[1] = jnp.dot(inner, down_w[...], preferred_element_type=jnp.float32)
+    store(4, shares.at[1])
     wait_all(copies)
 
 
@@ -652,11 +651,11 @@
         [ANYWHERE] * (2 * m + 3),
         [act, act, act, share, share] * m,
         [ANYWHERE] * (5 * m),
-        [pltpu.VMEM((m, rows, depth), jnp.bfloat16)] * 2
+        [pltpu.VMEM((m * rows, depth), jnp.bfloat16)] * 2
         + [pltpu.VMEM((units, depth), jnp.bfloat16)] * 3
         + [
-            pltpu.VMEM((3 * m, rows, padded(units)), jnp.bfloat16),
-            pltpu.VMEM((2 * m, rows, depth), jnp.float32),
+            pltpu.VMEM((3, m * rows, padded(units)), jnp.bfloat16),
+            pltpu.VMEM((2, m * rows, depth), jnp.float32),
             pltpu.SemaphoreType.DMA((3 + 2 * m,)),
             pltpu.SemaphoreType.DMA((5 * m,)),
         ],
@@ -739,19 +738,18 @@
     for r in range(n):
         cols = pl.ds(aligned(me ^ r, share), share)
         copies.append(pltpu.make_async_copy(blocks[r], mixed.at[:, cols], sems.at[nd + r]))
-    wait_all(start_all(copies))
+    start_all(copies[nd:] + copies[:nd])
+    wait_all(copies[nd:])
     depth = x.shape[1]
-    piece = 512
-
-    def step(c, total):
-        cols = pl.ds(aligned(c, piece), piece)
+    total = jnp.zeros((x.shape[0], 1), jnp.float32)
+    for r in range(nd):
+        copies[r].wait()
+        cols = pl.ds(aligned(dp ^ r, quarter), quarter)
         v = x[:, cols].astype(jnp.float32) + jnp.dot(
             mixed[...], weight[:, cols], preferred_element_type=jnp.float32
         )
         hidden[:, cols] = v
-        return total + jnp.sum(v * v, axis=-1, keepdims=True)
-
-    total = lax.fori_loop(0, depth // piece, step, jnp.zeros((x.shape[0], 1), jnp.float32))
+        total = total + jnp.sum(v * v, axis=-1, keepdims=True)
     normed[...] = (
         hidden[...] * lax.rsqrt(total / depth + EPSILON) * gains[1:2, :]
     ).astype(jnp.bfloat16)
@@ -1161,10 +1159,13 @@
             return [net.swap(sent, "dp", r) for r in range(2, nd, 2)]
 
         grad_sum = RowSum(net, lambda key: made[key][3])
+        out_sum = RowSum(net, lambda key: made[key][4])
         arrived = grad_sum.step()
-        kept, deps, swapped, mixed_parts = [], (), None, ()
+        kept, deps, swapped, mixed_parts, out_1 = [], (), None, (), ()
         for k in range(3):
-            upcoming = grad_sum.step(*deps, *((query_parts, mixed_near, mixed_parts)[k]))
+            upcoming = grad_sum.step(*deps, *out_1, *((query_parts, mixed_near, mixed_parts)[k]))
+            if k == 1:
+                out_1 = out_sum.step(*arrived)
             if k == 1:
                 mixed_parts = cores(mixed_near, *arrived)
             lhs = tie([made[key][(1, 2, 0)[k]] for key in ring_order], *arrived)
@@ -1186,22 +1187,21 @@
             sent = tie(cols, *deps)
             return [b if r == 0 else net.swap(b, "dp", r) for r, b in zip(dp_order, sent)]
 
-        out_sum = RowSum(net, lambda key: made[key][4])
-        out_1 = out_sum.step(*grad_sums[1:])
+        out_2 = out_sum.step(*grad_sums[1:])
         gm_sent, branch_cols, grad_hidden, ffn_gain_part = branch_gradient(
             n, nd, info, hidden, gains, cotangent, grad_sums, out_parts
         )
-        gm_blocks = exchange(tie(gm_sent, *out_1, *others[1]))
+        gm_blocks = exchange(tie(gm_sent, *others[1]))
         branch_got = dp_cols(branch_cols, *gm_sent)
-        gm_blocks = tie(gm_blocks, *branch_got)
+        gm_blocks = tie(gm_blocks, *branch_got, *out_2)
         others.append(exchange_x(kept[1][:top], *gm_blocks))
-        out_2 = out_sum.step(*gm_blocks)
+        out_3 = out_sum.step(*gm_blocks)
         dq_sent, dkv_sent = attention_backward(
             heads_info, q_blocks, kv_blocks, gm_blocks, stats, ot
         )
 
 
-        dq_sent = tie(dq_sent, *out_2, *others[2])
+        dq_sent = tie(dq_sent, *out_3, *others[2])
         others.append(exchange_x(kept[1][top:], *dq_sent))
         dq_blocks = tie(exchange(dq_sent), *others[3])
 
@@ -1212,18 +1212,17 @@
         query_cols = sort_columns(n, nd, info, dq_blocks)
 
         query_got = dp_cols(query_cols)
-        out_3 = out_sum.step(*query_cols)
-        early = (n - 1) // 2
+        out_4 = out_sum.step(*query_cols)
+        early = (n - 1) * 2 // 7
         dkv_early = [
             net.swap(b, "seq", r + 1) for r, b in enumerate(tie(dkv_sent[1 : early + 1], *query_cols))
         ]
         input_grad, attn_gain_part = input_gradient(
             nd, layer_input, gains, grad_hidden, query_cols, query_parts
         )
-        out_4 = out_sum.step(attn_gain_part, *dkv_early)
         dkv_more = [
             net.swap(b, "seq", early + 1 + r)
-            for r, b in enumerate(tie(dkv_sent[early + 1 :], *out_3, attn_gain_part))
+            for r, b in enumerate(tie(dkv_sent[early + 1 :], attn_gain_part))
         ]
         dkv_blocks = [dkv_sent[0], *dkv_early, *dkv_more]
         for rows in (slice(top), slice(top, units)):
@@ -1249,9 +1248,9 @@
             return shares[ring_order.index(key)]
 
         share_sum = RowSum(net, share_of)
-        shared = share_sum.step(*out_3, *dkv_early)
+        shared = share_sum.step(*out_4, *dkv_early)
         gate_grad = spread_columns(info, *tie(gate_total, *shared))
-        share_sum.step(*out_4, *dkv_more[: len(dkv_more) // 2])
+        share_sum.step(*dkv_more[: len(dkv_more) // 2])
         up_grad = spread_columns(info, *tie(up_total, *shared))
         for _ in range(half_way - 3):
             share_sum.step(gate_grad, *dkv_more)

time: 776 us -> 768 us (0.990)
    ppermute x24, waiting for transfers between devices: 39.2 us -> 29.8 us  [to_left(): return lax.ppermute(x, 'seq', self.left)]
    ppermute x68, waiting for transfers between devices: 101 us -> 109 us  [swap(): return lax.ppermute(x, axis, [(k, k ^ r) for k in range(count)])]
  transfers between devices with their start and end apart: 124 -> 124, of which waited for: 51 -> 56; matrix products, arithmetic and copies ran while one was open for 5% -> 5% of each run, Pallas kernels for 32% -> 32%
where the time goes in v4:
time: 768 us; the launch traced here: 758 us
  waiting for transfers between devices  276 us (36%)
  Pallas kernels  250 us (33%)
  starting transfers between devices  171 us (22%)
  other arithmetic  34 us (4%)
  local copies, waits for them, and re-layouts  23.8 us (3%)
    pallas_call x25, Pallas kernels, call(): pl.pallas_call(body, name=name, in_specs=specs, out_specs=tuple(out_specs...  250 us
    ppermute x24, waiting for transfers between devices, to_right(): return lax.ppermute(x, 'seq', self.right)  116 us
    ppermute x68, waiting for transfers between devices, swap(): return lax.ppermute(x, axis, [(k, k ^ r) for k in range(count)])  109 us
    ppermute x68, starting transfers between devices, swap(): return lax.ppermute(x, axis, [(k, k ^ r) for k in range(count)])  76.9 us
    ppermute x24, starting transfers between devices, to_left(): return lax.ppermute(x, 'seq', self.left)  41.4 us
    ppermute x24, waiting for transfers between devices, to_left(): return lax.ppermute(x, 'seq', self.left)  29.8 us
    ppermute x24, starting transfers between devices, to_right(): return lax.ppermute(x, 'seq', self.right)  29.1 us
    convert_element_type x21, other arithmetic, low(): return value.astype(jnp.bfloat16)  25.6 us
  transfers between devices with their start and end apart: 124, of which 56 were waited for; matrix products, arithmetic and copies ran while one was open for 5% of the time, Pallas kernels for 32%

profile of v4, /device:TPU:0, one launch (start us, length us, event | category | flops | bytes accessed | tf_op | source)
XLA Modules:
  0.0 758.2 jit_solution(16476078090530182490)
XLA Ops:
  2.5 3.0 collective-permute-start.1
  5.6 12.6 %collective-permute-done.1.refs_5_ = bf16[544,512]{1,0:T(8,128)(2,1)S(1)} collective-permute-done((bf16[544,512]{1,0:T(8,128)(2,1)S(1)}, bf16[544,512]{1,0:T(8,128)(2,1)S(1)}, u32[]{:S(2)}, u32[]{:S(2)}) %collective-permute-start.1) | collective-permute-done | bytes 557088 | tf_op jit(solution)/shard_map/ppermute | solution.py:85
  22.2 3.7 pack_keys_values.1
  30.7 9.0 %collective-permute-done.5.refs_9_ = bf16[256,512]{1,0:T(8,128)(2,1)S(1)} collective-permute-done((bf16[256,512]{1,0:T(8,128)(2,1)}, bf16[256,512]{1,0:T(8,128)(2,1)S(1)}, u32[]{:S(2)}, u32[]{:S(2)}) %collective-permute-start.5) | collective-permute-done | bytes 262176 | tf_op jit(solution)/shard_map/ppermute | solution.py:103
  45.0 15.4 %collective-permute-done.7.refs_9_ = bf16[544,512]{1,0:T(8,128)(2,1)S(1)} collective-permute-done((bf16[544,512]{1,0:T(8,128)(2,1)}, bf16[544,512]{1,0:T(8,128)(2,1)S(1)}, u32[]{:S(2)}, u32[]{:S(2)}) %collective-permute-start.7) | collective-permute-done | bytes 557088 | tf_op jit(solution)/shard_map/ppermute | solution.py:85
  60.5 4.2 collective-permute-done.9.refs_11_
  66.7 4.5 collective-permute-done.11.refs_11_
  80.9 11.4 %project_queries.1 = (bf16[256,256]{1,0:T(8,128)(2,1)}, bf16[256,256]{1,0:T(8,128)(2,1)}, bf16[256,256]{1,0:T(8,128)(2,1)}, bf16[256,256]{1,0:T(8,128)(2,1)}, bf...) custom-call(s32[11]{0:T(128)} %stack.54.info, ...), custom_call_target="tpu_custom_call" | custom-call | flops 536870912 | bytes 6291456 | tf_op jit(solution)/shard_map/project_queries/pallas_call | solution.py:180
  92.3 8.3 %collective-permute-done.15.refs_13_ = bf16[256,512]{1,0:T(8,128)(2,1)} collective-permute-done((bf16[256,512]{1,0:T(8,128)(2,1)}, bf16[256,512]{1,0:T(8,128)(2,1)}, u32[]{:S(2)}, u32[]{:S(2)}) %collective-permute-start.15) | collective-permute-done | bytes 262176 | tf_op jit(solution)/shard_map/ppermute | solution.py:103
  103.7 15.8 %collective-permute-start.20 = (bf16[256,256]{1,0:T(8,128)(2,1)}, bf16[256,256]{1,0:T(8,128)(2,1)S(1)}, u32[]{:S(2)}, u32[]{:S(2)}) collective-permute-start(bf16[256,256]{1,0:T(8,128)(2,1)} %get-tuple-element.382), channel_id=1, source_target_pairs={{0,16},{1,17},{2,0},{3,1},{4,24},{5,25},{6,8},{7,9},{8,20},{9,21},... | collective-permute-start | bytes 393224 | tf_op jit(solution)/shard_map/ppermute | solution.py:99
  124.5 13.0 %collective-permute-done.20.refs_2_ = bf16[256,256]{1,0:T(8,128)(2,1)S(1)} collective-permute-done((bf16[256,256]{1,0:T(8,128)(2,1)}, bf16[256,256]{1,0:T(8,128)(2,1)S(1)}, u32[]{:S(2)}, u32[]{:S(2)}) %collective-permute-start.20) | collective-permute-done | bytes 131104 | tf_op jit(solution)/shard_map/ppermute | solution.py:99
  137.7 8.0 %collective-permute-done.25.refs_7_ = bf16[256,256]{1,0:T(8,128)(2,1)S(1)} collective-permute-done((bf16[256,256]{1,0:T(8,128)(2,1)}, bf16[256,256]{1,0:T(8,128)(2,1)S(1)}, u32[]{:S(2)}, u32[]{:S(2)}) %collective-permute-start.25) | collective-permute-done | bytes 131104 | tf_op jit(solution)/shard_map/ppermute | solution.py:99
  152.6 17.4 %attention_forward.1 = (bf16[256,256]{1,0:T(8,128)(2,1)}, bf16[256,256]{1,0:T(8,128)(2,1)}, bf16[256,256]{1,0:T(8,128)(2,1)}, bf16[256,256]{1,0:T(8,128)(2,1)}, ...) custom-call(s32[3]{0:T(128)} %pad_add_fusion.info, ...), custom_call_target="tpu_custom_call" | custom-call | flops 4294967296 | bytes 1310720 | tf_op jit(solution)/shard_map/attention_forward/pallas_call | solution.py:180
  170.0 5.3 collective-permute-done.26.refs_2_.refs_10_
  184.6 4.2 collective-permute-done.30.refs_3_
  190.7 6.8 collective-permute-done.31.refs_4_
  202.4 3.9 collective-permute-start.41
  208.4 8.5 %project_mixed.1 = (f32[256,2048]{1,0:T(8,128)}, bf16[256,2048]{1,0:T(8,128)(2,1)}, bf16[256,2048]{1,0:T(8,128)(2,1)}) custom-call(s32[11]{0:T(128)} %stack.54.info, bf16[256,2048]{1,0:T(8,128)(2,1)} %x.3, f32[8,2048]{1,0:T(8,128)} %get-tuple-element.364.gains, bf16[256,256]{1,0:T(8,128)(2,1)} %get-tuple-element.397.refs_0_, bf16[256,256]{1,0:T(8,128)(2,1)} %copy-done.91, ...), custom_call_target="tpu_custom_call" | custom-call | flops 536870912 | bytes 6291456 | tf_op jit(solution)/shard_map/project_mixed/pallas_call | solution.py:180
  219.0 3.5 collective-permute-start.39
  222.5 10.4 %ffn_blocks.5 = (bf16[256,768]{1,0:T(8,128)(2,1)}, bf16[256,768]{1,0:T(8,128)(2,1)}, bf16[256,768]{1,0:T(8,128)(2,1)}, f32[256,2048]{1,0:T(8,128)}, f32[256,2048]{1,0:T(8,128)}) custom-call(bf16[256,2048]{1,0:T(8,128)(2,1)} %get-tuple-element.410.refs_0_.refs_9_, bf16[256,2048]{1,0:T(8,128)(2,1)} %cotangent.1, bf16[688,2048]{1,0:T(8,128)(2,1)} %refs_4_.9, ...), custom_call_target="tpu_custom_call" | custom-call | flops 1082130432 | bytes 3686400 | tf_op jit(solution)/shard_map/ffn_blocks/pallas_call | solution.py:180
  233.0 19.0 %collective-permute-done.38.refs_0_.refs_10_ = bf16[256,2048]{1,0:T(8,128)(2,1)S(1)} collective-permute-done((bf16[256,2048]{1,0:T(8,128)(2,1)}, bf16[256,2048]{1,0:T(8,128)(2,1)S(1)}, u32[]{:S(2)}, u32[]{:S(2)}) %collective-permute-start.38) | collective-permute-done | bytes 1048608 | tf_op jit(solution)/shard_map/ppermute | solution.py:85
  258.7 17.6 %ffn_blocks.6 = (bf16[256,768]{1,0:T(8,128)(2,1)}, bf16[256,768]{1,0:T(8,128)(2,1)}, bf16[256,768]{1,0:T(8,128)(2,1)}, f32[256,2048]{1,0:T(8,128)}, f32[256,2048...) custom-call(bf16[256,2048]{1,0:T(8,128)(2,1)} %copy-done.6, ...), custom_call_target="tpu_custom_call" | custom-call | flops 2164260864 | bytes 5259264 | tf_op jit(solution)/shard_map/ffn_blocks/pallas_call | solution.py:180
  276.3 3.1 collective-permute-done.42.refs_0_.refs_12_
  281.2 18.9 %collective-permute-done.44.refs_2_.refs_14_ = bf16[256,2048]{1,0:T(8,128)(2,1)S(1)} collective-permute-done((bf16[256,2048]{1,0:T(8,128)(2,1)}, bf16[256,2048]{1,0:T(8,128)(2,1)S(1)}, u32[]{:S(2)}, u32[]{:S(2)}) %collective-permute-start.44) | collective-permute-done | bytes 1048608 | tf_op jit(solution)/shard_map/ppermute | solution.py:85
  306.7 17.6 %ffn_blocks.7 = (bf16[256,768]{1,0:T(8,128)(2,1)}, bf16[256,768]{1,0:T(8,128)(2,1)}, bf16[256,768]{1,0:T(8,128)(2,1)}, f32[256,2048]{1,0:T(8,128)}, f32[256,2048...) custom-call(bf16[256,2048]{1,0:T(8,128)(2,1)} %copy-done.8, ...), custom_call_target="tpu_custom_call" | custom-call | flops 2164260864 | bytes 5259264 | tf_op jit(solution)/shard_map/ffn_blocks/pallas_call | solution.py:180
  324.4 3.0 collective-permute-done.46.refs_0_.refs_14_
  327.9 7.8 %collective-permute-done.48.refs_2_.refs_16_ = bf16[128,2048]{1,0:T(8,128)(2,1)S(1)} collective-permute-done((bf16[128,2048]{1,0:T(8,128)(2,1)S(1)}, bf16[128,2048]{1,0:T(8,128)(2,1)S(1)}, u32[]{:S(2)}, u32[]{:S(2)}) %collective-permute-start.48) | collective-permute-done | bytes 524320 | tf_op jit(solution)/shard_map/ppermute | solution.py:85
  338.2 17.7 %ffn_blocks.8 = (bf16[256,768]{1,0:T(8,128)(2,1)}, bf16[256,768]{1,0:T(8,128)(2,1)}, bf16[256,768]{1,0:T(8,128)(2,1)}, f32[256,2048]{1,0:T(8,128)}, f32[256,2048...) custom-call(bf16[256,2048]{1,0:T(8,128)(2,1)} %copy-done, ...), custom_call_target="tpu_custom_call" | custom-call | flops 2164260864 | bytes 5259264 | tf_op jit(solution)/shard_map/ffn_blocks/pallas_call | solution.py:180
  356.9 10.6 %ffn_blocks.9 = (bf16[128,768]{1,0:T(8,128)(2,1)}, bf16[128,768]{1,0:T(8,128)(2,1)}, bf16[128,768]{1,0:T(8,128)(2,1)}, f32[128,2048]{1,0:T(8,128)}, f32[128,2048...) custom-call(bf16[128,2048]{1,0:T(8,128)(2,1)} %copy-done.18, ...), custom_call_target="tpu_custom_call" | custom-call | flops 1082130432 | bytes 3686400 | tf_op jit(solution)/shard_map/ffn_blocks/pallas_call | solution.py:180
  372.7 11.3 %collective-permute-done.53 = bf16[128,2048]{1,0:T(8,128)(2,1)S(1)} collective-permute-done((bf16[128,2048]{1,0:T(8,128)(2,1)S(1)}, bf16[128,2048]{1,0:T(8,128)(2,1)S(1)}, u32[]{:S(2)}, u32[]{:S(2)}) %collective-permute-start.53) | collective-permute-done | bytes 524320 | tf_op jit(solution)/shard_map/ppermute | solution.py:88
  389.7 15.2 %weight_gradient.3 = (bf16[688,1024]{1,0:T(8,128)(2,1)}, bf16[688,1024]{1,0:T(8,128)(2,1)}) custom-call(s32[11]{0:T(128)} %stack.54.info, bf16[256,768]{1,0:T(8,128)(2,1)} %get-tuple-element.466.refs_0_, bf16[256,768]{1,0:T(8,128)(2,1)} %get-tuple-element.467.refs_1_, bf16[256,768]{1,0:T(8,128)(2,1)} %get-tuple-element.468.refs_2_, ...), custom_call_target="tpu_custom_call" | custom-call | flops 1442840576 | bytes 2097152 | tf_op jit(solution)/shard_map/weight_gradient/pallas_call | solution.py:180
  405.0 5.1 collective-permute-done.57
  423.3 15.1 %weight_gradient.4 = (bf16[688,1024]{1,0:T(8,128)(2,1)}, bf16[688,1024]{1,0:T(8,128)(2,1)}) custom-call(s32[11]{0:T(128)} %stack.54.info, bf16[256,768]{1,0:T(8,128)(2,1)} %get-tuple-element.490.refs_0_, bf16[256,768]{1,0:T(8,128)(2,1)} %get-tuple-element.491.refs_1_, bf16[256,768]{1,0:T(8,128)(2,1)} %get-tuple-element.492.refs_2_, ...), custom_call_target="tpu_custom_call" | custom-call | flops 1442840576 | bytes 2097152 | tf_op jit(solution)/shard_map/weight_gradient/pallas_call | solution.py:180
  448.4 3.7 collective-permute-done.60
  457.7 15.0 %weight_gradient.5 = (bf16[688,1024]{1,0:T(8,128)(2,1)}, bf16[688,1024]{1,0:T(8,128)(2,1)}) custom-call(s32[11]{0:T(128)} %stack.54.info, bf16[256,768]{1,0:T(8,128)(2,1)} %get-tuple-element.514.refs_0_, bf16[256,768]{1,0:T(8,128)(2,1)} %get-tuple-element.515.refs_1_, bf16[256,768]{1,0:T(8,128)(2,1)} %get-tuple-element.516.refs_2_, ...), custom_call_target="tpu_custom_call" | custom-call | flops 1442840576 | bytes 2097152 | tf_op jit(solution)/shard_map/weight_gradient/pallas_call | solution.py:180
  479.5 10.5 %branch_gradient.1 = (bf16[256,256]{1,0:T(8,128)(2,1)}, bf16[256,256]{1,0:T(8,128)(2,1)}, bf16[256,256]{1,0:T(8,128)(2,1)}, bf16[256,256]{1,0:T(8,128)(2,1)}, bf...) custom-call(s32[11]{0:T(128)} %stack.54.info, ...), custom_call_target="tpu_custom_call" | custom-call | flops 536870912 | bytes 6291456 | tf_op jit(solution)/shard_map/branch_gradient/pallas_call | solution.py:180
  492.2 7.1 collective-permute-done.81.refs_1_
  507.5 3.6 collective-permute-done.76.refs_19_
  513.2 7.7 %collective-permute-done.77.refs_20_ = bf16[256,256]{1,0:T(8,128)(2,1)S(1)} collective-permute-done((bf16[256,256]{1,0:T(8,128)(2,1)}, bf16[256,256]{1,0:T(8,128)(2,1)S(1)}, u32[]{:S(2)}, u32[]{:S(2)}) %collective-permute-start.77) | collective-permute-done | bytes 131104 | tf_op jit(solution)/shard_map/ppermute | solution.py:103
  525.1 4.4 collective-permute-done.80.refs_23_
  536.6 22.0 %attention_backward.1 = (bf16[256,256]{1,0:T(8,128)(2,1)}, bf16[256,256]{1,0:T(8,128)(2,1)}, bf16[256,256]{1,0:T(8,128)(2,1)}, bf16[256,256]{1,0:T(8,128)(2,1)},...) custom-call(s32[3]{0:T(128)} %pad_add_fusion.info, ...), custom_call_target="tpu_custom_call" | custom-call | flops 10737418240 | bytes 2621440 | tf_op jit(solution)/shard_map/attention_backward/pallas_call | solution.py:180
  572.9 3.7 collective-permute-done.91.refs_5_
  578.7 3.0 sort_columns.1
  587.7 7.2 collective-permute-done.104.refs_5_
  594.9 10.4 %input_gradient.1 = (bf16[256,2048]{1,0:T(8,128)(2,1)}, f32[8,2048]{1,0:T(8,128)}) custom-call(bf16[256,2048]{1,0:T(8,128)(2,1)} %x.3, f32[8,2048]{1,0:T(8,128)} %get-tuple-element.364.gains, f32[256,2048]{1,0:T(8,128)} %get-tuple-element.601.grad_hidden, bf16[256,512]{1,0:T(8,128)(2,1)} %get-tuple-element.595.refs_0_, ...), custom_call_target="tpu_custom_call" | custom-call | flops 536870912 | bytes 6291456 | tf_op jit(solution)/shard_map/input_gradient/pallas_call | solution.py:180
  608.4 12.2 %projection_gradients.1 = (f32[544,512]{1,0:T(8,128)}, f32[544,512]{1,0:T(8,128)}, f32[544,512]{1,0:T(8,128)}, f32[544,512]{1,0:T(8,128)}, f32[544,512]{1,0:T(8,...) custom-call(s32[11]{0:T(128)} %stack.54.info, bf16[1024,2048]{1,0:T(8,128)(2,1)} %get-tuple-element.621.normed, ...), custom_call_target="tpu_custom_call" | custom-call | flops 1073741824 | bytes 2097152 | tf_op jit(solution)/shard_map/projection_gradients/pallas_call | solution.py:180
  622.8 3.3 chip_sum.3.mine
  628.6 3.1 chip_sum.4.mine
  633.4 7.8 %collective-permute-done.108 = bf16[272,512]{1,0:T(8,128)(2,1)S(1)} collective-permute-done((bf16[272,512]{1,0:T(8,128)(2,1)S(1)}, bf16[272,512]{1,0:T(8,128)(2,1)S(1)}, u32[]{:S(2)}, u32[]{:S(2)}) %collective-permute-start.108) | collective-permute-done | bytes 278560 | tf_op jit(solution)/shard_map/ppermute | solution.py:85
  643.0 4.3 collective-permute-start.109
  649.9 3.1 collective-permute-start.101
  654.1 4.6 spread_columns.3
  664.3 8.7 %collective-permute-done.101.refs_5_ = bf16[256,512]{1,0:T(8,128)(2,1)S(1)} collective-permute-done((bf16[256,512]{1,0:T(8,128)(2,1)}, bf16[256,512]{1,0:T(8,128)(2,1)S(1)}, u32[]{:S(2)}, u32[]{:S(2)}) %collective-permute-start.101) | collective-permute-done | bytes 262176 | tf_op jit(solution)/shard_map/ppermute | solution.py:103
  673.0 4.0 collective-permute-start.102
  679.9 4.4 collective-permute-done.102.refs_6_
  684.3 4.4 collective-permute-done.103.refs_7_
  688.8 8.7 %collective-permute-start.112 = (bf16[544,512]{1,0:T(8,128)(2,1)S(1)}, bf16[544,512]{1,0:T(8,128)(2,1)S(1)}, u32[]{:S(2)}, u32[]{:S(2)}) collective-permute-start(bf16[544,512]{1,0:T(8,128)(2,1)S(1)} %add_convert_fusion.16), channel_id=1, source_target_pairs={{3,1},{5,3},{7,5},{6,7},{4,6},{2,4},{0,2},{1,0},{11,9},{13,11},{15... | collective-permute-start | bytes 1671176 | tf_op jit(solution)/shard_map/ppermute | solution.py:88
  698.4 3.1 chip_sum.5.mine
  702.8 4.6 spread_columns.4
  707.6 9.2 %collective-permute-done.113 = bf16[544,512]{1,0:T(8,128)(2,1)} collective-permute-done((bf16[544,512]{1,0:T(8,128)(2,1)S(1)}, bf16[544,512]{1,0:T(8,128)(2,1)}, u32[]{:S(2)}, u32[]{:S(2)}) %collective-permute-start.113) | collective-permute-done | bytes 557088 | tf_op jit(solution)/shard_map/ppermute | solution.py:85
  720.9 3.7 split_keys_values.1
  725.8 4.8 spread_columns.5
  736.2 12.9 %collective-permute-done.121.refs_1_ = bf16[544,512]{1,0:T(8,128)(2,1)S(1)} collective-permute-done((bf16[544,512]{1,0:T(8,128)(2,1)S(1)}, bf16[544,512]{1,0:T(8,128)(2,1)S(1)}, u32[]{:S(2)}, u32[]{:S(2)}) %collective-permute-start.121) | collective-permute-done | bytes 557088 | tf_op jit(solution)/shard_map/ppermute | solution.py:103
  752.9 3.8 join_projections.1
  (528 shorter events, 214.7 us)
Async XLA Ops:
  19.6 20.1 %collective-permute-start.3 = (bf16[544,512]{1,0:T(8,128)(2,1)S(1)}, bf16[544,512]{1,0:T(8,128)(2,1)}, u32[]{:S(2)}, u32[]{:S(2)}) collective-permute-start(bf16[544,512]{1,0:T(8,128)(2,1)S(1)} %collective-permute-done.1.refs_5_), channel_id=1, source_target_pairs={{1,3},{3,5},{5,7},{7,6},{6,4},{4,2},{2,0},{0,1},{9,11},{11,13},{13... | collective-permute-start | bytes 1671176 | tf_op jit(solution)/shard_map/ppermute | solution.py:85
  29.2 37.5 %collective-permute-start = (bf16[256,2048]{1,0:T(8,128)(2,1)S(1)}, bf16[256,2048]{1,0:T(8,128)(2,1)S(1)}, u32[]{:S(2)}, u32[]{:S(2)}) collective-permute-start(bf16[256,2048]{1,0:T(8,128)(2,1)S(1)} %copy-done.10), channel_id=1, source_target_pairs={{0,16},{8,24},{16,0},{24,8},{1,17},{9,25},{17,1},{25,9},{2,18},{10... | collective-permute-start | bytes 3145736 | tf_op jit(solution)/shard_map/ppermute | solution.py:103
  39.7 20.7 %collective-permute-start.7 = (bf16[544,512]{1,0:T(8,128)(2,1)}, bf16[544,512]{1,0:T(8,128)(2,1)S(1)}, u32[]{:S(2)}, u32[]{:S(2)}) collective-permute-start(bf16[544,512]{1,0:T(8,128)(2,1)} %collective-permute-done.3.refs_7_), channel_id=1, source_target_pairs={{1,3},{3,5},{5,7},{7,6},{6,4},{4,2},{2,0},{0,1},{9,11},{11,13},{13... | collective-permute-start | bytes 1671176 | tf_op jit(solution)/shard_map/ppermute | solution.py:85
  41.3 19.1 %collective-permute-start.8 = (bf16[544,512]{1,0:T(8,128)(2,1)}, bf16[544,512]{1,0:T(8,128)(2,1)S(1)}, u32[]{:S(2)}, u32[]{:S(2)}) collective-permute-start(bf16[544,512]{1,0:T(8,128)(2,1)} %collective-permute-done.4.refs_8_), channel_id=1, source_target_pairs={{3,1},{5,3},{7,5},{6,7},{4,6},{2,4},{0,2},{1,0},{11,9},{13,11},{15... | collective-permute-start | bytes 1671176 | tf_op jit(solution)/shard_map/ppermute | solution.py:88
  41.8 22.8 %collective-permute-start.9 = (bf16[256,512]{1,0:T(8,128)(2,1)}, bf16[256,512]{1,0:T(8,128)(2,1)S(1)}, u32[]{:S(2)}, u32[]{:S(2)}) collective-permute-start(bf16[256,512]{1,0:T(8,128)(2,1)} %get-tuple-element.358), channel_id=1, source_target_pairs={{0,3},{1,2},{2,1},{3,0},{4,7},{5,6},{6,5},{7,4},{8,11},{9,10},{10,... | collective-permute-start | bytes 786440 | tf_op jit(solution)/shard_map/ppermute | solution.py:103
  43.1 21.5 %collective-permute-start.10 = (bf16[256,512]{1,0:T(8,128)(2,1)}, bf16[256,512]{1,0:T(8,128)(2,1)S(1)}, u32[]{:S(2)}, u32[]{:S(2)}) collective-permute-start(bf16[256,512]{1,0:T(8,128)(2,1)} %get-tuple-element.359), channel_id=1, source_target_pairs={{0,4},{1,5},{2,6},{3,7},{4,0},{5,1},{6,2},{7,3},{8,12},{9,13},{10,... | collective-permute-start | bytes 786440 | tf_op jit(solution)/shard_map/ppermute | solution.py:103
  73.3 27.3 %collective-permute-start.15 = (bf16[256,512]{1,0:T(8,128)(2,1)}, bf16[256,512]{1,0:T(8,128)(2,1)}, u32[]{:S(2)}, u32[]{:S(2)}) collective-permute-start(bf16[256,512]{1,0:T(8,128)(2,1)} %get-tuple-element.377), channel_id=1, source_target_pairs={{0,5},{1,4},{2,7},{3,6},{4,1},{5,0},{6,3},{7,2},{8,13},{9,12},{10,... | collective-permute-start | bytes 786440 | tf_op jit(solution)/shard_map/ppermute | solution.py:103
  74.7 25.8 %collective-permute-start.16 = (bf16[256,512]{1,0:T(8,128)(2,1)}, bf16[256,512]{1,0:T(8,128)(2,1)}, u32[]{:S(2)}, u32[]{:S(2)}) collective-permute-start(bf16[256,512]{1,0:T(8,128)(2,1)} %get-tuple-element.378), channel_id=1, source_target_pairs={{0,6},{1,7},{2,4},{3,5},{4,2},{5,3},{6,0},{7,1},{8,14},{9,15},{10,... | collective-permute-start | bytes 786440 | tf_op jit(solution)/shard_map/ppermute | solution.py:103
  77.2 23.4 %collective-permute-start.17 = (bf16[256,512]{1,0:T(8,128)(2,1)}, bf16[256,512]{1,0:T(8,128)(2,1)}, u32[]{:S(2)}, u32[]{:S(2)}) collective-permute-start(bf16[256,512]{1,0:T(8,128)(2,1)} %get-tuple-element.379), channel_id=1, source_target_pairs={{0,7},{1,6},{2,5},{3,4},{4,3},{5,2},{6,1},{7,0},{8,15},{9,14},{10,... | collective-permute-start | bytes 786440 | tf_op jit(solution)/shard_map/ppermute | solution.py:103
  100.6 21.5 %collective-permute-start.18 = (bf16[256,256]{1,0:T(8,128)(2,1)}, bf16[256,256]{1,0:T(8,128)(2,1)S(1)}, u32[]{:S(2)}, u32[]{:S(2)}) collective-permute-start(bf16[256,256]{1,0:T(8,128)(2,1)} %get-tuple-element.380), channel_id=1, source_target_pairs={{0,0},{1,1},{2,16},{3,17},{4,8},{5,9},{6,24},{7,25},{8,4},{9,5},{1... | collective-permute-start | bytes 393224 | tf_op jit(solution)/shard_map/ppermute | solution.py:99
  102.1 20.7 %collective-permute-start.19 = (bf16[256,256]{1,0:T(8,128)(2,1)}, bf16[256,256]{1,0:T(8,128)(2,1)S(1)}, u32[]{:S(2)}, u32[]{:S(2)}) collective-permute-start(bf16[256,256]{1,0:T(8,128)(2,1)} %get-tuple-element.381), channel_id=1, source_target_pairs={{0,1},{1,0},{2,17},{3,16},{4,9},{5,8},{6,25},{7,24},{8,5},{9,4},{1... | collective-permute-start | bytes 393224 | tf_op jit(solution)/shard_map/ppermute | solution.py:99
  103.7 33.8 %collective-permute-start.20 = (bf16[256,256]{1,0:T(8,128)(2,1)}, bf16[256,256]{1,0:T(8,128)(2,1)S(1)}, u32[]{:S(2)}, u32[]{:S(2)}) collective-permute-start(bf16[256,256]{1,0:T(8,128)(2,1)} %get-tuple-element.382), channel_id=1, source_target_pairs={{0,16},{1,17},{2,0},{3,1},{4,24},{5,25},{6,8},{7,9},{8,20},{9,21},... | collective-permute-start | bytes 393224 | tf_op jit(solution)/shard_map/ppermute | solution.py:99
  146.3 53.4 %collective-permute-start.35 = (bf16[2048,512]{1,0:T(8,128)(2,1)}, bf16[2048,512]{1,0:T(8,128)(2,1)S(1)}, u32[]{:S(2)}, u32[]{:S(2)}) collective-permute-start(bf16[2048,512]{1,0:T(8,128)(2,1)} %get-tuple-element.407.refs_8_.refs_0_), channel_id=1, source_target_pairs={{0,16},{8,24},{16,0},{24,8},{1,17},{9,25},{17,1},{25,9},{2,18},{10... | collective-permute-start | bytes 6291464 | tf_op jit(solution)/shard_map/ppermute | solution.py:103
  149.3 26.0 %collective-permute-start.26 = (bf16[256,2048]{1,0:T(8,128)(2,1)S(1)}, bf16[256,2048]{1,0:T(8,128)(2,1)}, u32[]{:S(2)}, u32[]{:S(2)}) collective-permute-start(bf16[256,2048]{1,0:T(8,128)(2,1)S(1)} %copy-done.5), channel_id=1, source_target_pairs={{1,3},{3,5},{5,7},{7,6},{6,4},{4,2},{2,0},{0,1},{9,11},{11,13},{13... | collective-permute-start | bytes 3145736 | tf_op jit(solution)/shard_map/ppermute | solution.py:85
  149.3 26.0 %collective-permute-start.27 = (bf16[256,2048]{1,0:T(8,128)(2,1)S(1)}, bf16[256,2048]{1,0:T(8,128)(2,1)}, u32[]{:S(2)}, u32[]{:S(2)}) collective-permute-start(bf16[256,2048]{1,0:T(8,128)(2,1)S(1)} %copy-done.5), channel_id=1, source_target_pairs={{3,1},{5,3},{7,5},{6,7},{4,6},{2,4},{0,2},{1,0},{11,9},{13,11},{15... | collective-permute-start | bytes 3145736 | tf_op jit(solution)/shard_map/ppermute | solution.py:88
  178.8 18.7 %collective-permute-start.31 = (bf16[256,256]{1,0:T(8,128)(2,1)}, bf16[256,256]{1,0:T(8,128)(2,1)S(1)}, u32[]{:S(2)}, u32[]{:S(2)}) collective-permute-start(bf16[256,256]{1,0:T(8,128)(2,1)} %get-tuple-element.401), channel_id=1, source_target_pairs={{0,4},{1,5},{2,6},{3,7},{4,0},{5,1},{6,2},{7,3},{8,12},{9,13},{10,... | collective-permute-start | bytes 393224 | tf_op jit(solution)/shard_map/ppermute | solution.py:103
  181.1 18.6 %collective-permute-start.32 = (bf16[256,256]{1,0:T(8,128)(2,1)}, bf16[256,256]{1,0:T(8,128)(2,1)S(1)}, u32[]{:S(2)}, u32[]{:S(2)}) collective-permute-start(bf16[256,256]{1,0:T(8,128)(2,1)} %get-tuple-element.402), channel_id=1, source_target_pairs={{0,5},{1,4},{2,7},{3,6},{4,1},{5,0},{6,3},{7,2},{8,13},{9,12},{10,... | collective-permute-start | bytes 393224 | tf_op jit(solution)/shard_map/ppermute | solution.py:103
  200.3 32.6 %collective-permute-start.40 = (bf16[256,2048]{1,0:T(8,128)(2,1)}, bf16[256,2048]{1,0:T(8,128)(2,1)}, u32[]{:S(2)}, u32[]{:S(2)}) collective-permute-start(bf16[256,2048]{1,0:T(8,128)(2,1)} %collective-permute-done.26.refs_2_.refs_10_), channel_id=1, source_target_pairs={{1,3},{3,5},{5,7},{7,6},{6,4},{4,2},{2,0},{0,1},{9,11},{11,13},{13... | collective-permute-start | bytes 3145736 | tf_op jit(solution)/shard_map/ppermute | solution.py:85
  202.4 30.5 %collective-permute-start.41 = (bf16[256,2048]{1,0:T(8,128)(2,1)}, bf16[256,2048]{1,0:T(8,128)(2,1)S(1)}, u32[]{:S(2)}, u32[]{:S(2)}) collective-permute-start(bf16[256,2048]{1,0:T(8,128)(2,1)} %collective-permute-done.27.refs_3_.refs_11_), channel_id=1, source_target_pairs={{3,1},{5,3},{7,5},{6,7},{4,6},{2,4},{0,2},{1,0},{11,9},{13,11},{15... | collective-permute-start | bytes 3145736 | tf_op jit(solution)/shard_map/ppermute | solution.py:88
  216.9 35.0 %collective-permute-start.38 = (bf16[256,2048]{1,0:T(8,128)(2,1)}, bf16[256,2048]{1,0:T(8,128)(2,1)S(1)}, u32[]{:S(2)}, u32[]{:S(2)}) collective-permute-start(bf16[256,2048]{1,0:T(8,128)(2,1)} %get-tuple-element.410.refs_0_.refs_9_), channel_id=1, source_target_pairs={{1,3},{3,5},{5,7},{7,6},{6,4},{4,2},{2,0},{0,1},{9,11},{11,13},{13... | collective-permute-start | bytes 3145736 | tf_op jit(solution)/shard_map/ppermute | solution.py:85
  219.0 34.2 %collective-permute-start.39 = (bf16[256,2048]{1,0:T(8,128)(2,1)}, bf16[256,2048]{1,0:T(8,128)(2,1)S(1)}, u32[]{:S(2)}, u32[]{:S(2)}) collective-permute-start(bf16[256,2048]{1,0:T(8,128)(2,1)} %get-tuple-element.410.refs_0_.refs_9_), channel_id=1, source_target_pairs={{3,1},{5,3},{7,5},{6,7},{4,6},{2,4},{0,2},{1,0},{11,9},{13,11},{15... | collective-permute-start | bytes 3145736 | tf_op jit(solution)/shard_map/ppermute | solution.py:88
  253.3 26.1 %collective-permute-start.42 = (bf16[256,2048]{1,0:T(8,128)(2,1)S(1)}, bf16[256,2048]{1,0:T(8,128)(2,1)S(1)}, u32[]{:S(2)}, u32[]{:S(2)}) collective-permute-start(bf16[256,2048]{1,0:T(8,128)(2,1)S(1)} %collective-permute-done.38.refs_0_.refs_10_), channel_id=1, source_target_pairs={{1,3},{3,5},{5,7},{7,6},{6,4},{4,2},{2,0},{0,1},{9,11},{11,13},{13... | collective-permute-start | bytes 3145736 | tf_op jit(solution)/shard_map/ppermute | solution.py:85
  255.1 26.1 %collective-permute-start.43 = (bf16[256,2048]{1,0:T(8,128)(2,1)S(1)}, bf16[256,2048]{1,0:T(8,128)(2,1)S(1)}, u32[]{:S(2)}, u32[]{:S(2)}) collective-permute-start(bf16[256,2048]{1,0:T(8,128)(2,1)S(1)} %collective-permute-done.39.refs_1_.refs_11_), channel_id=1, source_target_pairs={{3,1},{5,3},{7,5},{6,7},{4,6},{2,4},{0,2},{1,0},{11,9},{13,11},{15... | collective-permute-start | bytes 3145736 | tf_op jit(solution)/shard_map/ppermute | solution.py:88
  255.3 44.7 %collective-permute-start.44 = (bf16[256,2048]{1,0:T(8,128)(2,1)}, bf16[256,2048]{1,0:T(8,128)(2,1)S(1)}, u32[]{:S(2)}, u32[]{:S(2)}) collective-permute-start(bf16[256,2048]{1,0:T(8,128)(2,1)} %collective-permute-done.40.refs_2_.refs_12_), channel_id=1, source_target_pairs={{1,3},{3,5},{5,7},{7,6},{6,4},{4,2},{2,0},{0,1},{9,11},{11,13},{13... | collective-permute-start | bytes 3145736 | tf_op jit(solution)/shard_map/ppermute | solution.py:85
  257.1 44.2 %collective-permute-start.45 = (bf16[256,2048]{1,0:T(8,128)(2,1)}, bf16[256,2048]{1,0:T(8,128)(2,1)}, u32[]{:S(2)}, u32[]{:S(2)}) collective-permute-start(bf16[256,2048]{1,0:T(8,128)(2,1)} %copy-done.20), channel_id=1, source_target_pairs={{3,1},{5,3},{7,5},{6,7},{4,6},{2,4},{0,2},{1,0},{11,9},{13,11},{15... | collective-permute-start | bytes 3145736 | tf_op jit(solution)/shard_map/ppermute | solution.py:88
  257.5 70.4 %collective-permute-start.50 = (bf16[2048,512]{1,0:T(8,128)(2,1)}, bf16[2048,512]{1,0:T(8,128)(2,1)}, u32[]{:S(2)}, u32[]{:S(2)}) collective-permute-start(bf16[2048,512]{1,0:T(8,128)(2,1)} %get-tuple-element.450.refs_4_), channel_id=1, source_target_pairs={{0,16},{8,24},{16,0},{24,8},{1,17},{9,25},{17,1},{25,9},{2,18},{10... | collective-permute-start | bytes 6291464 | tf_op jit(solution)/shard_map/ppermute | solution.py:103
  301.3 26.1 %collective-permute-start.46 = (bf16[256,2048]{1,0:T(8,128)(2,1)S(1)}, bf16[256,2048]{1,0:T(8,128)(2,1)S(1)}, u32[]{:S(2)}, u32[]{:S(2)}) collective-permute-start(bf16[256,2048]{1,0:T(8,128)(2,1)S(1)} %collective-permute-done.42.refs_0_.refs_12_), channel_id=1, source_target_pairs={{1,3},{3,5},{5,7},{7,6},{6,4},{4,2},{2,0},{0,1},{9,11},{11,13},{13... | collective-permute-start | bytes 3145736 | tf_op jit(solution)/shard_map/ppermute | solution.py:85
  301.8 26.1 %collective-permute-start.47 = (bf16[256,2048]{1,0:T(8,128)(2,1)S(1)}, bf16[256,2048]{1,0:T(8,128)(2,1)S(1)}, u32[]{:S(2)}, u32[]{:S(2)}) collective-permute-start(bf16[256,2048]{1,0:T(8,128)(2,1)S(1)} %collective-permute-done.43.refs_1_.refs_13_), channel_id=1, source_target_pairs={{3,1},{5,3},{7,5},{6,7},{4,6},{2,4},{0,2},{1,0},{11,9},{13,11},{15... | collective-permute-start | bytes 3145736 | tf_op jit(solution)/shard_map/ppermute | solution.py:88
  304.5 31.3 %collective-permute-start.48 = (bf16[128,2048]{1,0:T(8,128)(2,1)S(1)}, bf16[128,2048]{1,0:T(8,128)(2,1)S(1)}, u32[]{:S(2)}, u32[]{:S(2)}) collective-permute-start(bf16[128,2048]{1,0:T(8,128)(2,1)S(1)} %slice.139), channel_id=1, source_target_pairs={{1,3},{3,5},{5,7},{7,6},{6,4},{4,2},{2,0},{0,1},{9,11},{11,13},{13... | collective-permute-start | bytes 1572872 | tf_op jit(solution)/shard_map/ppermute | solution.py:85
  305.0 30.8 %collective-permute-start.49 = (bf16[128,2048]{1,0:T(8,128)(2,1)S(1)}, bf16[128,2048]{1,0:T(8,128)(2,1)S(1)}, u32[]{:S(2)}, u32[]{:S(2)}) collective-permute-start(bf16[128,2048]{1,0:T(8,128)(2,1)S(1)} %slice.140), channel_id=1, source_target_pairs={{3,1},{5,3},{7,5},{6,7},{4,6},{2,4},{0,2},{1,0},{11,9},{13,11},{15... | collective-permute-start | bytes 1572872 | tf_op jit(solution)/shard_map/ppermute | solution.py:88
  335.8 20.2 %collective-permute-start.51 = (bf16[128,2048]{1,0:T(8,128)(2,1)S(1)}, bf16[128,2048]{1,0:T(8,128)(2,1)S(1)}, u32[]{:S(2)}, u32[]{:S(2)}) collective-permute-start(bf16[128,2048]{1,0:T(8,128)(2,1)S(1)} %slice.137), channel_id=1, source_target_pairs={{1,3},{3,5},{5,7},{7,6},{6,4},{4,2},{2,0},{0,1},{9,11},{11,13},{13... | collective-permute-start | bytes 1572872 | tf_op jit(solution)/shard_map/ppermute | solution.py:85
  336.4 19.5 %collective-permute-start.52 = (bf16[128,2048]{1,0:T(8,128)(2,1)S(1)}, bf16[128,2048]{1,0:T(8,128)(2,1)S(1)}, u32[]{:S(2)}, u32[]{:S(2)}) collective-permute-start(bf16[128,2048]{1,0:T(8,128)(2,1)S(1)} %slice.138), channel_id=1, source_target_pairs={{3,1},{5,3},{7,5},{6,7},{4,6},{2,4},{0,2},{1,0},{11,9},{13,11},{15... | collective-permute-start | bytes 1572872 | tf_op jit(solution)/shard_map/ppermute | solution.py:88
  356.0 30.5 %collective-permute-start.55 = (bf16[2048,512]{1,0:T(8,128)(2,1)}, bf16[2048,512]{1,0:T(8,128)(2,1)S(1)}, u32[]{:S(2)}, u32[]{:S(2)}) collective-permute-start(bf16[2048,512]{1,0:T(8,128)(2,1)} %get-tuple-element.450.refs_4_), channel_id=1, source_target_pairs={{0,8},{8,0},{16,24},{24,16},{1,9},{9,1},{17,25},{25,17},{2,10},{10... | collective-permute-start | bytes 6291464 | tf_op jit(solution)/shard_map/ppermute | solution.py:103
  356.0 30.4 %collective-permute-start.56 = (bf16[2048,512]{1,0:T(8,128)(2,1)}, bf16[2048,512]{1,0:T(8,128)(2,1)S(1)}, u32[]{:S(2)}, u32[]{:S(2)}) collective-permute-start(bf16[2048,512]{1,0:T(8,128)(2,1)} %collective-permute-done.50.refs_5_), channel_id=1, source_target_pairs={{0,8},{8,0},{16,24},{24,16},{1,9},{9,1},{17,25},{25,17},{2,10},{10... | collective-permute-start | bytes 6291464 | tf_op jit(solution)/shard_map/ppermute | solution.py:103
  386.5 23.6 %collective-permute-start.57 = (bf16[256,2048]{1,0:T(8,128)(2,1)S(1)}, bf16[256,2048]{1,0:T(8,128)(2,1)S(1)}, u32[]{:S(2)}, u32[]{:S(2)}) collective-permute-start(bf16[256,2048]{1,0:T(8,128)(2,1)S(1)} %pad_maximum_fusion), channel_id=1, source_target_pairs={{3,1},{5,3},{7,5},{6,7},{4,6},{2,4},{0,2},{1,0},{11,9},{13,11},{15... | collective-permute-start | bytes 3145736 | tf_op jit(solution)/shard_map/ppermute | solution.py:88
  387.4 24.0 %collective-permute-start.58 = (bf16[256,2048]{1,0:T(8,128)(2,1)}, bf16[256,2048]{1,0:T(8,128)(2,1)}, u32[]{:S(2)}, u32[]{:S(2)}) collective-permute-start(bf16[256,2048]{1,0:T(8,128)(2,1)} %pad_maximum_fusion.1), channel_id=1, source_target_pairs={{1,3},{3,5},{5,7},{7,6},{6,4},{4,2},{2,0},{0,1},{9,11},{11,13},{13... | collective-permute-start | bytes 3145736 | tf_op jit(solution)/shard_map/ppermute | solution.py:85
  388.6 25.5 %collective-permute-start.61 = (bf16[256,2048]{1,0:T(8,128)(2,1)}, bf16[256,2048]{1,0:T(8,128)(2,1)}, u32[]{:S(2)}, u32[]{:S(2)}) collective-permute-start(bf16[256,2048]{1,0:T(8,128)(2,1)} %get-tuple-element.500.refs_8_), channel_id=1, source_target_pairs={{0,16},{8,24},{16,0},{24,8},{1,17},{9,25},{17,1},{25,9},{2,18},{10... | collective-permute-start | bytes 3145736 | tf_op jit(solution)/shard_map/ppermute | solution.py:103
  414.1 26.5 %collective-permute-start.62 = (bf16[256,2048]{1,0:T(8,128)(2,1)}, bf16[256,2048]{1,0:T(8,128)(2,1)}, u32[]{:S(2)}, u32[]{:S(2)}) collective-permute-start(bf16[256,2048]{1,0:T(8,128)(2,1)} %add_convert_fusion.11), channel_id=1, source_target_pairs={{3,1},{5,3},{7,5},{6,7},{4,6},{2,4},{0,2},{1,0},{11,9},{13,11},{15... | collective-permute-start | bytes 3145736 | tf_op jit(solution)/shard_map/ppermute | solution.py:88
  418.1 26.3 %collective-permute-start.63 = (bf16[256,2048]{1,0:T(8,128)(2,1)}, bf16[256,2048]{1,0:T(8,128)(2,1)S(1)}, u32[]{:S(2)}, u32[]{:S(2)}) collective-permute-start(bf16[256,2048]{1,0:T(8,128)(2,1)} %add_convert_fusion.10), channel_id=1, source_target_pairs={{1,3},{3,5},{5,7},{7,6},{6,4},{4,2},{2,0},{0,1},{9,11},{11,13},{13... | collective-permute-start | bytes 3145736 | tf_op jit(solution)/shard_map/ppermute | solution.py:85
  421.2 27.2 %collective-permute-start.59 = (bf16[128,2048]{1,0:T(8,128)(2,1)}, bf16[128,2048]{1,0:T(8,128)(2,1)}, u32[]{:S(2)}, u32[]{:S(2)}) collective-permute-start(bf16[128,2048]{1,0:T(8,128)(2,1)} %convert_element_type.155), channel_id=1, source_target_pairs={{3,1},{5,3},{7,5},{6,7},{4,6},{2,4},{0,2},{1,0},{11,9},{13,11},{15... | collective-permute-start | bytes 1572872 | tf_op jit(solution)/shard_map/ppermute | solution.py:88
  422.1 30.0 %collective-permute-start.60 = (bf16[128,2048]{1,0:T(8,128)(2,1)}, bf16[128,2048]{1,0:T(8,128)(2,1)}, u32[]{:S(2)}, u32[]{:S(2)}) collective-permute-start(bf16[128,2048]{1,0:T(8,128)(2,1)} %convert_element_type.156), channel_id=1, source_target_pairs={{1,3},{3,5},{5,7},{7,6},{6,4},{4,2},{2,0},{0,1},{9,11},{11,13},{13... | collective-permute-start | bytes 1572872 | tf_op jit(solution)/shard_map/ppermute | solution.py:85
  423.3 28.9 %collective-permute-start.65 = (bf16[256,2048]{1,0:T(8,128)(2,1)}, bf16[256,2048]{1,0:T(8,128)(2,1)}, u32[]{:S(2)}, u32[]{:S(2)}) collective-permute-start(bf16[256,2048]{1,0:T(8,128)(2,1)} %get-tuple-element.500.refs_8_), channel_id=1, source_target_pairs={{0,8},{8,0},{16,24},{24,16},{1,9},{9,1},{17,25},{25,17},{2,10},{10... | collective-permute-start | bytes 3145736 | tf_op jit(solution)/shard_map/ppermute | solution.py:103
  445.4 27.4 %collective-permute-start.69 = (bf16[688,1024]{1,0:T(8,128)(2,1)}, bf16[688,1024]{1,0:T(8,128)(2,1)S(1)}, u32[]{:S(2)}, u32[]{:S(2)}) collective-permute-start(bf16[688,1024]{1,0:T(8,128)(2,1)} %get-tuple-element.504), channel_id=1, source_target_pairs={{0,8},{8,0},{16,24},{24,16},{1,9},{9,1},{17,25},{25,17},{2,10},{10... | collective-permute-start | bytes 4227080 | tf_op jit(solution)/shard_map/ppermute | solution.py:103
  452.1 21.9 %collective-permute-start.67 = (bf16[256,2048]{1,0:T(8,128)(2,1)}, bf16[256,2048]{1,0:T(8,128)(2,1)}, u32[]{:S(2)}, u32[]{:S(2)}) collective-permute-start(bf16[256,2048]{1,0:T(8,128)(2,1)} %add_convert_fusion.9), channel_id=1, source_target_pairs={{3,1},{5,3},{7,5},{6,7},{4,6},{2,4},{0,2},{1,0},{11,9},{13,11},{15... | collective-permute-start | bytes 3145736 | tf_op jit(solution)/shard_map/ppermute | solution.py:88
  453.1 21.6 %collective-permute-start.68 = (bf16[256,2048]{1,0:T(8,128)(2,1)}, bf16[256,2048]{1,0:T(8,128)(2,1)}, u32[]{:S(2)}, u32[]{:S(2)}) collective-permute-start(bf16[256,2048]{1,0:T(8,128)(2,1)} %add_convert_fusion.8), channel_id=1, source_target_pairs={{1,3},{3,5},{5,7},{7,6},{6,4},{4,2},{2,0},{0,1},{9,11},{11,13},{13... | collective-permute-start | bytes 3145736 | tf_op jit(solution)/shard_map/ppermute | solution.py:85
  477.2 52.3 %collective-permute-start.71 = (bf16[256,2048]{1,0:T(8,128)(2,1)S(1)}, bf16[256,2048]{1,0:T(8,128)(2,1)S(1)}, u32[]{:S(2)}, u32[]{:S(2)}) collective-permute-start(bf16[256,2048]{1,0:T(8,128)(2,1)S(1)} %pad_maximum_fusion.2), channel_id=1, source_target_pairs={{3,1},{5,3},{7,5},{6,7},{4,6},{2,4},{0,2},{1,0},{11,9},{13,11},{15... | collective-permute-start | bytes 3145736 | tf_op jit(solution)/shard_map/ppermute | solution.py:88
  477.9 51.6 %collective-permute-start.72 = (bf16[256,2048]{1,0:T(8,128)(2,1)S(1)}, bf16[256,2048]{1,0:T(8,128)(2,1)}, u32[]{:S(2)}, u32[]{:S(2)}) collective-permute-start(bf16[256,2048]{1,0:T(8,128)(2,1)S(1)} %pad_maximum_fusion.3), channel_id=1, source_target_pairs={{1,3},{3,5},{5,7},{7,6},{6,4},{4,2},{2,0},{0,1},{9,11},{11,13},{13... | collective-permute-start | bytes 3145736 | tf_op jit(solution)/shard_map/ppermute | solution.py:85
  505.8 19.3 %collective-permute-start.78 = (bf16[256,256]{1,0:T(8,128)(2,1)}, bf16[256,256]{1,0:T(8,128)(2,1)S(1)}, u32[]{:S(2)}, u32[]{:S(2)}) collective-permute-start(bf16[256,256]{1,0:T(8,128)(2,1)} %get-tuple-element.545), channel_id=1, source_target_pairs={{0,5},{1,4},{2,7},{3,6},{4,1},{5,0},{6,3},{7,2},{8,13},{9,12},{10,... | collective-permute-start | bytes 393224 | tf_op jit(solution)/shard_map/ppermute | solution.py:103
  533.3 25.3 %collective-permute-start.84 = (bf16[256,2048]{1,0:T(8,128)(2,1)S(1)}, bf16[256,2048]{1,0:T(8,128)(2,1)S(1)}, u32[]{:S(2)}, u32[]{:S(2)}) collective-permute-start(bf16[256,2048]{1,0:T(8,128)(2,1)S(1)} %add_convert_fusion.7), channel_id=1, source_target_pairs={{3,1},{5,3},{7,5},{6,7},{4,6},{2,4},{0,2},{1,0},{11,9},{13,11},{15... | collective-permute-start | bytes 3145736 | tf_op jit(solution)/shard_map/ppermute | solution.py:88
  534.1 24.5 %collective-permute-start.85 = (bf16[256,2048]{1,0:T(8,128)(2,1)S(1)}, bf16[256,2048]{1,0:T(8,128)(2,1)S(1)}, u32[]{:S(2)}, u32[]{:S(2)}) collective-permute-start(bf16[256,2048]{1,0:T(8,128)(2,1)S(1)} %add_convert_fusion.6), channel_id=1, source_target_pairs={{1,3},{3,5},{5,7},{7,6},{6,4},{4,2},{2,0},{0,1},{9,11},{11,13},{13... | collective-permute-start | bytes 3145736 | tf_op jit(solution)/shard_map/ppermute | solution.py:85
  536.4 22.3 %collective-permute-start.86 = (bf16[344,1024]{1,0:T(8,128)(2,1)S(1)}, bf16[344,1024]{1,0:T(8,128)(2,1)S(1)}, u32[]{:S(2)}, u32[]{:S(2)}) collective-permute-start(bf16[344,1024]{1,0:T(8,128)(2,1)S(1)} %get-tuple-element.577), channel_id=1, source_target_pairs={{0,16},{8,24},{16,0},{24,8},{1,17},{9,25},{17,1},{25,9},{2,18},{10... | collective-permute-start | bytes 2113544 | tf_op jit(solution)/shard_map/ppermute | solution.py:103
  581.7 40.3 %collective-permute-start.96 = (bf16[256,2048]{1,0:T(8,128)(2,1)S(1)}, bf16[256,2048]{1,0:T(8,128)(2,1)S(1)}, u32[]{:S(2)}, u32[]{:S(2)}) collective-permute-start(bf16[256,2048]{1,0:T(8,128)(2,1)S(1)} %add_convert_fusion.4), channel_id=1, source_target_pairs={{1,3},{3,5},{5,7},{7,6},{6,4},{4,2},{2,0},{0,1},{9,11},{11,13},{13... | collective-permute-start | bytes 3145736 | tf_op jit(solution)/shard_map/ppermute | solution.py:85
  583.1 38.9 %collective-permute-start.95 = (bf16[256,2048]{1,0:T(8,128)(2,1)S(1)}, bf16[256,2048]{1,0:T(8,128)(2,1)S(1)}, u32[]{:S(2)}, u32[]{:S(2)}) collective-permute-start(bf16[256,2048]{1,0:T(8,128)(2,1)S(1)} %add_convert_fusion.5), channel_id=1, source_target_pairs={{3,1},{5,3},{7,5},{6,7},{4,6},{2,4},{0,2},{1,0},{11,9},{13,11},{15... | collective-permute-start | bytes 3145736 | tf_op jit(solution)/shard_map/ppermute | solution.py:88
  586.1 19.3 %collective-permute-start.105 = (bf16[256,512]{1,0:T(8,128)(2,1)}, bf16[256,512]{1,0:T(8,128)(2,1)S(1)}, u32[]{:S(2)}, u32[]{:S(2)}) collective-permute-start(bf16[256,512]{1,0:T(8,128)(2,1)} %get-tuple-element.597.refs_2_), channel_id=1, source_target_pairs={{0,8},{8,0},{16,24},{24,16},{1,9},{9,1},{17,25},{25,17},{2,10},{10... | collective-permute-start | bytes 786440 | tf_op jit(solution)/shard_map/ppermute | solution.py:103
  586.1 20.3 %collective-permute-start.106 = (bf16[256,512]{1,0:T(8,128)(2,1)}, bf16[256,512]{1,0:T(8,128)(2,1)S(1)}, u32[]{:S(2)}, u32[]{:S(2)}) collective-permute-start(bf16[256,512]{1,0:T(8,128)(2,1)} %get-tuple-element.598.refs_3_), channel_id=1, source_target_pairs={{0,24},{8,16},{16,8},{24,0},{1,25},{9,17},{17,9},{25,1},{2,26},{10... | collective-permute-start | bytes 786440 | tf_op jit(solution)/shard_map/ppermute | solution.py:103
  594.9 52.4 %collective-permute-start.117 = (bf16[688,1024]{1,0:T(8,128)(2,1)}, bf16[688,1024]{1,0:T(8,128)(2,1)S(1)}, u32[]{:S(2)}, u32[]{:S(2)}) collective-permute-start(bf16[688,1024]{1,0:T(8,128)(2,1)} %get-tuple-element.653), channel_id=1, source_target_pairs={{0,8},{8,0},{16,24},{24,16},{1,9},{9,1},{17,25},{25,17},{2,10},{10... | collective-permute-start | bytes 4227080 | tf_op jit(solution)/shard_map/ppermute | solution.py:103
  626.1 27.0 %collective-permute-start.111 = (bf16[688,1024]{1,0:T(8,128)(2,1)}, bf16[688,1024]{1,0:T(8,128)(2,1)S(1)}, u32[]{:S(2)}, u32[]{:S(2)}) collective-permute-start(bf16[688,1024]{1,0:T(8,128)(2,1)} %chip_sum.3.mine), channel_id=1, source_target_pairs={{0,8},{8,0},{16,24},{24,16},{1,9},{9,1},{17,25},{25,17},{2,10},{10... | collective-permute-start | bytes 4227080 | tf_op jit(solution)/shard_map/ppermute | solution.py:103
  641.2 60.5 %collective-permute-start.114 = (bf16[688,1024]{1,0:T(8,128)(2,1)S(1)}, bf16[688,1024]{1,0:T(8,128)(2,1)S(1)}, u32[]{:S(2)}, u32[]{:S(2)}) collective-permute-start(bf16[688,1024]{1,0:T(8,128)(2,1)S(1)} %copy-done.17), channel_id=1, source_target_pairs={{0,8},{8,0},{16,24},{24,16},{1,9},{9,1},{17,25},{25,17},{2,10},{10... | collective-permute-start | bytes 4227080 | tf_op jit(solution)/shard_map/ppermute | solution.py:103
  647.9 29.1 %collective-permute-start.110 = (bf16[544,512]{1,0:T(8,128)(2,1)}, bf16[544,512]{1,0:T(8,128)(2,1)}, u32[]{:S(2)}, u32[]{:S(2)}) collective-permute-start(bf16[544,512]{1,0:T(8,128)(2,1)} %pad_maximum_fusion.6), channel_id=1, source_target_pairs={{1,3},{3,5},{5,7},{7,6},{6,4},{4,2},{2,0},{0,1},{9,11},{11,13},{13... | collective-permute-start | bytes 1671176 | tf_op jit(solution)/shard_map/ppermute | solution.py:85
  649.9 23.1 %collective-permute-start.101 = (bf16[256,512]{1,0:T(8,128)(2,1)}, bf16[256,512]{1,0:T(8,128)(2,1)S(1)}, u32[]{:S(2)}, u32[]{:S(2)}) collective-permute-start(bf16[256,512]{1,0:T(8,128)(2,1)} %get-tuple-element.616), channel_id=1, source_target_pairs={{0,5},{1,4},{2,7},{3,6},{4,1},{5,0},{6,3},{7,2},{8,13},{9,12},{10,... | collective-permute-start | bytes 786440 | tf_op jit(solution)/shard_map/ppermute | solution.py:103
  653.0 44.5 %collective-permute-start.118 = (bf16[344,1024]{1,0:T(8,128)(2,1)}, bf16[344,1024]{1,0:T(8,128)(2,1)}, u32[]{:S(2)}, u32[]{:S(2)}) collective-permute-start(bf16[344,1024]{1,0:T(8,128)(2,1)} %get-tuple-element.654), channel_id=1, source_target_pairs={{0,16},{8,24},{16,0},{24,8},{1,17},{9,25},{17,1},{25,9},{2,18},{10... | collective-permute-start | bytes 2113544 | tf_op jit(solution)/shard_map/ppermute | solution.py:103
  660.7 36.8 %collective-permute-start.119 = (bf16[344,1024]{1,0:T(8,128)(2,1)}, bf16[344,1024]{1,0:T(8,128)(2,1)S(1)}, u32[]{:S(2)}, u32[]{:S(2)}) collective-permute-start(bf16[344,1024]{1,0:T(8,128)(2,1)} %get-tuple-element.655), channel_id=1, source_target_pairs={{0,16},{8,24},{16,0},{24,8},{1,17},{9,25},{17,1},{25,9},{2,18},{10... | collective-permute-start | bytes 2113544 | tf_op jit(solution)/shard_map/ppermute | solution.py:103
  688.8 18.7 %collective-permute-start.112 = (bf16[544,512]{1,0:T(8,128)(2,1)S(1)}, bf16[544,512]{1,0:T(8,128)(2,1)S(1)}, u32[]{:S(2)}, u32[]{:S(2)}) collective-permute-start(bf16[544,512]{1,0:T(8,128)(2,1)S(1)} %add_convert_fusion.16), channel_id=1, source_target_pairs={{3,1},{5,3},{7,5},{6,7},{4,6},{2,4},{0,2},{1,0},{11,9},{13,11},{15... | collective-permute-start | bytes 1671176 | tf_op jit(solution)/shard_map/ppermute | solution.py:88
  701.5 23.1 %collective-permute-start.120 = (bf16[688,1024]{1,0:T(8,128)(2,1)}, bf16[688,1024]{1,0:T(8,128)(2,1)S(1)}, u32[]{:S(2)}, u32[]{:S(2)}) collective-permute-start(bf16[688,1024]{1,0:T(8,128)(2,1)} %chip_sum.5.mine), channel_id=1, source_target_pairs={{0,8},{8,0},{16,24},{24,16},{1,9},{9,1},{17,25},{25,17},{2,10},{10... | collective-permute-start | bytes 4227080 | tf_op jit(solution)/shard_map/ppermute | solution.py:103
  (191 other events, 2468.4 us)

commit v5 on v4

--- a/solution.py
+++ b/solution.py
@@ -930,7 +930,7 @@
 def projections_body(n, nd, info, normed, attn_part, ffn_part, *refs):
     branch_cols, query_cols, mixed_in = refs[:nd], refs[nd : 2 * nd], refs[2 * nd : 3 * nd]
     outs = refs[3 * nd : 3 * nd + n]
-    branch, query, mixed = refs[3 * nd + n :]
+    branch, query, mixed, made, sems = refs[3 * nd + n :]
     count = branch_cols[0].shape[0]
     share = mixed.shape[1] // n
     for k in range(nd):
@@ -938,13 +938,18 @@
         mixed[rows, :] = mixed_in[k][...]
         branch[rows, :] = branch_cols[k][...]
         query[rows, :] = query_cols[k][...]
+    copies = []
     for k in range(n):
         cols = pl.ds(aligned(info[3 + k], share), share)
-        outs[k][:share, :] = tn_dot(mixed[:, cols], branch[...])
-        outs[k][share : 2 * share, :] = tn_dot(normed[:, cols], query[...])
-        outs[k][2 * share :, :] = jnp.zeros((GAIN_ROWS, branch.shape[1]), jnp.float32)
-        outs[k][2 * share : 2 * share + 8, :share] = attn_part[:, cols]
-        outs[k][2 * share : 2 * share + 8, share : 2 * share] = ffn_part[:, cols]
+        block = made.at[k]
+        block[:share, :] = tn_dot(mixed[:, cols], branch[...])
+        block[share : 2 * share, :] = tn_dot(normed[:, cols], query[...])
+        block[2 * share :, :] = jnp.zeros((GAIN_ROWS, branch.shape[1]), jnp.float32)
+        block[2 * share : 2 * share + 8, :share] = attn_part[:, cols]
+        block[2 * share : 2 * share + 8, share : 2 * share] = ffn_part[:, cols]
+        copies.append(pltpu.make_async_copy(block, outs[k], sems.at[k]))
+        copies[-1].start()
+    wait_all(copies)
 
 
 def projection_gradients(n, nd, info, mixed, normed, attn_part, ffn_part, branch_cols, query_cols):
@@ -955,9 +960,13 @@
         [info, normed, attn_part, ffn_part, *branch_cols, *query_cols, *mixed],
         [IN_SMEM] + [IN_VMEM] * (3 + 3 * nd),
         [((2 * depth // n + GAIN_ROWS, quarter), jnp.float32)] * n,
-        [IN_VMEM] * n,
+        [ANYWHERE] * n,
         [pltpu.VMEM((rows, quarter), jnp.bfloat16)] * 2
-        + [pltpu.VMEM((rows, depth), jnp.bfloat16)],
+        + [
+            pltpu.VMEM((rows, depth), jnp.bfloat16),
+            pltpu.VMEM((n, 2 * depth // n + GAIN_ROWS, quarter), jnp.float32),
+            pltpu.SemaphoreType.DMA((n,)),
+        ],
         4 * rows * depth * quarter,
         4 * rows * depth,
         "projection_gradients",

time: 768 us -> 767 us (level)
  Pallas kernels: 250 us -> 224 us
  waiting for transfers between devices: 276 us -> 299 us
    pallas_call x25, Pallas kernels: 250 us -> 224 us  [call(): pl.pallas_call(body, name=name, in_specs=specs, out_specs=tuple(out_specs...]
    ppermute x68, waiting for transfers between devices: 109 us -> 122 us  [swap(): return lax.ppermute(x, axis, [(k, k ^ r) for k in range(count)])]
  transfers between devices with their start and end apart: 124 -> 124, of which waited for: 56 -> 57; matrix products, arithmetic and copies ran while one was open for 5% -> 5% of each run, Pallas kernels for 32% -> 29%
where the time goes in v5:
time: 767 us; the launch traced here: 760 us
  waiting for transfers between devices  299 us (39%)
  Pallas kernels  224 us (29%)
  starting transfers between devices  175 us (23%)
  other arithmetic  34 us (4%)
  local copies, waits for them, and re-layouts  24.5 us (3%)
    pallas_call x25, Pallas kernels, call(): pl.pallas_call(body, name=name, in_specs=specs, out_specs=tuple(out_specs...  224 us
    ppermute x24, waiting for transfers between devices, to_right(): return lax.ppermute(x, 'seq', self.right)  122 us
    ppermute x68, waiting for transfers between devices, swap(): return lax.ppermute(x, axis, [(k, k ^ r) for k in range(count)])  122 us
    ppermute x68, starting transfers between devices, swap(): return lax.ppermute(x, axis, [(k, k ^ r) for k in range(count)])  81.7 us
    ppermute x24, starting transfers between devices, to_left(): return lax.ppermute(x, 'seq', self.left)  38.7 us
    ppermute x24, waiting for transfers between devices, to_left(): return lax.ppermute(x, 'seq', self.left)  34 us
    ppermute x24, starting transfers between devices, to_right(): return lax.ppermute(x, 'seq', self.right)  30.3 us
    convert_element_type x21, other arithmetic, low(): return value.astype(jnp.bfloat16)  25.6 us
  transfers between devices with their start and end apart: 124, of which 57 were waited for; matrix products, arithmetic and copies ran while one was open for 5% of the time, Pallas kernels for 29%

profile of v5, /device:TPU:0, one launch (start us, length us, event | category | flops | bytes accessed | tf_op | source)
XLA Modules:
  0.0 760.2 jit_solution(2472958228275724835)
XLA Ops:
  5.6 12.6 %collective-permute-done.1.refs_5_ = bf16[544,512]{1,0:T(8,128)(2,1)S(1)} collective-permute-done((bf16[544,512]{1,0:T(8,128)(2,1)S(1)}, bf16[544,512]{1,0:T(8,128)(2,1)S(1)}, u32[]{:S(2)}, u32[]{:S(2)}) %collective-permute-start.1) | collective-permute-done | bytes 557088 | tf_op jit(solution)/shard_map/ppermute | solution.py:85
  22.2 3.7 pack_keys_values.1
  30.7 9.0 %collective-permute-done.5.refs_9_ = bf16[256,512]{1,0:T(8,128)(2,1)S(1)} collective-permute-done((bf16[256,512]{1,0:T(8,128)(2,1)}, bf16[256,512]{1,0:T(8,128)(2,1)S(1)}, u32[]{:S(2)}, u32[]{:S(2)}) %collective-permute-start.5) | collective-permute-done | bytes 262176 | tf_op jit(solution)/shard_map/ppermute | solution.py:103
  45.0 15.4 %collective-permute-done.7.refs_9_ = bf16[544,512]{1,0:T(8,128)(2,1)S(1)} collective-permute-done((bf16[544,512]{1,0:T(8,128)(2,1)}, bf16[544,512]{1,0:T(8,128)(2,1)S(1)}, u32[]{:S(2)}, u32[]{:S(2)}) %collective-permute-start.7) | collective-permute-done | bytes 557088 | tf_op jit(solution)/shard_map/ppermute | solution.py:85
  60.5 4.2 collective-permute-done.9.refs_11_
  66.7 4.5 collective-permute-done.11.refs_11_
  80.9 11.4 %project_queries.1 = (bf16[256,256]{1,0:T(8,128)(2,1)}, bf16[256,256]{1,0:T(8,128)(2,1)}, bf16[256,256]{1,0:T(8,128)(2,1)}, bf16[256,256]{1,0:T(8,128)(2,1)}, bf...) custom-call(s32[11]{0:T(128)} %stack.54.info, ...), custom_call_target="tpu_custom_call" | custom-call | flops 536870912 | bytes 6291456 | tf_op jit(solution)/shard_map/project_queries/pallas_call | solution.py:180
  92.3 8.2 %collective-permute-done.15.refs_13_ = bf16[256,512]{1,0:T(8,128)(2,1)} collective-permute-done((bf16[256,512]{1,0:T(8,128)(2,1)}, bf16[256,512]{1,0:T(8,128)(2,1)}, u32[]{:S(2)}, u32[]{:S(2)}) %collective-permute-start.15) | collective-permute-done | bytes 262176 | tf_op jit(solution)/shard_map/ppermute | solution.py:103
  103.7 15.8 %collective-permute-start.20 = (bf16[256,256]{1,0:T(8,128)(2,1)}, bf16[256,256]{1,0:T(8,128)(2,1)S(1)}, u32[]{:S(2)}, u32[]{:S(2)}) collective-permute-start(bf16[256,256]{1,0:T(8,128)(2,1)} %get-tuple-element.382), channel_id=1, source_target_pairs={{0,16},{1,17},{2,0},{3,1},{4,24},{5,25},{6,8},{7,9},{8,20},{9,21},... | collective-permute-start | bytes 393224 | tf_op jit(solution)/shard_map/ppermute | solution.py:99
  124.5 13.0 %collective-permute-done.20.refs_2_ = bf16[256,256]{1,0:T(8,128)(2,1)S(1)} collective-permute-done((bf16[256,256]{1,0:T(8,128)(2,1)}, bf16[256,256]{1,0:T(8,128)(2,1)S(1)}, u32[]{:S(2)}, u32[]{:S(2)}) %collective-permute-start.20) | collective-permute-done | bytes 131104 | tf_op jit(solution)/shard_map/ppermute | solution.py:99
  137.7 8.0 %collective-permute-done.25.refs_7_ = bf16[256,256]{1,0:T(8,128)(2,1)S(1)} collective-permute-done((bf16[256,256]{1,0:T(8,128)(2,1)}, bf16[256,256]{1,0:T(8,128)(2,1)S(1)}, u32[]{:S(2)}, u32[]{:S(2)}) %collective-permute-start.25) | collective-permute-done | bytes 131104 | tf_op jit(solution)/shard_map/ppermute | solution.py:99
  152.6 7.0 attention_forward.1
  159.6 15.8 %collective-permute-done.26.refs_2_.refs_10_ = bf16[256,2048]{1,0:T(8,128)(2,1)} collective-permute-done((bf16[256,2048]{1,0:T(8,128)(2,1)S(1)}, bf16[256,2048]{1,0:T(8,128)(2,1)}, u32[]{:S(2)}, u32[]{:S(2)}) %collective-permute-start.26) | collective-permute-done | bytes 1048608 | tf_op jit(solution)/shard_map/ppermute | solution.py:85
  184.6 4.2 collective-permute-done.30.refs_3_
  190.7 6.8 collective-permute-done.31.refs_4_
  202.4 3.6 collective-permute-start.41
  208.3 8.5 %project_mixed.1 = (f32[256,2048]{1,0:T(8,128)}, bf16[256,2048]{1,0:T(8,128)(2,1)}, bf16[256,2048]{1,0:T(8,128)(2,1)}) custom-call(s32[11]{0:T(128)} %stack.54.info, bf16[256,2048]{1,0:T(8,128)(2,1)} %x.3, f32[8,2048]{1,0:T(8,128)} %get-tuple-element.364.gains, bf16[256,256]{1,0:T(8,128)(2,1)} %get-tuple-element.397.refs_0_, bf16[256,256]{1,0:T(8,128)(2,1)} %copy-done.91, ...), custom_call_target="tpu_custom_call" | custom-call | flops 536870912 | bytes 6291456 | tf_op jit(solution)/shard_map/project_mixed/pallas_call | solution.py:180
  219.0 3.5 collective-permute-start.39
  222.5 10.4 %ffn_blocks.5 = (bf16[256,768]{1,0:T(8,128)(2,1)}, bf16[256,768]{1,0:T(8,128)(2,1)}, bf16[256,768]{1,0:T(8,128)(2,1)}, f32[256,2048]{1,0:T(8,128)}, f32[256,2048]{1,0:T(8,128)}) custom-call(bf16[256,2048]{1,0:T(8,128)(2,1)} %get-tuple-element.410.refs_0_.refs_9_, bf16[256,2048]{1,0:T(8,128)(2,1)} %cotangent.1, bf16[688,2048]{1,0:T(8,128)(2,1)} %refs_4_.9, ...), custom_call_target="tpu_custom_call" | custom-call | flops 1082130432 | bytes 3686400 | tf_op jit(solution)/shard_map/ffn_blocks/pallas_call | solution.py:180
  233.0 19.0 %collective-permute-done.38.refs_0_.refs_10_ = bf16[256,2048]{1,0:T(8,128)(2,1)S(1)} collective-permute-done((bf16[256,2048]{1,0:T(8,128)(2,1)}, bf16[256,2048]{1,0:T(8,128)(2,1)S(1)}, u32[]{:S(2)}, u32[]{:S(2)}) %collective-permute-start.38) | collective-permute-done | bytes 1048608 | tf_op jit(solution)/shard_map/ppermute | solution.py:85
  258.6 17.6 %ffn_blocks.6 = (bf16[256,768]{1,0:T(8,128)(2,1)}, bf16[256,768]{1,0:T(8,128)(2,1)}, bf16[256,768]{1,0:T(8,128)(2,1)}, f32[256,2048]{1,0:T(8,128)}, f32[256,2048...) custom-call(bf16[256,2048]{1,0:T(8,128)(2,1)} %copy-done.6, ...), custom_call_target="tpu_custom_call" | custom-call | flops 2164260864 | bytes 5259264 | tf_op jit(solution)/shard_map/ffn_blocks/pallas_call | solution.py:180
  280.8 18.9 %collective-permute-done.44.refs_2_.refs_14_ = bf16[256,2048]{1,0:T(8,128)(2,1)S(1)} collective-permute-done((bf16[256,2048]{1,0:T(8,128)(2,1)}, bf16[256,2048]{1,0:T(8,128)(2,1)S(1)}, u32[]{:S(2)}, u32[]{:S(2)}) %collective-permute-start.44) | collective-permute-done | bytes 1048608 | tf_op jit(solution)/shard_map/ppermute | solution.py:85
  306.4 17.6 %ffn_blocks.7 = (bf16[256,768]{1,0:T(8,128)(2,1)}, bf16[256,768]{1,0:T(8,128)(2,1)}, bf16[256,768]{1,0:T(8,128)(2,1)}, f32[256,2048]{1,0:T(8,128)}, f32[256,2048...) custom-call(bf16[256,2048]{1,0:T(8,128)(2,1)} %copy-done.8, ...), custom_call_target="tpu_custom_call" | custom-call | flops 2164260864 | bytes 5259264 | tf_op jit(solution)/shard_map/ffn_blocks/pallas_call | solution.py:180
  327.6 7.8 %collective-permute-done.48.refs_2_.refs_16_ = bf16[128,2048]{1,0:T(8,128)(2,1)S(1)} collective-permute-done((bf16[128,2048]{1,0:T(8,128)(2,1)S(1)}, bf16[128,2048]{1,0:T(8,128)(2,1)S(1)}, u32[]{:S(2)}, u32[]{:S(2)}) %collective-permute-start.48) | collective-permute-done | bytes 524320 | tf_op jit(solution)/shard_map/ppermute | solution.py:85
  337.7 17.7 %ffn_blocks.8 = (bf16[256,768]{1,0:T(8,128)(2,1)}, bf16[256,768]{1,0:T(8,128)(2,1)}, bf16[256,768]{1,0:T(8,128)(2,1)}, f32[256,2048]{1,0:T(8,128)}, f32[256,2048...) custom-call(bf16[256,2048]{1,0:T(8,128)(2,1)} %copy-done, ...), custom_call_target="tpu_custom_call" | custom-call | flops 2164260864 | bytes 5259264 | tf_op jit(solution)/shard_map/ffn_blocks/pallas_call | solution.py:180
  356.4 10.9 %ffn_blocks.9 = (bf16[128,768]{1,0:T(8,128)(2,1)}, bf16[128,768]{1,0:T(8,128)(2,1)}, bf16[128,768]{1,0:T(8,128)(2,1)}, f32[128,2048]{1,0:T(8,128)}, f32[128,2048...) custom-call(bf16[128,2048]{1,0:T(8,128)(2,1)} %copy-done.18, ...), custom_call_target="tpu_custom_call" | custom-call | flops 1082130432 | bytes 3686400 | tf_op jit(solution)/shard_map/ffn_blocks/pallas_call | solution.py:180
  372.4 11.3 %collective-permute-done.53 = bf16[128,2048]{1,0:T(8,128)(2,1)S(1)} collective-permute-done((bf16[128,2048]{1,0:T(8,128)(2,1)S(1)}, bf16[128,2048]{1,0:T(8,128)(2,1)S(1)}, u32[]{:S(2)}, u32[]{:S(2)}) %collective-permute-start.53) | collective-permute-done | bytes 524320 | tf_op jit(solution)/shard_map/ppermute | solution.py:88
  389.6 15.2 %weight_gradient.3 = (bf16[688,1024]{1,0:T(8,128)(2,1)}, bf16[688,1024]{1,0:T(8,128)(2,1)}) custom-call(s32[11]{0:T(128)} %stack.54.info, bf16[256,768]{1,0:T(8,128)(2,1)} %get-tuple-element.466.refs_0_, bf16[256,768]{1,0:T(8,128)(2,1)} %get-tuple-element.467.refs_1_, bf16[256,768]{1,0:T(8,128)(2,1)} %get-tuple-element.468.refs_2_, ...), custom_call_target="tpu_custom_call" | custom-call | flops 1442840576 | bytes 2097152 | tf_op jit(solution)/shard_map/weight_gradient/pallas_call | solution.py:180
  404.9 5.1 collective-permute-done.57
  423.2 15.1 %weight_gradient.4 = (bf16[688,1024]{1,0:T(8,128)(2,1)}, bf16[688,1024]{1,0:T(8,128)(2,1)}) custom-call(s32[11]{0:T(128)} %stack.54.info, bf16[256,768]{1,0:T(8,128)(2,1)} %get-tuple-element.490.refs_0_, bf16[256,768]{1,0:T(8,128)(2,1)} %get-tuple-element.491.refs_1_, bf16[256,768]{1,0:T(8,128)(2,1)} %get-tuple-element.492.refs_2_, ...), custom_call_target="tpu_custom_call" | custom-call | flops 1442840576 | bytes 2097152 | tf_op jit(solution)/shard_map/weight_gradient/pallas_call | solution.py:180
  448.3 3.7 collective-permute-done.60
  457.6 15.0 %weight_gradient.5 = (bf16[688,1024]{1,0:T(8,128)(2,1)}, bf16[688,1024]{1,0:T(8,128)(2,1)}) custom-call(s32[11]{0:T(128)} %stack.54.info, bf16[256,768]{1,0:T(8,128)(2,1)} %get-tuple-element.514.refs_0_, bf16[256,768]{1,0:T(8,128)(2,1)} %get-tuple-element.515.refs_1_, bf16[256,768]{1,0:T(8,128)(2,1)} %get-tuple-element.516.refs_2_, ...), custom_call_target="tpu_custom_call" | custom-call | flops 1442840576 | bytes 2097152 | tf_op jit(solution)/shard_map/weight_gradient/pallas_call | solution.py:180
  479.2 10.5 %branch_gradient.1 = (bf16[256,256]{1,0:T(8,128)(2,1)}, bf16[256,256]{1,0:T(8,128)(2,1)}, bf16[256,256]{1,0:T(8,128)(2,1)}, bf16[256,256]{1,0:T(8,128)(2,1)}, bf...) custom-call(s32[11]{0:T(128)} %stack.54.info, ...), custom_call_target="tpu_custom_call" | custom-call | flops 536870912 | bytes 6291456 | tf_op jit(solution)/shard_map/branch_gradient/pallas_call | solution.py:180
  491.9 7.1 collective-permute-done.81.refs_1_
  507.3 3.6 collective-permute-done.76.refs_19_
  513.0 7.3 collective-permute-done.77.refs_20_
  520.9 3.3 collective-permute-start.80
  524.8 4.1 collective-permute-done.80.refs_23_
  536.5 9.1 %attention_backward.1 = (bf16[256,256]{1,0:T(8,128)(2,1)}, bf16[256,256]{1,0:T(8,128)(2,1)}, bf16[256,256]{1,0:T(8,128)(2,1)}, bf16[256,256]{1,0:T(8,128)(2,1)},...) custom-call(s32[3]{0:T(128)} %pad_add_fusion.info, ...), custom_call_target="tpu_custom_call" | custom-call | flops 10737418240 | bytes 2621440 | tf_op jit(solution)/shard_map/attention_backward/pallas_call | solution.py:180
  545.6 3.9 collective-permute-done.86.refs_0_
  549.5 4.2 collective-permute-done.84
  559.4 5.4 collective-permute-start.94
  572.5 3.3 collective-permute-done.90.refs_4_
  575.8 4.9 collective-permute-done.91.refs_5_
  585.2 4.1 collective-permute-start.95
  591.5 7.3 collective-permute-done.104.refs_5_
  598.9 10.4 %input_gradient.1 = (bf16[256,2048]{1,0:T(8,128)(2,1)}, f32[8,2048]{1,0:T(8,128)}) custom-call(bf16[256,2048]{1,0:T(8,128)(2,1)} %x.3, f32[8,2048]{1,0:T(8,128)} %get-tuple-element.364.gains, f32[256,2048]{1,0:T(8,128)} %get-tuple-element.601.grad_hidden, bf16[256,512]{1,0:T(8,128)(2,1)} %get-tuple-element.595.refs_0_, ...), custom_call_target="tpu_custom_call" | custom-call | flops 536870912 | bytes 6291456 | tf_op jit(solution)/shard_map/input_gradient/pallas_call | solution.py:180
  611.4 10.0 %projection_gradients.1 = (f32[544,512]{1,0:T(8,128)}, f32[544,512]{1,0:T(8,128)}, f32[544,512]{1,0:T(8,128)}, f32[544,512]{1,0:T(8,128)}, f32[544,512]{1,0:T(8,...) custom-call(s32[11]{0:T(128)} %stack.54.info, bf16[1024,2048]{1,0:T(8,128)(2,1)} %get-tuple-element.621.normed, ...), custom_call_target="tpu_custom_call" | custom-call | flops 1073741824 | bytes 2097152 | tf_op jit(solution)/shard_map/projection_gradients/pallas_call | solution.py:180
  623.5 3.3 chip_sum.3.mine
  630.3 3.1 chip_sum.4.mine
  640.5 7.8 %collective-permute-done.100.refs_4_ = bf16[256,512]{1,0:T(8,128)(2,1)S(1)} collective-permute-done((bf16[256,512]{1,0:T(8,128)(2,1)S(1)}, bf16[256,512]{1,0:T(8,128)(2,1)S(1)}, u32[]{:S(2)}, u32[]{:S(2)}) %collective-permute-start.100) | collective-permute-done | bytes 262176 | tf_op jit(solution)/shard_map/ppermute | solution.py:103
  655.8 4.6 spread_columns.3
  664.9 9.8 %collective-permute-done.101.refs_5_ = bf16[256,512]{1,0:T(8,128)(2,1)S(1)} collective-permute-done((bf16[256,512]{1,0:T(8,128)(2,1)}, bf16[256,512]{1,0:T(8,128)(2,1)S(1)}, u32[]{:S(2)}, u32[]{:S(2)}) %collective-permute-start.101) | collective-permute-done | bytes 262176 | tf_op jit(solution)/shard_map/ppermute | solution.py:103
  674.7 4.0 collective-permute-start.102
  681.7 4.3 collective-permute-done.102.refs_6_
  686.0 4.5 collective-permute-done.103.refs_7_
  690.5 8.7 %collective-permute-start.112 = (bf16[544,512]{1,0:T(8,128)(2,1)S(1)}, bf16[544,512]{1,0:T(8,128)(2,1)S(1)}, u32[]{:S(2)}, u32[]{:S(2)}) collective-permute-start(bf16[544,512]{1,0:T(8,128)(2,1)S(1)} %add_convert_fusion.16), channel_id=1, source_target_pairs={{3,1},{5,3},{7,5},{6,7},{4,6},{2,4},{0,2},{1,0},{11,9},{13,11},{15... | collective-permute-start | bytes 1671176 | tf_op jit(solution)/shard_map/ppermute | solution.py:88
  700.0 3.1 chip_sum.5.mine
  704.5 4.6 spread_columns.4
  709.4 9.2 %collective-permute-done.113 = bf16[544,512]{1,0:T(8,128)(2,1)} collective-permute-done((bf16[544,512]{1,0:T(8,128)(2,1)S(1)}, bf16[544,512]{1,0:T(8,128)(2,1)}, u32[]{:S(2)}, u32[]{:S(2)}) %collective-permute-start.113) | collective-permute-done | bytes 557088 | tf_op jit(solution)/shard_map/ppermute | solution.py:85
  722.6 3.7 split_keys_values.1
  727.5 4.8 spread_columns.5
  737.4 13.5 %collective-permute-done.121.refs_1_ = bf16[544,512]{1,0:T(8,128)(2,1)S(1)} collective-permute-done((bf16[544,512]{1,0:T(8,128)(2,1)S(1)}, bf16[544,512]{1,0:T(8,128)(2,1)S(1)}, u32[]{:S(2)}, u32[]{:S(2)}) %collective-permute-start.121) | collective-permute-done | bytes 557088 | tf_op jit(solution)/shard_map/ppermute | solution.py:103
  754.6 3.8 join_projections.1
  (528 shorter events, 224.7 us)
Async XLA Ops:
  19.6 20.1 %collective-permute-start.3 = (bf16[544,512]{1,0:T(8,128)(2,1)S(1)}, bf16[544,512]{1,0:T(8,128)(2,1)}, u32[]{:S(2)}, u32[]{:S(2)}) collective-permute-start(bf16[544,512]{1,0:T(8,128)(2,1)S(1)} %collective-permute-done.1.refs_5_), channel_id=1, source_target_pairs={{1,3},{3,5},{5,7},{7,6},{6,4},{4,2},{2,0},{0,1},{9,11},{11,13},{13... | collective-permute-start | bytes 1671176 | tf_op jit(solution)/shard_map/ppermute | solution.py:85
  29.2 37.5 %collective-permute-start = (bf16[256,2048]{1,0:T(8,128)(2,1)S(1)}, bf16[256,2048]{1,0:T(8,128)(2,1)S(1)}, u32[]{:S(2)}, u32[]{:S(2)}) collective-permute-start(bf16[256,2048]{1,0:T(8,128)(2,1)S(1)} %copy-done.10), channel_id=1, source_target_pairs={{0,16},{8,24},{16,0},{24,8},{1,17},{9,25},{17,1},{25,9},{2,18},{10... | collective-permute-start | bytes 3145736 | tf_op jit(solution)/shard_map/ppermute | solution.py:103
  39.7 20.7 %collective-permute-start.7 = (bf16[544,512]{1,0:T(8,128)(2,1)}, bf16[544,512]{1,0:T(8,128)(2,1)S(1)}, u32[]{:S(2)}, u32[]{:S(2)}) collective-permute-start(bf16[544,512]{1,0:T(8,128)(2,1)} %collective-permute-done.3.refs_7_), channel_id=1, source_target_pairs={{1,3},{3,5},{5,7},{7,6},{6,4},{4,2},{2,0},{0,1},{9,11},{11,13},{13... | collective-permute-start | bytes 1671176 | tf_op jit(solution)/shard_map/ppermute | solution.py:85
  41.3 19.1 %collective-permute-start.8 = (bf16[544,512]{1,0:T(8,128)(2,1)}, bf16[544,512]{1,0:T(8,128)(2,1)S(1)}, u32[]{:S(2)}, u32[]{:S(2)}) collective-permute-start(bf16[544,512]{1,0:T(8,128)(2,1)} %collective-permute-done.4.refs_8_), channel_id=1, source_target_pairs={{3,1},{5,3},{7,5},{6,7},{4,6},{2,4},{0,2},{1,0},{11,9},{13,11},{15... | collective-permute-start | bytes 1671176 | tf_op jit(solution)/shard_map/ppermute | solution.py:88
  41.8 22.8 %collective-permute-start.9 = (bf16[256,512]{1,0:T(8,128)(2,1)}, bf16[256,512]{1,0:T(8,128)(2,1)S(1)}, u32[]{:S(2)}, u32[]{:S(2)}) collective-permute-start(bf16[256,512]{1,0:T(8,128)(2,1)} %get-tuple-element.358), channel_id=1, source_target_pairs={{0,3},{1,2},{2,1},{3,0},{4,7},{5,6},{6,5},{7,4},{8,11},{9,10},{10,... | collective-permute-start | bytes 786440 | tf_op jit(solution)/shard_map/ppermute | solution.py:103
  43.1 21.5 %collective-permute-start.10 = (bf16[256,512]{1,0:T(8,128)(2,1)}, bf16[256,512]{1,0:T(8,128)(2,1)S(1)}, u32[]{:S(2)}, u32[]{:S(2)}) collective-permute-start(bf16[256,512]{1,0:T(8,128)(2,1)} %get-tuple-element.359), channel_id=1, source_target_pairs={{0,4},{1,5},{2,6},{3,7},{4,0},{5,1},{6,2},{7,3},{8,12},{9,13},{10,... | collective-permute-start | bytes 786440 | tf_op jit(solution)/shard_map/ppermute | solution.py:103
  73.3 27.3 %collective-permute-start.15 = (bf16[256,512]{1,0:T(8,128)(2,1)}, bf16[256,512]{1,0:T(8,128)(2,1)}, u32[]{:S(2)}, u32[]{:S(2)}) collective-permute-start(bf16[256,512]{1,0:T(8,128)(2,1)} %get-tuple-element.377), channel_id=1, source_target_pairs={{0,5},{1,4},{2,7},{3,6},{4,1},{5,0},{6,3},{7,2},{8,13},{9,12},{10,... | collective-permute-start | bytes 786440 | tf_op jit(solution)/shard_map/ppermute | solution.py:103
  74.7 25.8 %collective-permute-start.16 = (bf16[256,512]{1,0:T(8,128)(2,1)}, bf16[256,512]{1,0:T(8,128)(2,1)}, u32[]{:S(2)}, u32[]{:S(2)}) collective-permute-start(bf16[256,512]{1,0:T(8,128)(2,1)} %get-tuple-element.378), channel_id=1, source_target_pairs={{0,6},{1,7},{2,4},{3,5},{4,2},{5,3},{6,0},{7,1},{8,14},{9,15},{10,... | collective-permute-start | bytes 786440 | tf_op jit(solution)/shard_map/ppermute | solution.py:103
  77.2 23.4 %collective-permute-start.17 = (bf16[256,512]{1,0:T(8,128)(2,1)}, bf16[256,512]{1,0:T(8,128)(2,1)}, u32[]{:S(2)}, u32[]{:S(2)}) collective-permute-start(bf16[256,512]{1,0:T(8,128)(2,1)} %get-tuple-element.379), channel_id=1, source_target_pairs={{0,7},{1,6},{2,5},{3,4},{4,3},{5,2},{6,1},{7,0},{8,15},{9,14},{10,... | collective-permute-start | bytes 786440 | tf_op jit(solution)/shard_map/ppermute | solution.py:103
  100.6 21.5 %collective-permute-start.18 = (bf16[256,256]{1,0:T(8,128)(2,1)}, bf16[256,256]{1,0:T(8,128)(2,1)S(1)}, u32[]{:S(2)}, u32[]{:S(2)}) collective-permute-start(bf16[256,256]{1,0:T(8,128)(2,1)} %get-tuple-element.380), channel_id=1, source_target_pairs={{0,0},{1,1},{2,16},{3,17},{4,8},{5,9},{6,24},{7,25},{8,4},{9,5},{1... | collective-permute-start | bytes 393224 | tf_op jit(solution)/shard_map/ppermute | solution.py:99
  102.1 20.7 %collective-permute-start.19 = (bf16[256,256]{1,0:T(8,128)(2,1)}, bf16[256,256]{1,0:T(8,128)(2,1)S(1)}, u32[]{:S(2)}, u32[]{:S(2)}) collective-permute-start(bf16[256,256]{1,0:T(8,128)(2,1)} %get-tuple-element.381), channel_id=1, source_target_pairs={{0,1},{1,0},{2,17},{3,16},{4,9},{5,8},{6,25},{7,24},{8,5},{9,4},{1... | collective-permute-start | bytes 393224 | tf_op jit(solution)/shard_map/ppermute | solution.py:99
  103.7 33.8 %collective-permute-start.20 = (bf16[256,256]{1,0:T(8,128)(2,1)}, bf16[256,256]{1,0:T(8,128)(2,1)S(1)}, u32[]{:S(2)}, u32[]{:S(2)}) collective-permute-start(bf16[256,256]{1,0:T(8,128)(2,1)} %get-tuple-element.382), channel_id=1, source_target_pairs={{0,16},{1,17},{2,0},{3,1},{4,24},{5,25},{6,8},{7,9},{8,20},{9,21},... | collective-permute-start | bytes 393224 | tf_op jit(solution)/shard_map/ppermute | solution.py:99
  146.3 53.4 %collective-permute-start.35 = (bf16[2048,512]{1,0:T(8,128)(2,1)}, bf16[2048,512]{1,0:T(8,128)(2,1)S(1)}, u32[]{:S(2)}, u32[]{:S(2)}) collective-permute-start(bf16[2048,512]{1,0:T(8,128)(2,1)} %get-tuple-element.407.refs_8_.refs_0_), channel_id=1, source_target_pairs={{0,16},{8,24},{16,0},{24,8},{1,17},{9,25},{17,1},{25,9},{2,18},{10... | collective-permute-start | bytes 6291464 | tf_op jit(solution)/shard_map/ppermute | solution.py:103
  149.3 26.0 %collective-permute-start.26 = (bf16[256,2048]{1,0:T(8,128)(2,1)S(1)}, bf16[256,2048]{1,0:T(8,128)(2,1)}, u32[]{:S(2)}, u32[]{:S(2)}) collective-permute-start(bf16[256,2048]{1,0:T(8,128)(2,1)S(1)} %copy-done.5), channel_id=1, source_target_pairs={{1,3},{3,5},{5,7},{7,6},{6,4},{4,2},{2,0},{0,1},{9,11},{11,13},{13... | collective-permute-start | bytes 3145736 | tf_op jit(solution)/shard_map/ppermute | solution.py:85
  149.3 26.0 %collective-permute-start.27 = (bf16[256,2048]{1,0:T(8,128)(2,1)S(1)}, bf16[256,2048]{1,0:T(8,128)(2,1)}, u32[]{:S(2)}, u32[]{:S(2)}) collective-permute-start(bf16[256,2048]{1,0:T(8,128)(2,1)S(1)} %copy-done.5), channel_id=1, source_target_pairs={{3,1},{5,3},{7,5},{6,7},{4,6},{2,4},{0,2},{1,0},{11,9},{13,11},{15... | collective-permute-start | bytes 3145736 | tf_op jit(solution)/shard_map/ppermute | solution.py:88
  178.8 18.7 %collective-permute-start.31 = (bf16[256,256]{1,0:T(8,128)(2,1)}, bf16[256,256]{1,0:T(8,128)(2,1)S(1)}, u32[]{:S(2)}, u32[]{:S(2)}) collective-permute-start(bf16[256,256]{1,0:T(8,128)(2,1)} %get-tuple-element.401), channel_id=1, source_target_pairs={{0,4},{1,5},{2,6},{3,7},{4,0},{5,1},{6,2},{7,3},{8,12},{9,13},{10,... | collective-permute-start | bytes 393224 | tf_op jit(solution)/shard_map/ppermute | solution.py:103
  181.1 18.6 %collective-permute-start.32 = (bf16[256,256]{1,0:T(8,128)(2,1)}, bf16[256,256]{1,0:T(8,128)(2,1)S(1)}, u32[]{:S(2)}, u32[]{:S(2)}) collective-permute-start(bf16[256,256]{1,0:T(8,128)(2,1)} %get-tuple-element.402), channel_id=1, source_target_pairs={{0,5},{1,4},{2,7},{3,6},{4,1},{5,0},{6,3},{7,2},{8,13},{9,12},{10,... | collective-permute-start | bytes 393224 | tf_op jit(solution)/shard_map/ppermute | solution.py:103
  200.3 32.6 %collective-permute-start.40 = (bf16[256,2048]{1,0:T(8,128)(2,1)}, bf16[256,2048]{1,0:T(8,128)(2,1)}, u32[]{:S(2)}, u32[]{:S(2)}) collective-permute-start(bf16[256,2048]{1,0:T(8,128)(2,1)} %collective-permute-done.26.refs_2_.refs_10_), channel_id=1, source_target_pairs={{1,3},{3,5},{5,7},{7,6},{6,4},{4,2},{2,0},{0,1},{9,11},{11,13},{13... | collective-permute-start | bytes 3145736 | tf_op jit(solution)/shard_map/ppermute | solution.py:85
  202.4 30.5 %collective-permute-start.41 = (bf16[256,2048]{1,0:T(8,128)(2,1)}, bf16[256,2048]{1,0:T(8,128)(2,1)S(1)}, u32[]{:S(2)}, u32[]{:S(2)}) collective-permute-start(bf16[256,2048]{1,0:T(8,128)(2,1)} %collective-permute-done.27.refs_3_.refs_11_), channel_id=1, source_target_pairs={{3,1},{5,3},{7,5},{6,7},{4,6},{2,4},{0,2},{1,0},{11,9},{13,11},{15... | collective-permute-start | bytes 3145736 | tf_op jit(solution)/shard_map/ppermute | solution.py:88
  216.9 35.0 %collective-permute-start.38 = (bf16[256,2048]{1,0:T(8,128)(2,1)}, bf16[256,2048]{1,0:T(8,128)(2,1)S(1)}, u32[]{:S(2)}, u32[]{:S(2)}) collective-permute-start(bf16[256,2048]{1,0:T(8,128)(2,1)} %get-tuple-element.410.refs_0_.refs_9_), channel_id=1, source_target_pairs={{1,3},{3,5},{5,7},{7,6},{6,4},{4,2},{2,0},{0,1},{9,11},{11,13},{13... | collective-permute-start | bytes 3145736 | tf_op jit(solution)/shard_map/ppermute | solution.py:85
  219.0 33.9 %collective-permute-start.39 = (bf16[256,2048]{1,0:T(8,128)(2,1)}, bf16[256,2048]{1,0:T(8,128)(2,1)S(1)}, u32[]{:S(2)}, u32[]{:S(2)}) collective-permute-start(bf16[256,2048]{1,0:T(8,128)(2,1)} %get-tuple-element.410.refs_0_.refs_9_), channel_id=1, source_target_pairs={{3,1},{5,3},{7,5},{6,7},{4,6},{2,4},{0,2},{1,0},{11,9},{13,11},{15... | collective-permute-start | bytes 3145736 | tf_op jit(solution)/shard_map/ppermute | solution.py:88
  253.0 26.1 %collective-permute-start.42 = (bf16[256,2048]{1,0:T(8,128)(2,1)S(1)}, bf16[256,2048]{1,0:T(8,128)(2,1)S(1)}, u32[]{:S(2)}, u32[]{:S(2)}) collective-permute-start(bf16[256,2048]{1,0:T(8,128)(2,1)S(1)} %collective-permute-done.38.refs_0_.refs_10_), channel_id=1, source_target_pairs={{1,3},{3,5},{5,7},{7,6},{6,4},{4,2},{2,0},{0,1},{9,11},{11,13},{13... | collective-permute-start | bytes 3145736 | tf_op jit(solution)/shard_map/ppermute | solution.py:85
  254.7 26.1 %collective-permute-start.43 = (bf16[256,2048]{1,0:T(8,128)(2,1)S(1)}, bf16[256,2048]{1,0:T(8,128)(2,1)S(1)}, u32[]{:S(2)}, u32[]{:S(2)}) collective-permute-start(bf16[256,2048]{1,0:T(8,128)(2,1)S(1)} %collective-permute-done.39.refs_1_.refs_11_), channel_id=1, source_target_pairs={{3,1},{5,3},{7,5},{6,7},{4,6},{2,4},{0,2},{1,0},{11,9},{13,11},{15... | collective-permute-start | bytes 3145736 | tf_op jit(solution)/shard_map/ppermute | solution.py:88
  255.0 44.7 %collective-permute-start.44 = (bf16[256,2048]{1,0:T(8,128)(2,1)}, bf16[256,2048]{1,0:T(8,128)(2,1)S(1)}, u32[]{:S(2)}, u32[]{:S(2)}) collective-permute-start(bf16[256,2048]{1,0:T(8,128)(2,1)} %collective-permute-done.40.refs_2_.refs_12_), channel_id=1, source_target_pairs={{1,3},{3,5},{5,7},{7,6},{6,4},{4,2},{2,0},{0,1},{9,11},{11,13},{13... | collective-permute-start | bytes 3145736 | tf_op jit(solution)/shard_map/ppermute | solution.py:85
  256.8 44.2 %collective-permute-start.45 = (bf16[256,2048]{1,0:T(8,128)(2,1)}, bf16[256,2048]{1,0:T(8,128)(2,1)}, u32[]{:S(2)}, u32[]{:S(2)}) collective-permute-start(bf16[256,2048]{1,0:T(8,128)(2,1)} %copy-done.20), channel_id=1, source_target_pairs={{3,1},{5,3},{7,5},{6,7},{4,6},{2,4},{0,2},{1,0},{11,9},{13,11},{15... | collective-permute-start | bytes 3145736 | tf_op jit(solution)/shard_map/ppermute | solution.py:88
  257.4 70.2 %collective-permute-start.50 = (bf16[2048,512]{1,0:T(8,128)(2,1)}, bf16[2048,512]{1,0:T(8,128)(2,1)}, u32[]{:S(2)}, u32[]{:S(2)}) collective-permute-start(bf16[2048,512]{1,0:T(8,128)(2,1)} %get-tuple-element.450.refs_4_), channel_id=1, source_target_pairs={{0,16},{8,24},{16,0},{24,8},{1,17},{9,25},{17,1},{25,9},{2,18},{10... | collective-permute-start | bytes 6291464 | tf_op jit(solution)/shard_map/ppermute | solution.py:103
  301.0 26.1 %collective-permute-start.46 = (bf16[256,2048]{1,0:T(8,128)(2,1)S(1)}, bf16[256,2048]{1,0:T(8,128)(2,1)S(1)}, u32[]{:S(2)}, u32[]{:S(2)}) collective-permute-start(bf16[256,2048]{1,0:T(8,128)(2,1)S(1)} %collective-permute-done.42.refs_0_.refs_12_), channel_id=1, source_target_pairs={{1,3},{3,5},{5,7},{7,6},{6,4},{4,2},{2,0},{0,1},{9,11},{11,13},{13... | collective-permute-start | bytes 3145736 | tf_op jit(solution)/shard_map/ppermute | solution.py:85
  301.5 26.1 %collective-permute-start.47 = (bf16[256,2048]{1,0:T(8,128)(2,1)S(1)}, bf16[256,2048]{1,0:T(8,128)(2,1)S(1)}, u32[]{:S(2)}, u32[]{:S(2)}) collective-permute-start(bf16[256,2048]{1,0:T(8,128)(2,1)S(1)} %collective-permute-done.43.refs_1_.refs_13_), channel_id=1, source_target_pairs={{3,1},{5,3},{7,5},{6,7},{4,6},{2,4},{0,2},{1,0},{11,9},{13,11},{15... | collective-permute-start | bytes 3145736 | tf_op jit(solution)/shard_map/ppermute | solution.py:88
  304.2 31.3 %collective-permute-start.48 = (bf16[128,2048]{1,0:T(8,128)(2,1)S(1)}, bf16[128,2048]{1,0:T(8,128)(2,1)S(1)}, u32[]{:S(2)}, u32[]{:S(2)}) collective-permute-start(bf16[128,2048]{1,0:T(8,128)(2,1)S(1)} %slice.139), channel_id=1, source_target_pairs={{1,3},{3,5},{5,7},{7,6},{6,4},{4,2},{2,0},{0,1},{9,11},{11,13},{13... | collective-permute-start | bytes 1572872 | tf_op jit(solution)/shard_map/ppermute | solution.py:85
  304.7 30.8 %collective-permute-start.49 = (bf16[128,2048]{1,0:T(8,128)(2,1)S(1)}, bf16[128,2048]{1,0:T(8,128)(2,1)S(1)}, u32[]{:S(2)}, u32[]{:S(2)}) collective-permute-start(bf16[128,2048]{1,0:T(8,128)(2,1)S(1)} %slice.140), channel_id=1, source_target_pairs={{3,1},{5,3},{7,5},{6,7},{4,6},{2,4},{0,2},{1,0},{11,9},{13,11},{15... | collective-permute-start | bytes 1572872 | tf_op jit(solution)/shard_map/ppermute | solution.py:88
  335.5 20.0 %collective-permute-start.51 = (bf16[128,2048]{1,0:T(8,128)(2,1)S(1)}, bf16[128,2048]{1,0:T(8,128)(2,1)S(1)}, u32[]{:S(2)}, u32[]{:S(2)}) collective-permute-start(bf16[128,2048]{1,0:T(8,128)(2,1)S(1)} %slice.137), channel_id=1, source_target_pairs={{1,3},{3,5},{5,7},{7,6},{6,4},{4,2},{2,0},{0,1},{9,11},{11,13},{13... | collective-permute-start | bytes 1572872 | tf_op jit(solution)/shard_map/ppermute | solution.py:85
  336.1 19.3 %collective-permute-start.52 = (bf16[128,2048]{1,0:T(8,128)(2,1)S(1)}, bf16[128,2048]{1,0:T(8,128)(2,1)S(1)}, u32[]{:S(2)}, u32[]{:S(2)}) collective-permute-start(bf16[128,2048]{1,0:T(8,128)(2,1)S(1)} %slice.138), channel_id=1, source_target_pairs={{3,1},{5,3},{7,5},{6,7},{4,6},{2,4},{0,2},{1,0},{11,9},{13,11},{15... | collective-permute-start | bytes 1572872 | tf_op jit(solution)/shard_map/ppermute | solution.py:88
  355.5 30.9 %collective-permute-start.55 = (bf16[2048,512]{1,0:T(8,128)(2,1)}, bf16[2048,512]{1,0:T(8,128)(2,1)S(1)}, u32[]{:S(2)}, u32[]{:S(2)}) collective-permute-start(bf16[2048,512]{1,0:T(8,128)(2,1)} %get-tuple-element.450.refs_4_), channel_id=1, source_target_pairs={{0,8},{8,0},{16,24},{24,16},{1,9},{9,1},{17,25},{25,17},{2,10},{10... | collective-permute-start | bytes 6291464 | tf_op jit(solution)/shard_map/ppermute | solution.py:103
  355.5 30.8 %collective-permute-start.56 = (bf16[2048,512]{1,0:T(8,128)(2,1)}, bf16[2048,512]{1,0:T(8,128)(2,1)S(1)}, u32[]{:S(2)}, u32[]{:S(2)}) collective-permute-start(bf16[2048,512]{1,0:T(8,128)(2,1)} %collective-permute-done.50.refs_5_), channel_id=1, source_target_pairs={{0,8},{8,0},{16,24},{24,16},{1,9},{9,1},{17,25},{25,17},{2,10},{10... | collective-permute-start | bytes 6291464 | tf_op jit(solution)/shard_map/ppermute | solution.py:103
  386.4 23.6 %collective-permute-start.57 = (bf16[256,2048]{1,0:T(8,128)(2,1)S(1)}, bf16[256,2048]{1,0:T(8,128)(2,1)S(1)}, u32[]{:S(2)}, u32[]{:S(2)}) collective-permute-start(bf16[256,2048]{1,0:T(8,128)(2,1)S(1)} %pad_maximum_fusion), channel_id=1, source_target_pairs={{3,1},{5,3},{7,5},{6,7},{4,6},{2,4},{0,2},{1,0},{11,9},{13,11},{15... | collective-permute-start | bytes 3145736 | tf_op jit(solution)/shard_map/ppermute | solution.py:88
  387.1 24.2 %collective-permute-start.58 = (bf16[256,2048]{1,0:T(8,128)(2,1)}, bf16[256,2048]{1,0:T(8,128)(2,1)}, u32[]{:S(2)}, u32[]{:S(2)}) collective-permute-start(bf16[256,2048]{1,0:T(8,128)(2,1)} %pad_maximum_fusion.1), channel_id=1, source_target_pairs={{1,3},{3,5},{5,7},{7,6},{6,4},{4,2},{2,0},{0,1},{9,11},{11,13},{13... | collective-permute-start | bytes 3145736 | tf_op jit(solution)/shard_map/ppermute | solution.py:85
  388.5 25.5 %collective-permute-start.61 = (bf16[256,2048]{1,0:T(8,128)(2,1)}, bf16[256,2048]{1,0:T(8,128)(2,1)}, u32[]{:S(2)}, u32[]{:S(2)}) collective-permute-start(bf16[256,2048]{1,0:T(8,128)(2,1)} %get-tuple-element.500.refs_8_), channel_id=1, source_target_pairs={{0,16},{8,24},{16,0},{24,8},{1,17},{9,25},{17,1},{25,9},{2,18},{10... | collective-permute-start | bytes 3145736 | tf_op jit(solution)/shard_map/ppermute | solution.py:103
  414.0 26.5 %collective-permute-start.62 = (bf16[256,2048]{1,0:T(8,128)(2,1)}, bf16[256,2048]{1,0:T(8,128)(2,1)}, u32[]{:S(2)}, u32[]{:S(2)}) collective-permute-start(bf16[256,2048]{1,0:T(8,128)(2,1)} %add_convert_fusion.11), channel_id=1, source_target_pairs={{3,1},{5,3},{7,5},{6,7},{4,6},{2,4},{0,2},{1,0},{11,9},{13,11},{15... | collective-permute-start | bytes 3145736 | tf_op jit(solution)/shard_map/ppermute | solution.py:88
  417.8 26.3 %collective-permute-start.63 = (bf16[256,2048]{1,0:T(8,128)(2,1)}, bf16[256,2048]{1,0:T(8,128)(2,1)S(1)}, u32[]{:S(2)}, u32[]{:S(2)}) collective-permute-start(bf16[256,2048]{1,0:T(8,128)(2,1)} %add_convert_fusion.10), channel_id=1, source_target_pairs={{1,3},{3,5},{5,7},{7,6},{6,4},{4,2},{2,0},{0,1},{9,11},{11,13},{13... | collective-permute-start | bytes 3145736 | tf_op jit(solution)/shard_map/ppermute | solution.py:85
  421.1 27.2 %collective-permute-start.59 = (bf16[128,2048]{1,0:T(8,128)(2,1)}, bf16[128,2048]{1,0:T(8,128)(2,1)}, u32[]{:S(2)}, u32[]{:S(2)}) collective-permute-start(bf16[128,2048]{1,0:T(8,128)(2,1)} %convert_element_type.155), channel_id=1, source_target_pairs={{3,1},{5,3},{7,5},{6,7},{4,6},{2,4},{0,2},{1,0},{11,9},{13,11},{15... | collective-permute-start | bytes 1572872 | tf_op jit(solution)/shard_map/ppermute | solution.py:88
  421.8 30.3 %collective-permute-start.60 = (bf16[128,2048]{1,0:T(8,128)(2,1)}, bf16[128,2048]{1,0:T(8,128)(2,1)}, u32[]{:S(2)}, u32[]{:S(2)}) collective-permute-start(bf16[128,2048]{1,0:T(8,128)(2,1)} %convert_element_type.156), channel_id=1, source_target_pairs={{1,3},{3,5},{5,7},{7,6},{6,4},{4,2},{2,0},{0,1},{9,11},{11,13},{13... | collective-permute-start | bytes 1572872 | tf_op jit(solution)/shard_map/ppermute | solution.py:85
  423.2 28.9 %collective-permute-start.65 = (bf16[256,2048]{1,0:T(8,128)(2,1)}, bf16[256,2048]{1,0:T(8,128)(2,1)}, u32[]{:S(2)}, u32[]{:S(2)}) collective-permute-start(bf16[256,2048]{1,0:T(8,128)(2,1)} %get-tuple-element.500.refs_8_), channel_id=1, source_target_pairs={{0,8},{8,0},{16,24},{24,16},{1,9},{9,1},{17,25},{25,17},{2,10},{10... | collective-permute-start | bytes 3145736 | tf_op jit(solution)/shard_map/ppermute | solution.py:103
  445.1 27.5 %collective-permute-start.69 = (bf16[688,1024]{1,0:T(8,128)(2,1)}, bf16[688,1024]{1,0:T(8,128)(2,1)S(1)}, u32[]{:S(2)}, u32[]{:S(2)}) collective-permute-start(bf16[688,1024]{1,0:T(8,128)(2,1)} %get-tuple-element.504), channel_id=1, source_target_pairs={{0,8},{8,0},{16,24},{24,16},{1,9},{9,1},{17,25},{25,17},{2,10},{10... | collective-permute-start | bytes 4227080 | tf_op jit(solution)/shard_map/ppermute | solution.py:103
  452.1 22.1 %collective-permute-start.67 = (bf16[256,2048]{1,0:T(8,128)(2,1)}, bf16[256,2048]{1,0:T(8,128)(2,1)}, u32[]{:S(2)}, u32[]{:S(2)}) collective-permute-start(bf16[256,2048]{1,0:T(8,128)(2,1)} %add_convert_fusion.9), channel_id=1, source_target_pairs={{3,1},{5,3},{7,5},{6,7},{4,6},{2,4},{0,2},{1,0},{11,9},{13,11},{15... | collective-permute-start | bytes 3145736 | tf_op jit(solution)/shard_map/ppermute | solution.py:88
  452.8 21.7 %collective-permute-start.68 = (bf16[256,2048]{1,0:T(8,128)(2,1)}, bf16[256,2048]{1,0:T(8,128)(2,1)}, u32[]{:S(2)}, u32[]{:S(2)}) collective-permute-start(bf16[256,2048]{1,0:T(8,128)(2,1)} %add_convert_fusion.8), channel_id=1, source_target_pairs={{1,3},{3,5},{5,7},{7,6},{6,4},{4,2},{2,0},{0,1},{9,11},{11,13},{13... | collective-permute-start | bytes 3145736 | tf_op jit(solution)/shard_map/ppermute | solution.py:85
  477.0 52.0 %collective-permute-start.71 = (bf16[256,2048]{1,0:T(8,128)(2,1)S(1)}, bf16[256,2048]{1,0:T(8,128)(2,1)S(1)}, u32[]{:S(2)}, u32[]{:S(2)}) collective-permute-start(bf16[256,2048]{1,0:T(8,128)(2,1)S(1)} %pad_maximum_fusion.2), channel_id=1, source_target_pairs={{3,1},{5,3},{7,5},{6,7},{4,6},{2,4},{0,2},{1,0},{11,9},{13,11},{15... | collective-permute-start | bytes 3145736 | tf_op jit(solution)/shard_map/ppermute | solution.py:88
  477.7 51.2 %collective-permute-start.72 = (bf16[256,2048]{1,0:T(8,128)(2,1)S(1)}, bf16[256,2048]{1,0:T(8,128)(2,1)}, u32[]{:S(2)}, u32[]{:S(2)}) collective-permute-start(bf16[256,2048]{1,0:T(8,128)(2,1)S(1)} %pad_maximum_fusion.3), channel_id=1, source_target_pairs={{1,3},{3,5},{5,7},{7,6},{6,4},{4,2},{2,0},{0,1},{9,11},{11,13},{13... | collective-permute-start | bytes 3145736 | tf_op jit(solution)/shard_map/ppermute | solution.py:85
  505.5 19.3 %collective-permute-start.78 = (bf16[256,256]{1,0:T(8,128)(2,1)}, bf16[256,256]{1,0:T(8,128)(2,1)S(1)}, u32[]{:S(2)}, u32[]{:S(2)}) collective-permute-start(bf16[256,256]{1,0:T(8,128)(2,1)} %get-tuple-element.545), channel_id=1, source_target_pairs={{0,5},{1,4},{2,7},{3,6},{4,1},{5,0},{6,3},{7,2},{8,13},{9,12},{10,... | collective-permute-start | bytes 393224 | tf_op jit(solution)/shard_map/ppermute | solution.py:103
  532.8 20.9 %collective-permute-start.84 = (bf16[256,2048]{1,0:T(8,128)(2,1)S(1)}, bf16[256,2048]{1,0:T(8,128)(2,1)S(1)}, u32[]{:S(2)}, u32[]{:S(2)}) collective-permute-start(bf16[256,2048]{1,0:T(8,128)(2,1)S(1)} %add_convert_fusion.7), channel_id=1, source_target_pairs={{3,1},{5,3},{7,5},{6,7},{4,6},{2,4},{0,2},{1,0},{11,9},{13,11},{15... | collective-permute-start | bytes 3145736 | tf_op jit(solution)/shard_map/ppermute | solution.py:88
  533.8 22.1 %collective-permute-start.85 = (bf16[256,2048]{1,0:T(8,128)(2,1)S(1)}, bf16[256,2048]{1,0:T(8,128)(2,1)S(1)}, u32[]{:S(2)}, u32[]{:S(2)}) collective-permute-start(bf16[256,2048]{1,0:T(8,128)(2,1)S(1)} %add_convert_fusion.6), channel_id=1, source_target_pairs={{1,3},{3,5},{5,7},{7,6},{6,4},{4,2},{2,0},{0,1},{9,11},{11,13},{13... | collective-permute-start | bytes 3145736 | tf_op jit(solution)/shard_map/ppermute | solution.py:85
  559.4 21.2 %collective-permute-start.94 = (bf16[344,1024]{1,0:T(8,128)(2,1)}, bf16[344,1024]{1,0:T(8,128)(2,1)S(1)}, u32[]{:S(2)}, u32[]{:S(2)}) collective-permute-start(bf16[344,1024]{1,0:T(8,128)(2,1)} %get-tuple-element.586), channel_id=1, source_target_pairs={{0,16},{8,24},{16,0},{24,8},{1,17},{9,25},{17,1},{25,9},{2,18},{10... | collective-permute-start | bytes 2113544 | tf_op jit(solution)/shard_map/ppermute | solution.py:103
  584.4 38.4 %collective-permute-start.96 = (bf16[256,2048]{1,0:T(8,128)(2,1)S(1)}, bf16[256,2048]{1,0:T(8,128)(2,1)S(1)}, u32[]{:S(2)}, u32[]{:S(2)}) collective-permute-start(bf16[256,2048]{1,0:T(8,128)(2,1)S(1)} %add_convert_fusion.4), channel_id=1, source_target_pairs={{1,3},{3,5},{5,7},{7,6},{6,4},{4,2},{2,0},{0,1},{9,11},{11,13},{13... | collective-permute-start | bytes 3145736 | tf_op jit(solution)/shard_map/ppermute | solution.py:85
  585.2 37.6 %collective-permute-start.95 = (bf16[256,2048]{1,0:T(8,128)(2,1)S(1)}, bf16[256,2048]{1,0:T(8,128)(2,1)S(1)}, u32[]{:S(2)}, u32[]{:S(2)}) collective-permute-start(bf16[256,2048]{1,0:T(8,128)(2,1)S(1)} %add_convert_fusion.5), channel_id=1, source_target_pairs={{3,1},{5,3},{7,5},{6,7},{4,6},{2,4},{0,2},{1,0},{11,9},{13,11},{15... | collective-permute-start | bytes 3145736 | tf_op jit(solution)/shard_map/ppermute | solution.py:88
  589.5 19.8 %collective-permute-start.105 = (bf16[256,512]{1,0:T(8,128)(2,1)}, bf16[256,512]{1,0:T(8,128)(2,1)S(1)}, u32[]{:S(2)}, u32[]{:S(2)}) collective-permute-start(bf16[256,512]{1,0:T(8,128)(2,1)} %get-tuple-element.597.refs_2_), channel_id=1, source_target_pairs={{0,8},{8,0},{16,24},{24,16},{1,9},{9,1},{17,25},{25,17},{2,10},{10... | collective-permute-start | bytes 786440 | tf_op jit(solution)/shard_map/ppermute | solution.py:103
  589.5 19.9 %collective-permute-start.106 = (bf16[256,512]{1,0:T(8,128)(2,1)}, bf16[256,512]{1,0:T(8,128)(2,1)S(1)}, u32[]{:S(2)}, u32[]{:S(2)}) collective-permute-start(bf16[256,512]{1,0:T(8,128)(2,1)} %get-tuple-element.598.refs_3_), channel_id=1, source_target_pairs={{0,24},{8,16},{16,8},{24,0},{1,25},{9,17},{17,9},{25,1},{2,26},{10... | collective-permute-start | bytes 786440 | tf_op jit(solution)/shard_map/ppermute | solution.py:103
  598.8 50.0 %collective-permute-start.117 = (bf16[688,1024]{1,0:T(8,128)(2,1)}, bf16[688,1024]{1,0:T(8,128)(2,1)S(1)}, u32[]{:S(2)}, u32[]{:S(2)}) collective-permute-start(bf16[688,1024]{1,0:T(8,128)(2,1)} %get-tuple-element.653), channel_id=1, source_target_pairs={{0,8},{8,0},{16,24},{24,16},{1,9},{9,1},{17,25},{25,17},{2,10},{10... | collective-permute-start | bytes 4227080 | tf_op jit(solution)/shard_map/ppermute | solution.py:103
  626.8 27.9 %collective-permute-start.111 = (bf16[688,1024]{1,0:T(8,128)(2,1)}, bf16[688,1024]{1,0:T(8,128)(2,1)S(1)}, u32[]{:S(2)}, u32[]{:S(2)}) collective-permute-start(bf16[688,1024]{1,0:T(8,128)(2,1)} %chip_sum.3.mine), channel_id=1, source_target_pairs={{0,8},{8,0},{16,24},{24,16},{1,9},{9,1},{17,25},{25,17},{2,10},{10... | collective-permute-start | bytes 4227080 | tf_op jit(solution)/shard_map/ppermute | solution.py:103
  636.7 66.7 %collective-permute-start.114 = (bf16[688,1024]{1,0:T(8,128)(2,1)S(1)}, bf16[688,1024]{1,0:T(8,128)(2,1)S(1)}, u32[]{:S(2)}, u32[]{:S(2)}) collective-permute-start(bf16[688,1024]{1,0:T(8,128)(2,1)S(1)} %copy-done.17), channel_id=1, source_target_pairs={{0,8},{8,0},{16,24},{24,16},{1,9},{9,1},{17,25},{25,17},{2,10},{10... | collective-permute-start | bytes 4227080 | tf_op jit(solution)/shard_map/ppermute | solution.py:103
  649.5 29.2 %collective-permute-start.110 = (bf16[544,512]{1,0:T(8,128)(2,1)}, bf16[544,512]{1,0:T(8,128)(2,1)}, u32[]{:S(2)}, u32[]{:S(2)}) collective-permute-start(bf16[544,512]{1,0:T(8,128)(2,1)} %pad_maximum_fusion.6), channel_id=1, source_target_pairs={{1,3},{3,5},{5,7},{7,6},{6,4},{4,2},{2,0},{0,1},{9,11},{11,13},{13... | collective-permute-start | bytes 1671176 | tf_op jit(solution)/shard_map/ppermute | solution.py:85
  652.2 22.5 %collective-permute-start.101 = (bf16[256,512]{1,0:T(8,128)(2,1)}, bf16[256,512]{1,0:T(8,128)(2,1)S(1)}, u32[]{:S(2)}, u32[]{:S(2)}) collective-permute-start(bf16[256,512]{1,0:T(8,128)(2,1)} %get-tuple-element.616), channel_id=1, source_target_pairs={{0,5},{1,4},{2,7},{3,6},{4,1},{5,0},{6,3},{7,2},{8,13},{9,12},{10,... | collective-permute-start | bytes 786440 | tf_op jit(solution)/shard_map/ppermute | solution.py:103
  654.7 44.5 %collective-permute-start.118 = (bf16[344,1024]{1,0:T(8,128)(2,1)}, bf16[344,1024]{1,0:T(8,128)(2,1)}, u32[]{:S(2)}, u32[]{:S(2)}) collective-permute-start(bf16[344,1024]{1,0:T(8,128)(2,1)} %get-tuple-element.654), channel_id=1, source_target_pairs={{0,16},{8,24},{16,0},{24,8},{1,17},{9,25},{17,1},{25,9},{2,18},{10... | collective-permute-start | bytes 2113544 | tf_op jit(solution)/shard_map/ppermute | solution.py:103
  662.2 37.0 %collective-permute-start.119 = (bf16[344,1024]{1,0:T(8,128)(2,1)}, bf16[344,1024]{1,0:T(8,128)(2,1)S(1)}, u32[]{:S(2)}, u32[]{:S(2)}) collective-permute-start(bf16[344,1024]{1,0:T(8,128)(2,1)} %get-tuple-element.655), channel_id=1, source_target_pairs={{0,16},{8,24},{16,0},{24,8},{1,17},{9,25},{17,1},{25,9},{2,18},{10... | collective-permute-start | bytes 2113544 | tf_op jit(solution)/shard_map/ppermute | solution.py:103
  690.5 18.7 %collective-permute-start.112 = (bf16[544,512]{1,0:T(8,128)(2,1)S(1)}, bf16[544,512]{1,0:T(8,128)(2,1)S(1)}, u32[]{:S(2)}, u32[]{:S(2)}) collective-permute-start(bf16[544,512]{1,0:T(8,128)(2,1)S(1)} %add_convert_fusion.16), channel_id=1, source_target_pairs={{3,1},{5,3},{7,5},{6,7},{4,6},{2,4},{0,2},{1,0},{11,9},{13,11},{15... | collective-permute-start | bytes 1671176 | tf_op jit(solution)/shard_map/ppermute | solution.py:88
  703.2 23.2 %collective-permute-start.120 = (bf16[688,1024]{1,0:T(8,128)(2,1)}, bf16[688,1024]{1,0:T(8,128)(2,1)S(1)}, u32[]{:S(2)}, u32[]{:S(2)}) collective-permute-start(bf16[688,1024]{1,0:T(8,128)(2,1)} %chip_sum.5.mine), channel_id=1, source_target_pairs={{0,8},{8,0},{16,24},{24,16},{1,9},{9,1},{17,25},{25,17},{2,10},{10... | collective-permute-start | bytes 4227080 | tf_op jit(solution)/shard_map/ppermute | solution.py:103
  (191 other events, 2471.9 us)
